TPU v7x, 32 devices: a whole 2x2x4 slice. The times are simulated.
32 devices in a mesh: dp: 4 (over x, core), row: 2 (over y), col: 4 (over z).
Axes of the slice: x: 2, y: 2, z: 4, core: 2. Of those that a mesh axis runs over, the one named last changes fastest.
Arguments:
- tokens: bfloat16 [2, 5120, 1024], P(None, ('dp', 'row'), 'col'), may hold values from -110 to 110
- segment_ids: int32 [2, 5120], P(None, 'dp'), may hold values from 0 to 2, as said below
- prompt_reach: int32 [2, 5120], P(None, 'dp'), may hold values from 0 to 1024, as said below
- attn_gain_1: float32 [1024], P('col'), may hold values from 0.5 to 1.5
- query_weight_1: bfloat16 [1024, 1024], P('row', 'col'), may hold values from -0.1875 to 0.1875
- key_weight_1: bfloat16 [1024, 1024], P('row', 'col'), may hold values from -0.1875 to 0.1875
- value_weight_1: bfloat16 [1024, 1024], P('row', 'col'), may hold values from -0.1875 to 0.1875
- out_weight_1: bfloat16 [1024, 1024], P('col', 'row'), may hold values from -3 to 3
- ffn_gain_1: float32 [1024], P('col'), may hold values from 0.5 to 1.5
- gate_weight_1: bfloat16 [1024, 2816], P('row', 'col'), may hold values from -0.1875 to 0.1875
- up_weight_1: bfloat16 [1024, 2816], P('row', 'col'), may hold values from -0.1875 to 0.1875
- down_weight_1: bfloat16 [2816, 1024], P('col', 'row'), may hold values from -0.109375 to 0.109375
- attn_gain_2: float32 [1024], P('col'), may hold values from 0.5 to 1.5
- query_weight_2: bfloat16 [1024, 1024], P('row', 'col'), may hold values from -0.1875 to 0.1875
- key_weight_2: bfloat16 [1024, 1024], P('row', 'col'), may hold values from -0.1875 to 0.1875
- value_weight_2: bfloat16 [1024, 1024], P('row', 'col'), may hold values from -0.1875 to 0.1875
- out_weight_2: bfloat16 [1024, 1024], P('col', 'row'), may hold values from -3 to 3
- ffn_gain_2: float32 [1024], P('col'), may hold values from 0.5 to 1.5
- gate_weight_2: bfloat16 [1024, 2816], P('row', 'col'), may hold values from -0.1875 to 0.1875
- up_weight_2: bfloat16 [1024, 2816], P('row', 'col'), may hold values from -0.1875 to 0.1875
- down_weight_2: bfloat16 [2816, 1024], P('col', 'row'), may hold values from -0.109375 to 0.109375
- out_grad: bfloat16 [2, 5120, 1024], P(None, ('dp', 'row'), 'col'), may hold values from -6 to 6
Outputs:
- output: bfloat16 [2, 5120, 1024], P(None, ('dp', 'row'), 'col')
- input_grad: float32 [2, 5120, 1024], P(None, ('dp', 'row'), 'col')
- grad_attn_gain_1: float32 [1024], P('col')
- grad_query_1: float32 [1024, 1024], P('row', 'col')
- grad_key_1: float32 [1024, 1024], P('row', 'col')
- grad_value_1: float32 [1024, 1024], P('row', 'col')
- grad_out_1: float32 [1024, 1024], P('col', 'row')
- grad_ffn_gain_1: float32 [1024], P('col')
- grad_gate_1: float32 [1024, 2816], P('row', 'col')
- grad_up_1: float32 [1024, 2816], P('row', 'col')
- grad_down_1: float32 [2816, 1024], P('col', 'row')
- grad_attn_gain_2: float32 [1024], P('col')
- grad_query_2: float32 [1024, 1024], P('row', 'col')
- grad_key_2: float32 [1024, 1024], P('row', 'col')
- grad_value_2: float32 [1024, 1024], P('row', 'col')
- grad_out_2: float32 [1024, 1024], P('col', 'row')
- grad_ffn_gain_2: float32 [1024], P('col')
- grad_gate_2: float32 [1024, 2816], P('row', 'col')
- grad_up_2: float32 [1024, 2816], P('row', 'col')
- grad_down_2: float32 [2816, 1024], P('col', 'row')
Inputs may be any that keep to these rules, and one draw needn't show every extreme that they name: `segment_ids`: in each group the first 1024 tokens are segment 0, the prompt; then come 2 continuations numbered 1 to 2 in order, of 64 to 192 tokens each, 256 tokens together, one of exactly the largest length in every group. `prompt_reach`: 0 on prompt tokens; one value for all tokens of a continuation, 512 or more; in every group some continuation has 1024.
All inputs are finite; a program needn't handle non-finite values.
Results may differ from a plain program's by a relative error of at most 0.033.
Values may be sent and summed in bfloat16 or wider, within the bound.
No kernel may reach another device: no remote copies, remote signals or barrier semaphores. Data moves between devices by JAX's collectives and lax.ppermute only.
A program may use at most 320 MiB of HBM per device.

v0:
```python
import jax
import jax.numpy as jnp
from jax import lax
from jax.sharding import PartitionSpec as P

D = 1024
HEAD_DIM = 64
BRANCHES = 2


norm_eps = 1e-06
rope_base = 10000.0


def token_positions(segments, reach, seg_count):
    seg_labels = jnp.arange(seg_count, dtype=jnp.int32)
    onehot = (segments[:, None] == seg_labels[None, :]).astype(jnp.int32)
    seg_sizes = jnp.sum(onehot, axis=0)
    seg_starts = jnp.cumsum(seg_sizes) - seg_sizes
    first_token = jnp.sum(onehot * seg_starts[None, :], axis=1)
    return jnp.arange(segments.shape[0], dtype=jnp.int32) - first_token + reach


def rope_tables(position, head_dim):
    half_dim = head_dim // 2
    inverse = rope_base ** (-(jnp.arange(half_dim, dtype=jnp.float32) * 2.0) / head_dim)
    angles = position.astype(jnp.float32)[:, None] * inverse[None, :]
    return (jnp.cos(angles)[:, None, :], jnp.sin(angles)[:, None, :])


def rotate(values, cosine, sine):
    half_dim = values.shape[-1] // 2
    first_half = values[..., :half_dim]
    second_half = values[..., half_dim:]
    return jnp.concatenate(
        [first_half * cosine - second_half * sine, second_half * cosine + first_half * sine],
        axis=-1,
    )


def product(left, right):
    return jnp.dot(left, right, preferred_element_type=jnp.float32)


def outer_sum(left, right):
    return lax.dot_general(
        left, right, (((0,), (0,)), ((), ())), preferred_element_type=jnp.float32
    )


def times_transposed(left, right):
    return lax.dot_general(
        left, right, (((1,), (1,)), ((), ())), preferred_element_type=jnp.float32
    )


def normalize(residual, gain):
    squares = lax.psum(jnp.sum(residual * residual, axis=1), "col")
    factor = lax.rsqrt(squares / D + norm_eps)
    normed_local = (residual * factor[:, None] * gain[None, :]).astype(jnp.bfloat16)
    normed = lax.all_gather(normed_local, "col", axis=1, tiled=True)
    return (normed, factor)


def normalize_back(partial_value, residual, factor, gain):
    grad_normed = lax.psum_scatter(
        partial_value.astype(jnp.bfloat16), "col", scatter_dimension=1, tiled=True
    ).astype(jnp.float32)
    unit_rows = residual * factor[:, None]
    gain_grad = jnp.sum(grad_normed * unit_rows, axis=0)
    grad_unit = grad_normed * gain[None, :]
    inner_sum = lax.psum(jnp.sum(grad_unit * unit_rows, axis=1), "col")
    grad_residual = factor[:, None] * (grad_unit - unit_rows * (inner_sum / D)[:, None])
    return (grad_residual, gain_grad)


def branch_sum(partial_value):
    return lax.psum_scatter(
        partial_value.astype(jnp.bfloat16), "col", scatter_dimension=1, tiled=True
    ).astype(jnp.float32)


def branch_grad(gradient):
    return lax.all_gather(gradient.astype(jnp.bfloat16), "col", axis=1, tiled=True)


def masked_scores(query_block, keys_all, query_index, query_seg, query_reach, segments):
    scores = jnp.einsum(
        "qhd,khd->hqk", query_block, keys_all, preferred_element_type=jnp.float32
    ) * HEAD_DIM ** (-0.5)
    key_index = jnp.arange(segments.shape[0], dtype=jnp.int32)
    allowed = (query_seg[:, None] == segments[None, :]) & (
        key_index[None, :] <= query_index[:, None]
    ) | (key_index[None, :] < query_reach[:, None])
    return jnp.where(allowed[None], scores, -1e30)


def body(
    tokens,
    segment_ids,
    prompt_reach,
    attn_gain_1,
    query_weight_1,
    key_weight_1,
    value_weight_1,
    out_weight_1,
    ffn_gain_1,
    gate_weight_1,
    up_weight_1,
    down_weight_1,
    attn_gain_2,
    query_weight_2,
    key_weight_2,
    value_weight_2,
    out_weight_2,
    ffn_gain_2,
    gate_weight_2,
    up_weight_2,
    down_weight_2,
    out_grad,
):
    row_count = lax.axis_size("row")
    row_index = lax.axis_index("row")
    tokens_run, grads_run, segs_run, reach_run = (tokens, out_grad, segment_ids, prompt_reach)
    local_rows = tokens_run.shape[1]
    local_width = query_weight_1.shape[1]
    heads_local = local_width // HEAD_DIM
    block_rows = local_rows // max(1, local_rows // 512)
    block_count = local_rows // block_rows
    first_row = row_index * local_rows
    attn_scale = HEAD_DIM ** (-0.5)
    gathered = (
        lax.all_gather(query_weight_1, "row", axis=0, tiled=True),
        lax.all_gather(key_weight_1, "row", axis=0, tiled=True),
        lax.all_gather(value_weight_1, "row", axis=0, tiled=True),
        lax.all_gather(out_weight_1, "row", axis=1, tiled=True),
        lax.all_gather(gate_weight_1, "row", axis=0, tiled=True),
        lax.all_gather(up_weight_1, "row", axis=0, tiled=True),
        lax.all_gather(down_weight_1, "row", axis=1, tiled=True),
        lax.all_gather(query_weight_2, "row", axis=0, tiled=True),
        lax.all_gather(key_weight_2, "row", axis=0, tiled=True),
        lax.all_gather(value_weight_2, "row", axis=0, tiled=True),
        lax.all_gather(out_weight_2, "row", axis=1, tiled=True),
        lax.all_gather(gate_weight_2, "row", axis=0, tiled=True),
        lax.all_gather(up_weight_2, "row", axis=0, tiled=True),
        lax.all_gather(down_weight_2, "row", axis=1, tiled=True),
    )
    layer_one = (attn_gain_1,) + tuple(gathered[0:4]) + (ffn_gain_1,) + tuple(gathered[4:7])
    layer_two = (attn_gain_2,) + tuple(gathered[7:11]) + (ffn_gain_2,) + tuple(gathered[11:14])

    def split_blocks(matrix):
        return matrix.reshape((block_count, block_rows) + matrix.shape[1:])

    def layer_forward(residual, weight_set, first_values, context):
        cosine, sine, query_index, query_seg, query_reach, segments = context
        attn_gain, w_query, w_key, w_value, w_out, ffn_gain, w_gate, w_up, w_down = weight_set
        attn_input = residual
        normed, attn_factor = normalize(residual, attn_gain)
        queries = rotate(
            product(normed, w_query).reshape(local_rows, heads_local, HEAD_DIM), cosine, sine
        ).astype(jnp.bfloat16)
        key_local = rotate(
            product(normed, w_key).reshape(local_rows, heads_local, HEAD_DIM), cosine, sine
        ).astype(jnp.bfloat16)
        raw_values = product(normed, w_value)
        if first_values is None:
            values = raw_values.astype(jnp.bfloat16)
        else:
            values = (0.5 * raw_values + 0.5 * first_values.astype(jnp.float32)).astype(
                jnp.bfloat16
            )
        keys_all, values_all = (
            lax.all_gather(key_local.reshape(local_rows, local_width), "row", axis=0, tiled=True),
            lax.all_gather(values, "row", axis=0, tiled=True),
        )
        keys_all = keys_all.reshape(-1, heads_local, HEAD_DIM)
        values_all = values_all.reshape(-1, heads_local, HEAD_DIM)

        def forward_block(block_item):
            query_block, block_index, block_seg, block_reach = block_item
            scores = masked_scores(
                query_block, keys_all, block_index, block_seg, block_reach, segments
            )
            peak_score = jnp.max(scores, axis=2, keepdims=True)
            exp_total = jnp.sum(jnp.exp(scores - peak_score), axis=2, keepdims=True)
            log_total = peak_score + jnp.log(exp_total)
            probability = jnp.exp(scores - log_total).astype(jnp.bfloat16)
            block_out = jnp.einsum(
                "hqk,khd->qhd", probability, values_all, preferred_element_type=jnp.float32
            )
            return (block_out.astype(jnp.bfloat16), log_total[..., 0])

        mixture, log_totals = lax.map(
            forward_block,
            (
                split_blocks(queries),
                split_blocks(query_index),
                split_blocks(query_seg),
                split_blocks(query_reach),
            ),
        )
        mixture = mixture.reshape(local_rows, local_width)
        residual = residual + branch_sum(product(mixture, w_out))
        ffn_input = residual
        normed_ffn, ffn_factor = normalize(residual, ffn_gain)
        gate_act = product(normed_ffn, w_gate)
        up_act = product(normed_ffn, w_up)
        hidden = (jax.nn.silu(gate_act) * up_act).astype(jnp.bfloat16)
        residual = residual + branch_sum(product(hidden, w_down))
        saved = (
            attn_input,
            attn_factor,
            normed,
            queries,
            keys_all,
            values_all,
            mixture,
            log_totals,
            ffn_input,
            ffn_factor,
            normed_ffn,
            gate_act,
            up_act,
            hidden,
        )
        return (residual, values, saved)

    def layer_backward(gradient, weight_set, saved, context, value_extra, is_second):
        cosine, sine, query_index, query_seg, query_reach, segments = context
        attn_gain, w_query, w_key, w_value, w_out, ffn_gain, w_gate, w_up, w_down = weight_set
        (
            attn_input,
            attn_factor,
            normed,
            queries,
            keys_all,
            values_all,
            mixture,
            log_totals,
            ffn_input,
            ffn_factor,
            normed_ffn,
            gate_act,
            up_act,
            hidden,
        ) = saved
        grad_full = branch_grad(gradient)
        grad_w_down = outer_sum(hidden, grad_full)
        grad_hidden = times_transposed(grad_full, w_down)
        sigmoid_gate = jax.nn.sigmoid(gate_act)
        grad_gate = (
            grad_hidden * up_act * sigmoid_gate * (1.0 + gate_act * (1.0 - sigmoid_gate))
        ).astype(jnp.bfloat16)
        grad_up = (grad_hidden * gate_act * sigmoid_gate).astype(jnp.bfloat16)
        grad_w_gate = outer_sum(normed_ffn, grad_gate)
        grad_w_up = outer_sum(normed_ffn, grad_up)
        partial_value = times_transposed(grad_gate, w_gate) + times_transposed(grad_up, w_up)
        grad_norm, grad_ffn_gain = normalize_back(partial_value, ffn_input, ffn_factor, ffn_gain)
        gradient = gradient + grad_norm
        grad_full = branch_grad(gradient)
        grad_w_out = outer_sum(mixture, grad_full)
        grad_mixture = times_transposed(grad_full, w_out).astype(jnp.bfloat16)

        def backward_block(carried_in, block_item):
            key_grad, value_grad = carried_in
            query_block, grad_block, total_block, block_index, block_seg, block_reach = block_item
            scores = masked_scores(
                query_block, keys_all, block_index, block_seg, block_reach, segments
            )
            probability = jnp.exp(scores - total_block[..., None])
            grad_probability = jnp.einsum(
                "qhd,khd->hqk", grad_block, values_all, preferred_element_type=jnp.float32
            )
            inner_sum = jnp.sum(probability * grad_probability, axis=2, keepdims=True)
            grad_scores = (probability * (grad_probability - inner_sum)).astype(jnp.bfloat16)
            query_grad = (
                jnp.einsum(
                    "hqk,khd->qhd", grad_scores, keys_all, preferred_element_type=jnp.float32
                )
                * attn_scale
            )
            key_grad = (
                key_grad
                + jnp.einsum(
                    "hqk,qhd->khd", grad_scores, query_block, preferred_element_type=jnp.float32
                )
                * attn_scale
            )
            value_grad = value_grad + jnp.einsum(
                "hqk,qhd->khd",
                probability.astype(jnp.bfloat16),
                grad_block,
                preferred_element_type=jnp.float32,
            )
            return ((key_grad, value_grad), query_grad)

        group_len = keys_all.shape[0]
        empty_grad = jnp.zeros((group_len, heads_local, HEAD_DIM), jnp.float32)
        (key_grad, value_grad), query_grad = lax.scan(
            backward_block,
            (empty_grad, empty_grad),
            (
                split_blocks(queries),
                split_blocks(grad_mixture.reshape(local_rows, heads_local, HEAD_DIM)),
                log_totals,
                split_blocks(query_index),
                split_blocks(query_seg),
                split_blocks(query_reach),
            ),
        )
        key_shard, value_shard = (
            lax.psum_scatter(
                key_grad.reshape(group_len, local_width).astype(jnp.bfloat16),
                "row",
                scatter_dimension=0,
                tiled=True,
            ).astype(jnp.float32),
            lax.psum_scatter(
                value_grad.reshape(group_len, local_width).astype(jnp.bfloat16),
                "row",
                scatter_dimension=0,
                tiled=True,
            ).astype(jnp.float32),
        )
        grad_query = (
            rotate(query_grad.reshape(local_rows, heads_local, HEAD_DIM), cosine, -sine)
            .reshape(local_rows, local_width)
            .astype(jnp.bfloat16)
        )
        grad_key = (
            rotate(key_shard.reshape(local_rows, heads_local, HEAD_DIM), cosine, -sine)
            .reshape(local_rows, local_width)
            .astype(jnp.bfloat16)
        )
        if is_second:
            grad_mix = value_shard.astype(jnp.bfloat16).astype(jnp.float32)
            grad_value = (0.5 * grad_mix).astype(jnp.bfloat16)
            passed_back = 0.5 * grad_mix
        else:
            grad_value = (value_shard + value_extra).astype(jnp.bfloat16)
            passed_back = value_extra
        grad_w_query = outer_sum(normed, grad_query)
        grad_w_key = outer_sum(normed, grad_key)
        grad_w_value = outer_sum(normed, grad_value)
        partial_value = (
            times_transposed(grad_query, w_query)
            + times_transposed(grad_key, w_key)
            + times_transposed(grad_value, w_value)
        )
        grad_norm, grad_attn_gain = normalize_back(
            partial_value, attn_input, attn_factor, attn_gain
        )
        gradient = gradient + grad_norm
        grad_set = (
            grad_attn_gain,
            grad_w_query,
            grad_w_key,
            grad_w_value,
            grad_w_out,
            grad_ffn_gain,
            grad_w_gate,
            grad_w_up,
            grad_w_down,
        )
        return (gradient, grad_set, passed_back)

    def micro_step(totals, micro_item):
        tokens_in, segments, reach, cotangent = micro_item
        positions = token_positions(segments, reach, BRANCHES + 1)
        local_positions = lax.dynamic_slice_in_dim(positions, first_row, local_rows, 0)
        cosine, sine = rope_tables(local_positions, HEAD_DIM)
        query_index = first_row + jnp.arange(local_rows, dtype=jnp.int32)
        query_seg = lax.dynamic_slice_in_dim(segments, first_row, local_rows, 0)
        query_reach = lax.dynamic_slice_in_dim(reach, first_row, local_rows, 0)
        context = (cosine, sine, query_index, query_seg, query_reach, segments)
        residual = tokens_in.astype(jnp.float32)
        residual, first_values, saved_one = layer_forward(residual, layer_one, None, context)
        residual, unused_values, saved_two = layer_forward(
            residual, layer_two, first_values, context
        )
        gradient = cotangent.astype(jnp.float32)
        gradient, grads_two, passed_back = layer_backward(
            gradient, layer_two, saved_two, context, None, True
        )
        gradient, grads_one, unused_extra = layer_backward(
            gradient, layer_one, saved_one, context, passed_back, False
        )
        totals = tuple(
            (left_term + right_term for left_term, right_term in zip(totals, grads_one + grads_two))
        )
        return (totals, (residual.astype(jnp.bfloat16), gradient))

    zeros_set = tuple((jnp.zeros(matrix.shape, jnp.float32) for matrix in layer_one + layer_two))
    totals, (outputs, input_grads) = lax.scan(
        micro_step, zeros_set, (tokens_run, segs_run, reach_run, grads_run)
    )
    stacks = [
        jnp.broadcast_to(totals[slot_index][None, :], (row_count, totals[slot_index].shape[0]))
        for slot_index in (0, 5, 9, 14)
    ]
    reduced = (
        lax.psum_scatter(
            totals[1].astype(jnp.bfloat16), "row", scatter_dimension=0, tiled=True
        ).astype(jnp.float32),
        lax.psum_scatter(
            totals[2].astype(jnp.bfloat16), "row", scatter_dimension=0, tiled=True
        ).astype(jnp.float32),
        lax.psum_scatter(
            totals[3].astype(jnp.bfloat16), "row", scatter_dimension=0, tiled=True
        ).astype(jnp.float32),
        lax.psum_scatter(
            totals[4].astype(jnp.bfloat16), "row", scatter_dimension=1, tiled=True
        ).astype(jnp.float32),
        lax.psum_scatter(
            totals[6].astype(jnp.bfloat16), "row", scatter_dimension=0, tiled=True
        ).astype(jnp.float32),
        lax.psum_scatter(
            totals[7].astype(jnp.bfloat16), "row", scatter_dimension=0, tiled=True
        ).astype(jnp.float32),
        lax.psum_scatter(
            totals[8].astype(jnp.bfloat16), "row", scatter_dimension=1, tiled=True
        ).astype(jnp.float32),
        lax.psum_scatter(
            totals[10].astype(jnp.bfloat16), "row", scatter_dimension=0, tiled=True
        ).astype(jnp.float32),
        lax.psum_scatter(
            totals[11].astype(jnp.bfloat16), "row", scatter_dimension=0, tiled=True
        ).astype(jnp.float32),
        lax.psum_scatter(
            totals[12].astype(jnp.bfloat16), "row", scatter_dimension=0, tiled=True
        ).astype(jnp.float32),
        lax.psum_scatter(
            totals[13].astype(jnp.bfloat16), "row", scatter_dimension=1, tiled=True
        ).astype(jnp.float32),
        lax.psum_scatter(
            totals[15].astype(jnp.bfloat16), "row", scatter_dimension=0, tiled=True
        ).astype(jnp.float32),
        lax.psum_scatter(
            totals[16].astype(jnp.bfloat16), "row", scatter_dimension=0, tiled=True
        ).astype(jnp.float32),
        lax.psum_scatter(
            totals[17].astype(jnp.bfloat16), "row", scatter_dimension=1, tiled=True
        ).astype(jnp.float32),
        lax.psum_scatter(
            stacks[0].astype(jnp.bfloat16), "row", scatter_dimension=0, tiled=True
        ).astype(jnp.float32),
        lax.psum_scatter(
            stacks[1].astype(jnp.bfloat16), "row", scatter_dimension=0, tiled=True
        ).astype(jnp.float32),
        lax.psum_scatter(
            stacks[2].astype(jnp.bfloat16), "row", scatter_dimension=0, tiled=True
        ).astype(jnp.float32),
        lax.psum_scatter(
            stacks[3].astype(jnp.bfloat16), "row", scatter_dimension=0, tiled=True
        ).astype(jnp.float32),
    )
    summed = (
        lax.psum(reduced[0].astype(jnp.bfloat16), "dp").astype(jnp.float32),
        lax.psum(reduced[1].astype(jnp.bfloat16), "dp").astype(jnp.float32),
        lax.psum(reduced[2].astype(jnp.bfloat16), "dp").astype(jnp.float32),
        lax.psum(reduced[3].astype(jnp.bfloat16), "dp").astype(jnp.float32),
        lax.psum(reduced[4].astype(jnp.bfloat16), "dp").astype(jnp.float32),
        lax.psum(reduced[5].astype(jnp.bfloat16), "dp").astype(jnp.float32),
        lax.psum(reduced[6].astype(jnp.bfloat16), "dp").astype(jnp.float32),
        lax.psum(reduced[7].astype(jnp.bfloat16), "dp").astype(jnp.float32),
        lax.psum(reduced[8].astype(jnp.bfloat16), "dp").astype(jnp.float32),
        lax.psum(reduced[9].astype(jnp.bfloat16), "dp").astype(jnp.float32),
        lax.psum(reduced[10].astype(jnp.bfloat16), "dp").astype(jnp.float32),
        lax.psum(reduced[11].astype(jnp.bfloat16), "dp").astype(jnp.float32),
        lax.psum(reduced[12].astype(jnp.bfloat16), "dp").astype(jnp.float32),
        lax.psum(reduced[13].astype(jnp.bfloat16), "dp").astype(jnp.float32),
        lax.psum(reduced[14].astype(jnp.bfloat16), "dp").astype(jnp.float32),
        lax.psum(reduced[15].astype(jnp.bfloat16), "dp").astype(jnp.float32),
        lax.psum(reduced[16].astype(jnp.bfloat16), "dp").astype(jnp.float32),
        lax.psum(reduced[17].astype(jnp.bfloat16), "dp").astype(jnp.float32),
    )
    return (
        outputs,
        input_grads,
        summed[14][0],
        summed[0],
        summed[1],
        summed[2],
        summed[3],
        summed[15][0],
        summed[4],
        summed[5],
        summed[6],
        summed[16][0],
        summed[7],
        summed[8],
        summed[9],
        summed[10],
        summed[17][0],
        summed[11],
        summed[12],
        summed[13],
    )


def solution(mesh):
    placed = (
        P(None, ("dp", "row"), "col"),
        P(None, "dp"),
        P(None, "dp"),
        P("col"),
        P("row", "col"),
        P("row", "col"),
        P("row", "col"),
        P("col", "row"),
        P("col"),
        P("row", "col"),
        P("row", "col"),
        P("col", "row"),
        P("col"),
        P("row", "col"),
        P("row", "col"),
        P("row", "col"),
        P("col", "row"),
        P("col"),
        P("row", "col"),
        P("row", "col"),
        P("col", "row"),
        P(None, ("dp", "row"), "col"),
    )
    return jax.shard_map(
        body,
        mesh=mesh,
        in_specs=placed,
        out_specs=(
            P(None, ("dp", "row"), "col"),
            P(None, ("dp", "row"), "col"),
            P("col"),
            P("row", "col"),
            P("row", "col"),
            P("row", "col"),
            P("col", "row"),
            P("col"),
            P("row", "col"),
            P("row", "col"),
            P("col", "row"),
            P("col"),
            P("row", "col"),
            P("row", "col"),
            P("row", "col"),
            P("col", "row"),
            P("col"),
            P("row", "col"),
            P("row", "col"),
            P("col", "row"),
        ),
        check_vma=False,
    )
```

profile of v0, /device:TPU:0, one launch (start us, length us, event | category | flops | bytes accessed | tf_op | source)
XLA Modules:
  0.0 2366.4 jit_solution(16276068852788450131)
XLA Ops:
  15.1 14.7 all_gather.127
  29.9 15.1 all_gather.126
  118.7 29.7 %all-gather.21.cloned.1.call-done = bf16[1024,704]{1,0:T(8,128)(2,1)} async-done(((bf16[512,704]{1,0:T(8,128)(2,1)}), bf16[1024,704]{1,0:T(8,128)(2,1)}) %all-gather.21.cloned.1.call-update) | async-done | bytes 1441808 | tf_op jit(solution)/shard_map/all_gather | solution.py:138
  148.4 28.6 %all-gather.29.cloned.1.call-done = bf16[1024,704]{1,0:T(8,128)(2,1)} async-done(((bf16[512,704]{1,0:T(8,128)(2,1)}), bf16[1024,704]{1,0:T(8,128)(2,1)}) %all-gather.29.cloned.1.call-update) | async-done | bytes 1441808 | tf_op jit(solution)/shard_map/all_gather | solution.py:144
  177.0 28.6 %all-gather.27.cloned.1.call-done = bf16[1024,704]{1,0:T(8,128)(2,1)} async-done(((bf16[512,704]{1,0:T(8,128)(2,1)}), bf16[1024,704]{1,0:T(8,128)(2,1)}) %all-gather.27.cloned.1.call-update) | async-done | bytes 1441808 | tf_op jit(solution)/shard_map/all_gather | solution.py:145
  205.7 1704.7 %while.51 = (s32[]{:T(128)}, f32[256]{0:T(256)}, f32[1024,256]{1,0:T(8,128)}, f32[1024,256]{1,0:T(8,128)}, f32[1024,256]{1,0:T(8,128)}, /*index=5*/f32[256,1024]...) while((s32[]{:T(128)}, f32[256]{0:T(256)}, ...), condition=%wide.region_42.43_spmd.clone, body=%wide.region_0.42_spmd.clone.sunk | while | flops 29948319744 | bytes 1019586048 | solution.py:394
  223.5 26.5 %all-gather.31.cloned.1.call-done = bf16[640,1024]{1,0:T(8,128)(2,1)} async-done(((bf16[640,256]{1,0:T(8,128)(2,1)}), bf16[640,1024]{1,0:T(8,128)(2,1)}) %all-gather.31.cloned.1.call-update) | async-done | bytes 1310736 | tf_op jit(solution)/shard_map/while/body/eval_jaxpr/all_gather | solution.py:61
  302.0 30.0 %reduce-scatter.63.cloned.1.call-done = bf16[640,256]{1,0:T(8,128)(2,1)} async-done(((bf16[640,1024]{1,0:T(8,128)(2,1)}), bf16[640,256]{1,0:T(8,128)(2,1)}) %reduce-scatter.63.cloned.1.call-update) | async-done | bytes 327696 | tf_op jit(solution)/shard_map/while/body/eval_jaxpr/reduce_scatter | solution.py:78
  344.9 31.7 %all-gather.33.cloned.1.call-done = bf16[640,1024]{1,0:T(8,128)(2,1)} async-done(((bf16[640,256]{1,0:T(8,128)(2,1)}), bf16[640,1024]{1,0:T(8,128)(2,1)}) %all-gather.33.cloned.1.call-update) | async-done | bytes 1310736 | tf_op jit(solution)/shard_map/while/body/eval_jaxpr/all_gather | solution.py:61
  386.0 29.8 %reduce-scatter.65.cloned.1.call-done = bf16[640,256]{1,0:T(8,128)(2,1)} async-done(((bf16[640,1024]{1,0:T(8,128)(2,1)}), bf16[640,256]{1,0:T(8,128)(2,1)}) %reduce-scatter.65.cloned.1.call-update) | async-done | bytes 327696 | tf_op jit(solution)/shard_map/while/body/eval_jaxpr/reduce_scatter | solution.py:78
  427.6 32.0 %all-gather.35.cloned.1.call-done = bf16[640,1024]{1,0:T(8,128)(2,1)} async-done(((bf16[640,256]{1,0:T(8,128)(2,1)}), bf16[640,1024]{1,0:T(8,128)(2,1)}) %all-gather.35.cloned.1.call-update) | async-done | bytes 1310736 | tf_op jit(solution)/shard_map/while/body/eval_jaxpr/all_gather | solution.py:61
  515.0 28.2 %reduce-scatter.67.cloned.1.call-done = bf16[640,256]{1,0:T(8,128)(2,1)} async-done(((bf16[640,1024]{1,0:T(8,128)(2,1)}), bf16[640,256]{1,0:T(8,128)(2,1)}) %reduce-scatter.67.cloned.1.call-update) | async-done | bytes 327696 | tf_op jit(solution)/shard_map/while/body/eval_jaxpr/reduce_scatter | solution.py:78
  557.4 20.3 all-gather.39.cloned.1.call-done
  582.0 29.7 %all-gather.37.cloned.1.call-done = bf16[640,1024]{1,0:T(8,128)(2,1)} async-done(((bf16[640,256]{1,0:T(8,128)(2,1)}), bf16[640,1024]{1,0:T(8,128)(2,1)}) %all-gather.37.cloned.1.call-update) | async-done | bytes 1310736 | tf_op jit(solution)/shard_map/while/body/eval_jaxpr/all_gather | solution.py:61
  621.6 29.9 %reduce-scatter.69.cloned.1.call-done = bf16[640,256]{1,0:T(8,128)(2,1)} async-done(((bf16[640,1024]{1,0:T(8,128)(2,1)}), bf16[640,256]{1,0:T(8,128)(2,1)}) %reduce-scatter.69.cloned.1.call-update) | async-done | bytes 327696 | tf_op jit(solution)/shard_map/while/body/eval_jaxpr/reduce_scatter | solution.py:66
  667.5 31.8 %all-gather.41.cloned.1.call-done = bf16[640,1024]{1,0:T(8,128)(2,1)} async-done(((bf16[640,256]{1,0:T(8,128)(2,1)}), bf16[640,1024]{1,0:T(8,128)(2,1)}) %all-gather.41.cloned.1.call-update) | async-done | bytes 1310736 | tf_op jit(solution)/shard_map/while/body/eval_jaxpr/all_gather | solution.py:84
  763.5 30.9 %reduce-scatter.75.cloned.1.call-done = bf16[640,256]{1,0:T(8,128)(2,1)} async-done(((bf16[640,1024]{1,0:T(8,128)(2,1)}), bf16[640,256]{1,0:T(8,128)(2,1)}) %reduce-scatter.75.cloned.1.call-update) | async-done | bytes 327696 | tf_op jit(solution)/shard_map/while/body/eval_jaxpr/reduce_scatter | solution.py:66
  809.9 32.0 %all-gather.43.cloned.1.call-done = bf16[640,1024]{1,0:T(8,128)(2,1)} async-done(((bf16[640,256]{1,0:T(8,128)(2,1)}), bf16[640,1024]{1,0:T(8,128)(2,1)}) %all-gather.43.cloned.1.call-update) | async-done | bytes 1310736 | tf_op jit(solution)/shard_map/while/body/eval_jaxpr/all_gather | solution.py:84
  859.5 21.3 reduce-scatter.77.cloned.1.call-done
  922.4 25.7 %all-gather.45.cloned.1.call-done = bf16[640,1024]{1,0:T(8,128)(2,1)} async-done(((bf16[640,256]{1,0:T(8,128)(2,1)}), bf16[640,1024]{1,0:T(8,128)(2,1)}) %all-gather.45.cloned.1.call-update) | async-done | bytes 1310736 | tf_op jit(solution)/shard_map/while/body/eval_jaxpr/all_gather | solution.py:84
  1027.7 15.5 reduce-scatter.83.cloned.1.call-done
  1072.2 28.0 %all-gather.31.cloned.1.call-done = bf16[640,1024]{1,0:T(8,128)(2,1)} async-done(((bf16[640,256]{1,0:T(8,128)(2,1)}), bf16[640,1024]{1,0:T(8,128)(2,1)}) %all-gather.31.cloned.1.call-update) | async-done | bytes 1310736 | tf_op jit(solution)/shard_map/while/body/eval_jaxpr/all_gather | solution.py:61
  1152.2 30.0 %reduce-scatter.63.cloned.1.call-done = bf16[640,256]{1,0:T(8,128)(2,1)} async-done(((bf16[640,1024]{1,0:T(8,128)(2,1)}), bf16[640,256]{1,0:T(8,128)(2,1)}) %reduce-scatter.63.cloned.1.call-update) | async-done | bytes 327696 | tf_op jit(solution)/shard_map/while/body/eval_jaxpr/reduce_scatter | solution.py:78
  1195.1 31.7 %all-gather.33.cloned.1.call-done = bf16[640,1024]{1,0:T(8,128)(2,1)} async-done(((bf16[640,256]{1,0:T(8,128)(2,1)}), bf16[640,1024]{1,0:T(8,128)(2,1)}) %all-gather.33.cloned.1.call-update) | async-done | bytes 1310736 | tf_op jit(solution)/shard_map/while/body/eval_jaxpr/all_gather | solution.py:61
  1236.3 29.8 %reduce-scatter.65.cloned.1.call-done = bf16[640,256]{1,0:T(8,128)(2,1)} async-done(((bf16[640,1024]{1,0:T(8,128)(2,1)}), bf16[640,256]{1,0:T(8,128)(2,1)}) %reduce-scatter.65.cloned.1.call-update) | async-done | bytes 327696 | tf_op jit(solution)/shard_map/while/body/eval_jaxpr/reduce_scatter | solution.py:78
  1277.9 32.0 %all-gather.35.cloned.1.call-done = bf16[640,1024]{1,0:T(8,128)(2,1)} async-done(((bf16[640,256]{1,0:T(8,128)(2,1)}), bf16[640,1024]{1,0:T(8,128)(2,1)}) %all-gather.35.cloned.1.call-update) | async-done | bytes 1310736 | tf_op jit(solution)/shard_map/while/body/eval_jaxpr/all_gather | solution.py:61
  1365.3 28.2 %reduce-scatter.67.cloned.1.call-done = bf16[640,256]{1,0:T(8,128)(2,1)} async-done(((bf16[640,1024]{1,0:T(8,128)(2,1)}), bf16[640,256]{1,0:T(8,128)(2,1)}) %reduce-scatter.67.cloned.1.call-update) | async-done | bytes 327696 | tf_op jit(solution)/shard_map/while/body/eval_jaxpr/reduce_scatter | solution.py:78
  1407.6 20.2 all-gather.39.cloned.1.call-done
  1432.1 29.8 %all-gather.37.cloned.1.call-done = bf16[640,1024]{1,0:T(8,128)(2,1)} async-done(((bf16[640,256]{1,0:T(8,128)(2,1)}), bf16[640,1024]{1,0:T(8,128)(2,1)}) %all-gather.37.cloned.1.call-update) | async-done | bytes 1310736 | tf_op jit(solution)/shard_map/while/body/eval_jaxpr/all_gather | solution.py:61
  1471.8 29.9 %reduce-scatter.69.cloned.1.call-done = bf16[640,256]{1,0:T(8,128)(2,1)} async-done(((bf16[640,1024]{1,0:T(8,128)(2,1)}), bf16[640,256]{1,0:T(8,128)(2,1)}) %reduce-scatter.69.cloned.1.call-update) | async-done | bytes 327696 | tf_op jit(solution)/shard_map/while/body/eval_jaxpr/reduce_scatter | solution.py:66
  1517.8 31.7 %all-gather.41.cloned.1.call-done = bf16[640,1024]{1,0:T(8,128)(2,1)} async-done(((bf16[640,256]{1,0:T(8,128)(2,1)}), bf16[640,1024]{1,0:T(8,128)(2,1)}) %all-gather.41.cloned.1.call-update) | async-done | bytes 1310736 | tf_op jit(solution)/shard_map/while/body/eval_jaxpr/all_gather | solution.py:84
  1613.8 30.9 %reduce-scatter.75.cloned.1.call-done = bf16[640,256]{1,0:T(8,128)(2,1)} async-done(((bf16[640,1024]{1,0:T(8,128)(2,1)}), bf16[640,256]{1,0:T(8,128)(2,1)}) %reduce-scatter.75.cloned.1.call-update) | async-done | bytes 327696 | tf_op jit(solution)/shard_map/while/body/eval_jaxpr/reduce_scatter | solution.py:66
  1660.3 31.9 %all-gather.43.cloned.1.call-done = bf16[640,1024]{1,0:T(8,128)(2,1)} async-done(((bf16[640,256]{1,0:T(8,128)(2,1)}), bf16[640,1024]{1,0:T(8,128)(2,1)}) %all-gather.43.cloned.1.call-update) | async-done | bytes 1310736 | tf_op jit(solution)/shard_map/while/body/eval_jaxpr/all_gather | solution.py:84
  1710.8 20.4 reduce-scatter.77.cloned.1.call-done
  1774.4 24.0 %all-gather.45.cloned.1.call-done = bf16[640,1024]{1,0:T(8,128)(2,1)} async-done(((bf16[640,256]{1,0:T(8,128)(2,1)}), bf16[640,1024]{1,0:T(8,128)(2,1)}) %all-gather.45.cloned.1.call-update) | async-done | bytes 1310736 | tf_op jit(solution)/shard_map/while/body/eval_jaxpr/all_gather | solution.py:84
  1944.0 17.3 reduce-scatter.39.cloned.1.call-done
  1961.3 17.5 reduce-scatter.41.cloned.1.call-done
  1978.8 17.3 reduce-scatter.49.cloned.1.call-done
  1996.0 17.5 reduce-scatter.51.cloned.1.call-done
  2013.5 17.3 reduce-scatter.53.cloned.1.call-done
  2030.8 17.5 reduce-scatter.55.cloned.1.call-done
  2048.3 27.5 %reduce-scatter.43.cloned.1.call-done = bf16[512,704]{0,1:T(8,128)(2,1)} async-done(((bf16[1024,704]{0,1:T(8,128)(2,1)}), bf16[512,704]{0,1:T(8,128)(2,1)}) %reduce-scatter.43.cloned.1.call-update) | async-done | bytes 720912 | tf_op jit(solution)/shard_map/reduce_scatter | solution.py:414
  2075.7 27.6 %reduce-scatter.45.cloned.1.call-done = bf16[512,704]{0,1:T(8,128)(2,1)} async-done(((bf16[1024,704]{0,1:T(8,128)(2,1)}), bf16[512,704]{0,1:T(8,128)(2,1)}) %reduce-scatter.45.cloned.1.call-update) | async-done | bytes 720912 | tf_op jit(solution)/shard_map/reduce_scatter | solution.py:417
  2103.3 27.5 %reduce-scatter.47.cloned.1.call-done = bf16[704,512]{1,0:T(8,128)(2,1)} async-done(((bf16[704,1024]{1,0:T(8,128)(2,1)}), bf16[704,512]{1,0:T(8,128)(2,1)}) %reduce-scatter.47.cloned.1.call-update) | async-done | bytes 720912 | tf_op jit(solution)/shard_map/reduce_scatter | solution.py:420
  2130.8 27.4 %reduce-scatter.57.cloned.1.call-done = bf16[512,704]{0,1:T(8,128)(2,1)} async-done(((bf16[1024,704]{0,1:T(8,128)(2,1)}), bf16[512,704]{0,1:T(8,128)(2,1)}) %reduce-scatter.57.cloned.1.call-update) | async-done | bytes 720912 | tf_op jit(solution)/shard_map/reduce_scatter | solution.py:435
  2158.2 27.4 %reduce-scatter.59.cloned.1.call-done = bf16[512,704]{0,1:T(8,128)(2,1)} async-done(((bf16[1024,704]{0,1:T(8,128)(2,1)}), bf16[512,704]{0,1:T(8,128)(2,1)}) %reduce-scatter.59.cloned.1.call-update) | async-done | bytes 720912 | tf_op jit(solution)/shard_map/reduce_scatter | solution.py:438
  2185.6 27.6 %reduce-scatter.61.cloned.1.call-done = bf16[704,512]{1,0:T(8,128)(2,1)} async-done(((bf16[704,1024]{1,0:T(8,128)(2,1)}), bf16[704,512]{1,0:T(8,128)(2,1)}) %reduce-scatter.61.cloned.1.call-update) | async-done | bytes 720912 | tf_op jit(solution)/shard_map/reduce_scatter | solution.py:441
  2229.1 111.6 %all-reduce.9.cloned.1.call-done = (bf16[512,256]{1,0:T(8,128)(2,1)}, bf16[512,256]{1,0:T(8,128)(2,1)}, bf16[512,256]{1,0:T(8,128)(2,1)}, bf16[256,512]{1,0:T(8,...) async-done(((bf16[512,256]{1,0:T(8,128)(2,1)}, ...) | async-done | bytes 6422544 | tf_op jit(solution)/shard_map/psum | solution.py:458
  (1003 shorter events, 1032.0 us)
Async XLA Ops:
  7.2 103.2 %all-gather.23.cloned.1.call-start = ((), (), s32[]{:S(2)}) async-start(), calls=%async_computation.28 | async-start | bytes 2162688 | tf_op jit(solution)/shard_map/all_gather | solution.py:139
  7.9 102.5 %all-gather.25.cloned.1.call-start = ((), (), s32[]{:S(2)}) async-start(), calls=%async_computation.29 | async-start | bytes 2162688 | tf_op jit(solution)/shard_map/all_gather | solution.py:146
  8.7 110.0 %all-gather.19.cloned.1.call-start = ((), (), s32[]{:S(2)}) async-start(), calls=%async_computation.26 | async-start | bytes 2359296 | tf_op jit(solution)/shard_map/all_gather | solution.py:137
  11.0 137.4 %all-gather.21.cloned.1.call-start = ((), (), s32[]{:S(2)}) async-start(), calls=%async_computation.27 | async-start | bytes 2359296 | tf_op jit(solution)/shard_map/all_gather | solution.py:138
  12.3 164.7 %all-gather.29.cloned.1.call-start = ((), (), s32[]{:S(2)}) async-start(), calls=%async_computation.31 | async-start | bytes 2359296 | tf_op jit(solution)/shard_map/all_gather | solution.py:144
  13.6 192.1 %all-gather.27.cloned.1.call-start = ((), (), s32[]{:S(2)}) async-start(), calls=%async_computation.30 | async-start | bytes 2359296 | tf_op jit(solution)/shard_map/all_gather | solution.py:145
  219.2 112.9 %reduce-scatter.63.cloned.1.call-start = ((), (), s32[]{:S(2)}) async-start(), calls=%async_computation.48 | async-start | bytes 1638400 | tf_op jit(solution)/shard_map/while/body/eval_jaxpr/reduce_scatter | solution.py:78
  301.9 74.7 %all-gather.33.cloned.1.call-start = ((), (), s32[]{:S(2)}) async-start(), calls=%async_computation.49 | async-start | bytes 1638400 | tf_op jit(solution)/shard_map/while/body/eval_jaxpr/all_gather | solution.py:61
  344.6 71.3 %reduce-scatter.65.cloned.1.call-start = ((), (), s32[]{:S(2)}) async-start(), calls=%async_computation.50 | async-start | bytes 1638400 | tf_op jit(solution)/shard_map/while/body/eval_jaxpr/reduce_scatter | solution.py:78
  386.0 73.6 %all-gather.35.cloned.1.call-start = ((), (), s32[]{:S(2)}) async-start(), calls=%async_computation.51 | async-start | bytes 1638400 | tf_op jit(solution)/shard_map/while/body/eval_jaxpr/all_gather | solution.py:61
  427.6 115.7 %reduce-scatter.67.cloned.1.call-start = ((), (), s32[]{:S(2)}) async-start(), calls=%async_computation.52 | async-start | bytes 1638400 | tf_op jit(solution)/shard_map/while/body/eval_jaxpr/reduce_scatter | solution.py:78
  513.2 64.5 %all-gather.39.cloned.1.call-start = ((), (), s32[]{:S(2)}) async-start(), calls=%async_computation.54 | async-start | bytes 1638400 | tf_op jit(solution)/shard_map/while/body/eval_jaxpr/all_gather | solution.py:84
  515.0 96.7 %all-gather.37.cloned.1.call-start = ((), (), s32[]{:S(2)}) async-start(), calls=%async_computation.53 | async-start | bytes 1638400 | tf_op jit(solution)/shard_map/while/body/eval_jaxpr/all_gather | solution.py:61
  557.1 94.3 %reduce-scatter.69.cloned.1.call-start = ((), (), s32[]{:S(2)}) async-start(), calls=%async_computation.55 | async-start | bytes 1638400 | tf_op jit(solution)/shard_map/while/body/eval_jaxpr/reduce_scatter | solution.py:66
  621.6 77.7 %all-gather.41.cloned.1.call-start = ((), (), s32[]{:S(2)}) async-start(), calls=%async_computation.56 | async-start | bytes 1638400 | tf_op jit(solution)/shard_map/while/body/eval_jaxpr/all_gather | solution.py:84
  667.3 76.1 %reduce-scatter.71.cloned.1.call-start = ((), (), s32[]{:S(2)}) async-start(), calls=%async_computation.57 | async-start | bytes 983040 | tf_op jit(solution)/shard_map/while
  763.0 78.8 %all-gather.43.cloned.1.call-start = ((), (), s32[]{:S(2)}) async-start(), calls=%async_computation.60 | async-start | bytes 1638400 | tf_op jit(solution)/shard_map/while/body/eval_jaxpr/all_gather | solution.py:84
  809.8 71.0 %reduce-scatter.77.cloned.1.call-start = ((), (), s32[]{:S(2)}) async-start(), calls=%async_computation.61 | async-start | bytes 1638400 | tf_op jit(solution)/shard_map/while/body/eval_jaxpr/reduce_scatter | solution.py:66
  850.9 62.8 %reduce-scatter.85.cloned.1.call-start = ((), (), s32[]{:S(2)}) async-start(), calls=%async_computation.66 | async-start | bytes 1638400 | tf_op jit(solution)/shard_map/while/body/eval_jaxpr/reduce_scatter | solution.py:78
  854.9 93.3 %all-gather.45.cloned.1.call-start = ((), (), s32[]{:S(2)}) async-start(), calls=%async_computation.62 | async-start | bytes 1638400 | tf_op jit(solution)/shard_map/while/body/eval_jaxpr/all_gather | solution.py:84
  894.2 97.0 %reduce-scatter.79.cloned.1.call-start = ((), (), s32[]{:S(2)}) async-start(), calls=%async_computation.63 | async-start | bytes 983040 | tf_op jit(solution)/shard_map/while
  1067.8 114.4 %reduce-scatter.63.cloned.1.call-start = ((), (), s32[]{:S(2)}) async-start(), calls=%async_computation.48 | async-start | bytes 1638400 | tf_op jit(solution)/shard_map/while/body/eval_jaxpr/reduce_scatter | solution.py:78
  1152.1 74.7 %all-gather.33.cloned.1.call-start = ((), (), s32[]{:S(2)}) async-start(), calls=%async_computation.49 | async-start | bytes 1638400 | tf_op jit(solution)/shard_map/while/body/eval_jaxpr/all_gather | solution.py:61
  1194.8 71.3 %reduce-scatter.65.cloned.1.call-start = ((), (), s32[]{:S(2)}) async-start(), calls=%async_computation.50 | async-start | bytes 1638400 | tf_op jit(solution)/shard_map/while/body/eval_jaxpr/reduce_scatter | solution.py:78
  1236.2 73.6 %all-gather.35.cloned.1.call-start = ((), (), s32[]{:S(2)}) async-start(), calls=%async_computation.51 | async-start | bytes 1638400 | tf_op jit(solution)/shard_map/while/body/eval_jaxpr/all_gather | solution.py:61
  1277.8 115.7 %reduce-scatter.67.cloned.1.call-start = ((), (), s32[]{:S(2)}) async-start(), calls=%async_computation.52 | async-start | bytes 1638400 | tf_op jit(solution)/shard_map/while/body/eval_jaxpr/reduce_scatter | solution.py:78
  1363.4 64.3 %all-gather.39.cloned.1.call-start = ((), (), s32[]{:S(2)}) async-start(), calls=%async_computation.54 | async-start | bytes 1638400 | tf_op jit(solution)/shard_map/while/body/eval_jaxpr/all_gather | solution.py:84
  1365.2 96.7 %all-gather.37.cloned.1.call-start = ((), (), s32[]{:S(2)}) async-start(), calls=%async_computation.53 | async-start | bytes 1638400 | tf_op jit(solution)/shard_map/while/body/eval_jaxpr/all_gather | solution.py:61
  1407.4 94.3 %reduce-scatter.69.cloned.1.call-start = ((), (), s32[]{:S(2)}) async-start(), calls=%async_computation.55 | async-start | bytes 1638400 | tf_op jit(solution)/shard_map/while/body/eval_jaxpr/reduce_scatter | solution.py:66
  1471.8 77.7 %all-gather.41.cloned.1.call-start = ((), (), s32[]{:S(2)}) async-start(), calls=%async_computation.56 | async-start | bytes 1638400 | tf_op jit(solution)/shard_map/while/body/eval_jaxpr/all_gather | solution.py:84
  1517.5 76.1 %reduce-scatter.71.cloned.1.call-start = ((), (), s32[]{:S(2)}) async-start(), calls=%async_computation.57 | async-start | bytes 983040 | tf_op jit(solution)/shard_map/while
  1613.4 78.8 %all-gather.43.cloned.1.call-start = ((), (), s32[]{:S(2)}) async-start(), calls=%async_computation.60 | async-start | bytes 1638400 | tf_op jit(solution)/shard_map/while/body/eval_jaxpr/all_gather | solution.py:84
  1660.2 70.9 %reduce-scatter.77.cloned.1.call-start = ((), (), s32[]{:S(2)}) async-start(), calls=%async_computation.61 | async-start | bytes 1638400 | tf_op jit(solution)/shard_map/while/body/eval_jaxpr/reduce_scatter | solution.py:66
  1701.3 62.8 %reduce-scatter.85.cloned.1.call-start = ((), (), s32[]{:S(2)}) async-start(), calls=%async_computation.66 | async-start | bytes 1638400 | tf_op jit(solution)/shard_map/while/body/eval_jaxpr/reduce_scatter | solution.py:78
  1705.3 93.1 %all-gather.45.cloned.1.call-start = ((), (), s32[]{:S(2)}) async-start(), calls=%async_computation.62 | async-start | bytes 1638400 | tf_op jit(solution)/shard_map/while/body/eval_jaxpr/all_gather | solution.py:84
  1744.6 98.1 %reduce-scatter.79.cloned.1.call-start = ((), (), s32[]{:S(2)}) async-start(), calls=%async_computation.63 | async-start | bytes 983040 | tf_op jit(solution)/shard_map/while
  1914.5 64.2 %reduce-scatter.41.cloned.1.call-start = ((), (), s32[]{:S(2)}) async-start(), calls=%async_computation.35 | async-start | bytes 786432 | tf_op jit(solution)/shard_map/reduce_scatter | solution.py:411
  1915.5 80.5 %reduce-scatter.49.cloned.1.call-start = ((), (), s32[]{:S(2)}) async-start(), calls=%async_computation.39 | async-start | bytes 786432 | tf_op jit(solution)/shard_map/reduce_scatter | solution.py:423
  1916.4 97.1 %reduce-scatter.51.cloned.1.call-start = ((), (), s32[]{:S(2)}) async-start(), calls=%async_computation.40 | async-start | bytes 786432 | tf_op jit(solution)/shard_map/reduce_scatter | solution.py:426
  1918.6 112.2 %reduce-scatter.53.cloned.1.call-start = ((), (), s32[]{:S(2)}) async-start(), calls=%async_computation.41 | async-start | bytes 786432 | tf_op jit(solution)/shard_map/reduce_scatter | solution.py:429
  1920.9 127.4 %reduce-scatter.55.cloned.1.call-start = ((), (), s32[]{:S(2)}) async-start(), calls=%async_computation.42 | async-start | bytes 786432 | tf_op jit(solution)/shard_map/reduce_scatter | solution.py:432
  1923.0 152.7 %reduce-scatter.43.cloned.1.call-start = ((), (), s32[]{:S(2)}) async-start(), calls=%async_computation.36 | async-start | bytes 2162688 | tf_op jit(solution)/shard_map/reduce_scatter | solution.py:414
  1924.4 178.9 %reduce-scatter.45.cloned.1.call-start = ((), (), s32[]{:S(2)}) async-start(), calls=%async_computation.37 | async-start | bytes 2162688 | tf_op jit(solution)/shard_map/reduce_scatter | solution.py:417
  1927.8 203.0 %reduce-scatter.47.cloned.1.call-start = ((), (), s32[]{:S(2)}) async-start(), calls=%async_computation.38 | async-start | bytes 2162688 | tf_op jit(solution)/shard_map/reduce_scatter | solution.py:420
  1929.3 228.9 %reduce-scatter.57.cloned.1.call-start = ((), (), s32[]{:S(2)}) async-start(), calls=%async_computation.43 | async-start | bytes 2162688 | tf_op jit(solution)/shard_map/reduce_scatter | solution.py:435
  1932.5 253.1 %reduce-scatter.59.cloned.1.call-start = ((), (), s32[]{:S(2)}) async-start(), calls=%async_computation.44 | async-start | bytes 2162688 | tf_op jit(solution)/shard_map/reduce_scatter | solution.py:438
  1935.9 277.3 %reduce-scatter.61.cloned.1.call-start = ((), (), s32[]{:S(2)}) async-start(), calls=%async_computation.45 | async-start | bytes 2162688 | tf_op jit(solution)/shard_map/reduce_scatter | solution.py:441
  1937.3 403.5 %all-reduce.9.cloned.1.call-start = ((), (), s32[]{:S(2)}) async-start(), calls=%async_computation.46 | async-start | bytes 12845056 | tf_op jit(solution)/shard_map/psum | solution.py:458
  (273 other events, 3472.8 us)
Sparse Core Ops, SparseCore 0:
  9.6 37.8 all-gather.22
  49.0 35.6 all-gather.24
  86.8 31.8 all-gather.18
  120.7 27.6 all-gather.20
  149.8 27.2 all-gather.28
  178.4 27.1 all-gather.26
  219.3 30.6 all-gather.30
  302.0 29.9 reduce-scatter.62
  344.7 31.8 all-gather.32
  386.1 29.7 reduce-scatter.64
  427.7 31.8 all-gather.34
  513.3 29.9 reduce-scatter.66
  545.4 32.2 all-gather.38
  579.7 31.9 all-gather.36
  621.7 29.7 reduce-scatter.68
  667.4 31.8 all-gather.40
  742.5 16.0 reduce-scatter.72
  763.1 31.2 reduce-scatter.74
  810.0 31.8 all-gather.42
  851.0 29.7 reduce-scatter.76
  883.7 29.9 reduce-scatter.84
  915.9 32.2 all-gather.44
  992.0 16.0 reduce-scatter.80
  1012.0 31.2 reduce-scatter.82
  1068.0 32.2 all-gather.30
  1152.3 29.9 reduce-scatter.62
  1195.0 31.8 all-gather.32
  1236.4 29.7 reduce-scatter.64
  1277.9 31.8 all-gather.34
  1363.5 29.9 reduce-scatter.66
  1395.5 32.2 all-gather.38
  1429.9 31.9 all-gather.36
  1471.9 29.7 reduce-scatter.68
  1517.6 31.8 all-gather.40
  1592.9 15.9 reduce-scatter.72
  1613.5 31.2 reduce-scatter.74
  1660.3 31.8 all-gather.42
  1701.4 29.7 reduce-scatter.76
  1734.0 30.0 reduce-scatter.84
  1766.1 32.2 all-gather.44
  1862.0 31.2 reduce-scatter.82
  2051.1 24.6 reduce-scatter.42
  2078.6 24.6 reduce-scatter.44
  2106.1 24.6 reduce-scatter.46
  2133.6 24.6 reduce-scatter.56
  2160.9 24.6 reduce-scatter.58
  2188.5 24.6 reduce-scatter.60
  2216.5 124.2 all-reduce.8
  (13 shorter events, 188.0 us)
where the time goes:
time: 2370 us
  waiting for transfers between devices  1370 us (58%)
  matrix products  381 us (16%)
  blocking collectives  345 us (15%)
  other arithmetic  179 us (8%)
  local copies, waits for them, and re-layouts  65.8 us (3%)
    all_gather x8, waiting for transfers between devices, normalize(): normed = lax.all_gather(normed_local, 'col', axis=1, tiled=True)  241 us
    all_gather x8, waiting for transfers between devices, branch_grad(): lax.all_gather(gradient.astype(jnp.bfloat16), 'col', axis=1, tiled=True)  218 us
    reduce_scatter x8, waiting for transfers between devices, branch_sum(): lax.psum_scatter(partial_value.astype(jnp.bfloat16), 'col', scatter_dimen...  197 us
    reduce_scatter x8, waiting for transfers between devices, normalize_back(): lax.psum_scatter(partial_value.astype(jnp.bfloat16), 'col', scatter_dimen...  194 us
    psum x1, waiting for transfers between devices, body(): lax.psum(reduced[0].astype(jnp.bfloat16), 'dp').astype(jnp.float32)  112 us
    psum x8, blocking collectives, normalize(): squares = lax.psum(jnp.sum(residual * residual, axis=1), 'col')  79.4 us
    psum x8, blocking collectives, normalize_back(): inner_sum = lax.psum(jnp.sum(grad_unit * unit_rows, axis=1), 'col')  79.2 us
    dot_general x28, matrix products, times_transposed(): lax.dot_general(left, right, (((1,), (1,)), ((), ())), preferred_element_...  72.1 us
  transfers between devices with their start and end apart: 61, of which 54 were waited for; matrix products, arithmetic and copies ran while one was open for 10% of the time, Pallas kernels for 0%

commit v1 on v0

v1 whole, which is shorter than its diff:
```python
import jax
import jax.numpy as jnp
from jax import lax
from jax.sharding import Mesh, PartitionSpec as P

D = 1024
HEAD_DIM = 64
norm_eps = 1e-06
rope_base = 10000.0
bf16 = jnp.bfloat16
f32 = jnp.float32

SWAP = [(0, 1), (1, 0)]


def dot_nt(left, right):
    return lax.dot_general(left, right, (((1,), (1,)), ((), ())), preferred_element_type=f32)


def dot_nn(left, right):
    return lax.dot_general(left, right, (((1,), (0,)), ((), ())), preferred_element_type=f32)


def dot_tn(left, right):
    return lax.dot_general(left, right, (((0,), (0,)), ((), ())), preferred_element_type=f32)


class Lane:
    def __init__(self, axis, window):
        self.axis, self.window, self.sent = axis, window, []

    def send(self, value, perm):
        if self.window and len(self.sent) >= self.window:
            value, _ = lax.optimization_barrier((value, self.sent[-self.window]))
        value = lax.ppermute(value, self.axis, perm)
        self.sent.append(value)
        return value


def swap_core(value):
    return lax.ppermute(value, "core", SWAP)


def make_body(col_count):
    ring_up = [(i, (i + 1) % col_count) for i in range(col_count)]
    ring_down = [(i, (i - 1) % col_count) for i in range(col_count)]
    rounds = []
    for k in range(col_count):
        pairs = []
        for core in range(2):
            for col in range(col_count):
                j = col ^ k
                pairs.append((core * col_count + col, (j & 1) * col_count + (j & ~1) + core))
        rounds.append(pairs)

    def body(
        tokens, segment_ids, prompt_reach,
        attn_gain_1, query_weight_1, key_weight_1, value_weight_1, out_weight_1,
        ffn_gain_1, gate_weight_1, up_weight_1, down_weight_1,
        attn_gain_2, query_weight_2, key_weight_2, value_weight_2, out_weight_2,
        ffn_gain_2, gate_weight_2, up_weight_2, down_weight_2,
        out_grad,
    ):
        xo_count = lax.axis_size("xo")
        xi, core = lax.axis_index("xi"), lax.axis_index("core")
        row, col = lax.axis_index("row"), lax.axis_index("col")
        chip_rows = tokens.shape[1]
        own_rows = chip_rows // 2
        half_d = D // 2
        quarter = tokens.shape[2]
        slot = (col // 2) * 2 + core

        lane_x, lane_y, lane_z = Lane("xi", 2), Lane("row", 2), Lane("col", 2)

        def spread(array):
            pieces = array.reshape(col_count, own_rows, quarter)
            got = []
            for k in range(col_count):
                piece = lax.dynamic_index_in_dim(pieces, col ^ k, 0, keepdims=False)
                got.append(lax.ppermute(piece, ("core", "col"), rounds[k]))
            got = jnp.stack(got)
            return jnp.concatenate(
                [
                    lax.dynamic_index_in_dim(got, p ^ (2 * row) ^ slot, 0, keepdims=False)
                    for p in range(col_count)
                ],
                axis=1,
            )

        def unspread(array):
            pieces = jnp.stack([array[:, p * quarter : (p + 1) * quarter] for p in range(col_count)])
            got = []
            for k in range(col_count):
                piece = lax.dynamic_index_in_dim(
                    pieces, slot ^ k ^ (2 * row), 0, keepdims=False
                )
                back = [(b, a) for a, b in rounds[k]]
                got.append(lax.ppermute(piece, ("core", "col"), back))
            got = jnp.stack(got)
            got = jnp.concatenate(
                [lax.dynamic_index_in_dim(got, j ^ col, 0) for j in range(col_count)], axis=0
            )
            return got.reshape(tokens.shape)

        def turn(array, by, axis):
            first, second = jnp.split(array, 2, axis=axis)
            return jnp.where(
                by == 0, array, jnp.concatenate([second, first], axis=axis)
            )

        residual = spread(tokens).astype(f32)

        both = jnp.stack([segment_ids, prompt_reach])
        both = jnp.where(core == col % 2, both, swap_core(both))
        both = lax.dynamic_index_in_dim(both, col // 2, 1, keepdims=False)
        segments, reach = both[0], both[1]
        group_len = segments.shape[0]
        size_0 = jnp.sum((segments == 0).astype(jnp.int32))
        size_1 = jnp.sum((segments == 1).astype(jnp.int32))
        starts = jnp.where(segments == 0, 0, jnp.where(segments == 1, size_0, size_0 + size_1))
        index = jnp.arange(group_len, dtype=jnp.int32)
        positions = index - starts + reach

        def mine(array):
            part = lax.dynamic_slice_in_dim(array, row * chip_rows, chip_rows, 0)
            return turn(part, core, 0)

        inverse = rope_base ** (-(jnp.arange(HEAD_DIM // 2, dtype=f32) * 2.0) / HEAD_DIM)
        angles = mine(positions).astype(f32)[:, None] * inverse[None, :]
        cosine, sine = jnp.cos(angles)[:, None, :], jnp.sin(angles)[:, None, :]
        query_index, query_seg, query_reach = mine(index), mine(segments), mine(reach)
        first_index = jnp.where(row == 0, group_len, turn(index[:chip_rows], core, 0))
        key_index = jnp.concatenate([first_index, query_index])
        key_seg = jnp.concatenate([turn(segments[:chip_rows], core, 0), query_seg])
        allowed = (query_seg[:, None] == key_seg[None, :]) & (
            key_index[None, :] <= query_index[:, None]
        ) | (key_index[None, :] < query_reach[:, None])
        bias = jnp.where(allowed, 0.0, -1e30).astype(f32)

        gains = jnp.stack([attn_gain_1, ffn_gain_1, attn_gain_2, ffn_gain_2])
        gains = turn(lax.all_gather(gains, "col", axis=1, tiled=True), row, 1)

        def units(block, transposed):
            if transposed:
                size = block.shape[1] // 2
                return lax.dynamic_slice_in_dim(block, core * size, size, 1).T
            size = block.shape[0] // 2
            return lax.dynamic_slice_in_dim(block, core * size, size, 0)

        def x_halves(blocks):
            packed = jnp.concatenate([b.reshape(2, -1, half_d) for b in blocks], axis=1)
            return turn(packed, xi, 0)

        def join(pieces, blocks):
            result, at = [], 0
            for b in blocks:
                size = b.shape[0] // 2
                result.append(
                    jnp.concatenate([p[at : at + size] for pair in pieces for p in pair], axis=0)
                )
                at += size
            return result

        def gather_y_first(blocks):
            halves = x_halves(blocks)
            rows = halves.shape[1]
            other = lane_y.send(halves.reshape(2 * rows, half_d), SWAP).reshape(halves.shape)
            here = jnp.concatenate([halves, other], axis=2)
            pieces, moving = [(here[0], here[1])], here[0]
            for _ in range(col_count - 1):
                moving = lane_z.send(moving, ring_up)
                pieces.append((moving, lane_x.send(moving, SWAP)))
            return join(pieces, blocks)

        def gather_y_last(blocks):
            halves = x_halves(blocks)
            rows = halves.shape[1]
            pairs, moving = [halves.reshape(2 * rows, half_d)], halves[0]
            for _ in range(col_count - 1):
                moving = lane_z.send(moving, ring_up)
                pairs.append(jnp.concatenate([moving, lane_x.send(moving, SWAP)], axis=0))
            pieces = []
            for pair in pairs:
                whole = jnp.concatenate([pair, lane_y.send(pair, SWAP)], axis=1)
                pieces.append((whole[:rows], whole[rows:]))
            return join(pieces, blocks)

        def gather_layer(w_query, w_key, w_value, w_out, w_gate, w_up, w_down, down_first):
            query, key = gather_y_first([units(w_query, True), units(w_key, True)])
            value, out = gather_y_last([units(w_value, True), units(w_out, False)])
            gate_u, up_u, down_u = units(w_gate, True), units(w_up, True), units(w_down, False)
            if down_first:
                gate, down = gather_y_first([gate_u, down_u])
                (up,) = gather_y_last([up_u])
            else:
                (gate,) = gather_y_first([gate_u])
                up, down = gather_y_last([up_u, down_u])
            return query, key, value, out, gate, up, down

        weights_one = gather_layer(
            query_weight_1, key_weight_1, value_weight_1, out_weight_1,
            gate_weight_1, up_weight_1, down_weight_1, True,
        )
        weights_two = gather_layer(
            query_weight_2, key_weight_2, value_weight_2, out_weight_2,
            gate_weight_2, up_weight_2, down_weight_2, False,
        )

        def settle(block_halves, blocks_units):
            result, at = [], 0
            for size in blocks_units:
                half = size // 2
                result.append(block_halves[:, at : at + half].reshape(size, half_d))
                at += half
            return result

        def pack(grads):
            return jnp.concatenate(
                [g.reshape(col_count, 2, -1, D) for g in grads], axis=2
            )

        def ring_sum(parts):
            total = parts[col_count - 1].astype(f32)
            for k in reversed(range(col_count - 1)):
                total = lane_z.send(total.astype(bf16), ring_down).astype(f32) + parts[k].astype(f32)
            return total

        def over_xo(total):
            if xo_count > 1:
                total = lax.psum(total.astype(bf16), "xo").astype(f32)
            return total

        def scatter_x_first(grads):
            packed = pack(grads)
            rows = packed.shape[2]
            parts = []
            for k in reversed(range(col_count)):
                parts.append(packed[k, 0].astype(f32) + lane_x.send(packed[k, 1], SWAP).astype(f32))
            total = ring_sum(parts[::-1])
            total = total[:, :half_d] + lane_y.send(
                total[:, half_d:].astype(bf16), SWAP
            ).astype(f32)
            total = over_xo(total).astype(bf16)
            halves = turn(jnp.stack([total, lane_x.send(total, SWAP)]), xi, 0)
            return settle(halves, [g.shape[0] // col_count for g in grads])

        def scatter_y_first(grads):
            packed = pack(grads)
            rows = packed.shape[2]
            packed = packed.reshape(col_count, 2 * rows, D)
            parts = []
            for k in reversed(range(col_count)):
                parts.append(
                    packed[k, :, :half_d].astype(f32)
                    + lane_y.send(packed[k, :, half_d:], SWAP).astype(f32)
                )
            total = over_xo(ring_sum(parts[::-1]))
            halves = turn(total.reshape(2, rows, half_d), xi, 0)
            halves = halves + lane_x.send(halves.astype(bf16), SWAP).astype(f32)
            return settle(halves.astype(bf16), [g.shape[0] // col_count for g in grads])

        def finish(block, transposed):
            pair = turn(jnp.concatenate([block, swap_core(block)], axis=0), core, 0)
            return (pair.T if transposed else pair).astype(f32)

        def rotate(values, sine_signed):
            values = values.reshape(chip_rows, -1, HEAD_DIM)
            half = HEAD_DIM // 2
            first, second = values[..., :half], values[..., half:]
            turned = jnp.concatenate(
                [first * cosine - second * sine_signed, second * cosine + first * sine_signed],
                axis=-1,
            )
            return turned.reshape(chip_rows, -1)

        def both_cores(own):
            return jnp.concatenate([own, swap_core(own)], axis=0)

        def core_sum(partial):
            sent = swap_core(partial[own_rows:].astype(bf16))
            return partial[:own_rows].astype(bf16).astype(f32) + sent.astype(f32)

        def normalize(value, gain):
            factor = lax.rsqrt(jnp.mean(value * value, axis=1, keepdims=True) + norm_eps)
            return both_cores((value * factor * gain[None, :]).astype(bf16)), factor

        def normalize_back(partial, value, factor, gain):
            grad_normed = core_sum(partial)
            unit = value * factor
            gain_grad = jnp.sum(grad_normed * unit, axis=0)
            grad_unit = grad_normed * gain[None, :]
            inner = jnp.mean(grad_unit * unit, axis=1, keepdims=True)
            return factor * (grad_unit - unit * inner), gain_grad

        def heads(array):
            return array.reshape(array.shape[0], -1, HEAD_DIM)

        def from_first(array):
            return lane_y.send(array, [(0, 1)])

        def to_first(array):
            return lane_y.send(array, [(1, 0)])

        def attend(queries, keys, values):
            scores = jnp.einsum("qhd,khd->hqk", heads(queries), heads(keys), preferred_element_type=f32)
            scores = scores * HEAD_DIM ** (-0.5) + bias[None]
            peak = jnp.max(scores, axis=2, keepdims=True)
            total = jnp.sum(jnp.exp(scores - peak), axis=2, keepdims=True)
            log_total = peak + jnp.log(total)
            probability = jnp.exp(scores - log_total).astype(bf16)
            mixed = jnp.einsum("hqk,khd->qhd", probability, heads(values), preferred_element_type=f32)
            return mixed.reshape(chip_rows, -1).astype(bf16), log_total

        def attend_back(queries, keys, values, log_total, grad_out):
            scores = jnp.einsum("qhd,khd->hqk", heads(queries), heads(keys), preferred_element_type=f32)
            scores = scores * HEAD_DIM ** (-0.5) + bias[None]
            probability = jnp.exp(scores - log_total)
            grad_p = jnp.einsum("qhd,khd->hqk", heads(grad_out), heads(values), preferred_element_type=f32)
            inner = jnp.sum(probability * grad_p, axis=2, keepdims=True)
            grad_s = (probability * (grad_p - inner)).astype(bf16)
            scale = HEAD_DIM ** (-0.5)
            gq = jnp.einsum("hqk,khd->qhd", grad_s, heads(keys), preferred_element_type=f32) * scale
            gk = jnp.einsum("hqk,qhd->khd", grad_s, heads(queries), preferred_element_type=f32) * scale
            gv = jnp.einsum(
                "hqk,qhd->khd", probability.astype(bf16), heads(grad_out), preferred_element_type=f32
            )
            flat = lambda a: a.reshape(a.shape[0], -1)
            return flat(gq), flat(gk), flat(gv)

        def layer_forward(value, weights, attn_gain, ffn_gain, first_values):
            w_query, w_key, w_value, w_out, w_gate, w_up, w_down = weights
            attn_input = value
            normed, attn_factor = normalize(value, attn_gain)
            key_own = rotate(dot_nt(normed, w_key), sine).astype(bf16)
            raw = dot_nt(normed, w_value)
            if first_values is not None:
                raw = 0.5 * raw + 0.5 * first_values.astype(f32)
            value_own = raw.astype(bf16)
            sent = from_first(jnp.concatenate([key_own, value_own], axis=1))
            width = key_own.shape[1]
            queries = rotate(dot_nt(normed, w_query), sine).astype(bf16)
            keys = jnp.concatenate([sent[:, :width], key_own], axis=0)
            values = jnp.concatenate([sent[:, width:], value_own], axis=0)
            mixture, log_total = attend(queries, keys, values)
            value = value + core_sum(dot_nn(mixture, w_out))
            ffn_input = value
            normed_ffn, ffn_factor = normalize(value, ffn_gain)
            gate = dot_nt(normed_ffn, w_gate)
            up = dot_nt(normed_ffn, w_up)
            hidden = (jax.nn.silu(gate) * up).astype(bf16)
            value = value + core_sum(dot_nn(hidden, w_down))
            saved = (
                attn_input, attn_factor, normed, queries, keys, values, mixture, log_total,
                ffn_input, ffn_factor, normed_ffn, gate, up, hidden,
            )
            return value, value_own, saved

        def layer_backward(grad, weights, attn_gain, ffn_gain, saved, extra, is_second):
            w_query, w_key, w_value, w_out, w_gate, w_up, w_down = weights
            (
                attn_input, attn_factor, normed, queries, keys, values, mixture, log_total,
                ffn_input, ffn_factor, normed_ffn, gate, up, hidden,
            ) = saved
            grad_full = both_cores(grad.astype(bf16))
            grad_hidden = dot_nt(grad_full, w_down)
            sig = jax.nn.sigmoid(gate)
            grad_gate = (grad_hidden * up * sig * (1.0 + gate * (1.0 - sig))).astype(bf16)
            grad_up = (grad_hidden * gate * sig).astype(bf16)
            g_down = dot_tn(hidden, grad_full).astype(bf16)
            partial = dot_nn(grad_gate, w_gate) + dot_nn(grad_up, w_up)
            g_gate = dot_tn(grad_gate, normed_ffn).astype(bf16)
            g_up = dot_tn(grad_up, normed_ffn).astype(bf16)
            if is_second:
                b_down, b_up = scatter_y_first([g_down, g_up])
                (b_gate,) = scatter_x_first([g_gate])
            else:
                b_down, b_gate = scatter_x_first([g_down, g_gate])
                (b_up,) = scatter_y_first([g_up])
            grad_norm, g_ffn_gain = normalize_back(partial, ffn_input, ffn_factor, ffn_gain)
            grad = grad + grad_norm
            grad_full = both_cores(grad.astype(bf16))
            g_out = dot_tn(mixture, grad_full).astype(bf16)
            grad_mixture = dot_nt(grad_full, w_out).astype(bf16)
            gq, gk, gv = attend_back(queries, keys, values, log_total, grad_mixture)
            width = gk.shape[1]
            sent = to_first(
                jnp.concatenate([gk[:chip_rows].astype(bf16), gv[:chip_rows].astype(bf16)], axis=1)
            )
            gk = gk[chip_rows:] + sent[:, :width].astype(f32)
            gv = gv[chip_rows:] + sent[:, width:].astype(f32)
            grad_query = rotate(gq, -sine).astype(bf16)
            grad_key = rotate(gk, -sine).astype(bf16)
            if is_second:
                grad_mix = gv.astype(bf16).astype(f32)
                grad_value = (0.5 * grad_mix).astype(bf16)
                extra = 0.5 * grad_mix
            else:
                grad_value = (gv + extra).astype(bf16)
            partial = (
                dot_nn(grad_query, w_query) + dot_nn(grad_key, w_key) + dot_nn(grad_value, w_value)
            )
            g_query = dot_tn(grad_query, normed).astype(bf16)
            g_key = dot_tn(grad_key, normed).astype(bf16)
            g_value = dot_tn(grad_value, normed).astype(bf16)
            b_out, b_value = scatter_y_first([g_out, g_value])
            b_query, b_key = scatter_x_first([g_query, g_key])
            grad_norm, g_attn_gain = normalize_back(partial, attn_input, attn_factor, attn_gain)
            grad = grad + grad_norm
            blocks = (b_query, b_key, b_value, b_out, b_gate, b_up, b_down)
            return grad, blocks, (g_attn_gain, g_ffn_gain), extra

        residual, first_values, saved_one = layer_forward(
            residual, weights_one, gains[0], gains[1], None
        )
        residual, _, saved_two = layer_forward(
            residual, weights_two, gains[2], gains[3], first_values
        )
        output = unspread(residual.astype(bf16))
        grad = spread(out_grad).astype(f32)
        grad, blocks_two, gains_two, extra = layer_backward(
            grad, weights_two, gains[2], gains[3], saved_two, None, True
        )
        grad, blocks_one, gains_one, _ = layer_backward(
            grad, weights_one, gains[0], gains[1], saved_one, extra, False
        )
        input_grad = unspread(grad.astype(bf16)).astype(f32)

        gain_grads = turn(jnp.stack(gains_one + gains_two), row, 1)
        gain_grads = lax.psum(gain_grads, ("xo", "xi", "core", "row", "col"))
        gain_grads = lax.dynamic_slice_in_dim(gain_grads, col * quarter, quarter, 1)

        def outs(blocks):
            kinds = (True, True, True, False, True, True, False)
            return [finish(b, t) for b, t in zip(blocks, kinds)]

        one, two = outs(blocks_one), outs(blocks_two)
        return (
            output, input_grad,
            gain_grads[0], *one[:4], gain_grads[1], *one[4:],
            gain_grads[2], *two[:4], gain_grads[3], *two[4:],
        )

    return body


def solution(mesh):
    devices = mesh.devices
    dp, rows, cols = devices.shape
    split = Mesh(
        devices.reshape(dp // 4, 2, 2, rows, cols), ("xo", "xi", "core", "row", "col")
    )
    dp_axes = ("xo", "xi", "core")
    token = P(None, dp_axes + ("row",), "col")
    group = P(None, dp_axes)
    gain = P("col")
    tall, wide = P("row", "col"), P("col", "row")
    layer = (gain, tall, tall, tall, wide, gain, tall, tall, wide)
    return jax.shard_map(
        make_body(cols),
        mesh=split,
        in_specs=(token, group, group) + layer + layer + (token,),
        out_specs=(token, token) + layer + layer,
        check_vma=False,
    )
```

time: 2370 us -> 1250 us (0.53)
  waiting for transfers between devices: 1370 us -> 441 us
  blocking collectives: 345 us -> 52.4 us
  starting transfers between devices: 5.4 us -> 197 us
  matrix products: 381 us -> 234 us
  local copies, waits for them, and re-layouts: 65.8 us -> 102 us
    reduce_scatter x34 -> x0, waiting for transfers between devices: 699 us -> none  [the longest x8 197 us: branch_sum(): lax.psum_scatter(partial_value.astype(jnp.bfloat16), 'col', scatter_dimen...]
    all_gather x22 -> x0, waiting for transfers between devices: 554 us -> none  [the longest x8 241 us: normalize(): normed = lax.all_gather(normed_local, 'col', axis=1, tiled=True)]
    ppermute x0 -> x187, waiting for transfers between devices: none -> 441 us  [the longest x140 420 us: send(): value = lax.ppermute(value, self.axis, perm)]
    ppermute x0 -> x187, starting transfers between devices: none -> 197 us  [the longest x140 174 us: send(): value = lax.ppermute(value, self.axis, perm)]
    all_gather x16 -> x1, blocking collectives: 175 us -> 13.8 us  [body(): gains = turn(lax.all_gather(gains, 'col', axis=1, tiled=True), row, 1)]
    dot_general x108 -> x54, matrix products: 381 us -> 234 us  [the longest x2 38.5 us: attend_back(): jnp.einsum('qhd,khd->hqk', heads(grad_out), heads(values), preferred_elem...]
    psum x17 -> x1, blocking collectives: 165 us -> 38.6 us  [body(): gain_grads = lax.psum(gain_grads, ('xo', 'xi', 'core', 'row', 'col'))]
    psum x1 -> x0, waiting for transfers between devices: 112 us -> none  [body(): lax.psum(reduced[0].astype(jnp.bfloat16), 'dp').astype(jnp.float32)]
  transfers between devices with their start and end apart: 61 -> 187, of which waited for: 54 -> 84; matrix products, arithmetic and copies ran while one was open for 10% -> 40% of each run, Pallas kernels for 0% -> 0%
where the time goes in v1:
time: 1250 us; the launch traced here: 1240 us
  waiting for transfers between devices  441 us (35%)
  matrix products  234 us (19%)
  other arithmetic  202 us (16%)
  starting transfers between devices  197 us (16%)
  local copies, waits for them, and re-layouts  102 us (8%)
  blocking collectives  52.4 us (4%)
    ppermute x140, waiting for transfers between devices, send(): value = lax.ppermute(value, self.axis, perm)  420 us
    ppermute x140, starting transfers between devices, send(): value = lax.ppermute(value, self.axis, perm)  174 us
    psum x1, blocking collectives, body(): gain_grads = lax.psum(gain_grads, ('xo', 'xi', 'core', 'row', 'col'))  38.6 us
    dot_general x2, matrix products, attend_back(): jnp.einsum('qhd,khd->hqk', heads(grad_out), heads(values), preferred_elem...  38.5 us
    unnamed x810, local copies, waits for them, and re-layouts  33.3 us
    convert_element_type x2, other arithmetic, attend_back(): grad_s = (probability * (grad_p - inner)).astype(bf16)  32.4 us
    dot_general x14, matrix products, dot_nt(): lax.dot_general(left, right, (((1,), (1,)), ((), ())), preferred_element_...  31.2 us
    dot_general x14, matrix products, dot_tn(): lax.dot_general(left, right, (((0,), (0,)), ((), ())), preferred_element_...  28.8 us
  transfers between devices with their start and end apart: 187, of which 84 were waited for; matrix products, arithmetic and copies ran while one was open for 40% of the time, Pallas kernels for 0%

profile of v1, /device:TPU:0, one launch (start us, length us, event | category | flops | bytes accessed | tf_op | source)
XLA Modules:
  0.0 1236.3 jit_solution(579859006849164820)
XLA Ops:
  9.4 13.8 %all_gather.3 = f32[4,1024]{1,0:T(4,128)S(1)} all-gather(f32[4,256]{1,0:T(4,128)S(1)} %pad_maximum_fusion.75), channel_id=1, replica_groups=mesh['xo'=1,'xi'=2,'core'=2,'row'=2,'col'=4] {'col'}, dimensions={1}, use_global_device_ids=true | all-gather | bytes 20480 | tf_op jit(solution)/shard_map/all_gather | solution.py:141
  41.6 6.3 collective-permute-done.8
  57.7 6.7 collective-permute-done.17
  83.2 12.6 %collective-permute-done.23 = bf16[704,512]{1,0:T(8,128)(2,1)S(1)} collective-permute-done((bf16[704,512]{1,0:T(8,128)(2,1)S(1)}, bf16[704,512]{1,0:T(8,128)(2,1)S(1)}, u32[]{:S(2)}, u32[]{:S(2)}) %collective-permute-start.23) | collective-permute-done | bytes 720928 | tf_op jit(solution)/shard_map/ppermute | solution.py:35
  98.3 21.0 %collective-permute-done.20 = bf16[128,512]{1,0:T(8,128)(2,1)S(1)} collective-permute-done((bf16[128,512]{1,0:T(8,128)(2,1)S(1)}, bf16[128,512]{1,0:T(8,128)(2,1)S(1)}, u32[]{:S(2)}, u32[]{:S(2)}) %collective-permute-start.20) | collective-permute-done | bytes 131104 | tf_op jit(solution)/shard_map/ppermute | solution.py:35
  122.4 17.0 %collective-permute-done.25 = bf16[352,1024]{1,0:T(8,128)(2,1)S(1)} collective-permute-done((bf16[352,1024]{1,0:T(8,128)(2,1)S(1)}, bf16[352,1024]{1,0:T(8,128)(2,1)S(1)}, u32[]{:S(2)}, u32[]{:S(2)}) %collective-permute-start.25) | collective-permute-done | bytes 720928 | tf_op jit(solution)/shard_map/ppermute | solution.py:35
  150.4 14.7 %collective-permute-done.15 = bf16[128,512]{1,0:T(8,128)(2,1)S(1)} collective-permute-done((bf16[128,512]{1,0:T(8,128)(2,1)S(1)}, bf16[128,512]{1,0:T(8,128)(2,1)S(1)}, u32[]{:S(2)}, u32[]{:S(2)}) %collective-permute-start.15) | collective-permute-done | bytes 131104 | tf_op jit(solution)/shard_map/ppermute | solution.py:35
  174.9 6.2 collective-permute-done.26
  202.0 8.5 collective-permute-done.33
  218.2 7.6 collective-permute-done.44
  251.5 6.6 collective-permute-done.40
  264.3 6.6 collective-permute-done.50
  283.3 11.0 collective-permute-done.53
  297.9 9.6 collective-permute-done.54
  333.0 6.6 collective-permute-done.60
  342.3 14.7 %collective-permute-done.67 = bf16[704,512]{1,0:T(8,128)(2,1)S(1)} collective-permute-done((bf16[704,512]{1,0:T(8,128)(2,1)S(1)}, bf16[704,512]{1,0:T(8,128)(2,1)S(1)}, u32[]{:S(2)}, u32[]{:S(2)}) %collective-permute-start.67) | collective-permute-done | bytes 720928 | tf_op jit(solution)/shard_map/ppermute | solution.py:35
  366.9 19.7 %collective-permute-done.68 = bf16[640,1024]{1,0:T(8,128)(2,1)S(1)} collective-permute-done((bf16[640,1024]{1,0:T(8,128)(2,1)S(1)}, bf16[640,1024]{1,0:T(8,128)(2,1)S(1)}, u32[]{:S(2)}, u32[]{:S(2)}) %collective-permute-start.68) | collective-permute-done | bytes 1310752 | tf_op jit(solution)/shard_map/ppermute | solution.py:35
  395.9 13.9 %fusion = (f32[8,640]{1,0:T(8,128)S(1)}, f32[8,640,1280]{2,1,0:T(8,128)}) fusion(f32[640,1280]{1,0:T(8,128)S(1)} %or_select_fusion, bf16[1280,8,64]{0,2,1:T(8,128)(2,1)} %bitcast.666, bf16[640,8,32]{0,2,1:T(8,128)(2,1)} %get-tuple-element.408, bf16[640,8,32]{0,2,1:T(8,128)(2,1)} %get-tuple-element.407), kind=kOutput, calls=%fused_computation.10 | convolution fusion | flops 859827200 | bytes 31477760 | tf_op jit(solution)/shard_map/qhd,khd->hqk/dot_general | solution.py:305
  409.9 12.9 %exponential_reduce_fusion.1 = f32[8,640]{1,0:T(8,128)S(1)} fusion(f32[8,640,1280]{2,1,0:T(8,128)} %get-tuple-element.594, f32[8,640]{1,0:T(8,128)S(1)} %get-tuple-element.593, f32[640,1280]{1,0:T(8,128)S(1)} %or_select_fusion), kind=kLoop, calls=%fused_computation.8 | loop fusion | flops 26209280 | bytes 29532160 | tf_op jit(solution)/shard_map/reduce_sum | solution.py:308
  422.8 12.6 %convolution_convert_fusion.21 = bf16[8,64,640]{2,1,0:T(8,128)(2,1)} fusion(bf16[1280,8,64]{0,2,1:T(8,128)(2,1)} %bitcast.675, f32[8,640,1280]{2,1,0:T(8,128)} %get-tuple-element.594, f32[8,640]{1,0:T(8,128)S(1)} %log_add_fusion.1, f32[640,1280]{1,0:T(8,128)S(1)} %or_select_fusion), kind=kOutput, calls=%fused_computation.172 | convolution fusion | flops 865402880 | bytes 31477760 | tf_op jit(solution)/shard_map/hqk,khd->qhd/dot_general | solution.py:311
  458.2 6.7 collective-permute-done.75
  473.8 6.7 collective-permute-done.76
  494.7 6.0 collective-permute-done.78
  508.8 21.1 %collective-permute-done.79 = bf16[640,1024]{1,0:T(8,128)(2,1)S(1)} collective-permute-done((bf16[640,1024]{1,0:T(8,128)(2,1)S(1)}, bf16[640,1024]{1,0:T(8,128)(2,1)S(1)}, u32[]{:S(2)}, u32[]{:S(2)}) %collective-permute-start.79) | collective-permute-done | bytes 1310752 | tf_op jit(solution)/shard_map/ppermute | solution.py:35
  539.3 13.9 %fusion.1 = (f32[8,640]{1,0:T(8,128)S(1)}, f32[8,640,1280]{2,1,0:T(8,128)}) fusion(f32[640,1280]{1,0:T(8,128)S(1)} %or_select_fusion, bf16[1280,8,64]{0,2,1:T(8,128)(2,1)} %bitcast.668, bf16[640,8,32]{0,2,1:T(8,128)(2,1)} %get-tuple-element.404, bf16[640,8,32]{0,2,1:T(8,128)(2,1)} %get-tuple-element.403), kind=kOutput, calls=%fused_computation.11 | convolution fusion | flops 859827200 | bytes 31477760 | tf_op jit(solution)/shard_map/qhd,khd->hqk/dot_general | solution.py:305
  553.2 12.9 %exponential_reduce_fusion = f32[8,640]{1,0:T(8,128)S(1)} fusion(f32[8,640,1280]{2,1,0:T(8,128)} %get-tuple-element.598, f32[8,640]{1,0:T(8,128)S(1)} %get-tuple-element.597, f32[640,1280]{1,0:T(8,128)S(1)} %or_select_fusion), kind=kLoop, calls=%fused_computation.5 | loop fusion | flops 26209280 | bytes 29532160 | tf_op jit(solution)/shard_map/reduce_sum | solution.py:308
  566.1 12.5 %convolution_convert_fusion.20 = bf16[8,64,640]{2,1,0:T(8,128)(2,1)} fusion(bf16[1280,8,64]{0,2,1:T(8,128)(2,1)} %bitcast.677, f32[8,640,1280]{2,1,0:T(8,128)} %get-tuple-element.598, f32[8,640]{1,0:T(8,128)S(1)} %log_add_fusion, f32[640,1280]{1,0:T(8,128)S(1)} %or_select_fusion), kind=kOutput, calls=%fused_computation.171 | convolution fusion | flops 865402880 | bytes 31477760 | tf_op jit(solution)/shard_map/hqk,khd->qhd/dot_general | solution.py:311
  634.4 8.1 collective-permute-done.94
  644.6 13.4 %collective-permute-done.102 = bf16[704,512]{1,0:T(8,128)(2,1)S(1)} collective-permute-done((bf16[704,512]{1,0:T(8,128)(2,1)S(1)}, bf16[704,512]{1,0:T(8,128)(2,1)S(1)}, u32[]{:S(2)}, u32[]{:S(2)}) %collective-permute-start.102) | collective-permute-done | bytes 720928 | tf_op jit(solution)/shard_map/ppermute | solution.py:35
  667.0 13.1 %convolution_bitcast_fusion.1 = f32[1280,8,64]{0,2,1:T(8,128)} fusion(bf16[640,8,64]{0,2,1:T(8,128)(2,1)} %bitcast.741, f32[8,640,1280]{2,1,0:T(8,128)} %get-tuple-element.598, f32[8,640]{1,0:T(8,128)S(1)} %log_add_fusion, f32[640,1280]{1,0:T(8,128)S(1)} %or_select_fusion), kind=kOutput, calls=%fused_computation.77 | convolution fusion | flops 865075200 | bytes 32788480 | tf_op jit(solution)/shard_map/hqk,qhd->khd/dot_general | solution.py:324
  680.0 24.7 %multiply_reduce_fusion.1 = (f32[8,640]{1,0:T(8,128)S(1)}, f32[8,640,1280]{2,1,0:T(8,128)}) fusion(f32[8,640,1280]{2,1,0:T(8,128)} %get-tuple-element.598, f32[8,640]{1,0:T(8,128)S(1)} %log_add_fusion, f32[640,1280]{1,0:T(8,128)S(1)} %or_select_fusion, bf16[640,8,64]{0,2,1:T(8,128)(2,1)} %bitcast.742, bf16[1280,8,64]{0,2,1:T(8,128)(2,1)} %bitcast.678), kind=kOutput, calls=%fused_computation.3 | convolution fusion | flops 871623680 | bytes 57712640 | tf_op jit(solution)/shard_map/qhd,khd->hqk/dot_general | solution.py:318
  704.8 16.2 %multiply_convert_fusion.1 = bf16[8,640,1280]{2,1,0:T(8,128)(2,1)} fusion(f32[8,640,1280]{2,1,0:T(8,128)} %get-tuple-element.600, f32[8,640,1280]{2,1,0:T(8,128)S(1)} %bitcast.628, f32[8,640]{1,0:T(8,128)S(1)} %get-tuple-element.599, f32[8,640]{1,0:T(8,128)S(1)} %log_add_fusion, f32[640,1280]{1,0:T(8,128)S(1)} %or_select_fusion), kind=kLoop, calls=%fused_computation.2 | loop fusion | flops 39321600 | bytes 68853760 | tf_op jit(solution)/shard_map/convert_element_type | solution.py:320
  720.9 7.4 fusion.4
  751.7 9.8 fusion.24
  808.3 6.7 collective-permute-done.86
  823.0 8.4 collective-permute-done.109
  834.6 8.4 collective-permute-start.110
  868.8 8.1 collective-permute-done.112
  907.8 13.9 %multiply_reduce_fusion = (f32[8,640]{1,0:T(8,128)S(1)}, f32[8,640,1280]{2,1,0:T(8,128)}) fusion(f32[8,640,1280]{2,1,0:T(8,128)S(1)} %bitcast.626, f32[8,640]{1,0:T(8,128)S(1)} %copy-done.145, f32[640,1280]{1,0:T(8,128)S(1)} %or_select_fusion, bf16[640,8,64]{0,2,1:T(8,128)(2,1)S(1)} %bitcast.739, bf16[1280,8,64]{0,2,1:T(8,128)(2,1)} %bitcast.676), kind=kOutput, calls=%fused_computation.1 | convolution fusion | flops 871623680 | bytes 57712640 | tf_op jit(solution)/shard_map/qhd,khd->hqk/dot_general | solution.py:318
  922.9 16.2 %multiply_convert_fusion = bf16[8,640,1280]{2,1,0:T(8,128)(2,1)} fusion(f32[8,640,1280]{2,1,0:T(8,128)} %get-tuple-element.602, f32[8,640,1280]{2,1,0:T(8,128)S(1)} %bitcast.626, f32[8,640]{1,0:T(8,128)S(1)} %get-tuple-element.601, f32[8,640]{1,0:T(8,128)S(1)} %copy-done.145, f32[640,1280]{1,0:T(8,128)S(1)} %or_select_fusion), kind=kLoop, calls=%fused_computation | loop fusion | flops 39321600 | bytes 68853760 | tf_op jit(solution)/shard_map/convert_element_type | solution.py:320
  941.9 11.4 convolution_bitcast_fusion
  955.0 9.8 fusion.23
  966.5 7.1 fusion.5
  1005.6 7.3 collective-permute-done.142
  1052.9 6.8 collective-permute-done.134
  1087.4 7.5 collective-permute-done.149
  1096.4 7.4 collective-permute-done.150
  1110.4 38.6 %psum.7 = f32[4,1024]{1,0:T(4,128)S(1)} all-reduce(f32[4,1024]{1,0:T(4,128)S(1)} %maximum_select_fusion.23), channel_id=1, replica_groups=mesh['xo'=1,'xi'=2,'core'=2,'row'=2,'col'=4] {'xo','xi','core','row','col'}, use_global_device_ids=true, to_apply=%region_20.21 | all-reduce | flops 4096 | bytes 32768 | tf_op jit(solution)/shard_map/psum | solution.py:429
  (1516 shorter events, 669.5 us)
Async XLA Ops:
  2.1 77.6 %collective-permute-start.12 = (s32[2,2,1280]{2,1,0:T(2,128)}, s32[2,2,1280]{2,1,0:T(2,128)}, u32[]{:S(2)}, u32[]{:S(2)}) collective-permute-start(s32[2,2,1280]{2,1,0:T(2,128)} %pad_add_fusion), channel_id=1, source_target_pairs={{0,8},{8,0},{1,9},{9,1},{2,10},{10,2},{3,11},{11,3},{4,12},{12,4},... | collective-permute-start | bytes 61448 | tf_op jit(solution)/shard_map/ppermute | solution.py:41
  4.7 65.5 %collective-permute-start.13 = (bf16[256,512]{1,0:T(8,128)(2,1)S(1)}, bf16[256,512]{1,0:T(8,128)(2,1)S(1)}, u32[]{:S(2)}, u32[]{:S(2)}) collective-permute-start(bf16[256,512]{1,0:T(8,128)(2,1)S(1)} %bitcast.705), channel_id=1, source_target_pairs={{0,4},{4,0},{1,5},{5,1},{2,6},{6,2},{3,7},{7,3},{8,12},{12,8},{9,1... | collective-permute-start | bytes 786440 | tf_op jit(solution)/shard_map/ppermute | solution.py:35
  51.5 88.1 %collective-permute-start = (bf16[320,256]{1,0:T(8,128)(2,1)}, bf16[320,256]{1,0:T(8,128)(2,1)}, u32[]{:S(2)}, u32[]{:S(2)}) collective-permute-start(bf16[320,256]{1,0:T(8,128)(2,1)} %get-tuple-element.490), channel_id=1, source_target_pairs={{0,0},{1,8},{2,2},{3,10},{8,1},{9,9},{10,3},{11,11},{4,4},{5,12},{... | collective-permute-start | bytes 491528 | tf_op jit(solution)/shard_map/ppermute | solution.py:80
  64.3 77.2 %collective-permute-start.3 = (bf16[320,256]{1,0:T(8,128)(2,1)}, bf16[320,256]{1,0:T(8,128)(2,1)}, u32[]{:S(2)}, u32[]{:S(2)}) collective-permute-start(bf16[320,256]{1,0:T(8,128)(2,1)} %get-tuple-element.491), channel_id=1, source_target_pairs={{0,10},{1,2},{2,8},{3,0},{8,11},{9,3},{10,9},{11,1},{4,14},{5,6},{... | collective-permute-start | bytes 491528 | tf_op jit(solution)/shard_map/ppermute | solution.py:80
  69.4 73.4 %collective-permute-start.2 = (bf16[320,256]{1,0:T(8,128)(2,1)}, bf16[320,256]{1,0:T(8,128)(2,1)}, u32[]{:S(2)}, u32[]{:S(2)}) collective-permute-start(bf16[320,256]{1,0:T(8,128)(2,1)} %get-tuple-element.492), channel_id=1, source_target_pairs={{0,2},{1,10},{2,0},{3,8},{8,3},{9,11},{10,1},{11,9},{4,6},{5,14},{... | collective-permute-start | bytes 491528 | tf_op jit(solution)/shard_map/ppermute | solution.py:80
  95.9 23.5 %collective-permute-start.24 = (bf16[352,1024]{1,0:T(8,128)(2,1)S(1)}, bf16[352,1024]{1,0:T(8,128)(2,1)S(1)}, u32[]{:S(2)}, u32[]{:S(2)}) collective-permute-start(bf16[352,1024]{1,0:T(8,128)(2,1)S(1)} %fusion.50), channel_id=1, source_target_pairs={{0,1},{1,2},{2,3},{3,0},{4,5},{5,6},{6,7},{7,4},{8,9},{9,10},{10,1... | collective-permute-start | bytes 2162696 | tf_op jit(solution)/shard_map/ppermute | solution.py:35
  119.3 24.1 %collective-permute-start.1 = (bf16[320,256]{1,0:T(8,128)(2,1)}, bf16[320,256]{1,0:T(8,128)(2,1)S(1)}, u32[]{:S(2)}, u32[]{:S(2)}) collective-permute-start(bf16[320,256]{1,0:T(8,128)(2,1)} %get-tuple-element.493), channel_id=1, source_target_pairs={{0,8},{1,0},{2,10},{3,2},{8,9},{9,1},{10,11},{11,3},{4,12},{5,4},{... | collective-permute-start | bytes 491528 | tf_op jit(solution)/shard_map/ppermute | solution.py:80
  139.6 27.7 %collective-permute-start.29 = (bf16[352,1024]{1,0:T(8,128)(2,1)S(1)}, bf16[352,1024]{1,0:T(8,128)(2,1)S(1)}, u32[]{:S(2)}, u32[]{:S(2)}) collective-permute-start(bf16[352,1024]{1,0:T(8,128)(2,1)S(1)} %collective-permute-done.24), channel_id=1, source_target_pairs={{0,16},{16,0},{1,17},{17,1},{2,18},{18,2},{3,19},{19,3},{4,20},{20... | collective-permute-start | bytes 2162696 | tf_op jit(solution)/shard_map/ppermute | solution.py:35
  141.5 26.1 %collective-permute-start.27 = (bf16[352,1024]{1,0:T(8,128)(2,1)S(1)}, bf16[352,1024]{1,0:T(8,128)(2,1)S(1)}, u32[]{:S(2)}, u32[]{:S(2)}) collective-permute-start(bf16[352,1024]{1,0:T(8,128)(2,1)S(1)} %collective-permute-done.25), channel_id=1, source_target_pairs={{0,1},{1,2},{2,3},{3,0},{4,5},{5,6},{6,7},{7,4},{8,9},{9,10},{10,1... | collective-permute-start | bytes 2162696 | tf_op jit(solution)/shard_map/ppermute | solution.py:35
  142.8 38.3 %collective-permute-start.87 = (bf16[320,256]{1,0:T(8,128)(2,1)S(1)}, bf16[320,256]{1,0:T(8,128)(2,1)S(1)}, u32[]{:S(2)}, u32[]{:S(2)}) collective-permute-start(bf16[320,256]{1,0:T(8,128)(2,1)S(1)} %copy-done.277), channel_id=1, source_target_pairs={{0,0},{1,8},{2,2},{3,10},{8,1},{9,9},{10,3},{11,11},{4,4},{5,12},{... | collective-permute-start | bytes 491528 | tf_op jit(solution)/shard_map/ppermute | solution.py:80
  143.5 38.2 %collective-permute-start.90 = (bf16[320,256]{1,0:T(8,128)(2,1)S(1)}, bf16[320,256]{1,0:T(8,128)(2,1)S(1)}, u32[]{:S(2)}, u32[]{:S(2)}) collective-permute-start(bf16[320,256]{1,0:T(8,128)(2,1)S(1)} %copy-done.276), channel_id=1, source_target_pairs={{0,10},{1,2},{2,8},{3,0},{8,11},{9,3},{10,9},{11,1},{4,14},{5,6},{... | collective-permute-start | bytes 491528 | tf_op jit(solution)/shard_map/ppermute | solution.py:80
  167.6 22.7 %collective-permute-start.30 = (bf16[352,1024]{1,0:T(8,128)(2,1)S(1)}, bf16[352,1024]{1,0:T(8,128)(2,1)S(1)}, u32[]{:S(2)}, u32[]{:S(2)}) collective-permute-start(bf16[352,1024]{1,0:T(8,128)(2,1)S(1)} %collective-permute-done.27), channel_id=1, source_target_pairs={{0,16},{16,0},{1,17},{17,1},{2,18},{18,2},{3,19},{19,3},{4,20},{20... | collective-permute-start | bytes 2162696 | tf_op jit(solution)/shard_map/ppermute | solution.py:35
  191.7 67.2 %collective-permute-start.4 = (bf16[320,1024]{1,0:T(8,128)(2,1)S(1)}, bf16[320,1024]{1,0:T(8,128)(2,1)S(1)}, u32[]{:S(2)}, u32[]{:S(2)}) collective-permute-start(bf16[320,1024]{1,0:T(8,128)(2,1)S(1)} %fusion.26), channel_id=1, source_target_pairs={{0,8},{8,0},{1,9},{9,1},{2,10},{10,2},{3,11},{11,3},{4,12},{12,4},... | collective-permute-start | bytes 1966088 | tf_op jit(solution)/shard_map/ppermute | solution.py:41
  295.9 25.5 %collective-permute-start.58 = (bf16[176,1024]{1,0:T(8,128)(2,1)S(1)}, bf16[176,1024]{1,0:T(8,128)(2,1)S(1)}, u32[]{:S(2)}, u32[]{:S(2)}) collective-permute-start(bf16[176,1024]{1,0:T(8,128)(2,1)S(1)} %collective-permute-done.52), channel_id=1, source_target_pairs={{0,16},{16,0},{1,17},{17,1},{2,18},{18,2},{3,19},{19,3},{4,20},{20... | collective-permute-start | bytes 1081352 | tf_op jit(solution)/shard_map/ppermute | solution.py:35
  313.2 275.1 %collective-permute-start.91 = (bf16[320,1024]{1,0:T(8,128)(2,1)}, bf16[320,1024]{1,0:T(8,128)(2,1)}, u32[]{:S(2)}, u32[]{:S(2)}) collective-permute-start(bf16[320,1024]{1,0:T(8,128)(2,1)} %pad_maximum_fusion.38), channel_id=1, source_target_pairs={{0,8},{8,0},{1,9},{9,1},{2,10},{10,2},{3,11},{11,3},{4,12},{12,4},... | collective-permute-start | bytes 1966088 | tf_op jit(solution)/shard_map/ppermute | solution.py:41
  357.0 29.6 %collective-permute-start.68 = (bf16[640,1024]{1,0:T(8,128)(2,1)S(1)}, bf16[640,1024]{1,0:T(8,128)(2,1)S(1)}, u32[]{:S(2)}, u32[]{:S(2)}) collective-permute-start(bf16[640,1024]{1,0:T(8,128)(2,1)S(1)} %pad_maximum_fusion.4), channel_id=1, source_target_pairs={{0,4},{1,5},{2,6},{3,7},{8,12},{9,13},{10,14},{11,15},{16,20},{17,... | collective-permute-start | bytes 3932168 | tf_op jit(solution)/shard_map/ppermute | solution.py:35
  500.7 29.2 %collective-permute-start.79 = (bf16[640,1024]{1,0:T(8,128)(2,1)S(1)}, bf16[640,1024]{1,0:T(8,128)(2,1)S(1)}, u32[]{:S(2)}, u32[]{:S(2)}) collective-permute-start(bf16[640,1024]{1,0:T(8,128)(2,1)S(1)} %pad_maximum_fusion.9), channel_id=1, source_target_pairs={{0,4},{1,5},{2,6},{3,7},{8,12},{9,13},{10,14},{11,15},{16,20},{17,... | collective-permute-start | bytes 3932168 | tf_op jit(solution)/shard_map/ppermute | solution.py:35
  607.6 24.8 %collective-permute-start.101 = (bf16[176,1024]{1,0:T(8,128)(2,1)}, bf16[176,1024]{1,0:T(8,128)(2,1)}, u32[]{:S(2)}, u32[]{:S(2)}) collective-permute-start(bf16[176,1024]{1,0:T(8,128)(2,1)} %get-tuple-element.221), channel_id=1, source_target_pairs={{0,16},{16,0},{1,17},{17,1},{2,18},{18,2},{3,19},{19,3},{4,20},{20... | collective-permute-start | bytes 1081352 | tf_op jit(solution)/shard_map/ppermute | solution.py:35
  625.6 32.4 %collective-permute-start.102 = (bf16[704,512]{1,0:T(8,128)(2,1)S(1)}, bf16[704,512]{1,0:T(8,128)(2,1)S(1)}, u32[]{:S(2)}, u32[]{:S(2)}) collective-permute-start(bf16[704,512]{1,0:T(8,128)(2,1)S(1)} %get-tuple-element.222), channel_id=1, source_target_pairs={{0,4},{4,0},{1,5},{5,1},{2,6},{6,2},{3,7},{7,3},{8,12},{12,8},{9,1... | collective-permute-start | bytes 2162696 | tf_op jit(solution)/shard_map/ppermute | solution.py:35
  627.2 37.9 %collective-permute-start.93 = (bf16[320,1024]{1,0:T(8,128)(2,1)S(1)}, bf16[320,1024]{1,0:T(8,128)(2,1)S(1)}, u32[]{:S(2)}, u32[]{:S(2)}) collective-permute-start(bf16[320,1024]{1,0:T(8,128)(2,1)S(1)} %fusion.266), channel_id=1, source_target_pairs={{0,8},{8,0},{1,9},{9,1},{2,10},{10,2},{3,11},{11,3},{4,12},{12,4},... | collective-permute-start | bytes 1966088 | tf_op jit(solution)/shard_map/ppermute | solution.py:41
  632.4 164.8 %collective-permute-start.82 = (bf16[320,1024]{1,0:T(8,128)(2,1)}, bf16[320,1024]{1,0:T(8,128)(2,1)}, u32[]{:S(2)}, u32[]{:S(2)}) collective-permute-start(bf16[320,1024]{1,0:T(8,128)(2,1)} %slice.1422), channel_id=1, source_target_pairs={{0,8},{8,0},{1,9},{9,1},{2,10},{10,2},{3,11},{11,3},{4,12},{12,4},... | collective-permute-start | bytes 1966088 | tf_op jit(solution)/shard_map/ppermute | solution.py:41
  642.5 103.7 %collective-permute-start.95 = (bf16[704,512]{1,0:T(8,128)(2,1)}, bf16[704,512]{1,0:T(8,128)(2,1)}, u32[]{:S(2)}, u32[]{:S(2)}) collective-permute-start(bf16[704,512]{1,0:T(8,128)(2,1)} %get-tuple-element.219), channel_id=1, source_target_pairs={{0,4},{4,0},{1,5},{5,1},{2,6},{6,2},{3,7},{7,3},{8,12},{12,8},{9,1... | collective-permute-start | bytes 2162696 | tf_op jit(solution)/shard_map/ppermute | solution.py:35
  659.1 88.5 %collective-permute-start.103 = (bf16[704,512]{1,0:T(8,128)(2,1)}, bf16[704,512]{1,0:T(8,128)(2,1)}, u32[]{:S(2)}, u32[]{:S(2)}) collective-permute-start(bf16[704,512]{1,0:T(8,128)(2,1)} %fusion.21), channel_id=1, source_target_pairs={{0,3},{1,0},{2,1},{3,2},{4,7},{5,4},{6,5},{7,6},{8,11},{9,8},{10,9... | collective-permute-start | bytes 2162696 | tf_op jit(solution)/shard_map/ppermute | solution.py:35
  663.0 102.5 %collective-permute-start.106 = (bf16[704,512]{1,0:T(8,128)(2,1)}, bf16[704,512]{1,0:T(8,128)(2,1)}, u32[]{:S(2)}, u32[]{:S(2)}) collective-permute-start(bf16[704,512]{1,0:T(8,128)(2,1)} %get-tuple-element.226), channel_id=1, source_target_pairs={{0,4},{4,0},{1,5},{5,1},{2,6},{6,2},{3,7},{7,3},{8,12},{12,8},{9,1... | collective-permute-start | bytes 2162696 | tf_op jit(solution)/shard_map/ppermute | solution.py:35
  746.2 30.7 %collective-permute-start.96 = (bf16[640,1024]{1,0:T(8,128)(2,1)S(1)}, bf16[640,1024]{1,0:T(8,128)(2,1)S(1)}, u32[]{:S(2)}, u32[]{:S(2)}) collective-permute-start(bf16[640,1024]{1,0:T(8,128)(2,1)S(1)} %pad_maximum_fusion.15), channel_id=1, source_target_pairs={{4,0},{5,1},{6,2},{7,3},{12,8},{13,9},{14,10},{15,11},{20,16},{21,... | collective-permute-start | bytes 3932168 | tf_op jit(solution)/shard_map/ppermute | solution.py:35
  768.0 23.2 %collective-permute-start.107 = (bf16[704,512]{1,0:T(8,128)(2,1)}, bf16[704,512]{1,0:T(8,128)(2,1)}, u32[]{:S(2)}, u32[]{:S(2)}) collective-permute-start(bf16[704,512]{1,0:T(8,128)(2,1)} %fusion.18), channel_id=1, source_target_pairs={{0,3},{1,0},{2,1},{3,2},{4,7},{5,4},{6,5},{7,6},{8,11},{9,8},{10,9... | collective-permute-start | bytes 2162696 | tf_op jit(solution)/shard_map/ppermute | solution.py:35
  794.0 26.5 %collective-permute-start.108 = (bf16[2,352,512]{2,1,0:T(8,128)(2,1)S(1)}, bf16[2,352,512]{2,1,0:T(8,128)(2,1)S(1)}, u32[]{:S(2)}, u32[]{:S(2)}) collective-permute-start(bf16[2,352,512]{2,1,0:T(8,128)(2,1)S(1)} %fusion.101), channel_id=1, source_target_pairs={{0,16},{16,0},{1,17},{17,1},{2,18},{18,2},{3,19},{19,3},{4,20},{20... | collective-permute-start | bytes 2162696 | tf_op jit(solution)/shard_map/ppermute | solution.py:35
  807.5 55.5 %collective-permute-start.111 = (bf16[176,1024]{1,0:T(8,128)(2,1)S(1)}, bf16[176,1024]{1,0:T(8,128)(2,1)S(1)}, u32[]{:S(2)}, u32[]{:S(2)}) collective-permute-start(bf16[176,1024]{1,0:T(8,128)(2,1)S(1)} %copy-done.228), channel_id=1, source_target_pairs={{0,16},{16,0},{1,17},{17,1},{2,18},{18,2},{3,19},{19,3},{4,20},{20... | collective-permute-start | bytes 1081352 | tf_op jit(solution)/shard_map/ppermute | solution.py:35
  820.3 26.0 %collective-permute-start.98 = (bf16[320,1024]{1,0:T(8,128)(2,1)S(1)}, bf16[320,1024]{1,0:T(8,128)(2,1)S(1)}, u32[]{:S(2)}, u32[]{:S(2)}) collective-permute-start(bf16[320,1024]{1,0:T(8,128)(2,1)S(1)} %get-tuple-element.348), channel_id=1, source_target_pairs={{0,8},{8,0},{1,9},{9,1},{2,10},{10,2},{3,11},{11,3},{4,12},{12,4},... | collective-permute-start | bytes 1966088 | tf_op jit(solution)/shard_map/ppermute | solution.py:41
  831.4 107.7 %collective-permute-start.124 = (bf16[256,512]{1,0:T(8,128)(2,1)}, bf16[256,512]{1,0:T(8,128)(2,1)S(1)}, u32[]{:S(2)}, u32[]{:S(2)}) collective-permute-start(bf16[256,512]{1,0:T(8,128)(2,1)} %get-tuple-element.244), channel_id=1, source_target_pairs={{0,4},{4,0},{1,5},{5,1},{2,6},{6,2},{3,7},{7,3},{8,12},{12,8},{9,1... | collective-permute-start | bytes 786440 | tf_op jit(solution)/shard_map/ppermute | solution.py:35
  834.6 28.4 %collective-permute-start.110 = (bf16[176,1024]{1,0:T(8,128)(2,1)S(1)}, bf16[176,1024]{1,0:T(8,128)(2,1)S(1)}, u32[]{:S(2)}, u32[]{:S(2)}) collective-permute-start(bf16[176,1024]{1,0:T(8,128)(2,1)S(1)} %fusion.65), channel_id=1, source_target_pairs={{0,3},{1,0},{2,1},{3,2},{4,7},{5,4},{6,5},{7,6},{8,11},{9,8},{10,9... | collective-permute-start | bytes 1081352 | tf_op jit(solution)/shard_map/ppermute | solution.py:35
  844.3 24.5 %collective-permute-start.113 = (bf16[176,1024]{1,0:T(8,128)(2,1)S(1)}, bf16[176,1024]{1,0:T(8,128)(2,1)S(1)}, u32[]{:S(2)}, u32[]{:S(2)}) collective-permute-start(bf16[176,1024]{1,0:T(8,128)(2,1)S(1)} %copy-done.227), channel_id=1, source_target_pairs={{0,16},{16,0},{1,17},{17,1},{2,18},{18,2},{3,19},{19,3},{4,20},{20... | collective-permute-start | bytes 1081352 | tf_op jit(solution)/shard_map/ppermute | solution.py:35
  855.2 23.3 %collective-permute-start.99 = (bf16[320,1024]{1,0:T(8,128)(2,1)S(1)}, bf16[320,1024]{1,0:T(8,128)(2,1)S(1)}, u32[]{:S(2)}, u32[]{:S(2)}) collective-permute-start(bf16[320,1024]{1,0:T(8,128)(2,1)S(1)} %slice.1444), channel_id=1, source_target_pairs={{0,8},{8,0},{1,9},{9,1},{2,10},{10,2},{3,11},{11,3},{4,12},{12,4},... | collective-permute-start | bytes 1966088 | tf_op jit(solution)/shard_map/ppermute | solution.py:41
  892.1 110.3 %collective-permute-start.184 = (bf16[352,512]{1,0:T(8,128)(2,1)}, bf16[352,512]{1,0:T(8,128)(2,1)}, u32[]{:S(2)}, u32[]{:S(2)}) collective-permute-start(bf16[352,512]{1,0:T(8,128)(2,1)} %bitcast.289), channel_id=1, source_target_pairs={{0,8},{8,0},{1,9},{9,1},{2,10},{10,2},{3,11},{11,3},{4,12},{12,4},... | collective-permute-start | bytes 1081352 | tf_op jit(solution)/shard_map/ppermute | solution.py:41
  896.3 25.3 %collective-permute-start.122 = (bf16[256,512]{1,0:T(8,128)(2,1)}, bf16[256,512]{1,0:T(8,128)(2,1)}, u32[]{:S(2)}, u32[]{:S(2)}) collective-permute-start(bf16[256,512]{1,0:T(8,128)(2,1)} %get-tuple-element.242), channel_id=1, source_target_pairs={{0,4},{4,0},{1,5},{5,1},{2,6},{6,2},{3,7},{7,3},{8,12},{12,8},{9,1... | collective-permute-start | bytes 786440 | tf_op jit(solution)/shard_map/ppermute | solution.py:35
  898.4 88.2 %collective-permute-start.128 = (bf16[128,1024]{1,0:T(8,128)(2,1)}, bf16[128,1024]{1,0:T(8,128)(2,1)}, u32[]{:S(2)}, u32[]{:S(2)}) collective-permute-start(bf16[128,1024]{1,0:T(8,128)(2,1)} %get-tuple-element.248), channel_id=1, source_target_pairs={{0,16},{16,0},{1,17},{17,1},{2,18},{18,2},{3,19},{19,3},{4,20},{20... | collective-permute-start | bytes 786440 | tf_op jit(solution)/shard_map/ppermute | solution.py:35
  1027.2 22.8 %collective-permute-start.146 = (bf16[352,1024]{1,0:T(8,128)(2,1)}, bf16[352,1024]{1,0:T(8,128)(2,1)}, u32[]{:S(2)}, u32[]{:S(2)}) collective-permute-start(bf16[352,1024]{1,0:T(8,128)(2,1)} %get-tuple-element.261), channel_id=1, source_target_pairs={{0,16},{16,0},{1,17},{17,1},{2,18},{18,2},{3,19},{19,3},{4,20},{20... | collective-permute-start | bytes 2162696 | tf_op jit(solution)/shard_map/ppermute | solution.py:35
  1028.3 31.4 %collective-permute-start.134 = (bf16[640,1024]{1,0:T(8,128)(2,1)}, bf16[640,1024]{1,0:T(8,128)(2,1)}, u32[]{:S(2)}, u32[]{:S(2)}) collective-permute-start(bf16[640,1024]{1,0:T(8,128)(2,1)} %pad_maximum_fusion.18), channel_id=1, source_target_pairs={{4,0},{5,1},{6,2},{7,3},{12,8},{13,9},{14,10},{15,11},{20,16},{21,... | collective-permute-start | bytes 3932168 | tf_op jit(solution)/shard_map/ppermute | solution.py:35
  1045.2 38.0 %collective-permute-start.148 = (bf16[352,1024]{1,0:T(8,128)(2,1)}, bf16[352,1024]{1,0:T(8,128)(2,1)}, u32[]{:S(2)}, u32[]{:S(2)}) collective-permute-start(bf16[352,1024]{1,0:T(8,128)(2,1)} %get-tuple-element.263), channel_id=1, source_target_pairs={{0,16},{16,0},{1,17},{17,1},{2,18},{18,2},{3,19},{19,3},{4,20},{20... | collective-permute-start | bytes 2162696 | tf_op jit(solution)/shard_map/ppermute | solution.py:35
  1047.8 56.0 %collective-permute-start.145 = (bf16[352,512]{1,0:T(8,128)(2,1)}, bf16[352,512]{1,0:T(8,128)(2,1)}, u32[]{:S(2)}, u32[]{:S(2)}) collective-permute-start(bf16[352,512]{1,0:T(8,128)(2,1)} %fusion.60), channel_id=1, source_target_pairs={{0,3},{1,0},{2,1},{3,2},{4,7},{5,4},{6,5},{7,6},{8,11},{9,8},{10,9... | collective-permute-start | bytes 1081352 | tf_op jit(solution)/shard_map/ppermute | solution.py:35
  1052.7 30.5 %collective-permute-start.147 = (bf16[352,1024]{1,0:T(8,128)(2,1)}, bf16[352,1024]{1,0:T(8,128)(2,1)}, u32[]{:S(2)}, u32[]{:S(2)}) collective-permute-start(bf16[352,1024]{1,0:T(8,128)(2,1)} %fusion.12), channel_id=1, source_target_pairs={{0,3},{1,0},{2,1},{3,2},{4,7},{5,4},{6,5},{7,6},{8,11},{9,8},{10,9... | collective-permute-start | bytes 2162696 | tf_op jit(solution)/shard_map/ppermute | solution.py:35
  1105.8 48.5 %collective-permute-start.151 = (bf16[352,512]{1,0:T(8,128)(2,1)}, bf16[352,512]{1,0:T(8,128)(2,1)}, u32[]{:S(2)}, u32[]{:S(2)}) collective-permute-start(bf16[352,512]{1,0:T(8,128)(2,1)} %fusion.59), channel_id=1, source_target_pairs={{0,3},{1,0},{2,1},{3,2},{4,7},{5,4},{6,5},{7,6},{8,11},{9,8},{10,9... | collective-permute-start | bytes 1081352 | tf_op jit(solution)/shard_map/ppermute | solution.py:35
  1106.2 47.9 %collective-permute-start.153 = (bf16[352,512]{1,0:T(8,128)(2,1)S(1)}, bf16[352,512]{1,0:T(8,128)(2,1)S(1)}, u32[]{:S(2)}, u32[]{:S(2)}) collective-permute-start(bf16[352,512]{1,0:T(8,128)(2,1)S(1)} %copy-done.225), channel_id=1, source_target_pairs={{0,4},{4,0},{1,5},{5,1},{2,6},{6,2},{3,7},{7,3},{8,12},{12,8},{9,1... | collective-permute-start | bytes 1081352 | tf_op jit(solution)/shard_map/ppermute | solution.py:35
  1107.2 42.5 %collective-permute-start.139 = (bf16[320,256]{1,0:T(8,128)(2,1)S(1)}, bf16[320,256]{1,0:T(8,128)(2,1)S(1)}, u32[]{:S(2)}, u32[]{:S(2)}) collective-permute-start(bf16[320,256]{1,0:T(8,128)(2,1)S(1)} %get-tuple-element.459), channel_id=1, source_target_pairs={{10,0},{2,1},{8,2},{0,3},{11,8},{3,9},{9,10},{1,11},{14,4},{6,5},{... | collective-permute-start | bytes 491528 | tf_op jit(solution)/shard_map/ppermute | solution.py:98
  1107.3 44.8 %collective-permute-start.138 = (bf16[320,256]{1,0:T(8,128)(2,1)S(1)}, bf16[320,256]{1,0:T(8,128)(2,1)S(1)}, u32[]{:S(2)}, u32[]{:S(2)}) collective-permute-start(bf16[320,256]{1,0:T(8,128)(2,1)S(1)} %get-tuple-element.460), channel_id=1, source_target_pairs={{2,0},{10,1},{0,2},{8,3},{3,8},{11,9},{1,10},{9,11},{6,4},{14,5},{... | collective-permute-start | bytes 491528 | tf_op jit(solution)/shard_map/ppermute | solution.py:98
  1110.2 41.8 %collective-permute-start.137 = (bf16[320,256]{1,0:T(8,128)(2,1)S(1)}, bf16[320,256]{1,0:T(8,128)(2,1)S(1)}, u32[]{:S(2)}, u32[]{:S(2)}) collective-permute-start(bf16[320,256]{1,0:T(8,128)(2,1)S(1)} %get-tuple-element.461), channel_id=1, source_target_pairs={{8,0},{0,1},{10,2},{2,3},{9,8},{1,9},{11,10},{3,11},{12,4},{4,5},{... | collective-permute-start | bytes 491528 | tf_op jit(solution)/shard_map/ppermute | solution.py:98
  1149.7 34.4 %collective-permute-start.163 = (bf16[256,512]{1,0:T(8,128)(2,1)}, bf16[256,512]{1,0:T(8,128)(2,1)S(1)}, u32[]{:S(2)}, u32[]{:S(2)}) collective-permute-start(bf16[256,512]{1,0:T(8,128)(2,1)} %get-tuple-element.278), channel_id=1, source_target_pairs={{0,4},{4,0},{1,5},{5,1},{2,6},{6,2},{3,7},{7,3},{8,12},{12,8},{9,1... | collective-permute-start | bytes 786440 | tf_op jit(solution)/shard_map/ppermute | solution.py:35
  1158.4 23.7 %collective-permute-start.164 = (bf16[352,512]{1,0:T(8,128)(2,1)S(1)}, bf16[352,512]{1,0:T(8,128)(2,1)S(1)}, u32[]{:S(2)}, u32[]{:S(2)}) collective-permute-start(bf16[352,512]{1,0:T(8,128)(2,1)S(1)} %fusion.51), channel_id=1, source_target_pairs={{0,16},{16,0},{1,17},{17,1},{2,18},{18,2},{3,19},{19,3},{4,20},{20... | collective-permute-start | bytes 1081352 | tf_op jit(solution)/shard_map/ppermute | solution.py:35
  (522 other events, 6015.7 us)

commit v2 on v1

v2 whole, which is shorter than its diff:
```python
import jax
import jax.numpy as jnp
from jax import lax
from jax.experimental import pallas as pl
from jax.experimental.pallas import tpu as pltpu
from jax.sharding import Mesh, PartitionSpec as P

D = 1024
HEAD_DIM = 64
norm_eps = 1e-06
rope_base = 10000.0
scale = HEAD_DIM ** (-0.5)
bf16 = jnp.bfloat16
f32 = jnp.float32
PAIR = 2 * HEAD_DIM

SWAP = [(0, 1), (1, 0)]
VMEM = pltpu.CompilerParams(vmem_limit_bytes=56 << 20)


def dot_nt(left, right):
    return lax.dot_general(left, right, (((1,), (1,)), ((), ())), preferred_element_type=f32)


def dot_nn(left, right):
    return lax.dot_general(left, right, (((1,), (0,)), ((), ())), preferred_element_type=f32)


def dot_tn(left, right):
    return lax.dot_general(left, right, (((0,), (0,)), ((), ())), preferred_element_type=f32)


def swap_core(value):
    return lax.ppermute(value, "core", SWAP)


def swap_x(value):
    return lax.ppermute(value, "xi", SWAP)


def swap_y(value):
    return lax.ppermute(value, "row", SWAP)


def after(value, *milestones):
    return lax.optimization_barrier((value,) + milestones)[0] if milestones else value


def turn(array, by, axis):
    first, second = jnp.split(array, 2, axis=axis)
    return jnp.where(by == 0, array, jnp.concatenate([second, first], axis=axis))


def rotated(values, cos_ref, sin_ref):
    width = values.shape[1]
    half = HEAD_DIM // 2
    lane = lax.broadcasted_iota(jnp.int32, values.shape, 1) % HEAD_DIM
    other = jnp.where(
        lane < half, pltpu.roll(values, width - half, 1), pltpu.roll(values, half, 1)
    )
    cos, sin = cos_ref[...], sin_ref[...]
    times = width // PAIR
    if times > 1:
        cos = jnp.concatenate([cos] * times, axis=1)
        sin = jnp.concatenate([sin] * times, axis=1)
    return values * cos + other * sin


def project(normed, weight, cos, sin, kinds, mix):
    rows, block = normed.shape[0], 256
    steps = weight.shape[0] // block
    turned = sum(kinds)

    def kernel(n_ref, w_ref, cos_ref, sin_ref, *rest):
        out_ref = rest[-1]
        step = pl.program_id(0)
        result = dot_nt(n_ref[...], w_ref[...])

        @pl.when(step < turned)
        def _():
            out_ref[...] = rotated(result, cos_ref, sin_ref).astype(bf16)

        @pl.when(step >= turned)
        def _():
            if mix is None:
                out_ref[...] = result.astype(bf16)
            else:
                out_ref[...] = (0.5 * result + 0.5 * rest[0][...].astype(f32)).astype(bf16)

    whole = lambda shape: pl.BlockSpec(shape, lambda i: (0, 0))
    in_specs = [
        whole((rows, D)),
        pl.BlockSpec((block, D), lambda i: (i, 0)),
        whole((rows, PAIR)),
        whole((rows, PAIR)),
    ]
    operands = [normed, weight, cos, sin]
    if mix is not None:
        skip = mix.shape[1] // block - (steps - turned)
        in_specs.append(
            pl.BlockSpec((rows, block), lambda i: (0, jnp.maximum(i - turned, 0) + skip))
        )
        operands.append(mix)
    return pl.pallas_call(
        kernel,
        grid=(steps,),
        in_specs=in_specs,
        out_specs=pl.BlockSpec((rows, block), lambda i: (0, i)),
        out_shape=jax.ShapeDtypeStruct((rows, weight.shape[0]), bf16),
        compiler_params=VMEM,
        cost_estimate=pl.CostEstimate(
            flops=1,
            bytes_accessed=1,
            transcendentals=0,
        ),
    )(*operands)


def assemble(whole, by_y, by_x, low, high, cols, counts):
    rows, width = whole.shape[0] // cols, whole.shape[1]
    size = rows // sum(counts)
    half = cols // 2

    def kernel(whole_ref, y_ref, x_ref, low_ref, high_ref, *outs):
        step = pl.program_id(0)
        at = 0
        for out, count in zip(outs, counts):
            for j in range(count):
                piece = slice(at, at + size)
                out[j, :, :width] = whole_ref[piece]
                out[j, :, width : 2 * width] = y_ref[piece]
                out[j, :, 2 * width : 3 * width] = x_ref[piece]

                @pl.when(step < half)
                def _():
                    out[j, :, 3 * width :] = low_ref[piece]

                @pl.when(step >= half)
                def _():
                    out[j, :, 3 * width :] = high_ref[piece]

                at += size

    block = lambda index: pl.BlockSpec((rows, width), index)
    outs = pl.pallas_call(
        kernel,
        grid=(cols,),
        in_specs=[
            block(lambda i: (i, 0)),
            block(lambda i: (i, 0)),
            block(lambda i: (i, 0)),
            block(lambda i: (jnp.minimum(i, half - 1), 0)),
            block(lambda i: (jnp.maximum(i - half, 0), 0)),
        ],
        out_specs=[pl.BlockSpec((c, size, 4 * width), lambda i: (0, i, 0)) for c in counts],
        out_shape=[jax.ShapeDtypeStruct((c, cols * size, 4 * width), bf16) for c in counts],
        compiler_params=VMEM,
        cost_estimate=pl.CostEstimate(flops=1, bytes_accessed=1, transcendentals=0),
    )(whole, by_y, by_x, low, high)
    return [o.reshape(-1, 4 * width) for o in outs]


def pair_block(rows, first):
    return pl.BlockSpec((rows, PAIR), lambda i: (0, first + i))


def attend(own, first, bias):
    n, m = own.shape[0], first.shape[0]
    width = own.shape[1] // 3
    pairs = width // PAIR

    def kernel(q_ref, ka_ref, kb_ref, va_ref, vb_ref, bias_ref, out_ref, total_ref):
        for h in range(2):
            lanes = slice(h * HEAD_DIM, (h + 1) * HEAD_DIM)
            keys = jnp.concatenate([ka_ref[:, lanes], kb_ref[:, lanes]], axis=0)
            values = jnp.concatenate([va_ref[:, lanes], vb_ref[:, lanes]], axis=0)
            scores = dot_nt(keys, q_ref[:, lanes]) * scale + bias_ref[...]
            peak = jnp.max(scores, axis=0, keepdims=True)
            weight = jnp.exp(scores - peak)
            total = jnp.sum(weight, axis=0, keepdims=True)
            mixed = dot_tn(values, weight.astype(bf16))
            out_ref[:, lanes] = (mixed / total).T.astype(bf16)
            total_ref[0, h, :, :] = peak + jnp.log(total)

    return pl.pallas_call(
        kernel,
        grid=(pairs,),
        in_specs=[
            pair_block(n, 0),
            pair_block(m, 0),
            pair_block(n, pairs),
            pair_block(m, pairs),
            pair_block(n, 2 * pairs),
            pl.BlockSpec((m + n, n), lambda i: (0, 0)),
        ],
        out_specs=[pair_block(n, 0), pl.BlockSpec((1, 2, 1, n), lambda i: (i, 0, 0, 0))],
        out_shape=[
            jax.ShapeDtypeStruct((n, width), bf16),
            jax.ShapeDtypeStruct((pairs, 2, 1, n), f32),
        ],
        compiler_params=VMEM,
        cost_estimate=pl.CostEstimate(
            flops=1, bytes_accessed=1, transcendentals=0
        ),
    )(own, first, own, first, own, bias)


def attend_back(own, first, bias, totals, mixture, grad_out, tables, extra):
    n, m = own.shape[0], first.shape[0]
    width = own.shape[1] // 3
    pairs = width // PAIR
    cos_own, sin_own, cos_first, sin_first = tables

    def kernel(
        q_ref, ka_ref, kb_ref, va_ref, vb_ref, bias_ref, total_ref, mix_ref, go_ref,
        co_ref, so_ref, cf_ref, sf_ref, *rest
    ):
        gq_ref, gka_ref, gkb_ref, gva_ref, gvb_ref = rest[-5:]
        queries_back, keys_back, values_back = [], [], []
        for h in range(2):
            lanes = slice(h * HEAD_DIM, (h + 1) * HEAD_DIM)
            keys = jnp.concatenate([ka_ref[:, lanes], kb_ref[:, lanes]], axis=0)
            values = jnp.concatenate([va_ref[:, lanes], vb_ref[:, lanes]], axis=0)
            queries, grads = q_ref[:, lanes], go_ref[:, lanes]
            inner = jnp.sum(
                grads.astype(f32) * mix_ref[:, lanes].astype(f32), axis=1, keepdims=True
            )
            inner = jnp.broadcast_to(inner, (n, 128)).T[:1]
            scores = dot_nt(keys, queries) * scale + bias_ref[...]
            weight = jnp.exp(scores - total_ref[0, h, :, :])
            grad_weight = dot_nt(values, grads)
            grad_scores = (weight * (grad_weight - inner)).astype(bf16)
            values_back.append(dot_nn(weight.astype(bf16), grads))
            keys_back.append(dot_nn(grad_scores, queries))
            queries_back.append(dot_tn(keys, grad_scores).T)
        side = lambda pair: jnp.concatenate(pair, axis=1)
        gq_ref[...] = rotated(side(queries_back) * scale, co_ref, so_ref).astype(bf16)
        gk, gv = side(keys_back) * scale, side(values_back)
        gka_ref[...] = rotated(gk[:m], cf_ref, sf_ref).astype(bf16)
        gkb_ref[...] = rotated(gk[m:], co_ref, so_ref).astype(bf16)
        if extra is None:
            gva_ref[...] = (0.5 * gv[:m].astype(bf16).astype(f32)).astype(bf16)
            gvb_ref[...] = (0.5 * gv[m:].astype(bf16).astype(f32)).astype(bf16)
        else:
            gva_ref[...] = (gv[:m] + rest[0][...].astype(f32)).astype(bf16)
            gvb_ref[...] = (gv[m:] + rest[1][...].astype(f32)).astype(bf16)

    whole = lambda shape: pl.BlockSpec(shape, lambda i: (0, 0))
    in_specs = [
        pair_block(n, 0),
        pair_block(m, 0),
        pair_block(n, pairs),
        pair_block(m, pairs),
        pair_block(n, 2 * pairs),
        whole((m + n, n)),
        pl.BlockSpec((1, 2, 1, n), lambda i: (i, 0, 0, 0)),
        pair_block(n, 0),
        pair_block(n, 0),
        whole((n, PAIR)),
        whole((n, PAIR)),
        whole((m, PAIR)),
        whole((m, PAIR)),
    ]
    operands = [own, first, own, first, own, bias, totals, mixture, grad_out]
    operands += [cos_own, -sin_own, cos_first, -sin_first]
    if extra is not None:
        in_specs += [pair_block(m, 0), pair_block(n, 0)]
        operands += list(extra)
    shape = lambda rows: jax.ShapeDtypeStruct((rows, width), bf16)
    return pl.pallas_call(
        kernel,
        grid=(pairs,),
        in_specs=in_specs,
        out_specs=[pair_block(r, 0) for r in (n, m, n, m, n)],
        out_shape=[shape(r) for r in (n, m, n, m, n)],
        compiler_params=VMEM,
        cost_estimate=pl.CostEstimate(
            flops=1, bytes_accessed=1, transcendentals=0
        ),
    )(*operands)


def make_body(col_count):
    ring_up = [(i, (i + 1) % col_count) for i in range(col_count)]
    rounds = []
    for k in range(col_count):
        pairs = []
        for core in range(2):
            for col in range(col_count):
                j = col ^ k
                pairs.append((core * col_count + col, (j & 1) * col_count + (j & ~1) + core))
        rounds.append(pairs)
    backs = [[(b, a) for a, b in pairs] for pairs in rounds]

    def body(
        tokens, segment_ids, prompt_reach,
        attn_gain_1, query_weight_1, key_weight_1, value_weight_1, out_weight_1,
        ffn_gain_1, gate_weight_1, up_weight_1, down_weight_1,
        attn_gain_2, query_weight_2, key_weight_2, value_weight_2, out_weight_2,
        ffn_gain_2, gate_weight_2, up_weight_2, down_weight_2,
        out_grad,
    ):
        xo_count = lax.axis_size("xo")
        xi, core = lax.axis_index("xi"), lax.axis_index("core")
        row, col = lax.axis_index("row"), lax.axis_index("col")
        chip_rows = tokens.shape[1]
        own_rows = chip_rows // 2
        quarter = tokens.shape[2]
        half_d = 2 * quarter
        slot = (col // 2) * 2 + core

        def place(p):
            return (2 * row + xi) ^ (0, 2, 1, 3)[p]

        gains = jnp.stack([attn_gain_1, ffn_gain_1, attn_gain_2, ffn_gain_2])
        high = gains.astype(bf16)
        middle = (gains - high.astype(f32)).astype(bf16)
        low = (gains - high.astype(f32) - middle.astype(f32)).astype(bf16)
        small = jnp.concatenate([high, middle, low, jnp.zeros_like(high)], axis=0)
        def unspread(array):
            pieces = jnp.stack([array[:, p * quarter : (p + 1) * quarter] for p in (0, 1, 2, 3)])
            got = []
            for k in range(col_count):
                p = slot ^ k ^ (2 * row + xi)
                p = (p & 1) * 2 + (p >> 1)
                piece = lax.dynamic_index_in_dim(pieces, p, 0, keepdims=False)
                got.append(lax.ppermute(piece, ("core", "col"), backs[k]))
            got = jnp.stack(got)
            got = jnp.concatenate(
                [lax.dynamic_index_in_dim(got, j ^ col, 0) for j in range(col_count)], axis=0
            )
            return got.reshape(tokens.shape)

        def units(block, transposed):
            if transposed:
                size = block.shape[1] // 2
                block = lax.dynamic_slice_in_dim(block, core * size, size, 1).T
            else:
                size = block.shape[0] // 2
                block = lax.dynamic_slice_in_dim(block, core * size, size, 0)
            return turn(block, xi, 1)

        def stack_attn(w_query, w_key, w_value, w_out):
            return jnp.concatenate(
                [units(w_query, True), units(w_key, True), units(w_value, True), units(w_out, False)]
            )

        def gather_col(block):
            return lax.all_gather(block, "col", axis=0, tiled=True)

        class Crossing:
            def __init__(self, whole, *milestones):
                self.whole = after(whole, *milestones)
                self.sides = (swap_x(self.whole), swap_y(self.whole))

            def complete(self, counts, *milestones):
                by_x, by_y = after(self.sides, *milestones)
                half = by_x.shape[0] // 2
                self.both = (swap_x(by_y[:half]), swap_y(by_x[half:]))
                return assemble(self.whole, by_y, by_x, *self.both, col_count, counts)

        def near_x(block):
            return block[:, :quarter]

        def local_ffn(w_gate, w_up, w_down):
            blocks = (units(w_gate, True), units(w_up, True), units(w_down, False))
            return jnp.concatenate([near_x(b) for b in blocks])

        attn_local_one = near_x(
            stack_attn(query_weight_1, key_weight_1, value_weight_1, out_weight_1)
        )
        attn_local_two = near_x(
            stack_attn(query_weight_2, key_weight_2, value_weight_2, out_weight_2)
        )
        ffn_local_one = local_ffn(gate_weight_1, up_weight_1, down_weight_1)
        ffn_local_two = local_ffn(gate_weight_2, up_weight_2, down_weight_2)
        half = attn_local_one.shape[0] // 2
        qk_whole_one = gather_col(attn_local_one[:half])
        vo_whole_one = gather_col(after(attn_local_one[half:], qk_whole_one))
        attn_whole_one = jnp.concatenate(
            [w.reshape(col_count, -1, quarter) for w in (qk_whole_one, vo_whole_one)], axis=1
        ).reshape(-1, quarter)
        ffn_whole_one = gather_col(after(ffn_local_one, vo_whole_one))
        attn_whole_two = gather_col(after(attn_local_two, ffn_whole_one))

        pieces = jnp.concatenate(
            [
                tokens.reshape(col_count, own_rows, quarter),
                out_grad.reshape(col_count, own_rows, quarter),
                jnp.broadcast_to(small[None], (col_count,) + small.shape),
            ],
            axis=1,
        )
        got = []
        for k in range(col_count):
            piece = lax.dynamic_index_in_dim(pieces, col ^ k, 0, keepdims=False)
            got.append(lax.ppermute(piece, ("core", "col"), rounds[k]))
        got = jnp.stack(got)
        got = jnp.concatenate(
            [
                lax.dynamic_index_in_dim(got, place(p) ^ slot, 0, keepdims=False)
                for p in range(col_count)
            ],
            axis=1,
        )
        residual = got[:own_rows].astype(f32)
        last_grad = got[own_rows : 2 * own_rows].astype(f32)
        small = got[2 * own_rows :].astype(f32)
        gains = small[0:4] + small[4:8] + small[8:12]

        both = jnp.stack([segment_ids, prompt_reach])
        both = jnp.where(core == col % 2, both, swap_core(both))
        both = lax.dynamic_index_in_dim(both, col // 2, 1, keepdims=False)
        segments, reach = both[0], both[1]
        group_len = segments.shape[0]
        size_0 = jnp.sum((segments == 0).astype(jnp.int32))
        size_1 = jnp.sum((segments == 1).astype(jnp.int32))
        starts = jnp.where(segments == 0, 0, jnp.where(segments == 1, size_0, size_0 + size_1))
        index = jnp.arange(group_len, dtype=jnp.int32)
        positions = index - starts + reach

        def mine(array):
            return turn(lax.dynamic_slice_in_dim(array, row * chip_rows, chip_rows, 0), core, 0)

        def leading(array):
            return turn(array[:chip_rows], core, 0)

        inverse = rope_base ** (-(jnp.arange(HEAD_DIM // 2, dtype=f32) * 2.0) / HEAD_DIM)

        def tables(position):
            angles = position.astype(f32)[:, None] * inverse[None, :]
            cosine, sine = jnp.cos(angles), jnp.sin(angles)
            return (
                jnp.concatenate([cosine] * 4, axis=1),
                jnp.concatenate([-sine, sine, -sine, sine], axis=1),
            )

        cos_own, sin_own = tables(mine(positions))
        cos_first, sin_first = tables(leading(positions))
        rope = (cos_own, sin_own, cos_first, sin_first)
        query_index, query_seg, query_reach = mine(index), mine(segments), mine(reach)
        first_index = jnp.where(row == 0, group_len, leading(index))
        key_index = jnp.concatenate([first_index, query_index])
        key_seg = jnp.concatenate([leading(segments), query_seg])
        allowed = (query_seg[None, :] == key_seg[:, None]) & (
            key_index[:, None] <= query_index[None, :]
        ) | (key_index[:, None] < query_reach[None, :])
        bias = jnp.where(allowed, 0.0, -1e30).astype(f32)

        def over_xo(total):
            if xo_count > 1:
                total = lax.psum(total, "xo")
            return total

        def scatter_col(array):
            return lax.psum_scatter(array, "col", scatter_dimension=0, tiled=True)

        def add(left, right):
            return (left.astype(f32) + right.astype(f32)).astype(bf16)

        def both_blocks(block):
            return jnp.stack([block, swap_core(block)])

        def finish(pair, at, size, transposed):
            pair = turn(pair[:, at : at + size].reshape(2 * size, half_d), core, 0)
            return (pair.T if transposed else pair).astype(f32)

        def quarters(array, *places):
            if len(places) == 1:
                return array[:, places[0] * quarter : (places[0] + 1) * quarter]
            return jnp.concatenate(
                [array[:, p * quarter : (p + 1) * quarter] for p in places], axis=1
            )

        class Return:
            def __init__(self, by_x, by_y):
                stack = lambda parts: jnp.concatenate(parts) if len(parts) > 1 else parts[0]
                self.near = [stack([n for n, _ in parts]) for parts in (by_x, by_y)]
                far = [stack([f for _, f in parts]) for parts in (by_x, by_y)]
                self.sent = (swap_x(far[0]), swap_y(far[1]))

            def second(self, *milestones):
                sent = after(self.sent, *milestones)
                totals = [add(a, b) for a, b in zip(self.near, sent)]
                self.near = [t[:, :quarter] for t in totals]
                self.sent = (swap_y(totals[0][:, quarter:]), swap_x(totals[1][:, quarter:]))

            def last(self, *milestones):
                sent = after(self.sent, *milestones)
                return [add(a, b) for a, b in zip(self.near, sent)]

        def pack_parts(parts):
            packed = [p.reshape(col_count, -1, quarter) for p in parts]
            return jnp.concatenate(packed, axis=1).reshape(-1, quarter)

        def scatter(packed):
            return over_xo(scatter_col(packed))

        def return_ffn(gate, up, down):
            half = down[0].shape[0] // 2
            low = (quarters(down[0], 0, 1)[:half], quarters(down[0], 2, 3)[:half])
            high = (quarters(down[0], 0, 2)[half:], quarters(down[0], 1, 3)[half:])
            return Return([gate, low], [up, high])

        def last_ffn(returned, *milestones):
            first, second = returned.last(*milestones)
            rows = first.shape[0] * 2 // 3
            down = jnp.concatenate([first[rows:], second[rows:]])
            return pack_parts([first[:rows], second[:rows], down])

        def sides(left, right, x_first):
            stay, go = ((0, 1), (2, 3)) if x_first else ((0, 2), (1, 3))
            return (
                dot_tn(left, quarters(right, *stay)).astype(bf16),
                dot_tn(left, quarters(right, *go)).astype(bf16),
            )

        def finish_all(total, kinds, spare=0):
            total = turn(jnp.concatenate([total, swap_x(total)], axis=1), xi, 1)
            pair = both_blocks(total)
            size = (total.shape[0] - spare) // len(kinds)
            blocks = [finish(pair, j * size, size, kind) for j, kind in enumerate(kinds)]
            return (blocks, pair[:, len(kinds) * size :]) if spare else blocks

        def finish_ffn(total, *milestones):
            return finish_all(after(total, *milestones), (True, True, False))

        def finish_attn(total, *milestones, spare=0):
            return finish_all(after(total, *milestones), (True, True, True, False), spare)

        def return_attn(grads, extra_rows=None):
            pack = lambda pair: jnp.concatenate(
                [g.reshape(col_count, -1, D) for g in pair], axis=1
            ).reshape(-1, D)
            rest = list(grads[2:])
            if extra_rows is not None:
                rest.append(jnp.concatenate([extra_rows] * col_count))
            qk, vo = pack(grads[:2]), pack(rest)
            pairs = [
                (quarters(qk, 0, 1), quarters(qk, 2, 3)),
                (quarters(vo, 0, 2), quarters(vo, 1, 3)),
            ]
            return Return(pairs[:1], pairs[1:])

        def both_cores(own):
            return jnp.concatenate([own, swap_core(own)], axis=0)

        def core_sum(partial):
            sent = swap_core(partial[own_rows:].astype(bf16))
            return partial[:own_rows] + sent.astype(f32)

        def normalize(value, gain):
            factor = lax.rsqrt(jnp.mean(value * value, axis=1, keepdims=True) + norm_eps)
            return (value * factor * gain[None, :]).astype(bf16), factor

        def normalize_back(grad_normed, value, factor, gain):
            unit = value * factor
            gain_grad = jnp.sum(grad_normed * unit, axis=0)
            grad_unit = grad_normed * gain[None, :]
            inner = jnp.mean(grad_unit * unit, axis=1, keepdims=True)
            return factor * (grad_unit - unit * inner), gain_grad

        def flip_row(array):
            return jnp.concatenate(
                [array[:, p * quarter : (p + 1) * quarter] for p in (1, 0, 3, 2)], axis=1
            )

        def attn_forward(value, weights, gain, mix, start):
            w_qkv, w_out = weights
            width = w_out.shape[0]
            normed_own, factor = normalize(value, gain)
            normed_first = both_cores(flip_row(lax.ppermute(normed_own, "row", [(0, 1)])))
            normed = both_cores(normed_own)
            own = project(normed, w_qkv, cos_own, sin_own, (1, 1, 1, 1, 0, 0), mix and mix[0])
            first = project(
                normed_first, w_qkv[width:], cos_first, sin_first, (1, 1, 0, 0), mix and mix[1]
            )
            mixture, totals = attend(own, first, bias)
            mixture = after(mixture, *start(normed_first))
            result = value + core_sum(dot_nn(mixture, w_out))
            return result, (value, factor, normed, normed_first, own, first, mixture, totals)

        def ffn_forward(value, weights, gain, deadline):
            w_gate, w_up, w_down = weights
            normed_own, factor = normalize(value, gain)
            normed = both_cores(normed_own)
            gate = dot_nt(normed, w_gate)
            up = dot_nt(normed, w_up)
            hidden = (jax.nn.silu(gate) * up).astype(bf16)
            hidden = after(hidden, *deadline)
            return value + core_sum(dot_nn(hidden, w_down)), (value, factor, normed, gate, up, hidden)

        def ffn_backward(grad, weights, gain, saved, kinds):
            w_gate, w_up, w_down = weights
            value, factor, normed, gate, up, hidden = saved
            grad_full = both_cores(grad.astype(bf16))
            grad_hidden = dot_nt(grad_full, w_down)
            sig = jax.nn.sigmoid(gate)
            grad_gate = (grad_hidden * up * sig * (1.0 + gate * (1.0 - sig))).astype(bf16)
            grad_up = (grad_hidden * gate * sig).astype(bf16)
            grad_normed = core_sum(dot_nn(grad_gate, w_gate) + dot_nn(grad_up, w_up))
            pairs = ((grad_gate, normed), (grad_up, normed), (hidden, grad_full))
            grads = [sides(*pair, k) for pair, k in zip(pairs[:2], kinds)]
            grads.append((dot_tn(*pairs[2]).astype(bf16),))
            step, gain_grad = normalize_back(grad_normed, value, factor, gain)
            return grad + step, grads, gain_grad

        def attn_backward(grad, weights, gain, saved, extra, milestones, late):
            w_qkv, w_out = weights
            width = w_out.shape[0]
            value, factor, normed, normed_first, own, first, mixture, totals = saved
            grad_full = both_cores(grad.astype(bf16))
            grad_mixture = after(dot_nt(grad_full, w_out).astype(bf16), *milestones)
            gq, gk_first, gk, gv_first, gv = attend_back(
                own, first, bias, totals, mixture, grad_mixture, rope, extra
            )
            gk_first, gv_first = after((gk_first, gv_first), *late)
            w_query, w_key, w_value = w_qkv[:width], w_qkv[width : 2 * width], w_qkv[2 * width :]
            operand = core_sum(dot_nn(gk_first, w_key) + dot_nn(gv_first, w_value)).astype(bf16)
            sent = flip_row(lax.ppermute(operand, "row", [(1, 0)])).astype(f32)
            grad_normed = core_sum(dot_nn(gq, w_query) + dot_nn(gk, w_key) + dot_nn(gv, w_value))
            done = gq
            gq, gk, gv, gk_first, gv_first = after((gq, gk, gv, gk_first, gv_first), operand)
            grads = [
                dot_tn(gq, normed).astype(bf16),
                (dot_tn(gk, normed) + dot_tn(gk_first, normed_first)).astype(bf16),
                (dot_tn(gv, normed) + dot_tn(gv_first, normed_first)).astype(bf16),
                dot_tn(mixture, grad_full).astype(bf16),
            ]
            step, gain_grad = normalize_back(grad_normed + sent, value, factor, gain)
            return grad + step, grads, gain_grad, (gv_first, gv), done

        cross = Crossing(attn_whole_one, got)
        attn_one = cross.complete((3, 1), bias, cos_own, cos_first)
        cross_ffn = Crossing(ffn_whole_one, *cross.both)
        residual, kept_attn_one = attn_forward(
            residual, attn_one, gains[0], None, lambda _: (*cross_ffn.sides, attn_whole_two)
        )
        own_one, first_one = kept_attn_one[4], kept_attn_one[5]
        ffn_one = cross_ffn.complete((1, 1, 1))
        cross = Crossing(attn_whole_two, *cross_ffn.both)
        ffn_whole_two = gather_col(after(ffn_local_two, attn_whole_two))
        residual, kept_ffn_one = ffn_forward(residual, ffn_one, gains[1], (*cross.sides, ffn_whole_two))
        attn_two = cross.complete((3, 1))
        ffn_two = []

        def start_ffn_two(normed_first):
            ffn_two.append(Crossing(ffn_whole_two, normed_first, *cross.both))
            return ffn_two[0].sides

        residual, kept_attn_two = attn_forward(
            residual, attn_two, gains[2], (own_one, first_one), start_ffn_two
        )
        ffn_two = ffn_two[0].complete((1, 1, 1))
        residual, kept_ffn_two = ffn_forward(residual, ffn_two, gains[3], ())
        output = unspread(residual.astype(bf16))

        kinds = (True, False)

        def leaves(grads):
            return [a for pair in grads for a in pair]

        grad, g_ffn_two, gain_ffn_two = ffn_backward(
            last_grad, ffn_two, gains[3], kept_ffn_two, kinds
        )
        r_ffn_two = return_ffn(*g_ffn_two)
        grad, g_attn_two, gain_attn_two, extra, done_attn_two = attn_backward(
            grad, attn_two, gains[2], kept_attn_two, None, (output, *leaves(g_ffn_two)), ()
        )
        r_attn_two = return_attn(g_attn_two)
        r_ffn_two.second(grad)
        grad, g_ffn_one, gain_ffn_one = ffn_backward(grad, ffn_one, gains[1], kept_ffn_one, kinds)
        p_ffn_two = last_ffn(r_ffn_two, grad, *leaves(g_ffn_one))
        t_ffn_two = scatter(p_ffn_two)
        r_ffn_one = return_ffn(*g_ffn_one)
        grad, g_attn_one, gain_attn_one, _, done_attn_one = attn_backward(
            grad, attn_one, gains[0], kept_attn_one, extra,
            (p_ffn_two, *leaves(g_ffn_one)), r_ffn_one.sent,
        )
        r_attn_two.second(*r_ffn_one.sent)
        r_ffn_one.second()
        gain_rows = jnp.stack([gain_attn_one, gain_ffn_one, gain_attn_two, gain_ffn_two])
        gain_rows = jnp.pad(gain_rows, ((0, 12), (0, 0))).astype(bf16)
        r_attn_one = return_attn(g_attn_one, gain_rows)
        p_attn_two = pack_parts(r_attn_two.last(*r_attn_one.near))
        t_attn_two = scatter(p_attn_two)
        p_ffn_one = last_ffn(r_ffn_one)
        r_attn_one.second(p_ffn_one)
        t_ffn_one = scatter(p_ffn_one)
        p_attn_one = pack_parts(r_attn_one.last())
        t_attn_one = scatter(after(p_attn_one, t_ffn_one))
        b_ffn_two = finish_ffn(t_ffn_two, p_ffn_one)
        b_attn_two = finish_attn(t_attn_two, p_ffn_one)
        b_ffn_one = finish_ffn(t_ffn_one)
        b_attn_one, gain_sums = finish_attn(t_attn_one, spare=16)
        input_grad = unspread(grad.astype(bf16)).astype(f32)

        total = gain_sums[0, :4].astype(f32) + gain_sums[1, :4].astype(f32)
        total = turn(jnp.concatenate([total, swap_y(total)], axis=1), row, 1)
        total = lax.dynamic_slice_in_dim(total, col * quarter, quarter, 1)

        return (
            output, input_grad,
            total[0], *b_attn_one, total[1], *b_ffn_one,
            total[2], *b_attn_two, total[3], *b_ffn_two,
        )

    return body


def solution(mesh):
    devices = mesh.devices
    dp, rows, cols = devices.shape
    split = Mesh(devices.reshape(dp // 4, 2, 2, rows, cols), ("xo", "xi", "core", "row", "col"))
    dp_axes = ("xo", "xi", "core")
    token = P(None, dp_axes + ("row",), "col")
    group = P(None, dp_axes)
    gain = P("col")
    tall, wide = P("row", "col"), P("col", "row")
    layer = (gain, tall, tall, tall, wide, gain, tall, tall, wide)
    return jax.shard_map(
        make_body(cols),
        mesh=split,
        in_specs=(token, group, group) + layer + layer + (token,),
        out_specs=(token, token) + layer + layer,
        check_vma=False,
    )
```

time: 1250 us -> 836 us (0.67)
  waiting for transfers between devices: 441 us -> 268 us
  Pallas kernels: 0 us -> 133 us
  matrix products: 234 us -> 115 us
  other arithmetic: 202 us -> 91.8 us
  starting transfers between devices: 197 us -> 88.8 us
  local copies, waits for them, and re-layouts: 102 us -> 60.7 us
    ppermute x156 -> x53, waiting for transfers between devices: 438 us -> 256 us  [the longest x20 141 us: swap_x(): return lax.ppermute(value, 'xi', SWAP)]
    dot_general x12 -> x0, matrix products: 150 us -> none  [the longest x2 38.5 us: attend_back(): jnp.einsum('qhd,khd->hqk', heads(grad_out), heads(values), preferred_elem...]
    pallas_call x0 -> x12, Pallas kernels: none -> 133 us  [the longest x2 48.3 us: attend_back(): pl.pallas_call(kernel, grid=(pairs,), in_specs=in_specs, out_specs=[pair_...]
    ppermute x156 -> x53, starting transfers between devices: 193 us -> 81.7 us  [the longest x17 27.5 us: swap_y(): return lax.ppermute(value, 'row', SWAP)]
    convert_element_type x47 -> x30, other arithmetic: 73.1 us -> 24.2 us  [the longest x16 15.6 us: add(): return (left.astype(f32) + right.astype(f32)).astype(bf16)]
    all_gather x1 -> x2, blocking collectives: 13.8 us -> 52.5 us  [gather_col(): return lax.all_gather(block, 'col', axis=0, tiled=True)]
    psum x1 -> x0, blocking collectives: 38.6 us -> none  [body(): gain_grads = lax.psum(gain_grads, ('xo', 'xi', 'core', 'row', 'col'))]
    reduce_sum x2 -> x0, other arithmetic: 25.8 us -> none  [attend(): total = jnp.sum(jnp.exp(scores - peak), axis=2, keepdims=True)]
  transfers between devices with their start and end apart: 187 -> 85, of which waited for: 84 -> 37; matrix products, arithmetic and copies ran while one was open for 40% -> 25% of each run, Pallas kernels for 0% -> 16%
where the time goes in v2:
time: 836 us; the launch traced here: 827 us
  waiting for transfers between devices  268 us (32%)
  Pallas kernels  133 us (16%)
  matrix products  115 us (14%)
  other arithmetic  91.8 us (11%)
  starting transfers between devices  88.8 us (11%)
  local copies, waits for them, and re-layouts  60.7 us (7%)
  blocking collectives  52.5 us (6%)
  between operations  18.4 us (2%)
    ppermute x20, waiting for transfers between devices, swap_x(): return lax.ppermute(value, 'xi', SWAP)  141 us
    ppermute x17, waiting for transfers between devices, swap_y(): return lax.ppermute(value, 'row', SWAP)  60.9 us
    all_gather x2, blocking collectives, gather_col(): return lax.all_gather(block, 'col', axis=0, tiled=True)  52.5 us
    pallas_call x2, Pallas kernels, attend_back(): pl.pallas_call(kernel, grid=(pairs,), in_specs=in_specs, out_specs=[pair_...  48.3 us
    dot_general x22, matrix products, dot_tn(): lax.dot_general(left, right, (((0,), (0,)), ((), ())), preferred_element_...  46 us
    dot_general x8, matrix products, dot_nt(): lax.dot_general(left, right, (((1,), (1,)), ((), ())), preferred_element_...  35.2 us
    dot_general x18, matrix products, dot_nn(): lax.dot_general(left, right, (((1,), (0,)), ((), ())), preferred_element_...  33.3 us
    pallas_call x4, Pallas kernels, project(): pl.pallas_call(kernel, grid=(steps,), in_specs=in_specs, out_specs=pl.Blo...  30 us
  transfers between devices with their start and end apart: 85, of which 37 were waited for; matrix products, arithmetic and copies ran while one was open for 25% of the time, Pallas kernels for 16%

profile of v2, /device:TPU:0, one launch (start us, length us, event | category | flops | bytes accessed | tf_op | source)
XLA Modules:
  0.0 827.4 jit_solution(15454489520126633617)
XLA Ops:
  16.7 4.3 collective-permute-start
  21.8 36.6 %all_gather.15 = bf16[1024,256]{1,0:T(8,128)(2,1)S(1)} all-gather(bf16[256,256]{1,0:T(8,128)(2,1)S(1)} %pad_maximum_fusion.72), channel_id=1, replica_groups=mesh['xo'=1,'xi'=2,'core'=2,'row'=2,'col'=4] {'col'}, dimensions={0}, use_global_device_ids=true | all-gather | bytes 655360 | tf_op jit(solution)/shard_map/all_gather | solution.py:349
  59.1 15.9 %all_gather.16 = bf16[1024,256]{1,0:T(8,128)(2,1)S(1)} all-gather(bf16[256,256]{1,0:T(8,128)(2,1)S(1)} %pad_maximum_fusion.71), channel_id=1, replica_groups=mesh['xo'=1,'xi'=2,'core'=2,'row'=2,'col'=4] {'col'}, dimensions={0}, use_global_device_ids=true | all-gather | bytes 655360 | tf_op jit(solution)/shard_map/all_gather | solution.py:349
  98.3 13.9 %collective-permute-done.5.x_ref = bf16[2048,256]{1,0:T(8,128)(2,1)S(1)} collective-permute-done((bf16[2048,256]{1,0:T(8,128)(2,1)S(1)}, bf16[2048,256]{1,0:T(8,128)(2,1)S(1)}, u32[]{:S(2)}, u32[]{:S(2)}) %collective-permute-start.5) | collective-permute-done | bytes 1048608 | tf_op jit(solution)/shard_map/ppermute | solution.py:38
  124.3 4.4 collective-permute-done.9.high_ref
  135.9 6.8 collective-permute-done.10
  150.2 4.7 shard_map.365
  154.9 8.6 %shard_map.366.q_ref.kb_ref.vb_ref.rest_0_ = bf16[640,1536]{1,0:T(8,128)(2,1)} custom-call(bf16[640,1024]{1,0:T(8,128)(2,1)} %pad_maximum_fusion.13.n_ref, bf16[1536,1024]{1,0:T(8,128)(2,1)} %bitcast.373, f32[640,128]{1,0:T(8,128)} %get-tuple-element.421.cos_ref.co_ref, f32[640,128]{1,0:T(8,128)} %get-tuple-element.424.sin_ref), custom_call_target="tpu_custom_call" | custom-call | flops 1 | bytes 1 | tf_op jit(solution)/shard_map/pallas_call | solution.py:104
  165.1 6.2 shard_map.367.ka_ref.va_ref.rest_0_
  172.0 15.0 %shard_map.368 = (bf16[640,512]{1,0:T(8,128)(2,1)}, f32[4,2,1,640]{3,2,1,0:T(1,128)}) custom-call(bf16[640,1536]{1,0:T(8,128)(2,1)} %shard_map.366.q_ref.kb_ref.vb_ref.rest_0_, bf16[640,1024]{1,0:T(8,128)(2,1)} %shard_map.367.ka_ref.va_ref.rest_0_, bf16[640,1536]{1,0:T(8,128)(2,1)} %shard_map.366.q_ref.kb_ref.vb_ref.rest_0_, ...), custom_call_target="tpu_custom_call" | custom-call | flops 1 | bytes 1 | tf_op jit(solution)/shard_map/pallas_call | solution.py:185
  201.5 18.2 %collective-permute-done.16.low_ref = bf16[2112,256]{1,0:T(8,128)(2,1)S(1)} collective-permute-done((bf16[2112,256]{1,0:T(8,128)(2,1)S(1)}, bf16[2112,256]{1,0:T(8,128)(2,1)S(1)}, u32[]{:S(2)}, u32[]{:S(2)}) %collective-permute-start.16) | collective-permute-done | bytes 1081376 | tf_op jit(solution)/shard_map/ppermute | solution.py:38
  225.5 7.3 shard_map.369
  232.8 4.4 fusion.30
  237.2 6.4 multiply_convert_fusion.5
  243.6 4.0 collective-permute-done.18.x_ref
  247.9 4.7 fusion.22
  260.0 14.3 %collective-permute-done.24 = bf16[320,1024]{1,0:T(8,128)(2,1)S(1)} collective-permute-done((bf16[320,1024]{1,0:T(8,128)(2,1)}, bf16[320,1024]{1,0:T(8,128)(2,1)S(1)}, u32[]{:S(2)}, u32[]{:S(2)}) %collective-permute-start.24) | collective-permute-done | bytes 655392 | tf_op jit(solution)/shard_map/ppermute | solution.py:572
  280.8 9.2 %collective-permute-done.22.low_ref = bf16[1024,256]{1,0:T(8,128)(2,1)S(1)} collective-permute-done((bf16[1024,256]{1,0:T(8,128)(2,1)S(1)}, bf16[1024,256]{1,0:T(8,128)(2,1)S(1)}, u32[]{:S(2)}, u32[]{:S(2)}) %collective-permute-start.22) | collective-permute-done | bytes 524320 | tf_op jit(solution)/shard_map/ppermute | solution.py:38
  294.6 4.7 shard_map.370
  304.9 8.7 %shard_map.371.q_ref.kb_ref.vb_ref = bf16[640,1536]{1,0:T(8,128)(2,1)} custom-call(bf16[640,1024]{1,0:T(8,128)(2,1)} %pad_maximum_fusion.15.n_ref, bf16[1536,1024]{1,0:T(8,128)(2,1)} %bitcast.374, f32[640,128]{1,0:T(8,128)} %get-tuple-element.421.cos_ref.co_ref, f32[640,128]{1,0:T(8,128)} %get-tuple-element.424.sin_ref, ...), custom_call_target="tpu_custom_call" | custom-call | flops 1 | bytes 1 | tf_op jit(solution)/shard_map/pallas_call | solution.py:104
  313.6 6.5 shard_map.372.ka_ref.va_ref
  320.1 15.0 %shard_map.373 = (bf16[640,512]{1,0:T(8,128)(2,1)}, f32[4,2,1,640]{3,2,1,0:T(1,128)}) custom-call(bf16[640,1536]{1,0:T(8,128)(2,1)} %shard_map.371.q_ref.kb_ref.vb_ref, bf16[640,1024]{1,0:T(8,128)(2,1)} %shard_map.372.ka_ref.va_ref, bf16[640,1536]{1,0:T(8,128)(2,1)} %shard_map.371.q_ref.kb_ref.vb_ref, bf16[640,1024]{1,0:T(8,128)(2,1)} %shard_map.372.ka_ref.va_ref, ...), custom_call_target="tpu_custom_call" | custom-call | flops 1 | bytes 1 | tf_op jit(solution)/shard_map/pallas_call | solution.py:185
  335.1 5.7 collective-permute-done.26.x_ref
  356.8 15.6 %collective-permute-done.30.low_ref = bf16[2112,256]{1,0:T(8,128)(2,1)} collective-permute-done((bf16[2112,256]{1,0:T(8,128)(2,1)}, bf16[2112,256]{1,0:T(8,128)(2,1)}, u32[]{:S(2)}, u32[]{:S(2)}) %collective-permute-start.30) | collective-permute-done | bytes 1081376 | tf_op jit(solution)/shard_map/ppermute | solution.py:38
  374.2 7.7 shard_map.374
  382.0 4.6 fusion.8
  390.3 5.1 multiply_convert_fusion.3
  397.6 3.7 convolution_convert_fusion.1
  431.5 4.5 collective-permute-done.36
  443.2 24.2 %shard_map.375 = (bf16[640,512]{1,0:T(8,128)(2,1)}, bf16[640,512]{1,0:T(8,128)(2,1)}, bf16[640,512]{1,0:T(8,128)(2,1)}, bf16[640,512]{1,0:T(8,128)(2,1)}, bf16[640,512]{1,0:T(8,128)(2,1)}) custom-call(bf16[640,1536]{1,0:T(8,128)(2,1)} %shard_map.371.q_ref.kb_ref.vb_ref, bf16[640,1024]{1,0:T(8,128)(2,1)} %shard_map.372.ka_ref.va_ref, ...), custom_call_target="tpu_custom_call" | custom-call | flops 1 | bytes 1 | tf_op jit(solution)/shard_map/pallas_call | solution.py:270
  488.1 7.6 collective-permute-done.42
  506.1 6.3 multiply_convert_fusion.1
  540.2 28.4 %collective-permute-done.51 = bf16[2112,512]{1,0:T(8,128)(2,1)S(1)} collective-permute-done((bf16[2112,512]{1,0:T(8,128)(2,1)S(1)}, bf16[2112,512]{1,0:T(8,128)(2,1)S(1)}, u32[]{:S(2)}, u32[]{:S(2)}) %collective-permute-start.51) | collective-permute-done | bytes 2162720 | tf_op jit(solution)/shard_map/ppermute | solution.py:38
  576.9 17.5 %collective-permute-done.48 = bf16[2112,256]{1,0:T(8,128)(2,1)S(1)} collective-permute-done((bf16[2112,256]{1,0:T(8,128)(2,1)S(1)}, bf16[2112,256]{1,0:T(8,128)(2,1)S(1)}, u32[]{:S(2)}, u32[]{:S(2)}) %collective-permute-start.48) | collective-permute-done | bytes 1081376 | tf_op jit(solution)/shard_map/ppermute | solution.py:42
  594.4 9.8 %collective-permute-done.72 = bf16[1024,256]{1,0:T(8,128)(2,1)S(1)} collective-permute-done((bf16[1024,256]{1,0:T(8,128)(2,1)S(1)}, bf16[1024,256]{1,0:T(8,128)(2,1)S(1)}, u32[]{:S(2)}, u32[]{:S(2)}) %collective-permute-start.72) | collective-permute-done | bytes 524320 | tf_op jit(solution)/shard_map/ppermute | solution.py:42
  615.9 24.1 %shard_map.376 = (bf16[640,512]{1,0:T(8,128)(2,1)}, bf16[640,512]{1,0:T(8,128)(2,1)}, bf16[640,512]{1,0:T(8,128)(2,1)}, bf16[640,512]{1,0:T(8,128)(2,1)}, bf16[640,512]{1,0:T(8,128)(2,1)}) custom-call(bf16[640,1536]{1,0:T(8,128)(2,1)} %shard_map.366.q_ref.kb_ref.vb_ref.rest_0_, bf16[640,1024]{1,0:T(8,128)(2,1)} %shard_map.367.ka_ref.va_ref.rest_0_, ...), custom_call_target="tpu_custom_call" | custom-call | flops 1 | bytes 1 | tf_op jit(solution)/shard_map/pallas_call | solution.py:270
  668.2 9.5 %collective-permute-done.62 = bf16[2112,256]{1,0:T(8,128)(2,1)S(1)} collective-permute-done((bf16[2112,256]{1,0:T(8,128)(2,1)S(1)}, bf16[2112,256]{1,0:T(8,128)(2,1)S(1)}, u32[]{:S(2)}, u32[]{:S(2)}) %collective-permute-start.62) | collective-permute-done | bytes 1081376 | tf_op jit(solution)/shard_map/ppermute | solution.py:38
  680.6 13.1 %collective-permute-done.54 = bf16[320,1024]{1,0:T(8,128)(2,1)S(1)} collective-permute-done((bf16[320,1024]{1,0:T(8,128)(2,1)S(1)}, bf16[320,1024]{1,0:T(8,128)(2,1)S(1)}, u32[]{:S(2)}, u32[]{:S(2)}) %collective-permute-start.54) | collective-permute-done | bytes 655392 | tf_op jit(solution)/shard_map/ppermute | solution.py:620
  696.5 4.8 collective-permute-start.58
  710.0 6.5 collective-permute-done.57
  719.0 10.3 %collective-permute-done.60 = bf16[1088,512]{1,0:T(8,128)(2,1)} collective-permute-done((bf16[1088,512]{1,0:T(8,128)(2,1)S(1)}, bf16[1088,512]{1,0:T(8,128)(2,1)}, u32[]{:S(2)}, u32[]{:S(2)}) %collective-permute-start.60) | collective-permute-done | bytes 1114144 | tf_op jit(solution)/shard_map/ppermute | solution.py:42
  737.0 3.8 collective-permute-done.74
  742.6 3.9 collective-permute-done.63
  747.8 5.1 collective-permute-done.64
  755.2 9.2 %collective-permute-done.76 = bf16[1056,256]{1,0:T(8,128)(2,1)S(1)} collective-permute-done((bf16[1056,256]{1,0:T(8,128)(2,1)}, bf16[1056,256]{1,0:T(8,128)(2,1)S(1)}, u32[]{:S(2)}, u32[]{:S(2)}) %collective-permute-start.76) | collective-permute-done | bytes 540704 | tf_op jit(solution)/shard_map/ppermute | solution.py:38
  779.7 9.1 %collective-permute-done.68 = bf16[1056,256]{1,0:T(8,128)(2,1)S(1)} collective-permute-done((bf16[1056,256]{1,0:T(8,128)(2,1)}, bf16[1056,256]{1,0:T(8,128)(2,1)S(1)}, u32[]{:S(2)}, u32[]{:S(2)}) %collective-permute-start.68) | collective-permute-done | bytes 540704 | tf_op jit(solution)/shard_map/ppermute | solution.py:38
  793.9 9.6 %reduce-scatter.7.cloned.1.call-done = bf16[528,256]{1,0:T(8,128)(2,1)} async-done(((bf16[2112,256]{1,0:T(8,128)(2,1)}), bf16[528,256]{1,0:T(8,128)(2,1)}) %reduce-scatter.7.cloned.1.call-update) | async-done | bytes 270352 | tf_op jit(solution)/shard_map/reduce_scatter | solution.py:456
  806.4 5.4 collective-permute-done.65
  (722 shorter events, 334.1 us)
Async XLA Ops:
  7.2 121.5 %all-gather.4.cloned.1.call-start = ((), (), s32[]{:S(2)}) async-start(), calls=%async_computation.4 | async-start | bytes 2703360 | tf_op jit(solution)/shard_map/all_gather | solution.py:349
  11.5 76.6 %collective-permute-start.3 = (bf16[656,256]{1,0:T(8,128)(2,1)}, bf16[656,256]{1,0:T(8,128)(2,1)}, u32[]{:S(2)}, u32[]{:S(2)}) collective-permute-start(bf16[656,256]{1,0:T(8,128)(2,1)} %get-tuple-element.258), channel_id=1, source_target_pairs={{0,10},{1,2},{2,8},{3,0},{8,11},{9,3},{10,9},{11,1},{4,14},{5,6},{... | collective-permute-start | bytes 1007624 | tf_op jit(solution)/shard_map/ppermute | solution.py:397
  15.0 73.1 %collective-permute-start.2 = (bf16[656,256]{1,0:T(8,128)(2,1)}, bf16[656,256]{1,0:T(8,128)(2,1)}, u32[]{:S(2)}, u32[]{:S(2)}) collective-permute-start(bf16[656,256]{1,0:T(8,128)(2,1)} %get-tuple-element.259), channel_id=1, source_target_pairs={{0,2},{1,10},{2,0},{3,8},{8,3},{9,11},{10,1},{11,9},{4,6},{5,14},{... | collective-permute-start | bytes 1007624 | tf_op jit(solution)/shard_map/ppermute | solution.py:397
  15.6 72.6 %collective-permute-start.1 = (bf16[656,256]{1,0:T(8,128)(2,1)}, bf16[656,256]{1,0:T(8,128)(2,1)}, u32[]{:S(2)}, u32[]{:S(2)}) collective-permute-start(bf16[656,256]{1,0:T(8,128)(2,1)} %get-tuple-element.260), channel_id=1, source_target_pairs={{0,8},{1,0},{2,10},{3,2},{8,9},{9,1},{10,11},{11,3},{4,12},{5,4},{... | collective-permute-start | bytes 1007624 | tf_op jit(solution)/shard_map/ppermute | solution.py:397
  16.7 71.5 %collective-permute-start = (bf16[656,256]{1,0:T(8,128)(2,1)}, bf16[656,256]{1,0:T(8,128)(2,1)}, u32[]{:S(2)}, u32[]{:S(2)}) collective-permute-start(bf16[656,256]{1,0:T(8,128)(2,1)} %get-tuple-element.257), channel_id=1, source_target_pairs={{0,0},{1,8},{2,2},{3,10},{8,1},{9,9},{10,3},{11,11},{4,4},{5,12},{... | collective-permute-start | bytes 1007624 | tf_op jit(solution)/shard_map/ppermute | solution.py:397
  21.0 60.5 %collective-permute-start.7 = (s32[2,2,1280]{2,1,0:T(2,128)S(1)}, s32[2,2,1280]{2,1,0:T(2,128)}, u32[]{:S(2)}, u32[]{:S(2)}) collective-permute-start(s32[2,2,1280]{2,1,0:T(2,128)S(1)} %pad_add_fusion), channel_id=1, source_target_pairs={{0,8},{8,0},{1,9},{9,1},{2,10},{10,2},{3,11},{11,3},{4,12},{12,4},... | collective-permute-start | bytes 61448 | tf_op jit(solution)/shard_map/ppermute | solution.py:34
  79.1 107.9 %all-gather.6.cloned.1.call-start = ((), (), s32[]{:S(2)}) async-start(), calls=%async_computation.5 | async-start | bytes 1310720 | tf_op jit(solution)/shard_map/all_gather | solution.py:349
  89.9 22.2 %collective-permute-start.5 = (bf16[2048,256]{1,0:T(8,128)(2,1)S(1)}, bf16[2048,256]{1,0:T(8,128)(2,1)S(1)}, u32[]{:S(2)}, u32[]{:S(2)}) collective-permute-start(bf16[2048,256]{1,0:T(8,128)(2,1)S(1)} %bitcast.395), channel_id=1, source_target_pairs={{0,16},{16,0},{1,17},{17,1},{2,18},{18,2},{3,19},{19,3},{4,20},{20... | collective-permute-start | bytes 3145736 | tf_op jit(solution)/shard_map/ppermute | solution.py:38
  91.5 22.7 %collective-permute-start.6 = (bf16[2048,256]{1,0:T(8,128)(2,1)S(1)}, bf16[2048,256]{1,0:T(8,128)(2,1)S(1)}, u32[]{:S(2)}, u32[]{:S(2)}) collective-permute-start(bf16[2048,256]{1,0:T(8,128)(2,1)S(1)} %bitcast.396), channel_id=1, source_target_pairs={{0,4},{4,0},{1,5},{5,1},{2,6},{6,2},{3,7},{7,3},{8,12},{12,8},{9,1... | collective-permute-start | bytes 3145736 | tf_op jit(solution)/shard_map/ppermute | solution.py:42
  116.6 26.2 %collective-permute-start.10 = (bf16[320,1024]{1,0:T(8,128)(2,1)S(1)}, bf16[320,1024]{1,0:T(8,128)(2,1)}, u32[]{:S(2)}, u32[]{:S(2)}) collective-permute-start(bf16[320,1024]{1,0:T(8,128)(2,1)S(1)} %fusion.50), channel_id=1, source_target_pairs={{0,4},{1,5},{2,6},{3,7},{8,12},{9,13},{10,14},{11,15},{16,20},{17,... | collective-permute-start | bytes 1966088 | tf_op jit(solution)/shard_map/ppermute | solution.py:572
  128.7 58.3 %collective-permute-start.12 = (bf16[4224,256]{1,0:T(8,128)(2,1)}, bf16[4224,256]{1,0:T(8,128)(2,1)}, u32[]{:S(2)}, u32[]{:S(2)}) collective-permute-start(bf16[4224,256]{1,0:T(8,128)(2,1)} %all-gather.4.cloned.1.call-done.whole_ref), channel_id=1, source_target_pairs={{0,16},{16,0},{1,17},{17,1},{2,18},{18,2},{3,19},{19,3},{4,20},{20... | collective-permute-start | bytes 6488072 | tf_op jit(solution)/shard_map/ppermute | solution.py:38
  130.3 56.7 %collective-permute-start.13 = (bf16[4224,256]{1,0:T(8,128)(2,1)}, bf16[4224,256]{1,0:T(8,128)(2,1)}, u32[]{:S(2)}, u32[]{:S(2)}) collective-permute-start(bf16[4224,256]{1,0:T(8,128)(2,1)} %all-gather.4.cloned.1.call-done.whole_ref), channel_id=1, source_target_pairs={{0,4},{4,0},{1,5},{5,1},{2,6},{6,2},{3,7},{7,3},{8,12},{12,8},{9,1... | collective-permute-start | bytes 6488072 | tf_op jit(solution)/shard_map/ppermute | solution.py:42
  135.7 112.2 %all-gather.8.cloned.1.call-start = ((), (), s32[]{:S(2)}) async-start(), calls=%async_computation.6 | async-start | bytes 2703360 | tf_op jit(solution)/shard_map/all_gather | solution.py:349
  192.4 539.3 %reduce-scatter.9.cloned.1.call-start = ((), (), s32[]{:S(2)}) async-start(), calls=%async_computation.9 | async-start | bytes 1310720 | tf_op jit(solution)/shard_map/reduce_scatter | solution.py:456
  194.1 25.6 %collective-permute-start.16 = (bf16[2112,256]{1,0:T(8,128)(2,1)S(1)}, bf16[2112,256]{1,0:T(8,128)(2,1)S(1)}, u32[]{:S(2)}, u32[]{:S(2)}) collective-permute-start(bf16[2112,256]{1,0:T(8,128)(2,1)S(1)} %slice.858), channel_id=1, source_target_pairs={{0,16},{16,0},{1,17},{17,1},{2,18},{18,2},{3,19},{19,3},{4,20},{20... | collective-permute-start | bytes 3244040 | tf_op jit(solution)/shard_map/ppermute | solution.py:38
  197.1 26.2 %collective-permute-start.17 = (bf16[2112,256]{1,0:T(8,128)(2,1)S(1)}, bf16[2112,256]{1,0:T(8,128)(2,1)S(1)}, u32[]{:S(2)}, u32[]{:S(2)}) collective-permute-start(bf16[2112,256]{1,0:T(8,128)(2,1)S(1)} %slice.859), channel_id=1, source_target_pairs={{0,4},{4,0},{1,5},{5,1},{2,6},{6,2},{3,7},{7,3},{8,12},{12,8},{9,1... | collective-permute-start | bytes 3244040 | tf_op jit(solution)/shard_map/ppermute | solution.py:42
  201.4 31.4 %collective-permute-start.15 = (bf16[320,1024]{1,0:T(8,128)(2,1)S(1)}, bf16[320,1024]{1,0:T(8,128)(2,1)}, u32[]{:S(2)}, u32[]{:S(2)}) collective-permute-start(bf16[320,1024]{1,0:T(8,128)(2,1)S(1)} %multiply_convert_fusion.8), channel_id=1, source_target_pairs={{0,8},{8,0},{1,9},{9,1},{2,10},{10,2},{3,11},{11,3},{4,12},{12,4},... | collective-permute-start | bytes 1966088 | tf_op jit(solution)/shard_map/ppermute | solution.py:34
  223.3 24.3 %collective-permute-start.18 = (bf16[2048,256]{1,0:T(8,128)(2,1)}, bf16[2048,256]{1,0:T(8,128)(2,1)S(1)}, u32[]{:S(2)}, u32[]{:S(2)}) collective-permute-start(bf16[2048,256]{1,0:T(8,128)(2,1)} %all-gather.6.cloned.1.call-done.whole_ref), channel_id=1, source_target_pairs={{0,16},{16,0},{1,17},{17,1},{2,18},{18,2},{3,19},{19,3},{4,20},{20... | collective-permute-start | bytes 3145736 | tf_op jit(solution)/shard_map/ppermute | solution.py:38
  223.7 24.1 %collective-permute-start.19 = (bf16[2048,256]{1,0:T(8,128)(2,1)}, bf16[2048,256]{1,0:T(8,128)(2,1)}, u32[]{:S(2)}, u32[]{:S(2)}) collective-permute-start(bf16[2048,256]{1,0:T(8,128)(2,1)} %all-gather.6.cloned.1.call-done.whole_ref), channel_id=1, source_target_pairs={{0,4},{4,0},{1,5},{5,1},{2,6},{6,2},{3,7},{7,3},{8,12},{12,8},{9,1... | collective-permute-start | bytes 3145736 | tf_op jit(solution)/shard_map/ppermute | solution.py:42
  291.9 48.9 %collective-permute-start.26 = (bf16[4224,256]{1,0:T(8,128)(2,1)}, bf16[4224,256]{1,0:T(8,128)(2,1)S(1)}, u32[]{:S(2)}, u32[]{:S(2)}) collective-permute-start(bf16[4224,256]{1,0:T(8,128)(2,1)} %all-gather.8.cloned.1.call-done.whole_ref), channel_id=1, source_target_pairs={{0,16},{16,0},{1,17},{17,1},{2,18},{18,2},{3,19},{19,3},{4,20},{20... | collective-permute-start | bytes 6488072 | tf_op jit(solution)/shard_map/ppermute | solution.py:38
  292.7 48.9 %collective-permute-start.27 = (bf16[4224,256]{1,0:T(8,128)(2,1)}, bf16[4224,256]{1,0:T(8,128)(2,1)S(1)}, u32[]{:S(2)}, u32[]{:S(2)}) collective-permute-start(bf16[4224,256]{1,0:T(8,128)(2,1)} %all-gather.8.cloned.1.call-done.whole_ref), channel_id=1, source_target_pairs={{0,4},{4,0},{1,5},{5,1},{2,6},{6,2},{3,7},{7,3},{8,12},{12,8},{9,1... | collective-permute-start | bytes 6488072 | tf_op jit(solution)/shard_map/ppermute | solution.py:42
  345.8 26.6 %collective-permute-start.30 = (bf16[2112,256]{1,0:T(8,128)(2,1)}, bf16[2112,256]{1,0:T(8,128)(2,1)}, u32[]{:S(2)}, u32[]{:S(2)}) collective-permute-start(bf16[2112,256]{1,0:T(8,128)(2,1)} %slice.874), channel_id=1, source_target_pairs={{0,16},{16,0},{1,17},{17,1},{2,18},{18,2},{3,19},{19,3},{4,20},{20... | collective-permute-start | bytes 3244040 | tf_op jit(solution)/shard_map/ppermute | solution.py:38
  347.9 26.3 %collective-permute-start.31 = (bf16[2112,256]{1,0:T(8,128)(2,1)}, bf16[2112,256]{1,0:T(8,128)(2,1)}, u32[]{:S(2)}, u32[]{:S(2)}) collective-permute-start(bf16[2112,256]{1,0:T(8,128)(2,1)} %slice.875), channel_id=1, source_target_pairs={{0,4},{4,0},{1,5},{5,1},{2,6},{6,2},{3,7},{7,3},{8,12},{12,8},{9,1... | collective-permute-start | bytes 3244040 | tf_op jit(solution)/shard_map/ppermute | solution.py:42
  351.6 30.3 %collective-permute-start.37 = (bf16[320,1024]{1,0:T(8,128)(2,1)}, bf16[320,1024]{1,0:T(8,128)(2,1)}, u32[]{:S(2)}, u32[]{:S(2)}) collective-permute-start(bf16[320,1024]{1,0:T(8,128)(2,1)} %slice.882), channel_id=1, source_target_pairs={{0,8},{8,0},{1,9},{9,1},{2,10},{10,2},{3,11},{11,3},{4,12},{12,4},... | collective-permute-start | bytes 1966088 | tf_op jit(solution)/shard_map/ppermute | solution.py:34
  354.1 32.5 %collective-permute-start.29 = (bf16[320,1024]{1,0:T(8,128)(2,1)}, bf16[320,1024]{1,0:T(8,128)(2,1)}, u32[]{:S(2)}, u32[]{:S(2)}) collective-permute-start(bf16[320,1024]{1,0:T(8,128)(2,1)} %multiply_convert_fusion.6), channel_id=1, source_target_pairs={{0,8},{8,0},{1,9},{9,1},{2,10},{10,2},{3,11},{11,3},{4,12},{12,4},... | collective-permute-start | bytes 1966088 | tf_op jit(solution)/shard_map/ppermute | solution.py:34
  435.9 61.0 %collective-permute-start.46 = (bf16[2112,512]{1,0:T(8,128)(2,1)}, bf16[2112,512]{1,0:T(8,128)(2,1)}, u32[]{:S(2)}, u32[]{:S(2)}) collective-permute-start(bf16[2112,512]{1,0:T(8,128)(2,1)} %pad_maximum_fusion.3), channel_id=1, source_target_pairs={{0,16},{16,0},{1,17},{17,1},{2,18},{18,2},{3,19},{19,3},{4,20},{20... | collective-permute-start | bytes 6488072 | tf_op jit(solution)/shard_map/ppermute | solution.py:38
  438.3 58.7 %collective-permute-start.47 = (bf16[2112,512]{1,0:T(8,128)(2,1)}, bf16[2112,512]{1,0:T(8,128)(2,1)}, u32[]{:S(2)}, u32[]{:S(2)}) collective-permute-start(bf16[2112,512]{1,0:T(8,128)(2,1)} %fusion.33), channel_id=1, source_target_pairs={{0,4},{4,0},{1,5},{5,1},{2,6},{6,2},{3,7},{7,3},{8,12},{12,8},{9,1... | collective-permute-start | bytes 6488072 | tf_op jit(solution)/shard_map/ppermute | solution.py:42
  473.6 22.1 %collective-permute-start.40 = (bf16[320,1024]{1,0:T(8,128)(2,1)S(1)}, bf16[320,1024]{1,0:T(8,128)(2,1)S(1)}, u32[]{:S(2)}, u32[]{:S(2)}) collective-permute-start(bf16[320,1024]{1,0:T(8,128)(2,1)S(1)} %slice.1222), channel_id=1, source_target_pairs={{0,8},{8,0},{1,9},{9,1},{2,10},{10,2},{3,11},{11,3},{4,12},{12,4},... | collective-permute-start | bytes 1966088 | tf_op jit(solution)/shard_map/ppermute | solution.py:34
  483.2 56.0 %collective-permute-start.70 = (bf16[1024,512]{1,0:T(8,128)(2,1)S(1)}, bf16[1024,512]{1,0:T(8,128)(2,1)S(1)}, u32[]{:S(2)}, u32[]{:S(2)}) collective-permute-start(bf16[1024,512]{1,0:T(8,128)(2,1)S(1)} %concatenate.600), channel_id=1, source_target_pairs={{0,16},{16,0},{1,17},{17,1},{2,18},{18,2},{3,19},{19,3},{4,20},{20... | collective-permute-start | bytes 3145736 | tf_op jit(solution)/shard_map/ppermute | solution.py:38
  495.6 44.6 %collective-permute-start.71 = (bf16[1024,512]{1,0:T(8,128)(2,1)S(1)}, bf16[1024,512]{1,0:T(8,128)(2,1)S(1)}, u32[]{:S(2)}, u32[]{:S(2)}) collective-permute-start(bf16[1024,512]{1,0:T(8,128)(2,1)S(1)} %pad_maximum_fusion.25), channel_id=1, source_target_pairs={{0,4},{4,0},{1,5},{5,1},{2,6},{6,2},{3,7},{7,3},{8,12},{12,8},{9,1... | collective-permute-start | bytes 3145736 | tf_op jit(solution)/shard_map/ppermute | solution.py:42
  518.5 50.0 %collective-permute-start.51 = (bf16[2112,512]{1,0:T(8,128)(2,1)S(1)}, bf16[2112,512]{1,0:T(8,128)(2,1)S(1)}, u32[]{:S(2)}, u32[]{:S(2)}) collective-permute-start(bf16[2112,512]{1,0:T(8,128)(2,1)S(1)} %pad_maximum_fusion.5), channel_id=1, source_target_pairs={{0,16},{16,0},{1,17},{17,1},{2,18},{18,2},{3,19},{19,3},{4,20},{20... | collective-permute-start | bytes 6488072 | tf_op jit(solution)/shard_map/ppermute | solution.py:38
  521.2 50.0 %collective-permute-start.52 = (bf16[2112,512]{1,0:T(8,128)(2,1)S(1)}, bf16[2112,512]{1,0:T(8,128)(2,1)S(1)}, u32[]{:S(2)}, u32[]{:S(2)}) collective-permute-start(bf16[2112,512]{1,0:T(8,128)(2,1)S(1)} %fusion.37), channel_id=1, source_target_pairs={{0,4},{4,0},{1,5},{5,1},{2,6},{6,2},{3,7},{7,3},{8,12},{12,8},{9,1... | collective-permute-start | bytes 6488072 | tf_op jit(solution)/shard_map/ppermute | solution.py:42
  536.6 57.8 %collective-permute-start.48 = (bf16[2112,256]{1,0:T(8,128)(2,1)S(1)}, bf16[2112,256]{1,0:T(8,128)(2,1)S(1)}, u32[]{:S(2)}, u32[]{:S(2)}) collective-permute-start(bf16[2112,256]{1,0:T(8,128)(2,1)S(1)} %slice.908), channel_id=1, source_target_pairs={{0,4},{4,0},{1,5},{5,1},{2,6},{6,2},{3,7},{7,3},{8,12},{12,8},{9,1... | collective-permute-start | bytes 3244040 | tf_op jit(solution)/shard_map/ppermute | solution.py:42
  539.2 55.2 %collective-permute-start.49 = (bf16[2112,256]{1,0:T(8,128)(2,1)S(1)}, bf16[2112,256]{1,0:T(8,128)(2,1)S(1)}, u32[]{:S(2)}, u32[]{:S(2)}) collective-permute-start(bf16[2112,256]{1,0:T(8,128)(2,1)S(1)} %slice.911), channel_id=1, source_target_pairs={{0,16},{16,0},{1,17},{17,1},{2,18},{18,2},{3,19},{19,3},{4,20},{20... | collective-permute-start | bytes 3244040 | tf_op jit(solution)/shard_map/ppermute | solution.py:38
  571.7 32.5 %collective-permute-start.72 = (bf16[1024,256]{1,0:T(8,128)(2,1)S(1)}, bf16[1024,256]{1,0:T(8,128)(2,1)S(1)}, u32[]{:S(2)}, u32[]{:S(2)}) collective-permute-start(bf16[1024,256]{1,0:T(8,128)(2,1)S(1)} %slice.971), channel_id=1, source_target_pairs={{0,4},{4,0},{1,5},{5,1},{2,6},{6,2},{3,7},{7,3},{8,12},{12,8},{9,1... | collective-permute-start | bytes 1572872 | tf_op jit(solution)/shard_map/ppermute | solution.py:42
  574.1 30.1 %collective-permute-start.73 = (bf16[1024,256]{1,0:T(8,128)(2,1)S(1)}, bf16[1024,256]{1,0:T(8,128)(2,1)S(1)}, u32[]{:S(2)}, u32[]{:S(2)}) collective-permute-start(bf16[1024,256]{1,0:T(8,128)(2,1)S(1)} %slice.974), channel_id=1, source_target_pairs={{0,16},{16,0},{1,17},{17,1},{2,18},{18,2},{3,19},{19,3},{4,20},{20... | collective-permute-start | bytes 1572872 | tf_op jit(solution)/shard_map/ppermute | solution.py:38
  576.9 35.0 %collective-permute-start.45 = (bf16[320,1024]{1,0:T(8,128)(2,1)}, bf16[320,1024]{1,0:T(8,128)(2,1)}, u32[]{:S(2)}, u32[]{:S(2)}) collective-permute-start(bf16[320,1024]{1,0:T(8,128)(2,1)} %get-tuple-element.206), channel_id=1, source_target_pairs={{0,8},{8,0},{1,9},{9,1},{2,10},{10,2},{3,11},{11,3},{4,12},{12,4},... | collective-permute-start | bytes 1966088 | tf_op jit(solution)/shard_map/ppermute | solution.py:34
  605.6 130.9 %reduce-scatter.11.cloned.1.call-start = ((), (), s32[]{:S(2)}) async-start(), calls=%async_computation.10 | async-start | bytes 2703360 | tf_op jit(solution)/shard_map/reduce_scatter | solution.py:456
  611.7 162.3 %reduce-scatter.5.cloned.1.call-start = ((), (), s32[]{:S(2)}) async-start(), calls=%async_computation.7 | async-start | bytes 2703360 | tf_op jit(solution)/shard_map/reduce_scatter | solution.py:456
  644.1 49.7 %collective-permute-start.50 = (bf16[320,1024]{1,0:T(8,128)(2,1)S(1)}, bf16[320,1024]{1,0:T(8,128)(2,1)S(1)}, u32[]{:S(2)}, u32[]{:S(2)}) collective-permute-start(bf16[320,1024]{1,0:T(8,128)(2,1)S(1)} %slice.1219), channel_id=1, source_target_pairs={{0,8},{8,0},{1,9},{9,1},{2,10},{10,2},{3,11},{11,3},{4,12},{12,4},... | collective-permute-start | bytes 1966088 | tf_op jit(solution)/shard_map/ppermute | solution.py:34
  651.0 26.8 %collective-permute-start.62 = (bf16[2112,256]{1,0:T(8,128)(2,1)S(1)}, bf16[2112,256]{1,0:T(8,128)(2,1)S(1)}, u32[]{:S(2)}, u32[]{:S(2)}) collective-permute-start(bf16[2112,256]{1,0:T(8,128)(2,1)S(1)} %slice.949), channel_id=1, source_target_pairs={{0,16},{16,0},{1,17},{17,1},{2,18},{18,2},{3,19},{19,3},{4,20},{20... | collective-permute-start | bytes 3244040 | tf_op jit(solution)/shard_map/ppermute | solution.py:38
  653.4 26.7 %collective-permute-start.61 = (bf16[2112,256]{1,0:T(8,128)(2,1)S(1)}, bf16[2112,256]{1,0:T(8,128)(2,1)S(1)}, u32[]{:S(2)}, u32[]{:S(2)}) collective-permute-start(bf16[2112,256]{1,0:T(8,128)(2,1)S(1)} %slice.944), channel_id=1, source_target_pairs={{0,4},{4,0},{1,5},{5,1},{2,6},{6,2},{3,7},{7,3},{8,12},{12,8},{9,1... | collective-permute-start | bytes 3244040 | tf_op jit(solution)/shard_map/ppermute | solution.py:42
  655.5 38.2 %collective-permute-start.54 = (bf16[320,1024]{1,0:T(8,128)(2,1)S(1)}, bf16[320,1024]{1,0:T(8,128)(2,1)S(1)}, u32[]{:S(2)}, u32[]{:S(2)}) collective-permute-start(bf16[320,1024]{1,0:T(8,128)(2,1)S(1)} %fusion.58), channel_id=1, source_target_pairs={{4,0},{5,1},{6,2},{7,3},{12,8},{13,9},{14,10},{15,11},{20,16},{21,... | collective-permute-start | bytes 1966088 | tf_op jit(solution)/shard_map/ppermute | solution.py:620
  664.0 55.0 %collective-permute-start.59 = (bf16[1024,512]{1,0:T(8,128)(2,1)}, bf16[1024,512]{1,0:T(8,128)(2,1)}, u32[]{:S(2)}, u32[]{:S(2)}) collective-permute-start(bf16[1024,512]{1,0:T(8,128)(2,1)} %concatenate.598), channel_id=1, source_target_pairs={{0,16},{16,0},{1,17},{17,1},{2,18},{18,2},{3,19},{19,3},{4,20},{20... | collective-permute-start | bytes 3145736 | tf_op jit(solution)/shard_map/ppermute | solution.py:38
  702.8 26.5 %collective-permute-start.60 = (bf16[1088,512]{1,0:T(8,128)(2,1)S(1)}, bf16[1088,512]{1,0:T(8,128)(2,1)}, u32[]{:S(2)}, u32[]{:S(2)}) collective-permute-start(bf16[1088,512]{1,0:T(8,128)(2,1)S(1)} %pad_maximum_fusion.21), channel_id=1, source_target_pairs={{0,4},{4,0},{1,5},{5,1},{2,6},{6,2},{3,7},{7,3},{8,12},{12,8},{9,1... | collective-permute-start | bytes 3342344 | tf_op jit(solution)/shard_map/ppermute | solution.py:42
  709.7 93.8 %reduce-scatter.7.cloned.1.call-start = ((), (), s32[]{:S(2)}) async-start(), calls=%async_computation.8 | async-start | bytes 1351680 | tf_op jit(solution)/shard_map/reduce_scatter | solution.py:456
  736.5 27.9 %collective-permute-start.76 = (bf16[1056,256]{1,0:T(8,128)(2,1)}, bf16[1056,256]{1,0:T(8,128)(2,1)S(1)}, u32[]{:S(2)}, u32[]{:S(2)}) collective-permute-start(bf16[1056,256]{1,0:T(8,128)(2,1)} %reduce-scatter.11.cloned.1.call-done), channel_id=1, source_target_pairs={{0,16},{16,0},{1,17},{17,1},{2,18},{18,2},{3,19},{19,3},{4,20},{20... | collective-permute-start | bytes 1622024 | tf_op jit(solution)/shard_map/ppermute | solution.py:38
  741.0 26.1 %collective-permute-start.75 = (bf16[512,512]{1,0:T(8,128)(2,1)S(1)}, bf16[512,512]{1,0:T(8,128)(2,1)S(1)}, u32[]{:S(2)}, u32[]{:S(2)}) collective-permute-start(bf16[512,512]{1,0:T(8,128)(2,1)S(1)} %maximum_select_fusion.13), channel_id=1, source_target_pairs={{0,8},{8,0},{1,9},{9,1},{2,10},{10,2},{3,11},{11,3},{4,12},{12,4},... | collective-permute-start | bytes 1572872 | tf_op jit(solution)/shard_map/ppermute | solution.py:34
  (174 other events, 1675.8 us)
Sparse Core Ops, SparseCore 0:
  79.2 45.6 all-gather.3
  135.8 24.5 all-gather.5
  192.5 46.8 all-gather.7
  605.7 31.1 reduce-scatter.8
  639.2 43.5 reduce-scatter.10
  709.9 52.2 reduce-scatter.4
  776.9 26.6 reduce-scatter.6

commit v3 on v2

--- a/solution.py
+++ b/solution.py
@@ -66,53 +66,49 @@
     return values * cos + other * sin
 
 
-def project(normed, weight, cos, sin, kinds, mix):
+def project(normed, turned_weight, plain_weight, skip, cos, sin, mix):
     rows, block = normed.shape[0], 256
-    steps = weight.shape[0] // block
-    turned = sum(kinds)
-
-    def kernel(n_ref, w_ref, cos_ref, sin_ref, *rest):
+    turned = turned_weight.shape[0] // block - skip
+    plain = plain_weight.shape[0] // block
+
+    def kernel(n_ref, t_ref, p_ref, cos_ref, sin_ref, *rest):
         out_ref = rest[-1]
         step = pl.program_id(0)
-        result = dot_nt(n_ref[...], w_ref[...])
 
         @pl.when(step < turned)
         def _():
+            result = dot_nt(n_ref[...], t_ref[...])
             out_ref[...] = rotated(result, cos_ref, sin_ref).astype(bf16)
 
         @pl.when(step >= turned)
         def _():
-            if mix is None:
-                out_ref[...] = result.astype(bf16)
-            else:
-                out_ref[...] = (0.5 * result + 0.5 * rest[0][...].astype(f32)).astype(bf16)
+            result = dot_nt(n_ref[...], p_ref[...])
+            if mix is not None:
+                result = 0.5 * result + 0.5 * rest[0][...].astype(f32)
+            out_ref[...] = result.astype(bf16)
 
     whole = lambda shape: pl.BlockSpec(shape, lambda i: (0, 0))
+    later = lambda i: jnp.maximum(i - turned, 0)
     in_specs = [
         whole((rows, D)),
-        pl.BlockSpec((block, D), lambda i: (i, 0)),
+        pl.BlockSpec((block, D), lambda i: (skip + jnp.minimum(i, turned - 1), 0)),
+        pl.BlockSpec((block, D), lambda i: (later(i), 0)),
         whole((rows, PAIR)),
         whole((rows, PAIR)),
     ]
-    operands = [normed, weight, cos, sin]
+    operands = [normed, turned_weight, plain_weight, cos, sin]
     if mix is not None:
-        skip = mix.shape[1] // block - (steps - turned)
-        in_specs.append(
-            pl.BlockSpec((rows, block), lambda i: (0, jnp.maximum(i - turned, 0) + skip))
-        )
+        before = mix.shape[1] // block - plain
+        in_specs.append(pl.BlockSpec((rows, block), lambda i: (0, before + later(i))))
         operands.append(mix)
     return pl.pallas_call(
         kernel,
-        grid=(steps,),
+        grid=(turned + plain,),
         in_specs=in_specs,
         out_specs=pl.BlockSpec((rows, block), lambda i: (0, i)),
-        out_shape=jax.ShapeDtypeStruct((rows, weight.shape[0]), bf16),
+        out_shape=jax.ShapeDtypeStruct((rows, (turned + plain) * block), bf16),
         compiler_params=VMEM,
-        cost_estimate=pl.CostEstimate(
-            flops=1,
-            bytes_accessed=1,
-            transcendentals=0,
-        ),
+        cost_estimate=pl.CostEstimate(flops=1, bytes_accessed=1, transcendentals=0),
     )(*operands)
 
 
@@ -383,29 +379,28 @@
         ffn_whole_one = gather_col(after(ffn_local_one, vo_whole_one))
         attn_whole_two = gather_col(after(attn_local_two, ffn_whole_one))
 
-        pieces = jnp.concatenate(
-            [
-                tokens.reshape(col_count, own_rows, quarter),
-                out_grad.reshape(col_count, own_rows, quarter),
-                jnp.broadcast_to(small[None], (col_count,) + small.shape),
-            ],
-            axis=1,
-        )
-        got = []
-        for k in range(col_count):
-            piece = lax.dynamic_index_in_dim(pieces, col ^ k, 0, keepdims=False)
-            got.append(lax.ppermute(piece, ("core", "col"), rounds[k]))
-        got = jnp.stack(got)
-        got = jnp.concatenate(
-            [
-                lax.dynamic_index_in_dim(got, place(p) ^ slot, 0, keepdims=False)
-                for p in range(col_count)
-            ],
-            axis=1,
+        def spread(arrays, *milestones):
+            pieces = after(jnp.concatenate(arrays, axis=1), *milestones)
+            got = []
+            for k in range(col_count):
+                piece = lax.dynamic_index_in_dim(pieces, col ^ k, 0, keepdims=False)
+                got.append(lax.ppermute(piece, ("core", "col"), rounds[k]))
+            got = jnp.stack(got)
+            return jnp.concatenate(
+                [
+                    lax.dynamic_index_in_dim(got, place(p) ^ slot, 0, keepdims=False)
+                    for p in range(col_count)
+                ],
+                axis=1,
+            )
+
+        by_piece = lambda array: array.reshape(col_count, own_rows, quarter)
+        got = spread(
+            [by_piece(tokens), jnp.broadcast_to(small[None], (col_count,) + small.shape)],
+            vo_whole_one,
         )
         residual = got[:own_rows].astype(f32)
-        last_grad = got[own_rows : 2 * own_rows].astype(f32)
-        small = got[2 * own_rows :].astype(f32)
+        small = got[own_rows:].astype(f32)
         gains = small[0:4] + small[4:8] + small[8:12]
 
         both = jnp.stack([segment_ids, prompt_reach])
@@ -479,11 +474,12 @@
                 far = [stack([f for _, f in parts]) for parts in (by_x, by_y)]
                 self.sent = (swap_x(far[0]), swap_y(far[1]))
 
-            def second(self, *milestones):
+            def second(self, milestones=(), before_y=()):
                 sent = after(self.sent, *milestones)
                 totals = [add(a, b) for a, b in zip(self.near, sent)]
                 self.near = [t[:, :quarter] for t in totals]
-                self.sent = (swap_y(totals[0][:, quarter:]), swap_x(totals[1][:, quarter:]))
+                far = [t[:, quarter:] for t in totals]
+                self.sent = (swap_y(after(far[0], *before_y)), swap_x(far[1]))
 
             def last(self, *milestones):
                 sent = after(self.sent, *milestones)
@@ -505,8 +501,7 @@
         def last_ffn(returned, *milestones):
             first, second = returned.last(*milestones)
             rows = first.shape[0] * 2 // 3
-            down = jnp.concatenate([first[rows:], second[rows:]])
-            return pack_parts([first[:rows], second[:rows], down])
+            return [first[:rows], second[:rows], jnp.concatenate([first[rows:], second[rows:]])]
 
         def sides(left, right, x_first):
             stay, go = ((0, 1), (2, 3)) if x_first else ((0, 2), (1, 3))
@@ -565,16 +560,14 @@
                 [array[:, p * quarter : (p + 1) * quarter] for p in (1, 0, 3, 2)], axis=1
             )
 
-        def attn_forward(value, weights, gain, mix, start):
-            w_qkv, w_out = weights
-            width = w_out.shape[0]
+        def attn_forward(value, weights, gain, mix, start, *milestones):
+            w_qk, w_value, w_out = weights
             normed_own, factor = normalize(value, gain)
-            normed_first = both_cores(flip_row(lax.ppermute(normed_own, "row", [(0, 1)])))
+            normed_first = both_cores(flip_row(lax.ppermute(after(normed_own, *milestones), "row", [(0, 1)])))
             normed = both_cores(normed_own)
-            own = project(normed, w_qkv, cos_own, sin_own, (1, 1, 1, 1, 0, 0), mix and mix[0])
-            first = project(
-                normed_first, w_qkv[width:], cos_first, sin_first, (1, 1, 0, 0), mix and mix[1]
-            )
+            skip = w_qk.shape[0] // 512
+            own = project(normed, w_qk, w_value, 0, cos_own, sin_own, mix and mix[0])
+            first = project(normed_first, w_qk, w_value, skip, cos_first, sin_first, mix and mix[1])
             mixture, totals = attend(own, first, bias)
             mixture = after(mixture, *start(normed_first))
             result = value + core_sum(dot_nn(mixture, w_out))
@@ -590,7 +583,7 @@
             hidden = after(hidden, *deadline)
             return value + core_sum(dot_nn(hidden, w_down)), (value, factor, normed, gate, up, hidden)
 
-        def ffn_backward(grad, weights, gain, saved, kinds):
+        def ffn_backward(grad, weights, gain, saved, kinds, late):
             w_gate, w_up, w_down = weights
             value, factor, normed, gate, up, hidden = saved
             grad_full = both_cores(grad.astype(bf16))
@@ -599,15 +592,15 @@
             grad_gate = (grad_hidden * up * sig * (1.0 + gate * (1.0 - sig))).astype(bf16)
             grad_up = (grad_hidden * gate * sig).astype(bf16)
             grad_normed = core_sum(dot_nn(grad_gate, w_gate) + dot_nn(grad_up, w_up))
-            pairs = ((grad_gate, normed), (grad_up, normed), (hidden, grad_full))
+            lefts = after((grad_gate, grad_up, hidden), *late)
+            pairs = tuple(zip(lefts, (normed, normed, grad_full)))
             grads = [sides(*pair, k) for pair, k in zip(pairs[:2], kinds)]
             grads.append((dot_tn(*pairs[2]).astype(bf16),))
             step, gain_grad = normalize_back(grad_normed, value, factor, gain)
             return grad + step, grads, gain_grad
 
         def attn_backward(grad, weights, gain, saved, extra, milestones, late):
-            w_qkv, w_out = weights
-            width = w_out.shape[0]
+            w_qk, w_value, w_out = weights
             value, factor, normed, normed_first, own, first, mixture, totals = saved
             grad_full = both_cores(grad.astype(bf16))
             grad_mixture = after(dot_nt(grad_full, w_out).astype(bf16), *milestones)
@@ -615,9 +608,10 @@
                 own, first, bias, totals, mixture, grad_mixture, rope, extra
             )
             gk_first, gv_first = after((gk_first, gv_first), *late)
-            w_query, w_key, w_value = w_qkv[:width], w_qkv[width : 2 * width], w_qkv[2 * width :]
+            w_query, w_key = jnp.split(w_qk, 2)
             operand = core_sum(dot_nn(gk_first, w_key) + dot_nn(gv_first, w_value)).astype(bf16)
-            sent = flip_row(lax.ppermute(operand, "row", [(1, 0)])).astype(f32)
+            sent_raw = lax.ppermute(operand, "row", [(1, 0)])
+            sent = flip_row(sent_raw).astype(f32)
             grad_normed = core_sum(dot_nn(gq, w_query) + dot_nn(gk, w_key) + dot_nn(gv, w_value))
             done = gq
             gq, gk, gv, gk_first, gv_first = after((gq, gk, gv, gk_first, gv_first), operand)
@@ -628,20 +622,27 @@
                 dot_tn(mixture, grad_full).astype(bf16),
             ]
             step, gain_grad = normalize_back(grad_normed + sent, value, factor, gain)
-            return grad + step, grads, gain_grad, (gv_first, gv), done
-
-        cross = Crossing(attn_whole_one, got)
-        attn_one = cross.complete((3, 1), bias, cos_own, cos_first)
-        cross_ffn = Crossing(ffn_whole_one, *cross.both)
+            return grad + step, grads, gain_grad, (gv_first, gv), (done, operand, sent_raw)
+
+        cross_one = Crossing(attn_whole_one)
+        attn_one = cross_one.complete((2, 1, 1), bias, cos_own, cos_first)
+        crossings = []
+
+        def start_ffn_one(normed_first):
+            crossings.append(Crossing(ffn_whole_one, normed_first, *cross_one.both))
+            return (*crossings[0].sides, attn_whole_two)
+
         residual, kept_attn_one = attn_forward(
-            residual, attn_one, gains[0], None, lambda _: (*cross_ffn.sides, attn_whole_two)
+            residual, attn_one, gains[0], None, start_ffn_one, *cross_one.both
         )
         own_one, first_one = kept_attn_one[4], kept_attn_one[5]
+        cross_ffn = crossings[0]
         ffn_one = cross_ffn.complete((1, 1, 1))
         cross = Crossing(attn_whole_two, *cross_ffn.both)
         ffn_whole_two = gather_col(after(ffn_local_two, attn_whole_two))
         residual, kept_ffn_one = ffn_forward(residual, ffn_one, gains[1], (*cross.sides, ffn_whole_two))
-        attn_two = cross.complete((3, 1))
+        attn_two = cross.complete((2, 1, 1))
+        residual = after(residual, *cross.both)
         ffn_two = []
 
         def start_ffn_two(normed_first):
@@ -652,7 +653,8 @@
             residual, attn_two, gains[2], (own_one, first_one), start_ffn_two
         )
         ffn_two = ffn_two[0].complete((1, 1, 1))
-        residual, kept_ffn_two = ffn_forward(residual, ffn_two, gains[3], ())
+        last_grad = spread([by_piece(out_grad)], residual)
+        residual, kept_ffn_two = ffn_forward(residual, ffn_two, gains[3], (last_grad,))
         output = unspread(residual.astype(bf16))
 
         kinds = (True, False)
@@ -661,38 +663,41 @@
             return [a for pair in grads for a in pair]
 
         grad, g_ffn_two, gain_ffn_two = ffn_backward(
-            last_grad, ffn_two, gains[3], kept_ffn_two, kinds
+            last_grad.astype(f32), ffn_two, gains[3], kept_ffn_two, kinds, ()
         )
         r_ffn_two = return_ffn(*g_ffn_two)
         grad, g_attn_two, gain_attn_two, extra, done_attn_two = attn_backward(
             grad, attn_two, gains[2], kept_attn_two, None, (output, *leaves(g_ffn_two)), ()
         )
         r_attn_two = return_attn(g_attn_two)
-        r_ffn_two.second(grad)
-        grad, g_ffn_one, gain_ffn_one = ffn_backward(grad, ffn_one, gains[1], kept_ffn_one, kinds)
+        r_ffn_two.second((grad,))
+        grad, g_ffn_one, gain_ffn_one = ffn_backward(
+            grad, ffn_one, gains[1], kept_ffn_one, kinds, r_attn_two.sent
+        )
+        r_attn_two.second()
         p_ffn_two = last_ffn(r_ffn_two, grad, *leaves(g_ffn_one))
-        t_ffn_two = scatter(p_ffn_two)
-        r_ffn_one = return_ffn(*g_ffn_one)
-        grad, g_attn_one, gain_attn_one, _, done_attn_one = attn_backward(
+        r_ffn_one = return_ffn(*after(tuple(g_ffn_one), *r_attn_two.sent))
+        grad, g_attn_one, gain_attn_one, _, (done_attn_one, operand, sent) = attn_backward(
             grad, attn_one, gains[0], kept_attn_one, extra,
-            (p_ffn_two, *leaves(g_ffn_one)), r_ffn_one.sent,
-        )
-        r_attn_two.second(*r_ffn_one.sent)
-        r_ffn_one.second()
+            (*p_ffn_two, *leaves(g_ffn_one), *r_attn_two.sent), r_ffn_one.sent,
+        )
+        t_ffn_two = scatter(pack_parts(p_ffn_two))
+        r_ffn_one.second((), (sent,))
         gain_rows = jnp.stack([gain_attn_one, gain_ffn_one, gain_attn_two, gain_ffn_two])
         gain_rows = jnp.pad(gain_rows, ((0, 12), (0, 0))).astype(bf16)
         r_attn_one = return_attn(g_attn_one, gain_rows)
-        p_attn_two = pack_parts(r_attn_two.last(*r_attn_one.near))
+        p_attn_two = pack_parts(r_attn_two.last())
         t_attn_two = scatter(p_attn_two)
-        p_ffn_one = last_ffn(r_ffn_one)
-        r_attn_one.second(p_ffn_one)
+        p_ffn_one = pack_parts(last_ffn(r_ffn_one, t_attn_two, t_ffn_two))
         t_ffn_one = scatter(p_ffn_one)
-        p_attn_one = pack_parts(r_attn_one.last())
-        t_attn_one = scatter(after(p_attn_one, t_ffn_one))
+        r_attn_one.second((p_ffn_one,))
+        p_attn_one = pack_parts(r_attn_one.last(t_ffn_one))
+        t_attn_one = scatter(p_attn_one)
         b_ffn_two = finish_ffn(t_ffn_two, p_ffn_one)
         b_attn_two = finish_attn(t_attn_two, p_ffn_one)
         b_ffn_one = finish_ffn(t_ffn_one)
         b_attn_one, gain_sums = finish_attn(t_attn_one, spare=16)
+        grad = after(grad, p_ffn_one)
         input_grad = unspread(grad.astype(bf16)).astype(f32)
 
         total = gain_sums[0, :4].astype(f32) + gain_sums[1, :4].astype(f32)

time: 836 us -> 785 us (0.939)
  waiting for transfers between devices: 268 us -> 230 us
  blocking collectives: 52.5 us -> 33.8 us
  matrix products: 115 us -> 102 us
  starting transfers between devices: 88.8 us -> 98 us
    ppermute x20, waiting for transfers between devices: 141 us -> 96.3 us  [swap_x(): return lax.ppermute(value, 'xi', SWAP)]
    all_gather x2, blocking collectives: 52.5 us -> 33.8 us  [gather_col(): return lax.all_gather(block, 'col', axis=0, tiled=True)]
    ppermute x25, starting transfers between devices: 6.07 us -> 23.5 us  [swap_core(): return lax.ppermute(value, 'core', SWAP)]
    ppermute x8 -> x12, waiting for transfers between devices: 41.8 us -> 55.1 us  [the longest x2 24.6 us: attn_forward(): lax.ppermute(after(normed_own, *milestones), 'row', [(0, 1)])]
    dot_general x22, matrix products: 46 us -> 37.4 us  [dot_tn(): lax.dot_general(left, right, (((0,), (0,)), ((), ())), preferred_element_...]
    ppermute x8 -> x12, starting transfers between devices: 20.1 us -> 17.5 us  [the longest x8 8.29 us: spread(): got.append(lax.ppermute(piece, ('core', 'col'), rounds[k]))]
    unnamed x272 -> x302, local copies, waits for them, and re-layouts: 22.8 us -> 22.3 us
  transfers between devices with their start and end apart: 85 -> 89, of which waited for: 37 -> 33; matrix products, arithmetic and copies ran while one was open for 25% -> 27% of each run, Pallas kernels for 16% -> 17%
where the time goes in v3:
time: 785 us; the launch traced here: 777 us
  waiting for transfers between devices  230 us (29%)
  Pallas kernels  131 us (17%)
  matrix products  102 us (13%)
  other arithmetic  99.1 us (13%)
  starting transfers between devices  98 us (12%)
  local copies, waits for them, and re-layouts  64 us (8%)
  blocking collectives  33.8 us (4%)
  between operations  18.6 us (2%)
    ppermute x20, waiting for transfers between devices, swap_x(): return lax.ppermute(value, 'xi', SWAP)  96.3 us
    ppermute x17, waiting for transfers between devices, swap_y(): return lax.ppermute(value, 'row', SWAP)  54 us
    pallas_call x2, Pallas kernels, attend_back(): pl.pallas_call(kernel, grid=(pairs,), in_specs=in_specs, out_specs=[pair_...  48.2 us
    dot_general x22, matrix products, dot_tn(): lax.dot_general(left, right, (((0,), (0,)), ((), ())), preferred_element_...  37.4 us
    all_gather x2, blocking collectives, gather_col(): return lax.all_gather(block, 'col', axis=0, tiled=True)  33.8 us
    dot_general x8, matrix products, dot_nt(): lax.dot_general(left, right, (((1,), (1,)), ((), ())), preferred_element_...  33.1 us
    dot_general x18, matrix products, dot_nn(): lax.dot_general(left, right, (((1,), (0,)), ((), ())), preferred_element_...  31.7 us
    pallas_call x2, Pallas kernels, attend(): pl.pallas_call(kernel, grid=(pairs,), in_specs=[pair_block(n, 0), pair_bl...  30 us
  transfers between devices with their start and end apart: 89, of which 33 were waited for; matrix products, arithmetic and copies ran while one was open for 27% of the time, Pallas kernels for 17%

profile of v3, /device:TPU:0, one launch (start us, length us, event | category | flops | bytes accessed | tf_op | source)
XLA Modules:
  0.0 776.8 jit_solution(9729506540909618714)
XLA Ops:
  9.6 17.4 %all_gather.15 = bf16[1024,256]{1,0:T(8,128)(2,1)S(1)} all-gather(bf16[256,256]{1,0:T(8,128)(2,1)S(1)} %pad_maximum_fusion.70), channel_id=1, replica_groups=mesh['xo'=1,'xi'=2,'core'=2,'row'=2,'col'=4] {'col'}, dimensions={0}, use_global_device_ids=true | all-gather | bytes 655360 | tf_op jit(solution)/shard_map/all_gather | solution.py:345
  27.8 16.4 %all_gather.16 = bf16[1024,256]{1,0:T(8,128)(2,1)S(1)} all-gather(bf16[256,256]{1,0:T(8,128)(2,1)S(1)} %pad_maximum_fusion.71), channel_id=1, replica_groups=mesh['xo'=1,'xi'=2,'core'=2,'row'=2,'col'=4] {'col'}, dimensions={0}, use_global_device_ids=true | all-gather | bytes 655360 | tf_op jit(solution)/shard_map/all_gather | solution.py:345
  63.7 3.7 fusion.133
  72.3 7.7 collective-permute-done.8.low_ref
  85.5 11.3 %collective-permute-done.10 = bf16[320,1024]{1,0:T(8,128)(2,1)S(1)} collective-permute-done((bf16[320,1024]{1,0:T(8,128)(2,1)S(1)}, bf16[320,1024]{1,0:T(8,128)(2,1)S(1)}, u32[]{:S(2)}, u32[]{:S(2)}) %collective-permute-start.10) | collective-permute-done | bytes 655392 | tf_op jit(solution)/shard_map/ppermute | solution.py:566
  96.9 10.8 %collective-permute-start.11 = (bf16[320,1024]{1,0:T(8,128)(2,1)S(1)}, bf16[320,1024]{1,0:T(8,128)(2,1)S(1)}, u32[]{:S(2)}, u32[]{:S(2)}) collective-permute-start(bf16[320,1024]{1,0:T(8,128)(2,1)S(1)} %pad_maximum_fusion.40), channel_id=1, source_target_pairs={{0,8},{8,0},{1,9},{9,1},{2,10},{10,2},{3,11},{11,3},{4,12},{12,4},... | collective-permute-start | bytes 1966088 | tf_op jit(solution)/shard_map/ppermute | solution.py:34
  125.8 4.8 shard_map.365
  130.6 8.0 %shard_map.366.q_ref.kb_ref.vb_ref.rest_0_ = bf16[640,1536]{1,0:T(8,128)(2,1)} custom-call(bf16[640,1024]{1,0:T(8,128)(2,1)} %pad_maximum_fusion.10.n_ref, bf16[1024,1024]{1,0:T(8,128)(2,1)} %bitcast.391, bf16[512,1024]{1,0:T(8,128)(2,1)} %bitcast.395, f32[640,128]{1,0:T(8,128)} %get-tuple-element.457.cos_ref.co_ref, f32[640,128]{1,0:T(8,128)} %get-tuple-element.460.sin_ref), custom_call_target="tpu_custom_call" | custom-call | flops 1 | bytes 1 | tf_op jit(solution)/shard_map/pallas_call | solution.py:104
  138.6 5.9 shard_map.367.ka_ref.va_ref.rest_0_
  144.5 15.0 %shard_map.368 = (bf16[640,512]{1,0:T(8,128)(2,1)}, f32[4,2,1,640]{3,2,1,0:T(1,128)}) custom-call(bf16[640,1536]{1,0:T(8,128)(2,1)} %shard_map.366.q_ref.kb_ref.vb_ref.rest_0_, bf16[640,1024]{1,0:T(8,128)(2,1)} %shard_map.367.ka_ref.va_ref.rest_0_, bf16[640,1536]{1,0:T(8,128)(2,1)} %shard_map.366.q_ref.kb_ref.vb_ref.rest_0_, ...), custom_call_target="tpu_custom_call" | custom-call | flops 1 | bytes 1 | tf_op jit(solution)/shard_map/pallas_call | solution.py:181
  174.6 21.7 %collective-permute-done.16.low_ref = bf16[2112,256]{1,0:T(8,128)(2,1)S(1)} collective-permute-done((bf16[2112,256]{1,0:T(8,128)(2,1)S(1)}, bf16[2112,256]{1,0:T(8,128)(2,1)S(1)}, u32[]{:S(2)}, u32[]{:S(2)}) %collective-permute-start.16) | collective-permute-done | bytes 1081376 | tf_op jit(solution)/shard_map/ppermute | solution.py:38
  199.9 7.4 shard_map.369
  207.3 4.4 fusion.30
  211.7 6.5 multiply_convert_fusion.5
  218.2 3.9 collective-permute-done.18.x_ref
  222.8 4.5 fusion.22
  231.7 11.2 %collective-permute-done.21.low_ref = bf16[1024,256]{1,0:T(8,128)(2,1)S(1)} collective-permute-done((bf16[1024,256]{1,0:T(8,128)(2,1)S(1)}, bf16[1024,256]{1,0:T(8,128)(2,1)S(1)}, u32[]{:S(2)}, u32[]{:S(2)}) %collective-permute-start.21) | collective-permute-done | bytes 524320 | tf_op jit(solution)/shard_map/ppermute | solution.py:38
  244.4 3.5 collective-permute-start.24
  248.0 13.3 %collective-permute-done.24 = bf16[320,1024]{1,0:T(8,128)(2,1)S(1)} collective-permute-done((bf16[320,1024]{1,0:T(8,128)(2,1)S(1)}, bf16[320,1024]{1,0:T(8,128)(2,1)S(1)}, u32[]{:S(2)}, u32[]{:S(2)}) %collective-permute-start.24) | collective-permute-done | bytes 655392 | tf_op jit(solution)/shard_map/ppermute | solution.py:566
  268.4 4.8 shard_map.370
  274.4 8.1 %shard_map.371.q_ref.kb_ref.vb_ref = bf16[640,1536]{1,0:T(8,128)(2,1)} custom-call(bf16[640,1024]{1,0:T(8,128)(2,1)} %pad_maximum_fusion.12.n_ref, bf16[1024,1024]{1,0:T(8,128)(2,1)} %bitcast.393, bf16[512,1024]{1,0:T(8,128)(2,1)} %bitcast.397, f32[640,128]{1,0:T(8,128)} %get-tuple-element.457.cos_ref.co_ref, f32[640,128]{1,0:T(8,128)} %get-tuple-element.460.sin_ref, ...), custom_call_target="tpu_custom_call" | custom-call | flops 1 | bytes 1 | tf_op jit(solution)/shard_map/pallas_call | solution.py:104
  282.5 6.1 shard_map.372.ka_ref.va_ref
  288.6 15.0 %shard_map.373 = (bf16[640,512]{1,0:T(8,128)(2,1)}, f32[4,2,1,640]{3,2,1,0:T(1,128)}) custom-call(bf16[640,1536]{1,0:T(8,128)(2,1)} %shard_map.371.q_ref.kb_ref.vb_ref, bf16[640,1024]{1,0:T(8,128)(2,1)} %shard_map.372.ka_ref.va_ref, bf16[640,1536]{1,0:T(8,128)(2,1)} %shard_map.371.q_ref.kb_ref.vb_ref, bf16[640,1024]{1,0:T(8,128)(2,1)} %shard_map.372.ka_ref.va_ref, ...), custom_call_target="tpu_custom_call" | custom-call | flops 1 | bytes 1 | tf_op jit(solution)/shard_map/pallas_call | solution.py:181
  303.6 10.5 %collective-permute-done.26.x_ref = bf16[4224,256]{1,0:T(8,128)(2,1)S(1)} collective-permute-done((bf16[4224,256]{1,0:T(8,128)(2,1)}, bf16[4224,256]{1,0:T(8,128)(2,1)S(1)}, u32[]{:S(2)}, u32[]{:S(2)}) %collective-permute-start.26) | collective-permute-done | bytes 2162720 | tf_op jit(solution)/shard_map/ppermute | solution.py:38
  328.1 4.6 collective-permute-done.35
  336.6 4.0 collective-permute-done.34
  342.6 4.4 collective-permute-start.41
  349.2 7.5 shard_map.374
  358.2 4.6 fusion.14
  363.7 3.5 fusion.8
  367.2 5.0 multiply_convert_fusion.3
  392.6 3.5 convolution_convert_fusion.9
  407.0 6.0 collective-permute-done.40
  418.3 24.1 %shard_map.375 = (bf16[640,512]{1,0:T(8,128)(2,1)}, bf16[640,512]{1,0:T(8,128)(2,1)}, bf16[640,512]{1,0:T(8,128)(2,1)}, bf16[640,512]{1,0:T(8,128)(2,1)}, bf16[640,512]{1,0:T(8,128)(2,1)}) custom-call(bf16[640,1536]{1,0:T(8,128)(2,1)} %shard_map.371.q_ref.kb_ref.vb_ref, bf16[640,1024]{1,0:T(8,128)(2,1)} %shard_map.372.ka_ref.va_ref, ...), custom_call_target="tpu_custom_call" | custom-call | flops 1 | bytes 1 | tf_op jit(solution)/shard_map/pallas_call | solution.py:266
  459.4 12.3 %collective-permute-done.46 = bf16[320,1024]{1,0:T(8,128)(2,1)S(1)} collective-permute-done((bf16[320,1024]{1,0:T(8,128)(2,1)S(1)}, bf16[320,1024]{1,0:T(8,128)(2,1)S(1)}, u32[]{:S(2)}, u32[]{:S(2)}) %collective-permute-start.46) | collective-permute-done | bytes 655392 | tf_op jit(solution)/shard_map/ppermute | solution.py:613
  485.6 12.2 %collective-permute-done.55 = bf16[1024,512]{1,0:T(8,128)(2,1)S(1)} collective-permute-done((bf16[1024,512]{1,0:T(8,128)(2,1)S(1)}, bf16[1024,512]{1,0:T(8,128)(2,1)S(1)}, u32[]{:S(2)}, u32[]{:S(2)}) %collective-permute-start.55) | collective-permute-done | bytes 1048608 | tf_op jit(solution)/shard_map/ppermute | solution.py:42
  499.6 4.5 multiply_convert_fusion.1
  521.8 7.6 collective-permute-done.56
  555.3 24.1 %shard_map.376 = (bf16[640,512]{1,0:T(8,128)(2,1)}, bf16[640,512]{1,0:T(8,128)(2,1)}, bf16[640,512]{1,0:T(8,128)(2,1)}, bf16[640,512]{1,0:T(8,128)(2,1)}, bf16[640,512]{1,0:T(8,128)(2,1)}) custom-call(bf16[640,1536]{1,0:T(8,128)(2,1)} %shard_map.366.q_ref.kb_ref.vb_ref.rest_0_, bf16[640,1024]{1,0:T(8,128)(2,1)} %shard_map.367.ka_ref.va_ref.rest_0_, ...), custom_call_target="tpu_custom_call" | custom-call | flops 1 | bytes 1 | tf_op jit(solution)/shard_map/pallas_call | solution.py:266
  607.5 9.5 %collective-permute-done.62 = bf16[320,1024]{1,0:T(8,128)(2,1)S(1)} collective-permute-done((bf16[320,1024]{1,0:T(8,128)(2,1)S(1)}, bf16[320,1024]{1,0:T(8,128)(2,1)S(1)}, u32[]{:S(2)}, u32[]{:S(2)}) %collective-permute-start.62) | collective-permute-done | bytes 655392 | tf_op jit(solution)/shard_map/ppermute | solution.py:613
  624.0 20.1 %collective-permute-done.63 = bf16[2112,256]{1,0:T(8,128)(2,1)} collective-permute-done((bf16[2112,256]{1,0:T(8,128)(2,1)}, bf16[2112,256]{1,0:T(8,128)(2,1)}, u32[]{:S(2)}, u32[]{:S(2)}) %collective-permute-start.63) | collective-permute-done | bytes 1081376 | tf_op jit(solution)/shard_map/ppermute | solution.py:42
  652.3 5.6 collective-permute-start.67
  659.0 7.4 collective-permute-done.70
  677.7 15.3 %collective-permute-done.78 = bf16[512,256]{1,0:T(8,128)(2,1)S(1)} collective-permute-done((bf16[512,256]{1,0:T(8,128)(2,1)S(1)}, bf16[512,256]{1,0:T(8,128)(2,1)S(1)}, u32[]{:S(2)}, u32[]{:S(2)}) %collective-permute-start.78) | collective-permute-done | bytes 262176 | tf_op jit(solution)/shard_map/ppermute | solution.py:38
  693.4 8.7 %collective-permute-done.80 = bf16[1056,256]{1,0:T(8,128)(2,1)S(1)} collective-permute-done((bf16[1056,256]{1,0:T(8,128)(2,1)S(1)}, bf16[1056,256]{1,0:T(8,128)(2,1)S(1)}, u32[]{:S(2)}, u32[]{:S(2)}) %collective-permute-start.80) | collective-permute-done | bytes 540704 | tf_op jit(solution)/shard_map/ppermute | solution.py:38
  723.2 9.9 %collective-permute-done.76 = bf16[1056,256]{1,0:T(8,128)(2,1)S(1)} collective-permute-done((bf16[1056,256]{1,0:T(8,128)(2,1)}, bf16[1056,256]{1,0:T(8,128)(2,1)S(1)}, u32[]{:S(2)}, u32[]{:S(2)}) %collective-permute-start.76) | collective-permute-done | bytes 540704 | tf_op jit(solution)/shard_map/ppermute | solution.py:38
  738.2 14.6 %reduce-scatter.11.cloned.1.call-done = bf16[528,256]{1,0:T(8,128)(2,1)} async-done(((bf16[2112,256]{1,0:T(8,128)(2,1)}), bf16[528,256]{1,0:T(8,128)(2,1)}) %reduce-scatter.11.cloned.1.call-update) | async-done | bytes 270352 | tf_op jit(solution)/shard_map/reduce_scatter | solution.py:451
  755.6 5.4 collective-permute-done.73
  (758 shorter events, 312.2 us)
Async XLA Ops:
  7.2 103.7 %all-gather.4.cloned.1.call-start = ((), (), s32[]{:S(2)}) async-start(), calls=%async_computation.4 | async-start | bytes 2703360 | tf_op jit(solution)/shard_map/all_gather | solution.py:345
  44.3 25.0 %collective-permute-start.5 = (bf16[2048,256]{1,0:T(8,128)(2,1)S(1)}, bf16[2048,256]{1,0:T(8,128)(2,1)S(1)}, u32[]{:S(2)}, u32[]{:S(2)}) collective-permute-start(bf16[2048,256]{1,0:T(8,128)(2,1)S(1)} %bitcast.416), channel_id=1, source_target_pairs={{0,16},{16,0},{1,17},{17,1},{2,18},{18,2},{3,19},{19,3},{4,20},{20... | collective-permute-start | bytes 3145736 | tf_op jit(solution)/shard_map/ppermute | solution.py:38
  45.8 23.5 %collective-permute-start.6 = (bf16[2048,256]{1,0:T(8,128)(2,1)S(1)}, bf16[2048,256]{1,0:T(8,128)(2,1)}, u32[]{:S(2)}, u32[]{:S(2)}) collective-permute-start(bf16[2048,256]{1,0:T(8,128)(2,1)S(1)} %bitcast.417), channel_id=1, source_target_pairs={{0,4},{4,0},{1,5},{5,1},{2,6},{6,2},{3,7},{7,3},{8,12},{12,8},{9,1... | collective-permute-start | bytes 3145736 | tf_op jit(solution)/shard_map/ppermute | solution.py:42
  48.6 20.2 %collective-permute-start.2 = (bf16[336,256]{1,0:T(8,128)(2,1)}, bf16[336,256]{1,0:T(8,128)(2,1)S(1)}, u32[]{:S(2)}, u32[]{:S(2)}) collective-permute-start(bf16[336,256]{1,0:T(8,128)(2,1)} %get-tuple-element.320), channel_id=1, source_target_pairs={{0,2},{1,10},{2,0},{3,8},{8,3},{9,11},{10,1},{11,9},{4,6},{5,14},{... | collective-permute-start | bytes 516104 | tf_op jit(solution)/shard_map/ppermute | solution.py:387
  56.6 102.9 %all-gather.6.cloned.1.call-start = ((), (), s32[]{:S(2)}) async-start(), calls=%async_computation.5 | async-start | bytes 1310720 | tf_op jit(solution)/shard_map/all_gather | solution.py:345
  110.9 49.2 %collective-permute-start.12 = (bf16[4224,256]{1,0:T(8,128)(2,1)}, bf16[4224,256]{1,0:T(8,128)(2,1)S(1)}, u32[]{:S(2)}, u32[]{:S(2)}) collective-permute-start(bf16[4224,256]{1,0:T(8,128)(2,1)} %all-gather.4.cloned.1.call-done.whole_ref), channel_id=1, source_target_pairs={{0,16},{16,0},{1,17},{17,1},{2,18},{18,2},{3,19},{19,3},{4,20},{20... | collective-permute-start | bytes 6488072 | tf_op jit(solution)/shard_map/ppermute | solution.py:38
  112.7 49.5 %collective-permute-start.13 = (bf16[4224,256]{1,0:T(8,128)(2,1)}, bf16[4224,256]{1,0:T(8,128)(2,1)}, u32[]{:S(2)}, u32[]{:S(2)}) collective-permute-start(bf16[4224,256]{1,0:T(8,128)(2,1)} %all-gather.4.cloned.1.call-done.whole_ref), channel_id=1, source_target_pairs={{0,4},{4,0},{1,5},{5,1},{2,6},{6,2},{3,7},{7,3},{8,12},{12,8},{9,1... | collective-permute-start | bytes 6488072 | tf_op jit(solution)/shard_map/ppermute | solution.py:42
  118.8 104.0 %all-gather.8.cloned.1.call-start = ((), (), s32[]{:S(2)}) async-start(), calls=%async_computation.6 | async-start | bytes 2703360 | tf_op jit(solution)/shard_map/all_gather | solution.py:345
  167.9 454.8 %reduce-scatter.5.cloned.1.call-start = ((), (), s32[]{:S(2)}) async-start(), calls=%async_computation.7 | async-start | bytes 1310720 | tf_op jit(solution)/shard_map/reduce_scatter | solution.py:451
  169.9 26.3 %collective-permute-start.16 = (bf16[2112,256]{1,0:T(8,128)(2,1)S(1)}, bf16[2112,256]{1,0:T(8,128)(2,1)S(1)}, u32[]{:S(2)}, u32[]{:S(2)}) collective-permute-start(bf16[2112,256]{1,0:T(8,128)(2,1)S(1)} %slice.790), channel_id=1, source_target_pairs={{0,16},{16,0},{1,17},{17,1},{2,18},{18,2},{3,19},{19,3},{4,20},{20... | collective-permute-start | bytes 3244040 | tf_op jit(solution)/shard_map/ppermute | solution.py:38
  170.5 26.5 %collective-permute-start.17 = (bf16[2112,256]{1,0:T(8,128)(2,1)S(1)}, bf16[2112,256]{1,0:T(8,128)(2,1)S(1)}, u32[]{:S(2)}, u32[]{:S(2)}) collective-permute-start(bf16[2112,256]{1,0:T(8,128)(2,1)S(1)} %slice.791), channel_id=1, source_target_pairs={{0,4},{4,0},{1,5},{5,1},{2,6},{6,2},{3,7},{7,3},{8,12},{12,8},{9,1... | collective-permute-start | bytes 3244040 | tf_op jit(solution)/shard_map/ppermute | solution.py:42
  174.5 32.8 %collective-permute-start.15 = (bf16[320,1024]{1,0:T(8,128)(2,1)S(1)}, bf16[320,1024]{1,0:T(8,128)(2,1)}, u32[]{:S(2)}, u32[]{:S(2)}) collective-permute-start(bf16[320,1024]{1,0:T(8,128)(2,1)S(1)} %multiply_convert_fusion.8), channel_id=1, source_target_pairs={{0,8},{8,0},{1,9},{9,1},{2,10},{10,2},{3,11},{11,3},{4,12},{12,4},... | collective-permute-start | bytes 1966088 | tf_op jit(solution)/shard_map/ppermute | solution.py:34
  197.0 25.1 %collective-permute-start.18 = (bf16[2048,256]{1,0:T(8,128)(2,1)}, bf16[2048,256]{1,0:T(8,128)(2,1)S(1)}, u32[]{:S(2)}, u32[]{:S(2)}) collective-permute-start(bf16[2048,256]{1,0:T(8,128)(2,1)} %all-gather.6.cloned.1.call-done.whole_ref), channel_id=1, source_target_pairs={{0,16},{16,0},{1,17},{17,1},{2,18},{18,2},{3,19},{19,3},{4,20},{20... | collective-permute-start | bytes 3145736 | tf_op jit(solution)/shard_map/ppermute | solution.py:38
  198.2 24.6 %collective-permute-start.19 = (bf16[2048,256]{1,0:T(8,128)(2,1)}, bf16[2048,256]{1,0:T(8,128)(2,1)}, u32[]{:S(2)}, u32[]{:S(2)}) collective-permute-start(bf16[2048,256]{1,0:T(8,128)(2,1)} %all-gather.6.cloned.1.call-done.whole_ref), channel_id=1, source_target_pairs={{0,4},{4,0},{1,5},{5,1},{2,6},{6,2},{3,7},{7,3},{8,12},{12,8},{9,1... | collective-permute-start | bytes 3145736 | tf_op jit(solution)/shard_map/ppermute | solution.py:42
  264.8 49.3 %collective-permute-start.26 = (bf16[4224,256]{1,0:T(8,128)(2,1)}, bf16[4224,256]{1,0:T(8,128)(2,1)S(1)}, u32[]{:S(2)}, u32[]{:S(2)}) collective-permute-start(bf16[4224,256]{1,0:T(8,128)(2,1)} %all-gather.8.cloned.1.call-done.whole_ref), channel_id=1, source_target_pairs={{0,16},{16,0},{1,17},{17,1},{2,18},{18,2},{3,19},{19,3},{4,20},{20... | collective-permute-start | bytes 6488072 | tf_op jit(solution)/shard_map/ppermute | solution.py:38
  265.9 49.8 %collective-permute-start.27 = (bf16[4224,256]{1,0:T(8,128)(2,1)}, bf16[4224,256]{1,0:T(8,128)(2,1)S(1)}, u32[]{:S(2)}, u32[]{:S(2)}) collective-permute-start(bf16[4224,256]{1,0:T(8,128)(2,1)} %all-gather.8.cloned.1.call-done.whole_ref), channel_id=1, source_target_pairs={{0,4},{4,0},{1,5},{5,1},{2,6},{6,2},{3,7},{7,3},{8,12},{12,8},{9,1... | collective-permute-start | bytes 6488072 | tf_op jit(solution)/shard_map/ppermute | solution.py:42
  319.3 29.9 %collective-permute-start.30 = (bf16[2112,256]{1,0:T(8,128)(2,1)}, bf16[2112,256]{1,0:T(8,128)(2,1)}, u32[]{:S(2)}, u32[]{:S(2)}) collective-permute-start(bf16[2112,256]{1,0:T(8,128)(2,1)} %slice.806), channel_id=1, source_target_pairs={{0,16},{16,0},{1,17},{17,1},{2,18},{18,2},{3,19},{19,3},{4,20},{20... | collective-permute-start | bytes 3244040 | tf_op jit(solution)/shard_map/ppermute | solution.py:38
  321.3 27.9 %collective-permute-start.31 = (bf16[2112,256]{1,0:T(8,128)(2,1)}, bf16[2112,256]{1,0:T(8,128)(2,1)}, u32[]{:S(2)}, u32[]{:S(2)}) collective-permute-start(bf16[2112,256]{1,0:T(8,128)(2,1)} %slice.807), channel_id=1, source_target_pairs={{0,4},{4,0},{1,5},{5,1},{2,6},{6,2},{3,7},{7,3},{8,12},{12,8},{9,1... | collective-permute-start | bytes 3244040 | tf_op jit(solution)/shard_map/ppermute | solution.py:42
  342.6 20.3 %collective-permute-start.41 = (bf16[320,1024]{1,0:T(8,128)(2,1)S(1)}, bf16[320,1024]{1,0:T(8,128)(2,1)S(1)}, u32[]{:S(2)}, u32[]{:S(2)}) collective-permute-start(bf16[320,1024]{1,0:T(8,128)(2,1)S(1)} %pad_maximum_fusion.43), channel_id=1, source_target_pairs={{0,8},{8,0},{1,9},{9,1},{2,10},{10,2},{3,11},{11,3},{4,12},{12,4},... | collective-permute-start | bytes 1966088 | tf_op jit(solution)/shard_map/ppermute | solution.py:34
  413.0 61.6 %collective-permute-start.50 = (bf16[2112,512]{1,0:T(8,128)(2,1)}, bf16[2112,512]{1,0:T(8,128)(2,1)}, u32[]{:S(2)}, u32[]{:S(2)}) collective-permute-start(bf16[2112,512]{1,0:T(8,128)(2,1)} %pad_maximum_fusion.3), channel_id=1, source_target_pairs={{0,16},{16,0},{1,17},{17,1},{2,18},{18,2},{3,19},{19,3},{4,20},{20... | collective-permute-start | bytes 6488072 | tf_op jit(solution)/shard_map/ppermute | solution.py:38
  414.2 60.4 %collective-permute-start.51 = (bf16[2112,512]{1,0:T(8,128)(2,1)}, bf16[2112,512]{1,0:T(8,128)(2,1)S(1)}, u32[]{:S(2)}, u32[]{:S(2)}) collective-permute-start(bf16[2112,512]{1,0:T(8,128)(2,1)} %fusion.33), channel_id=1, source_target_pairs={{0,4},{4,0},{1,5},{5,1},{2,6},{6,2},{3,7},{7,3},{8,12},{12,8},{9,1... | collective-permute-start | bytes 6488072 | tf_op jit(solution)/shard_map/ppermute | solution.py:42
  448.8 22.9 %collective-permute-start.44 = (bf16[320,1024]{1,0:T(8,128)(2,1)S(1)}, bf16[320,1024]{1,0:T(8,128)(2,1)S(1)}, u32[]{:S(2)}, u32[]{:S(2)}) collective-permute-start(bf16[320,1024]{1,0:T(8,128)(2,1)S(1)} %slice.1100), channel_id=1, source_target_pairs={{0,8},{8,0},{1,9},{9,1},{2,10},{10,2},{3,11},{11,3},{4,12},{12,4},... | collective-permute-start | bytes 1966088 | tf_op jit(solution)/shard_map/ppermute | solution.py:34
  450.6 21.1 %collective-permute-start.46 = (bf16[320,1024]{1,0:T(8,128)(2,1)S(1)}, bf16[320,1024]{1,0:T(8,128)(2,1)S(1)}, u32[]{:S(2)}, u32[]{:S(2)}) collective-permute-start(bf16[320,1024]{1,0:T(8,128)(2,1)S(1)} %fusion.59), channel_id=1, source_target_pairs={{4,0},{5,1},{6,2},{7,3},{12,8},{13,9},{14,10},{15,11},{20,16},{21,... | collective-permute-start | bytes 1966088 | tf_op jit(solution)/shard_map/ppermute | solution.py:613
  455.7 28.7 %collective-permute-start.54 = (bf16[1024,512]{1,0:T(8,128)(2,1)S(1)}, bf16[1024,512]{1,0:T(8,128)(2,1)S(1)}, u32[]{:S(2)}, u32[]{:S(2)}) collective-permute-start(bf16[1024,512]{1,0:T(8,128)(2,1)S(1)} %concatenate.597), channel_id=1, source_target_pairs={{0,16},{16,0},{1,17},{17,1},{2,18},{18,2},{3,19},{19,3},{4,20},{20... | collective-permute-start | bytes 3145736 | tf_op jit(solution)/shard_map/ppermute | solution.py:38
  471.7 26.1 %collective-permute-start.55 = (bf16[1024,512]{1,0:T(8,128)(2,1)S(1)}, bf16[1024,512]{1,0:T(8,128)(2,1)S(1)}, u32[]{:S(2)}, u32[]{:S(2)}) collective-permute-start(bf16[1024,512]{1,0:T(8,128)(2,1)S(1)} %pad_maximum_fusion.21), channel_id=1, source_target_pairs={{0,4},{4,0},{1,5},{5,1},{2,6},{6,2},{3,7},{7,3},{8,12},{12,8},{9,1... | collective-permute-start | bytes 3145736 | tf_op jit(solution)/shard_map/ppermute | solution.py:42
  474.6 24.7 %collective-permute-start.47 = (bf16[320,1024]{1,0:T(8,128)(2,1)S(1)}, bf16[320,1024]{1,0:T(8,128)(2,1)S(1)}, u32[]{:S(2)}, u32[]{:S(2)}) collective-permute-start(bf16[320,1024]{1,0:T(8,128)(2,1)S(1)} %get-tuple-element.238), channel_id=1, source_target_pairs={{0,8},{8,0},{1,9},{9,1},{2,10},{10,2},{3,11},{11,3},{4,12},{12,4},... | collective-permute-start | bytes 1966088 | tf_op jit(solution)/shard_map/ppermute | solution.py:34
  479.5 63.9 %collective-permute-start.52 = (bf16[2112,256]{1,0:T(8,128)(2,1)}, bf16[2112,256]{1,0:T(8,128)(2,1)}, u32[]{:S(2)}, u32[]{:S(2)}) collective-permute-start(bf16[2112,256]{1,0:T(8,128)(2,1)} %slice.839), channel_id=1, source_target_pairs={{0,4},{4,0},{1,5},{5,1},{2,6},{6,2},{3,7},{7,3},{8,12},{12,8},{9,1... | collective-permute-start | bytes 3244040 | tf_op jit(solution)/shard_map/ppermute | solution.py:42
  483.2 60.1 %collective-permute-start.53 = (bf16[2112,256]{1,0:T(8,128)(2,1)}, bf16[2112,256]{1,0:T(8,128)(2,1)}, u32[]{:S(2)}, u32[]{:S(2)}) collective-permute-start(bf16[2112,256]{1,0:T(8,128)(2,1)} %slice.842), channel_id=1, source_target_pairs={{0,16},{16,0},{1,17},{17,1},{2,18},{18,2},{3,19},{19,3},{4,20},{20... | collective-permute-start | bytes 3244040 | tf_op jit(solution)/shard_map/ppermute | solution.py:38
  484.8 44.5 %collective-permute-start.56 = (bf16[1024,256]{1,0:T(8,128)(2,1)S(1)}, bf16[1024,256]{1,0:T(8,128)(2,1)S(1)}, u32[]{:S(2)}, u32[]{:S(2)}) collective-permute-start(bf16[1024,256]{1,0:T(8,128)(2,1)S(1)} %slice.858), channel_id=1, source_target_pairs={{0,4},{4,0},{1,5},{5,1},{2,6},{6,2},{3,7},{7,3},{8,12},{12,8},{9,1... | collective-permute-start | bytes 1572872 | tf_op jit(solution)/shard_map/ppermute | solution.py:42
  498.1 31.3 %collective-permute-start.57 = (bf16[1024,256]{1,0:T(8,128)(2,1)S(1)}, bf16[1024,256]{1,0:T(8,128)(2,1)S(1)}, u32[]{:S(2)}, u32[]{:S(2)}) collective-permute-start(bf16[1024,256]{1,0:T(8,128)(2,1)S(1)} %slice.861), channel_id=1, source_target_pairs={{0,16},{16,0},{1,17},{17,1},{2,18},{18,2},{3,19},{19,3},{4,20},{20... | collective-permute-start | bytes 1572872 | tf_op jit(solution)/shard_map/ppermute | solution.py:38
  509.6 28.0 %collective-permute-start.48 = (bf16[320,1024]{1,0:T(8,128)(2,1)}, bf16[320,1024]{1,0:T(8,128)(2,1)}, u32[]{:S(2)}, u32[]{:S(2)}) collective-permute-start(bf16[320,1024]{1,0:T(8,128)(2,1)} %slice.1098), channel_id=1, source_target_pairs={{0,8},{8,0},{1,9},{9,1},{2,10},{10,2},{3,11},{11,3},{4,12},{12,4},... | collective-permute-start | bytes 1966088 | tf_op jit(solution)/shard_map/ppermute | solution.py:34
  533.2 53.2 %collective-permute-start.59 = (bf16[2112,512]{1,0:T(8,128)(2,1)}, bf16[2112,512]{1,0:T(8,128)(2,1)}, u32[]{:S(2)}, u32[]{:S(2)}) collective-permute-start(bf16[2112,512]{1,0:T(8,128)(2,1)} %pad_maximum_fusion.4), channel_id=1, source_target_pairs={{0,16},{16,0},{1,17},{17,1},{2,18},{18,2},{3,19},{19,3},{4,20},{20... | collective-permute-start | bytes 6488072 | tf_op jit(solution)/shard_map/ppermute | solution.py:38
  535.8 50.5 %collective-permute-start.60 = (bf16[2112,512]{1,0:T(8,128)(2,1)}, bf16[2112,512]{1,0:T(8,128)(2,1)}, u32[]{:S(2)}, u32[]{:S(2)}) collective-permute-start(bf16[2112,512]{1,0:T(8,128)(2,1)} %fusion.37), channel_id=1, source_target_pairs={{0,4},{4,0},{1,5},{5,1},{2,6},{6,2},{3,7},{7,3},{8,12},{12,8},{9,1... | collective-permute-start | bytes 6488072 | tf_op jit(solution)/shard_map/ppermute | solution.py:42
  537.5 106.6 %reduce-scatter.7.cloned.1.call-start = ((), (), s32[]{:S(2)}) async-start(), calls=%async_computation.8 | async-start | bytes 2703360 | tf_op jit(solution)/shard_map/reduce_scatter | solution.py:451
  551.1 165.8 %reduce-scatter.9.cloned.1.call-start = ((), (), s32[]{:S(2)}) async-start(), calls=%async_computation.9 | async-start | bytes 2703360 | tf_op jit(solution)/shard_map/reduce_scatter | solution.py:451
  583.8 33.3 %collective-permute-start.58 = (bf16[320,1024]{1,0:T(8,128)(2,1)S(1)}, bf16[320,1024]{1,0:T(8,128)(2,1)S(1)}, u32[]{:S(2)}, u32[]{:S(2)}) collective-permute-start(bf16[320,1024]{1,0:T(8,128)(2,1)S(1)} %slice.1097), channel_id=1, source_target_pairs={{0,8},{8,0},{1,9},{9,1},{2,10},{10,2},{3,11},{11,3},{4,12},{12,4},... | collective-permute-start | bytes 1966088 | tf_op jit(solution)/shard_map/ppermute | solution.py:34
  597.0 27.0 %collective-permute-start.64 = (bf16[2112,256]{1,0:T(8,128)(2,1)}, bf16[2112,256]{1,0:T(8,128)(2,1)}, u32[]{:S(2)}, u32[]{:S(2)}) collective-permute-start(bf16[2112,256]{1,0:T(8,128)(2,1)} %slice.872), channel_id=1, source_target_pairs={{0,16},{16,0},{1,17},{17,1},{2,18},{18,2},{3,19},{19,3},{4,20},{20... | collective-permute-start | bytes 3244040 | tf_op jit(solution)/shard_map/ppermute | solution.py:38
  598.2 18.8 %collective-permute-start.62 = (bf16[320,1024]{1,0:T(8,128)(2,1)S(1)}, bf16[320,1024]{1,0:T(8,128)(2,1)S(1)}, u32[]{:S(2)}, u32[]{:S(2)}) collective-permute-start(bf16[320,1024]{1,0:T(8,128)(2,1)S(1)} %fusion.57), channel_id=1, source_target_pairs={{4,0},{5,1},{6,2},{7,3},{12,8},{13,9},{14,10},{15,11},{20,16},{21,... | collective-permute-start | bytes 1966088 | tf_op jit(solution)/shard_map/ppermute | solution.py:613
  604.3 53.6 %collective-permute-start.69 = (bf16[1024,512]{1,0:T(8,128)(2,1)}, bf16[1024,512]{1,0:T(8,128)(2,1)}, u32[]{:S(2)}, u32[]{:S(2)}) collective-permute-start(bf16[1024,512]{1,0:T(8,128)(2,1)} %concatenate.604), channel_id=1, source_target_pairs={{0,16},{16,0},{1,17},{17,1},{2,18},{18,2},{3,19},{19,3},{4,20},{20... | collective-permute-start | bytes 3145736 | tf_op jit(solution)/shard_map/ppermute | solution.py:38
  617.0 27.1 %collective-permute-start.63 = (bf16[2112,256]{1,0:T(8,128)(2,1)}, bf16[2112,256]{1,0:T(8,128)(2,1)}, u32[]{:S(2)}, u32[]{:S(2)}) collective-permute-start(bf16[2112,256]{1,0:T(8,128)(2,1)} %slice.871), channel_id=1, source_target_pairs={{0,4},{4,0},{1,5},{5,1},{2,6},{6,2},{3,7},{7,3},{8,12},{12,8},{9,1... | collective-permute-start | bytes 3244040 | tf_op jit(solution)/shard_map/ppermute | solution.py:42
  620.1 46.3 %collective-permute-start.70 = (bf16[1088,512]{1,0:T(8,128)(2,1)}, bf16[1088,512]{1,0:T(8,128)(2,1)}, u32[]{:S(2)}, u32[]{:S(2)}) collective-permute-start(bf16[1088,512]{1,0:T(8,128)(2,1)} %pad_maximum_fusion.18), channel_id=1, source_target_pairs={{0,4},{4,0},{1,5},{5,1},{2,6},{6,2},{3,7},{7,3},{8,12},{12,8},{9,1... | collective-permute-start | bytes 3342344 | tf_op jit(solution)/shard_map/ppermute | solution.py:42
  650.6 102.2 %reduce-scatter.11.cloned.1.call-start = ((), (), s32[]{:S(2)}) async-start(), calls=%async_computation.10 | async-start | bytes 1351680 | tf_op jit(solution)/shard_map/reduce_scatter | solution.py:451
  650.9 20.7 %collective-permute-start.68 = (bf16[320,256]{1,0:T(8,128)(2,1)S(1)}, bf16[320,256]{1,0:T(8,128)(2,1)S(1)}, u32[]{:S(2)}, u32[]{:S(2)}) collective-permute-start(bf16[320,256]{1,0:T(8,128)(2,1)S(1)} %get-tuple-element.327), channel_id=1, source_target_pairs={{10,0},{2,1},{8,2},{0,3},{11,8},{3,9},{9,10},{1,11},{14,4},{6,5},{... | collective-permute-start | bytes 491528 | tf_op jit(solution)/shard_map/ppermute | solution.py:323
  652.3 22.0 %collective-permute-start.67 = (bf16[320,256]{1,0:T(8,128)(2,1)S(1)}, bf16[320,256]{1,0:T(8,128)(2,1)S(1)}, u32[]{:S(2)}, u32[]{:S(2)}) collective-permute-start(bf16[320,256]{1,0:T(8,128)(2,1)S(1)} %get-tuple-element.328), channel_id=1, source_target_pairs={{2,0},{10,1},{0,2},{8,3},{3,8},{11,9},{1,10},{9,11},{6,4},{14,5},{... | collective-permute-start | bytes 491528 | tf_op jit(solution)/shard_map/ppermute | solution.py:323
  668.9 48.0 %collective-permute-start.71 = (bf16[1024,256]{1,0:T(8,128)(2,1)}, bf16[1024,256]{1,0:T(8,128)(2,1)}, u32[]{:S(2)}, u32[]{:S(2)}) collective-permute-start(bf16[1024,256]{1,0:T(8,128)(2,1)} %slice.887), channel_id=1, source_target_pairs={{0,4},{4,0},{1,5},{5,1},{2,6},{6,2},{3,7},{7,3},{8,12},{12,8},{9,1... | collective-permute-start | bytes 1572872 | tf_op jit(solution)/shard_map/ppermute | solution.py:42
  671.6 45.3 %collective-permute-start.72 = (bf16[1088,256]{1,0:T(8,128)(2,1)}, bf16[1088,256]{1,0:T(8,128)(2,1)}, u32[]{:S(2)}, u32[]{:S(2)}) collective-permute-start(bf16[1088,256]{1,0:T(8,128)(2,1)} %slice.890), channel_id=1, source_target_pairs={{0,16},{16,0},{1,17},{17,1},{2,18},{18,2},{3,19},{19,3},{4,20},{20... | collective-permute-start | bytes 1671176 | tf_op jit(solution)/shard_map/ppermute | solution.py:38
  674.3 18.7 %collective-permute-start.78 = (bf16[512,256]{1,0:T(8,128)(2,1)S(1)}, bf16[512,256]{1,0:T(8,128)(2,1)S(1)}, u32[]{:S(2)}, u32[]{:S(2)}) collective-permute-start(bf16[512,256]{1,0:T(8,128)(2,1)S(1)} %copy-done.84), channel_id=1, source_target_pairs={{0,16},{16,0},{1,17},{17,1},{2,18},{18,2},{3,19},{19,3},{4,20},{20... | collective-permute-start | bytes 786440 | tf_op jit(solution)/shard_map/ppermute | solution.py:38
  675.1 27.0 %collective-permute-start.80 = (bf16[1056,256]{1,0:T(8,128)(2,1)S(1)}, bf16[1056,256]{1,0:T(8,128)(2,1)S(1)}, u32[]{:S(2)}, u32[]{:S(2)}) collective-permute-start(bf16[1056,256]{1,0:T(8,128)(2,1)S(1)} %copy-done.59), channel_id=1, source_target_pairs={{0,16},{16,0},{1,17},{17,1},{2,18},{18,2},{3,19},{19,3},{4,20},{20... | collective-permute-start | bytes 1622024 | tf_op jit(solution)/shard_map/ppermute | solution.py:38
  (190 other events, 1822.5 us)
Sparse Core Ops, SparseCore 0:
  56.7 44.7 all-gather.3
  118.9 25.6 all-gather.5
  168.0 46.5 all-gather.7
  537.6 31.5 reduce-scatter.4
  571.5 43.5 reduce-scatter.6
  650.7 52.6 reduce-scatter.8
  721.4 31.4 reduce-scatter.10

commit v4 on v3

--- a/solution.py
+++ b/solution.py
@@ -154,6 +154,42 @@
         cost_estimate=pl.CostEstimate(flops=1, bytes_accessed=1, transcendentals=0),
     )(whole, by_y, by_x, low, high)
     return [o.reshape(-1, 4 * width) for o in outs]
+
+
+def assemble_sides(whole_x, far_x, whole_y, far_y, cols, outs):
+    rows, width = whole_x.shape[0] // cols, whole_x.shape[1]
+    quarter = width // 2
+
+    def kernel(x_ref, xf_ref, y_ref, yf_ref, *out_refs):
+        for out, pieces in zip(out_refs, outs):
+            for j, parts in enumerate(pieces):
+                at = 0
+                for over_x, first, size in parts:
+                    here, there = slice(at, at + size), slice(first, first + size)
+                    if over_x:
+                        out[j, here, :width] = x_ref[there]
+                        out[j, here, width:] = xf_ref[there]
+                    else:
+                        for q, ref in enumerate((y_ref, yf_ref, y_ref, yf_ref)):
+                            side = slice(q // 2 * quarter, (q // 2 + 1) * quarter)
+                            out[j, here, q * quarter : (q + 1) * quarter] = ref[there, side]
+                    at += size
+
+    sizes = [sum(p[2] for p in pieces[0]) for pieces in outs]
+    results = pl.pallas_call(
+        kernel,
+        grid=(cols,),
+        in_specs=[pl.BlockSpec((rows, width), lambda i: (i, 0))] * 4,
+        out_specs=[
+            pl.BlockSpec((len(p), n, 2 * width), lambda i: (0, i, 0)) for p, n in zip(outs, sizes)
+        ],
+        out_shape=[
+            jax.ShapeDtypeStruct((len(p), cols * n, 2 * width), bf16) for p, n in zip(outs, sizes)
+        ],
+        compiler_params=VMEM,
+        cost_estimate=pl.CostEstimate(flops=1, bytes_accessed=1, transcendentals=0),
+    )(whole_x, far_x, whole_y, far_y)
+    return [r.reshape(-1, 2 * width) for r in results]
 
 
 def pair_block(rows, first):
@@ -365,11 +401,17 @@
         attn_local_one = near_x(
             stack_attn(query_weight_1, key_weight_1, value_weight_1, out_weight_1)
         )
-        attn_local_two = near_x(
-            stack_attn(query_weight_2, key_weight_2, value_weight_2, out_weight_2)
-        )
         ffn_local_one = local_ffn(gate_weight_1, up_weight_1, down_weight_1)
-        ffn_local_two = local_ffn(gate_weight_2, up_weight_2, down_weight_2)
+        gate_two, up_two = units(gate_weight_2, True), units(up_weight_2, True)
+        down_two = units(down_weight_2, False)
+        wide, low = gate_two.shape[0], gate_two.shape[0] // 2
+        tall = query_weight_2.shape[1] // 2
+        qk_two = jnp.concatenate([units(query_weight_2, True), units(key_weight_2, True)])
+        attn_y_two = jnp.concatenate([units(value_weight_2, True), units(out_weight_2, False)])
+        ffn_y_two = jnp.concatenate([up_two, down_two[low:]])
+        own = jnp.concatenate([near_x(qk_two), near_x(gate_two), near_x(down_two[:low])])
+        both_rows = jnp.concatenate([own, swap_y(own)], axis=1)
+        attn_x_two, ffn_x_two = both_rows[: 2 * tall], both_rows[2 * tall :]
         half = attn_local_one.shape[0] // 2
         qk_whole_one = gather_col(attn_local_one[:half])
         vo_whole_one = gather_col(after(attn_local_one[half:], qk_whole_one))
@@ -377,7 +419,11 @@
             [w.reshape(col_count, -1, quarter) for w in (qk_whole_one, vo_whole_one)], axis=1
         ).reshape(-1, quarter)
         ffn_whole_one = gather_col(after(ffn_local_one, vo_whole_one))
-        attn_whole_two = gather_col(after(attn_local_two, ffn_whole_one))
+        attn_whole_two = gather_col(after(jnp.concatenate([attn_x_two, attn_y_two]), ffn_whole_one))
+
+        def halves(whole):
+            whole = whole.reshape(col_count, 2, -1, half_d)
+            return whole[:, 0].reshape(-1, half_d), whole[:, 1].reshape(-1, half_d)
 
         def spread(arrays, *milestones):
             pieces = after(jnp.concatenate(arrays, axis=1), *milestones)
@@ -485,6 +531,70 @@
                 sent = after(self.sent, *milestones)
                 return [add(a, b) for a, b in zip(self.near, sent)]
 
+        def return_sides(near_x, far_x, near_y, far_y):
+            return near_x, swap_x(far_x), near_y, swap_y(far_y)
+
+        def scatter_sides(sides, *milestones):
+            near_x, sent_x, near_y, sent_y = sides
+            sent_x, sent_y = after((sent_x, sent_y), *milestones)
+            parts = [
+                add(n, r).reshape(col_count, -1, half_d)
+                for n, r in ((near_x, sent_x), (near_y, sent_y))
+            ]
+            packed = jnp.concatenate(parts, axis=1).reshape(-1, half_d)
+            return packed, over_xo(scatter_col(packed))
+
+        def settle_sides(total, *milestones):
+            total = after(total, *milestones)
+            half = total.shape[0] // 2
+            first, second = total[:half], turn(total[half:], xi, 1)
+            first = add(first[:, :quarter], swap_y(first[:, quarter:]))
+            first = turn(jnp.concatenate([first, swap_x(first)], axis=1), xi, 1)
+            return first, add(second, swap_x(second))
+
+        def by_col(array):
+            return array.reshape(col_count, -1, array.shape[-1])
+
+        def flat(array):
+            return array.reshape(-1, array.shape[-1])
+
+        def return_ffn_two(gate, up, down):
+            down = by_col(down[0])
+            part = lambda rows, *places: quarters(flat(rows), *places)
+            lower, upper = down[:, :low], down[:, low:]
+            join = lambda a, b: flat(jnp.concatenate([by_col(a), by_col(b)], axis=1))
+            return return_sides(
+                join(gate[0], part(lower, 0, 1)), join(gate[1], part(lower, 2, 3)),
+                join(up[0], part(upper, 0, 2)), join(up[1], part(upper, 1, 3)),
+            )
+
+        def return_attn_two(grads):
+            qk = flat(jnp.concatenate([by_col(g) for g in grads[:2]], axis=1))
+            vo = flat(jnp.concatenate([by_col(g) for g in grads[2:]], axis=1))
+            return return_sides(
+                quarters(qk, 0, 1), quarters(qk, 2, 3), quarters(vo, 0, 2), quarters(vo, 1, 3)
+            )
+
+        def finish_rows(total, sizes):
+            pair, blocks, at = both_blocks(total), [], 0
+            for size, transposed in sizes:
+                blocks.append(finish(pair, at, size, transposed))
+                at += size
+            return blocks
+
+        def finish_ffn_two(total, *milestones):
+            first, second = settle_sides(total, *milestones)
+            rows = [first[:wide], second[:wide], first[wide:], second[wide:]]
+            return finish_rows(
+                jnp.concatenate(rows), ((wide, True), (wide, True), (wide, False))
+            )
+
+        def finish_attn_two(total, *milestones):
+            total = jnp.concatenate(settle_sides(total, *milestones))
+            return finish_rows(
+                total, ((tall, True), (tall, True), (tall, True), (tall, False))
+            )
+
         def pack_parts(parts):
             packed = [p.reshape(col_count, -1, quarter) for p in parts]
             return jnp.concatenate(packed, axis=1).reshape(-1, quarter)
@@ -592,7 +702,7 @@
             grad_gate = (grad_hidden * up * sig * (1.0 + gate * (1.0 - sig))).astype(bf16)
             grad_up = (grad_hidden * gate * sig).astype(bf16)
             grad_normed = core_sum(dot_nn(grad_gate, w_gate) + dot_nn(grad_up, w_up))
-            lefts = after((grad_gate, grad_up, hidden), *late)
+            lefts = (grad_gate, grad_up, after(hidden, *late))
             pairs = tuple(zip(lefts, (normed, normed, grad_full)))
             grads = [sides(*pair, k) for pair, k in zip(pairs[:2], kinds)]
             grads.append((dot_tn(*pairs[2]).astype(bf16),))
@@ -636,25 +746,41 @@
             residual, attn_one, gains[0], None, start_ffn_one, *cross_one.both
         )
         own_one, first_one = kept_attn_one[4], kept_attn_one[5]
+        ffn_whole_two = gather_col(after(jnp.concatenate([ffn_x_two, ffn_y_two]), attn_whole_two))
         cross_ffn = crossings[0]
         ffn_one = cross_ffn.complete((1, 1, 1))
-        cross = Crossing(attn_whole_two, *cross_ffn.both)
-        ffn_whole_two = gather_col(after(ffn_local_two, attn_whole_two))
-        residual, kept_ffn_one = ffn_forward(residual, ffn_one, gains[1], (*cross.sides, ffn_whole_two))
-        attn_two = cross.complete((2, 1, 1))
-        residual = after(residual, *cross.both)
-        ffn_two = []
+        wx, wy = halves(after(attn_whole_two, *cross_ffn.both))
+        far = (swap_x(wx), swap_y(wy))
+        residual, kept_ffn_one = ffn_forward(residual, ffn_one, gains[1], far)
+        attn_two = assemble_sides(
+            wx, far[0], wy, far[1], col_count,
+            (
+                (((True, 0, tall),), ((True, tall, tall),)),
+                (((False, 0, tall),),),
+                (((False, tall, tall),),),
+            ),
+        )
+        ffn_sides, grads = [], []
 
         def start_ffn_two(normed_first):
-            ffn_two.append(Crossing(ffn_whole_two, normed_first, *cross.both))
-            return ffn_two[0].sides
+            wx, wy = after(halves(ffn_whole_two), normed_first, *far)
+            ffn_sides.extend((wx, swap_x(wx), wy, swap_y(wy)))
+            grads.append(spread([by_piece(out_grad)], normed_first))
+            return ffn_sides[1], ffn_sides[3], grads[0]
 
         residual, kept_attn_two = attn_forward(
             residual, attn_two, gains[2], (own_one, first_one), start_ffn_two
         )
-        ffn_two = ffn_two[0].complete((1, 1, 1))
-        last_grad = spread([by_piece(out_grad)], residual)
-        residual, kept_ffn_two = ffn_forward(residual, ffn_two, gains[3], (last_grad,))
+        ffn_two = assemble_sides(
+            *ffn_sides, col_count,
+            (
+                (((True, 0, wide),),),
+                (((False, 0, wide),),),
+                (((True, wide, low), (False, wide, low)),),
+            ),
+        )
+        last_grad = grads[0]
+        residual, kept_ffn_two = ffn_forward(residual, ffn_two, gains[3], ())
         output = unspread(residual.astype(bf16))
 
         kinds = (True, False)
@@ -663,38 +789,35 @@
             return [a for pair in grads for a in pair]
 
         grad, g_ffn_two, gain_ffn_two = ffn_backward(
-            last_grad.astype(f32), ffn_two, gains[3], kept_ffn_two, kinds, ()
-        )
-        r_ffn_two = return_ffn(*g_ffn_two)
+            last_grad.astype(f32), ffn_two, gains[3], kept_ffn_two, kinds, (output,)
+        )
+        r_ffn_two = return_ffn_two(*g_ffn_two)
         grad, g_attn_two, gain_attn_two, extra, done_attn_two = attn_backward(
-            grad, attn_two, gains[2], kept_attn_two, None, (output, *leaves(g_ffn_two)), ()
-        )
-        r_attn_two = return_attn(g_attn_two)
-        r_ffn_two.second((grad,))
+            grad, attn_two, gains[2], kept_attn_two, None, tuple(leaves(g_ffn_two)), (r_ffn_two[1], r_ffn_two[3])
+        )
+        r_attn_two = return_attn_two(g_attn_two)
+        sent_attn_two = (r_attn_two[1], r_attn_two[3])
         grad, g_ffn_one, gain_ffn_one = ffn_backward(
-            grad, ffn_one, gains[1], kept_ffn_one, kinds, r_attn_two.sent
-        )
-        r_attn_two.second()
-        p_ffn_two = last_ffn(r_ffn_two, grad, *leaves(g_ffn_one))
-        r_ffn_one = return_ffn(*after(tuple(g_ffn_one), *r_attn_two.sent))
+            grad, ffn_one, gains[1], kept_ffn_one, kinds, ()
+        )
+        r_ffn_one = return_ffn(*after(tuple(g_ffn_one), *sent_attn_two))
+        p_ffn_two, t_ffn_two = scatter_sides(r_ffn_two, *leaves(g_ffn_one))
+        p_attn_two, t_attn_two = scatter_sides(r_attn_two, *leaves(g_ffn_one))
         grad, g_attn_one, gain_attn_one, _, (done_attn_one, operand, sent) = attn_backward(
             grad, attn_one, gains[0], kept_attn_one, extra,
-            (*p_ffn_two, *leaves(g_ffn_one), *r_attn_two.sent), r_ffn_one.sent,
-        )
-        t_ffn_two = scatter(pack_parts(p_ffn_two))
+            (p_attn_two, p_ffn_two, *leaves(g_ffn_one)), r_ffn_one.sent,
+        )
         r_ffn_one.second((), (sent,))
         gain_rows = jnp.stack([gain_attn_one, gain_ffn_one, gain_attn_two, gain_ffn_two])
         gain_rows = jnp.pad(gain_rows, ((0, 12), (0, 0))).astype(bf16)
         r_attn_one = return_attn(g_attn_one, gain_rows)
-        p_attn_two = pack_parts(r_attn_two.last())
-        t_attn_two = scatter(p_attn_two)
-        p_ffn_one = pack_parts(last_ffn(r_ffn_one, t_attn_two, t_ffn_two))
+        p_ffn_one = pack_parts(last_ffn(r_ffn_one, t_attn_two, t_ffn_two, *r_attn_one.near))
         t_ffn_one = scatter(p_ffn_one)
         r_attn_one.second((p_ffn_one,))
-        p_attn_one = pack_parts(r_attn_one.last(t_ffn_one))
+        b_ffn_two = finish_ffn_two(t_ffn_two, p_ffn_one)
+        b_attn_two = finish_attn_two(t_attn_two, p_ffn_one)
+        p_attn_one = pack_parts(r_attn_one.last(t_ffn_one, *b_ffn_two, *b_attn_two))
         t_attn_one = scatter(p_attn_one)
-        b_ffn_two = finish_ffn(t_ffn_two, p_ffn_one)
-        b_attn_two = finish_attn(t_attn_two, p_ffn_one)
         b_ffn_one = finish_ffn(t_ffn_one)
         b_attn_one, gain_sums = finish_attn(t_attn_one, spare=16)
         grad = after(grad, p_ffn_one)

time: 785 us -> 744 us (0.948)
  starting transfers between devices: 98 us -> 80.3 us
  local copies, waits for them, and re-layouts: 64 us -> 51.9 us
    all_gather x3, waiting for transfers between devices: 0.01 us -> 21.1 us  [gather_col(): return lax.all_gather(block, 'col', axis=0, tiled=True)]
    ppermute x25, starting transfers between devices: 23.5 us -> 7.01 us  [swap_core(): return lax.ppermute(value, 'core', SWAP)]
    pallas_call x4 -> x2, Pallas kernels: 24.4 us -> 12.1 us  [assemble(): pl.pallas_call(kernel, grid=(cols,), in_specs=[block(lambda i: (i, 0)), b...]
    pallas_call x0 -> x2, Pallas kernels: none -> 12.1 us  [assemble_sides(): pl.pallas_call(kernel, grid=(cols,), in_specs=[pl.BlockSpec((rows, width)...]
    concatenate x0 -> x14, other arithmetic: none -> 12.1 us  [the longest x4 4.76 us: return_ffn_two(): join = lambda a, b: flat(jnp.concatenate([by_col(a), by_col(b)], axis=1))]
    ppermute x2, waiting for transfers between devices: 24.6 us -> 14.2 us  [attn_forward(): lax.ppermute(after(normed_own, *milestones), 'row', [(0, 1)])]
    reduce_scatter x4, waiting for transfers between devices: 14.6 us -> 5.41 us  [scatter_col(): return lax.psum_scatter(array, 'col', scatter_dimension=0, tiled=True)]
    ppermute x20 -> x18, waiting for transfers between devices: 96.3 us -> 87.4 us  [swap_x(): return lax.ppermute(value, 'xi', SWAP)]
  transfers between devices with their start and end apart: 89 -> 86, of which waited for: 33 -> 38; matrix products, arithmetic and copies ran while one was open for 27% -> 26% of each run, Pallas kernels for 17% -> 18%
where the time goes in v4:
time: 744 us; the launch traced here: 736 us
  waiting for transfers between devices  230 us (31%)
  Pallas kernels  130 us (17%)
  matrix products  97.3 us (13%)
  other arithmetic  93.6 us (13%)
  starting transfers between devices  80.3 us (11%)
  local copies, waits for them, and re-layouts  51.9 us (7%)
  blocking collectives  33.9 us (5%)
  between operations  19 us (3%)
    ppermute x18, waiting for transfers between devices, swap_x(): return lax.ppermute(value, 'xi', SWAP)  87.4 us
    ppermute x16, waiting for transfers between devices, swap_y(): return lax.ppermute(value, 'row', SWAP)  57.4 us
    pallas_call x2, Pallas kernels, attend_back(): pl.pallas_call(kernel, grid=(pairs,), in_specs=in_specs, out_specs=[pair_...  48.2 us
    dot_general x22, matrix products, dot_tn(): lax.dot_general(left, right, (((0,), (0,)), ((), ())), preferred_element_...  36.7 us
    all_gather x2, blocking collectives, gather_col(): return lax.all_gather(block, 'col', axis=0, tiled=True)  33.9 us
    dot_general x18, matrix products, dot_nn(): lax.dot_general(left, right, (((1,), (0,)), ((), ())), preferred_element_...  30.5 us
    dot_general x8, matrix products, dot_nt(): lax.dot_general(left, right, (((1,), (1,)), ((), ())), preferred_element_...  30.2 us
    pallas_call x2, Pallas kernels, attend(): pl.pallas_call(kernel, grid=(pairs,), in_specs=[pair_block(n, 0), pair_bl...  29.9 us
  transfers between devices with their start and end apart: 86, of which 38 were waited for; matrix products, arithmetic and copies ran while one was open for 26% of the time, Pallas kernels for 18%

profile of v4, /device:TPU:0, one launch (start us, length us, event | category | flops | bytes accessed | tf_op | source)
XLA Modules:
  0.0 736.0 jit_solution(826604657706949670)
XLA Ops:
  9.6 17.5 %all_gather.15 = bf16[1024,256]{1,0:T(8,128)(2,1)S(1)} all-gather(bf16[256,256]{1,0:T(8,128)(2,1)S(1)} %pad_maximum_fusion.76), channel_id=1, replica_groups=mesh['xo'=1,'xi'=2,'core'=2,'row'=2,'col'=4] {'col'}, dimensions={0}, use_global_device_ids=true | all-gather | bytes 655360 | tf_op jit(solution)/shard_map/all_gather | solution.py:381
  28.8 16.4 %all_gather.16 = bf16[1024,256]{1,0:T(8,128)(2,1)S(1)} all-gather(bf16[256,256]{1,0:T(8,128)(2,1)S(1)} %pad_maximum_fusion.77), channel_id=1, replica_groups=mesh['xo'=1,'xi'=2,'core'=2,'row'=2,'col'=4] {'col'}, dimensions={0}, use_global_device_ids=true | all-gather | bytes 655360 | tf_op jit(solution)/shard_map/all_gather | solution.py:381
  67.0 3.7 fusion.135
  79.4 5.1 collective-permute-done.8.low_ref
  84.5 5.4 collective-permute-done.9.high_ref
  94.2 10.8 %all-gather.4.cloned.1.call-done.whole_ref = bf16[4224,256]{1,0:T(8,128)(2,1)} async-done(((bf16[1056,256]{1,0:T(8,128)(2,1)}), bf16[4224,256]{1,0:T(8,128)(2,1)}) %all-gather.4.cloned.1.call-update) | async-done | bytes 2162704 | tf_op jit(solution)/shard_map/all_gather | solution.py:381
  106.6 3.6 collective-permute-start.11
  120.3 4.7 shard_map.365
  125.0 7.9 %shard_map.366.q_ref.kb_ref.vb_ref.rest_0_ = bf16[640,1536]{1,0:T(8,128)(2,1)} custom-call(bf16[640,1024]{1,0:T(8,128)(2,1)} %pad_maximum_fusion.14.n_ref, bf16[1024,1024]{1,0:T(8,128)(2,1)} %bitcast.425, bf16[512,1024]{1,0:T(8,128)(2,1)} %bitcast.430, f32[640,128]{1,0:T(8,128)} %get-tuple-element.471.cos_ref.co_ref, f32[640,128]{1,0:T(8,128)} %get-tuple-element.474.sin_ref), custom_call_target="tpu_custom_call" | custom-call | flops 1 | bytes 1 | tf_op jit(solution)/shard_map/pallas_call | solution.py:104
  132.9 5.9 shard_map.367.ka_ref.va_ref.rest_0_
  138.8 15.0 %shard_map.368 = (bf16[640,512]{1,0:T(8,128)(2,1)}, f32[4,2,1,640]{3,2,1,0:T(1,128)}) custom-call(bf16[640,1536]{1,0:T(8,128)(2,1)} %shard_map.366.q_ref.kb_ref.vb_ref.rest_0_, bf16[640,1024]{1,0:T(8,128)(2,1)} %shard_map.367.ka_ref.va_ref.rest_0_, bf16[640,1536]{1,0:T(8,128)(2,1)} %shard_map.366.q_ref.kb_ref.vb_ref.rest_0_, ...), custom_call_target="tpu_custom_call" | custom-call | flops 1 | bytes 1 | tf_op jit(solution)/shard_map/pallas_call | solution.py:217
  153.8 9.3 %collective-permute-done.13.y_ref = bf16[4224,256]{1,0:T(8,128)(2,1)} collective-permute-done((bf16[4224,256]{1,0:T(8,128)(2,1)S(1)}, bf16[4224,256]{1,0:T(8,128)(2,1)}, u32[]{:S(2)}, u32[]{:S(2)}) %collective-permute-start.13) | collective-permute-done | bytes 2162720 | tf_op jit(solution)/shard_map/ppermute | solution.py:42
  178.5 19.5 %collective-permute-done.17.low_ref = bf16[2112,256]{1,0:T(8,128)(2,1)} collective-permute-done((bf16[2112,256]{1,0:T(8,128)(2,1)}, bf16[2112,256]{1,0:T(8,128)(2,1)}, u32[]{:S(2)}, u32[]{:S(2)}) %collective-permute-start.17) | collective-permute-done | bytes 1081376 | tf_op jit(solution)/shard_map/ppermute | solution.py:38
  198.0 3.5 collective-permute-done.18.high_ref
  202.7 7.3 shard_map.369
  210.0 4.3 fusion.28
  214.4 4.2 multiply_convert_fusion.5
  218.7 7.4 %collective-permute-done.19.xf_ref = bf16[1024,512]{1,0:T(8,128)(2,1)S(1)} collective-permute-done((bf16[1024,512]{1,0:T(8,128)(2,1)S(1)}, bf16[1024,512]{1,0:T(8,128)(2,1)S(1)}, u32[]{:S(2)}, u32[]{:S(2)}) %collective-permute-start.19) | collective-permute-done | bytes 1048608 | tf_op jit(solution)/shard_map/ppermute | solution.py:38
  234.7 14.2 %collective-permute-done.23 = bf16[320,1024]{1,0:T(8,128)(2,1)S(1)} collective-permute-done((bf16[320,1024]{1,0:T(8,128)(2,1)S(1)}, bf16[320,1024]{1,0:T(8,128)(2,1)S(1)}, u32[]{:S(2)}, u32[]{:S(2)}) %collective-permute-start.23) | collective-permute-done | bytes 655392 | tf_op jit(solution)/shard_map/ppermute | solution.py:676
  252.4 10.3 %all-gather.8.cloned.1.call-done = bf16[4224,512]{1,0:T(8,128)(2,1)} async-done(((bf16[1056,512]{1,0:T(8,128)(2,1)}), bf16[4224,512]{1,0:T(8,128)(2,1)}) %all-gather.8.cloned.1.call-update) | async-done | bytes 4325392 | tf_op jit(solution)/shard_map/all_gather | solution.py:381
  271.9 5.1 collective-permute-start.30
  276.9 4.7 shard_map.370
  282.8 8.1 %shard_map.371.q_ref.kb_ref.vb_ref = bf16[640,1536]{1,0:T(8,128)(2,1)} custom-call(bf16[640,1024]{1,0:T(8,128)(2,1)} %pad_maximum_fusion.16.n_ref, bf16[1024,1024]{1,0:T(8,128)(2,1)} %bitcast.427, bf16[512,1024]{1,0:T(8,128)(2,1)} %bitcast.432, f32[640,128]{1,0:T(8,128)} %get-tuple-element.471.cos_ref.co_ref, f32[640,128]{1,0:T(8,128)} %get-tuple-element.474.sin_ref, ...), custom_call_target="tpu_custom_call" | custom-call | flops 1 | bytes 1 | tf_op jit(solution)/shard_map/pallas_call | solution.py:104
  291.0 6.1 shard_map.372.ka_ref.va_ref
  297.1 14.9 %shard_map.373 = (bf16[640,512]{1,0:T(8,128)(2,1)}, f32[4,2,1,640]{3,2,1,0:T(1,128)}) custom-call(bf16[640,1536]{1,0:T(8,128)(2,1)} %shard_map.371.q_ref.kb_ref.vb_ref, bf16[640,1024]{1,0:T(8,128)(2,1)} %shard_map.372.ka_ref.va_ref, bf16[640,1536]{1,0:T(8,128)(2,1)} %shard_map.371.q_ref.kb_ref.vb_ref, bf16[640,1024]{1,0:T(8,128)(2,1)} %shard_map.372.ka_ref.va_ref, ...), custom_call_target="tpu_custom_call" | custom-call | flops 1 | bytes 1 | tf_op jit(solution)/shard_map/pallas_call | solution.py:217
  319.5 7.4 %shard_map.374 = (bf16[1,1408,1024]{2,1,0:T(8,128)(2,1)}, bf16[1,1408,1024]{2,1,0:T(8,128)(2,1)}, bf16[1,1408,1024]{2,1,0:T(8,128)(2,1)}) custom-call(bf16[2112,512]{1,0:T(8,128)(2,1)} %bitcast.441, bf16[2112,512]{1,0:T(8,128)(2,1)} %collective-permute-done.25.xf_ref, bf16[2112,512]{1,0:T(8,128)(2,1)} %bitcast.439, ...), custom_call_target="tpu_custom_call" | custom-call | flops 1 | bytes 1 | tf_op jit(solution)/shard_map/pallas_call | solution.py:179
  327.0 4.4 fusion.6
  331.5 3.5 fusion.12
  334.9 4.8 multiply_convert_fusion.3
  362.3 10.1 %collective-permute-done.36 = bf16[320,256]{1,0:T(8,128)(2,1)S(1)} collective-permute-done((bf16[320,256]{1,0:T(8,128)(2,1)S(1)}, bf16[320,256]{1,0:T(8,128)(2,1)S(1)}, u32[]{:S(2)}, u32[]{:S(2)}) %collective-permute-start.36) | collective-permute-done | bytes 163872 | tf_op jit(solution)/shard_map/ppermute | solution.py:359
  374.1 3.5 convolution_convert_fusion.1
  391.6 24.1 %shard_map.375 = (bf16[640,512]{1,0:T(8,128)(2,1)}, bf16[640,512]{1,0:T(8,128)(2,1)}, bf16[640,512]{1,0:T(8,128)(2,1)}, bf16[640,512]{1,0:T(8,128)(2,1)}, bf16[640,512]{1,0:T(8,128)(2,1)}) custom-call(bf16[640,1536]{1,0:T(8,128)(2,1)} %shard_map.371.q_ref.kb_ref.vb_ref, bf16[640,1024]{1,0:T(8,128)(2,1)} %shard_map.372.ka_ref.va_ref, ...), custom_call_target="tpu_custom_call" | custom-call | flops 1 | bytes 1 | tf_op jit(solution)/shard_map/pallas_call | solution.py:302
  418.7 6.9 collective-permute-done.43
  441.1 11.9 %collective-permute-done.45 = bf16[320,1024]{1,0:T(8,128)(2,1)S(1)} collective-permute-done((bf16[320,1024]{1,0:T(8,128)(2,1)S(1)}, bf16[320,1024]{1,0:T(8,128)(2,1)S(1)}, u32[]{:S(2)}, u32[]{:S(2)}) %collective-permute-start.45) | collective-permute-done | bytes 655392 | tf_op jit(solution)/shard_map/ppermute | solution.py:723
  461.2 4.5 multiply_convert_fusion.1
  477.9 3.7 fusion.22
  487.9 3.4 fusion.31
  491.4 3.9 fusion.38
  512.4 24.1 %shard_map.376 = (bf16[640,512]{1,0:T(8,128)(2,1)}, bf16[640,512]{1,0:T(8,128)(2,1)}, bf16[640,512]{1,0:T(8,128)(2,1)}, bf16[640,512]{1,0:T(8,128)(2,1)}, bf16[640,512]{1,0:T(8,128)(2,1)}) custom-call(bf16[640,1536]{1,0:T(8,128)(2,1)} %shard_map.366.q_ref.kb_ref.vb_ref.rest_0_, bf16[640,1024]{1,0:T(8,128)(2,1)} %shard_map.367.ka_ref.va_ref.rest_0_, ...), custom_call_target="tpu_custom_call" | custom-call | flops 1 | bytes 1 | tf_op jit(solution)/shard_map/pallas_call | solution.py:302
  547.3 11.8 %collective-permute-done.52 = bf16[2112,512]{1,0:T(8,128)(2,1)} collective-permute-done((bf16[2112,512]{1,0:T(8,128)(2,1)}, bf16[2112,512]{1,0:T(8,128)(2,1)}, u32[]{:S(2)}, u32[]{:S(2)}) %collective-permute-start.52) | collective-permute-done | bytes 2162720 | tf_op jit(solution)/shard_map/ppermute | solution.py:38
  574.5 9.5 %collective-permute-done.55 = bf16[320,1024]{1,0:T(8,128)(2,1)S(1)} collective-permute-done((bf16[320,1024]{1,0:T(8,128)(2,1)S(1)}, bf16[320,1024]{1,0:T(8,128)(2,1)S(1)}, u32[]{:S(2)}, u32[]{:S(2)}) %collective-permute-start.55) | collective-permute-done | bytes 655392 | tf_op jit(solution)/shard_map/ppermute | solution.py:723
  590.6 20.5 %collective-permute-done.56 = bf16[2112,256]{1,0:T(8,128)(2,1)} collective-permute-done((bf16[2112,256]{1,0:T(8,128)(2,1)}, bf16[2112,256]{1,0:T(8,128)(2,1)}, u32[]{:S(2)}, u32[]{:S(2)}) %collective-permute-start.56) | collective-permute-done | bytes 1081376 | tf_op jit(solution)/shard_map/ppermute | solution.py:42
  624.7 10.3 %collective-permute-done.63 = bf16[1088,512]{1,0:T(8,128)(2,1)} collective-permute-done((bf16[1088,512]{1,0:T(8,128)(2,1)}, bf16[1088,512]{1,0:T(8,128)(2,1)}, u32[]{:S(2)}, u32[]{:S(2)}) %collective-permute-start.63) | collective-permute-done | bytes 1114144 | tf_op jit(solution)/shard_map/ppermute | solution.py:42
  642.5 13.4 %collective-permute-done.71 = bf16[256,256]{1,0:T(8,128)(2,1)S(1)} collective-permute-done((bf16[256,256]{1,0:T(8,128)(2,1)S(1)}, bf16[256,256]{1,0:T(8,128)(2,1)S(1)}, u32[]{:S(2)}, u32[]{:S(2)}) %collective-permute-start.71) | collective-permute-done | bytes 131104 | tf_op jit(solution)/shard_map/ppermute | solution.py:38
  662.1 6.7 collective-permute-done.67
  686.6 10.1 %collective-permute-done.77 = bf16[1056,256]{1,0:T(8,128)(2,1)S(1)} collective-permute-done((bf16[1056,256]{1,0:T(8,128)(2,1)}, bf16[1056,256]{1,0:T(8,128)(2,1)S(1)}, u32[]{:S(2)}, u32[]{:S(2)}) %collective-permute-start.77) | collective-permute-done | bytes 540704 | tf_op jit(solution)/shard_map/ppermute | solution.py:38
  708.1 3.8 reduce-scatter.11.cloned.1.call-done
  714.7 5.5 collective-permute-done.74
  (770 shorter events, 294.3 us)
Async XLA Ops:
  7.2 97.8 %all-gather.4.cloned.1.call-start = ((), (), s32[]{:S(2)}) async-start(), calls=%async_computation.4 | async-start | bytes 2703360 | tf_op jit(solution)/shard_map/all_gather | solution.py:381
  45.3 28.8 %collective-permute-start.5 = (bf16[2048,256]{1,0:T(8,128)(2,1)S(1)}, bf16[2048,256]{1,0:T(8,128)(2,1)}, u32[]{:S(2)}, u32[]{:S(2)}) collective-permute-start(bf16[2048,256]{1,0:T(8,128)(2,1)S(1)} %bitcast.459), channel_id=1, source_target_pairs={{0,16},{16,0},{1,17},{17,1},{2,18},{18,2},{3,19},{19,3},{4,20},{20... | collective-permute-start | bytes 3145736 | tf_op jit(solution)/shard_map/ppermute | solution.py:38
  46.8 27.3 %collective-permute-start.6 = (bf16[2048,256]{1,0:T(8,128)(2,1)S(1)}, bf16[2048,256]{1,0:T(8,128)(2,1)}, u32[]{:S(2)}, u32[]{:S(2)}) collective-permute-start(bf16[2048,256]{1,0:T(8,128)(2,1)S(1)} %bitcast.460), channel_id=1, source_target_pairs={{0,4},{4,0},{1,5},{5,1},{2,6},{6,2},{3,7},{7,3},{8,12},{12,8},{9,1... | collective-permute-start | bytes 3145736 | tf_op jit(solution)/shard_map/ppermute | solution.py:42
  50.6 21.4 %collective-permute-start.2 = (bf16[336,256]{1,0:T(8,128)(2,1)}, bf16[336,256]{1,0:T(8,128)(2,1)}, u32[]{:S(2)}, u32[]{:S(2)}) collective-permute-start(bf16[336,256]{1,0:T(8,128)(2,1)} %get-tuple-element.331), channel_id=1, source_target_pairs={{0,2},{1,10},{2,0},{3,8},{8,3},{9,11},{10,1},{11,9},{4,6},{5,14},{... | collective-permute-start | bytes 516104 | tf_op jit(solution)/shard_map/ppermute | solution.py:433
  54.0 110.5 %all-gather.6.cloned.1.call-start = ((), (), s32[]{:S(2)}) async-start(), calls=%async_computation.5 | async-start | bytes 2621440 | tf_op jit(solution)/shard_map/all_gather | solution.py:381
  72.1 21.2 %collective-permute-start.14 = (bf16[784,256]{1,0:T(8,128)(2,1)S(1)}, bf16[784,256]{1,0:T(8,128)(2,1)S(1)}, u32[]{:S(2)}, u32[]{:S(2)}) collective-permute-start(bf16[784,256]{1,0:T(8,128)(2,1)S(1)} %copy-done.103), channel_id=1, source_target_pairs={{0,4},{4,0},{1,5},{5,1},{2,6},{6,2},{3,7},{7,3},{8,12},{12,8},{9,1... | collective-permute-start | bytes 1204232 | tf_op jit(solution)/shard_map/ppermute | solution.py:42
  105.0 157.7 %all-gather.8.cloned.1.call-start = ((), (), s32[]{:S(2)}) async-start(), calls=%async_computation.6 | async-start | bytes 5406720 | tf_op jit(solution)/shard_map/all_gather | solution.py:381
  113.1 50.0 %collective-permute-start.13 = (bf16[4224,256]{1,0:T(8,128)(2,1)S(1)}, bf16[4224,256]{1,0:T(8,128)(2,1)}, u32[]{:S(2)}, u32[]{:S(2)}) collective-permute-start(bf16[4224,256]{1,0:T(8,128)(2,1)S(1)} %copy-done.50), channel_id=1, source_target_pairs={{0,4},{4,0},{1,5},{5,1},{2,6},{6,2},{3,7},{7,3},{8,12},{12,8},{9,1... | collective-permute-start | bytes 6488072 | tf_op jit(solution)/shard_map/ppermute | solution.py:42
  115.4 49.1 %collective-permute-start.12 = (bf16[4224,256]{1,0:T(8,128)(2,1)S(1)}, bf16[4224,256]{1,0:T(8,128)(2,1)}, u32[]{:S(2)}, u32[]{:S(2)}) collective-permute-start(bf16[4224,256]{1,0:T(8,128)(2,1)S(1)} %copy-done.50), channel_id=1, source_target_pairs={{0,16},{16,0},{1,17},{17,1},{2,18},{18,2},{3,19},{19,3},{4,20},{20... | collective-permute-start | bytes 6488072 | tf_op jit(solution)/shard_map/ppermute | solution.py:38
  171.6 26.4 %collective-permute-start.17 = (bf16[2112,256]{1,0:T(8,128)(2,1)}, bf16[2112,256]{1,0:T(8,128)(2,1)}, u32[]{:S(2)}, u32[]{:S(2)}) collective-permute-start(bf16[2112,256]{1,0:T(8,128)(2,1)} %slice.794), channel_id=1, source_target_pairs={{0,16},{16,0},{1,17},{17,1},{2,18},{18,2},{3,19},{19,3},{4,20},{20... | collective-permute-start | bytes 3244040 | tf_op jit(solution)/shard_map/ppermute | solution.py:38
  175.4 26.1 %collective-permute-start.18 = (bf16[2112,256]{1,0:T(8,128)(2,1)}, bf16[2112,256]{1,0:T(8,128)(2,1)}, u32[]{:S(2)}, u32[]{:S(2)}) collective-permute-start(bf16[2112,256]{1,0:T(8,128)(2,1)} %slice.795), channel_id=1, source_target_pairs={{0,4},{4,0},{1,5},{5,1},{2,6},{6,2},{3,7},{7,3},{8,12},{12,8},{9,1... | collective-permute-start | bytes 3244040 | tf_op jit(solution)/shard_map/ppermute | solution.py:42
  175.7 414.9 %reduce-scatter.5.cloned.1.call-start = ((), (), s32[]{:S(2)}) async-start(), calls=%async_computation.7 | async-start | bytes 2621440 | tf_op jit(solution)/shard_map/reduce_scatter | solution.py:497
  178.4 31.6 %collective-permute-start.16 = (bf16[320,1024]{1,0:T(8,128)(2,1)S(1)}, bf16[320,1024]{1,0:T(8,128)(2,1)S(1)}, u32[]{:S(2)}, u32[]{:S(2)}) collective-permute-start(bf16[320,1024]{1,0:T(8,128)(2,1)S(1)} %multiply_convert_fusion.8), channel_id=1, source_target_pairs={{0,8},{8,0},{1,9},{9,1},{2,10},{10,2},{3,11},{11,3},{4,12},{12,4},... | collective-permute-start | bytes 1966088 | tf_op jit(solution)/shard_map/ppermute | solution.py:34
  201.8 24.3 %collective-permute-start.19 = (bf16[1024,512]{1,0:T(8,128)(2,1)S(1)}, bf16[1024,512]{1,0:T(8,128)(2,1)S(1)}, u32[]{:S(2)}, u32[]{:S(2)}) collective-permute-start(bf16[1024,512]{1,0:T(8,128)(2,1)S(1)} %bitcast.464), channel_id=1, source_target_pairs={{0,16},{16,0},{1,17},{17,1},{2,18},{18,2},{3,19},{19,3},{4,20},{20... | collective-permute-start | bytes 3145736 | tf_op jit(solution)/shard_map/ppermute | solution.py:38
  202.4 24.0 %collective-permute-start.20 = (bf16[1024,512]{1,0:T(8,128)(2,1)S(1)}, bf16[1024,512]{1,0:T(8,128)(2,1)S(1)}, u32[]{:S(2)}, u32[]{:S(2)}) collective-permute-start(bf16[1024,512]{1,0:T(8,128)(2,1)S(1)} %bitcast.462), channel_id=1, source_target_pairs={{0,4},{4,0},{1,5},{5,1},{2,6},{6,2},{3,7},{7,3},{8,12},{12,8},{9,1... | collective-permute-start | bytes 3145736 | tf_op jit(solution)/shard_map/ppermute | solution.py:42
  232.4 16.5 %collective-permute-start.23 = (bf16[320,1024]{1,0:T(8,128)(2,1)S(1)}, bf16[320,1024]{1,0:T(8,128)(2,1)S(1)}, u32[]{:S(2)}, u32[]{:S(2)}) collective-permute-start(bf16[320,1024]{1,0:T(8,128)(2,1)S(1)} %multiply_convert_fusion.7), channel_id=1, source_target_pairs={{0,4},{1,5},{2,6},{3,7},{8,12},{9,13},{10,14},{11,15},{16,20},{17,... | collective-permute-start | bytes 1966088 | tf_op jit(solution)/shard_map/ppermute | solution.py:676
  265.3 49.0 %collective-permute-start.25 = (bf16[2112,512]{1,0:T(8,128)(2,1)S(1)}, bf16[2112,512]{1,0:T(8,128)(2,1)}, u32[]{:S(2)}, u32[]{:S(2)}) collective-permute-start(bf16[2112,512]{1,0:T(8,128)(2,1)S(1)} %bitcast.440), channel_id=1, source_target_pairs={{0,16},{16,0},{1,17},{17,1},{2,18},{18,2},{3,19},{19,3},{4,20},{20... | collective-permute-start | bytes 6488072 | tf_op jit(solution)/shard_map/ppermute | solution.py:38
  266.9 48.6 %collective-permute-start.26 = (bf16[2112,512]{1,0:T(8,128)(2,1)S(1)}, bf16[2112,512]{1,0:T(8,128)(2,1)}, u32[]{:S(2)}, u32[]{:S(2)}) collective-permute-start(bf16[2112,512]{1,0:T(8,128)(2,1)S(1)} %bitcast.438), channel_id=1, source_target_pairs={{0,4},{4,0},{1,5},{5,1},{2,6},{6,2},{3,7},{7,3},{8,12},{12,8},{9,1... | collective-permute-start | bytes 6488072 | tf_op jit(solution)/shard_map/ppermute | solution.py:42
  269.1 42.9 %collective-permute-start.28 = (bf16[320,256]{1,0:T(8,128)(2,1)S(1)}, bf16[320,256]{1,0:T(8,128)(2,1)S(1)}, u32[]{:S(2)}, u32[]{:S(2)}) collective-permute-start(bf16[320,256]{1,0:T(8,128)(2,1)S(1)} %get-tuple-element.372), channel_id=1, source_target_pairs={{0,8},{1,0},{2,10},{3,2},{8,9},{9,1},{10,11},{11,3},{4,12},{5,4},{... | collective-permute-start | bytes 491528 | tf_op jit(solution)/shard_map/ppermute | solution.py:433
  270.9 41.1 %collective-permute-start.29 = (bf16[320,256]{1,0:T(8,128)(2,1)S(1)}, bf16[320,256]{1,0:T(8,128)(2,1)S(1)}, u32[]{:S(2)}, u32[]{:S(2)}) collective-permute-start(bf16[320,256]{1,0:T(8,128)(2,1)S(1)} %get-tuple-element.371), channel_id=1, source_target_pairs={{0,2},{1,10},{2,0},{3,8},{8,3},{9,11},{10,1},{11,9},{4,6},{5,14},{... | collective-permute-start | bytes 491528 | tf_op jit(solution)/shard_map/ppermute | solution.py:433
  271.9 40.1 %collective-permute-start.30 = (bf16[320,256]{1,0:T(8,128)(2,1)S(1)}, bf16[320,256]{1,0:T(8,128)(2,1)S(1)}, u32[]{:S(2)}, u32[]{:S(2)}) collective-permute-start(bf16[320,256]{1,0:T(8,128)(2,1)S(1)} %get-tuple-element.370), channel_id=1, source_target_pairs={{0,10},{1,2},{2,8},{3,0},{8,11},{9,3},{10,9},{11,1},{4,14},{5,6},{... | collective-permute-start | bytes 491528 | tf_op jit(solution)/shard_map/ppermute | solution.py:433
  379.7 45.9 %collective-permute-start.43 = (bf16[2112,512]{1,0:T(8,128)(2,1)}, bf16[2112,512]{1,0:T(8,128)(2,1)S(1)}, u32[]{:S(2)}, u32[]{:S(2)}) collective-permute-start(bf16[2112,512]{1,0:T(8,128)(2,1)} %bitcast.90), channel_id=1, source_target_pairs={{0,4},{4,0},{1,5},{5,1},{2,6},{6,2},{3,7},{7,3},{8,12},{12,8},{9,1... | collective-permute-start | bytes 6488072 | tf_op jit(solution)/shard_map/ppermute | solution.py:42
  382.8 45.7 %collective-permute-start.42 = (bf16[2112,512]{1,0:T(8,128)(2,1)}, bf16[2112,512]{1,0:T(8,128)(2,1)}, u32[]{:S(2)}, u32[]{:S(2)}) collective-permute-start(bf16[2112,512]{1,0:T(8,128)(2,1)} %bitcast.86), channel_id=1, source_target_pairs={{0,16},{16,0},{1,17},{17,1},{2,18},{18,2},{3,19},{19,3},{4,20},{20... | collective-permute-start | bytes 6488072 | tf_op jit(solution)/shard_map/ppermute | solution.py:38
  431.7 21.4 %collective-permute-start.41 = (bf16[320,1024]{1,0:T(8,128)(2,1)S(1)}, bf16[320,1024]{1,0:T(8,128)(2,1)S(1)}, u32[]{:S(2)}, u32[]{:S(2)}) collective-permute-start(bf16[320,1024]{1,0:T(8,128)(2,1)S(1)} %slice.1095), channel_id=1, source_target_pairs={{0,8},{8,0},{1,9},{9,1},{2,10},{10,2},{3,11},{11,3},{4,12},{12,4},... | collective-permute-start | bytes 1966088 | tf_op jit(solution)/shard_map/ppermute | solution.py:34
  433.4 19.6 %collective-permute-start.45 = (bf16[320,1024]{1,0:T(8,128)(2,1)S(1)}, bf16[320,1024]{1,0:T(8,128)(2,1)S(1)}, u32[]{:S(2)}, u32[]{:S(2)}) collective-permute-start(bf16[320,1024]{1,0:T(8,128)(2,1)S(1)} %fusion.53), channel_id=1, source_target_pairs={{4,0},{5,1},{6,2},{7,3},{12,8},{13,9},{14,10},{15,11},{20,16},{21,... | collective-permute-start | bytes 1966088 | tf_op jit(solution)/shard_map/ppermute | solution.py:723
  437.3 44.2 %collective-permute-start.50 = (bf16[1024,512]{1,0:T(8,128)(2,1)S(1)}, bf16[1024,512]{1,0:T(8,128)(2,1)S(1)}, u32[]{:S(2)}, u32[]{:S(2)}) collective-permute-start(bf16[1024,512]{1,0:T(8,128)(2,1)S(1)} %pad_maximum_fusion.30), channel_id=1, source_target_pairs={{0,4},{4,0},{1,5},{5,1},{2,6},{6,2},{3,7},{7,3},{8,12},{12,8},{9,1... | collective-permute-start | bytes 3145736 | tf_op jit(solution)/shard_map/ppermute | solution.py:42
  458.3 25.6 %collective-permute-start.49 = (bf16[1024,512]{1,0:T(8,128)(2,1)S(1)}, bf16[1024,512]{1,0:T(8,128)(2,1)S(1)}, u32[]{:S(2)}, u32[]{:S(2)}) collective-permute-start(bf16[1024,512]{1,0:T(8,128)(2,1)S(1)} %concatenate.577), channel_id=1, source_target_pairs={{0,16},{16,0},{1,17},{17,1},{2,18},{18,2},{3,19},{19,3},{4,20},{20... | collective-permute-start | bytes 3145736 | tf_op jit(solution)/shard_map/ppermute | solution.py:38
  487.6 125.1 %reduce-scatter.7.cloned.1.call-start = ((), (), s32[]{:S(2)}) async-start(), calls=%async_computation.8 | async-start | bytes 5406720 | tf_op jit(solution)/shard_map/reduce_scatter | solution.py:497
  491.3 52.4 %collective-permute-start.53 = (bf16[2112,512]{1,0:T(8,128)(2,1)}, bf16[2112,512]{1,0:T(8,128)(2,1)}, u32[]{:S(2)}, u32[]{:S(2)}) collective-permute-start(bf16[2112,512]{1,0:T(8,128)(2,1)} %fusion.31), channel_id=1, source_target_pairs={{0,4},{4,0},{1,5},{5,1},{2,6},{6,2},{3,7},{7,3},{8,12},{12,8},{9,1... | collective-permute-start | bytes 6488072 | tf_op jit(solution)/shard_map/ppermute | solution.py:42
  505.8 175.8 %reduce-scatter.9.cloned.1.call-start = ((), (), s32[]{:S(2)}) async-start(), calls=%async_computation.9 | async-start | bytes 2703360 | tf_op jit(solution)/shard_map/reduce_scatter | solution.py:497
  508.9 50.2 %collective-permute-start.52 = (bf16[2112,512]{1,0:T(8,128)(2,1)}, bf16[2112,512]{1,0:T(8,128)(2,1)}, u32[]{:S(2)}, u32[]{:S(2)}) collective-permute-start(bf16[2112,512]{1,0:T(8,128)(2,1)} %pad_maximum_fusion.8), channel_id=1, source_target_pairs={{0,16},{16,0},{1,17},{17,1},{2,18},{18,2},{3,19},{19,3},{4,20},{20... | collective-permute-start | bytes 6488072 | tf_op jit(solution)/shard_map/ppermute | solution.py:38
  541.0 43.1 %collective-permute-start.51 = (bf16[320,1024]{1,0:T(8,128)(2,1)S(1)}, bf16[320,1024]{1,0:T(8,128)(2,1)S(1)}, u32[]{:S(2)}, u32[]{:S(2)}) collective-permute-start(bf16[320,1024]{1,0:T(8,128)(2,1)S(1)} %slice.1092), channel_id=1, source_target_pairs={{0,8},{8,0},{1,9},{9,1},{2,10},{10,2},{3,11},{11,3},{4,12},{12,4},... | collective-permute-start | bytes 1966088 | tf_op jit(solution)/shard_map/ppermute | solution.py:34
  546.0 44.6 %collective-permute-start.57 = (bf16[2112,256]{1,0:T(8,128)(2,1)S(1)}, bf16[2112,256]{1,0:T(8,128)(2,1)}, u32[]{:S(2)}, u32[]{:S(2)}) collective-permute-start(bf16[2112,256]{1,0:T(8,128)(2,1)S(1)} %slice.865), channel_id=1, source_target_pairs={{0,16},{16,0},{1,17},{17,1},{2,18},{18,2},{3,19},{19,3},{4,20},{20... | collective-permute-start | bytes 3244040 | tf_op jit(solution)/shard_map/ppermute | solution.py:38
  565.9 18.1 %collective-permute-start.55 = (bf16[320,1024]{1,0:T(8,128)(2,1)S(1)}, bf16[320,1024]{1,0:T(8,128)(2,1)S(1)}, u32[]{:S(2)}, u32[]{:S(2)}) collective-permute-start(bf16[320,1024]{1,0:T(8,128)(2,1)S(1)} %fusion.51), channel_id=1, source_target_pairs={{4,0},{5,1},{6,2},{7,3},{12,8},{13,9},{14,10},{15,11},{20,16},{21,... | collective-permute-start | bytes 1966088 | tf_op jit(solution)/shard_map/ppermute | solution.py:723
  572.9 51.1 %collective-permute-start.62 = (bf16[1024,512]{1,0:T(8,128)(2,1)}, bf16[1024,512]{1,0:T(8,128)(2,1)}, u32[]{:S(2)}, u32[]{:S(2)}) collective-permute-start(bf16[1024,512]{1,0:T(8,128)(2,1)} %concatenate.584), channel_id=1, source_target_pairs={{0,16},{16,0},{1,17},{17,1},{2,18},{18,2},{3,19},{19,3},{4,20},{20... | collective-permute-start | bytes 3145736 | tf_op jit(solution)/shard_map/ppermute | solution.py:38
  584.0 27.1 %collective-permute-start.56 = (bf16[2112,256]{1,0:T(8,128)(2,1)}, bf16[2112,256]{1,0:T(8,128)(2,1)}, u32[]{:S(2)}, u32[]{:S(2)}) collective-permute-start(bf16[2112,256]{1,0:T(8,128)(2,1)} %slice.864), channel_id=1, source_target_pairs={{0,4},{4,0},{1,5},{5,1},{2,6},{6,2},{3,7},{7,3},{8,12},{12,8},{9,1... | collective-permute-start | bytes 3244040 | tf_op jit(solution)/shard_map/ppermute | solution.py:42
  587.2 47.8 %collective-permute-start.63 = (bf16[1088,512]{1,0:T(8,128)(2,1)}, bf16[1088,512]{1,0:T(8,128)(2,1)}, u32[]{:S(2)}, u32[]{:S(2)}) collective-permute-start(bf16[1088,512]{1,0:T(8,128)(2,1)} %pad_maximum_fusion.23), channel_id=1, source_target_pairs={{0,4},{4,0},{1,5},{5,1},{2,6},{6,2},{3,7},{7,3},{8,12},{12,8},{9,1... | collective-permute-start | bytes 3342344 | tf_op jit(solution)/shard_map/ppermute | solution.py:42
  619.0 92.8 %reduce-scatter.11.cloned.1.call-start = ((), (), s32[]{:S(2)}) async-start(), calls=%async_computation.10 | async-start | bytes 1351680 | tf_op jit(solution)/shard_map/reduce_scatter | solution.py:497
  620.1 19.1 %collective-permute-start.70 = (bf16[256,256]{1,0:T(8,128)(2,1)S(1)}, bf16[256,256]{1,0:T(8,128)(2,1)S(1)}, u32[]{:S(2)}, u32[]{:S(2)}) collective-permute-start(bf16[256,256]{1,0:T(8,128)(2,1)S(1)} %get-tuple-element.399), channel_id=1, source_target_pairs={{0,4},{4,0},{1,5},{5,1},{2,6},{6,2},{3,7},{7,3},{8,12},{12,8},{9,1... | collective-permute-start | bytes 393224 | tf_op jit(solution)/shard_map/ppermute | solution.py:42
  621.7 34.9 %collective-permute-start.72 = (bf16[256,512]{1,0:T(8,128)(2,1)S(1)}, bf16[256,512]{1,0:T(8,128)(2,1)S(1)}, u32[]{:S(2)}, u32[]{:S(2)}) collective-permute-start(bf16[256,512]{1,0:T(8,128)(2,1)S(1)} %maximum_select_fusion.15), channel_id=1, source_target_pairs={{0,16},{16,0},{1,17},{17,1},{2,18},{18,2},{3,19},{19,3},{4,20},{20... | collective-permute-start | bytes 786440 | tf_op jit(solution)/shard_map/ppermute | solution.py:38
  623.3 36.3 %collective-permute-start.66 = (bf16[528,256]{1,0:T(8,128)(2,1)S(1)}, bf16[528,256]{1,0:T(8,128)(2,1)S(1)}, u32[]{:S(2)}, u32[]{:S(2)}) collective-permute-start(bf16[528,256]{1,0:T(8,128)(2,1)S(1)} %get-tuple-element.314), channel_id=1, source_target_pairs={{0,4},{4,0},{1,5},{5,1},{2,6},{6,2},{3,7},{7,3},{8,12},{12,8},{9,1... | collective-permute-start | bytes 811016 | tf_op jit(solution)/shard_map/ppermute | solution.py:42
  624.1 37.2 %collective-permute-start.68 = (bf16[528,512]{1,0:T(8,128)(2,1)S(1)}, bf16[528,512]{1,0:T(8,128)(2,1)S(1)}, u32[]{:S(2)}, u32[]{:S(2)}) collective-permute-start(bf16[528,512]{1,0:T(8,128)(2,1)S(1)} %maximum_select_fusion.9), channel_id=1, source_target_pairs={{0,16},{16,0},{1,17},{17,1},{2,18},{18,2},{3,19},{19,3},{4,20},{20... | collective-permute-start | bytes 1622024 | tf_op jit(solution)/shard_map/ppermute | solution.py:38
  636.8 44.8 %collective-permute-start.65 = (bf16[1088,256]{1,0:T(8,128)(2,1)S(1)}, bf16[1088,256]{1,0:T(8,128)(2,1)}, u32[]{:S(2)}, u32[]{:S(2)}) collective-permute-start(bf16[1088,256]{1,0:T(8,128)(2,1)S(1)} %slice.881), channel_id=1, source_target_pairs={{0,16},{16,0},{1,17},{17,1},{2,18},{18,2},{3,19},{19,3},{4,20},{20... | collective-permute-start | bytes 1671176 | tf_op jit(solution)/shard_map/ppermute | solution.py:38
  655.9 23.7 %collective-permute-start.64 = (bf16[1024,256]{1,0:T(8,128)(2,1)S(1)}, bf16[1024,256]{1,0:T(8,128)(2,1)}, u32[]{:S(2)}, u32[]{:S(2)}) collective-permute-start(bf16[1024,256]{1,0:T(8,128)(2,1)S(1)} %slice.880), channel_id=1, source_target_pairs={{0,4},{4,0},{1,5},{5,1},{2,6},{6,2},{3,7},{7,3},{8,12},{12,8},{9,1... | collective-permute-start | bytes 1572872 | tf_op jit(solution)/shard_map/ppermute | solution.py:42
  656.6 41.4 %collective-permute-start.58 = (bf16[320,256]{1,0:T(8,128)(2,1)}, bf16[320,256]{1,0:T(8,128)(2,1)}, u32[]{:S(2)}, u32[]{:S(2)}) collective-permute-start(bf16[320,256]{1,0:T(8,128)(2,1)} %get-tuple-element.337), channel_id=1, source_target_pairs={{0,0},{8,1},{2,2},{10,3},{1,8},{9,9},{3,10},{11,11},{4,4},{12,5},{... | collective-permute-start | bytes 491528 | tf_op jit(solution)/shard_map/ppermute | solution.py:359
  661.3 36.6 %collective-permute-start.59 = (bf16[320,256]{1,0:T(8,128)(2,1)}, bf16[320,256]{1,0:T(8,128)(2,1)}, u32[]{:S(2)}, u32[]{:S(2)}) collective-permute-start(bf16[320,256]{1,0:T(8,128)(2,1)} %get-tuple-element.340), channel_id=1, source_target_pairs={{8,0},{0,1},{10,2},{2,3},{9,8},{1,9},{11,10},{3,11},{12,4},{4,5},{... | collective-permute-start | bytes 491528 | tf_op jit(solution)/shard_map/ppermute | solution.py:359
  673.4 24.5 %collective-permute-start.60 = (bf16[320,256]{1,0:T(8,128)(2,1)}, bf16[320,256]{1,0:T(8,128)(2,1)}, u32[]{:S(2)}, u32[]{:S(2)}) collective-permute-start(bf16[320,256]{1,0:T(8,128)(2,1)} %get-tuple-element.339), channel_id=1, source_target_pairs={{2,0},{10,1},{0,2},{8,3},{3,8},{11,9},{1,10},{9,11},{6,4},{14,5},{... | collective-permute-start | bytes 491528 | tf_op jit(solution)/shard_map/ppermute | solution.py:359
  679.6 18.3 %collective-permute-start.61 = (bf16[320,256]{1,0:T(8,128)(2,1)S(1)}, bf16[320,256]{1,0:T(8,128)(2,1)}, u32[]{:S(2)}, u32[]{:S(2)}) collective-permute-start(bf16[320,256]{1,0:T(8,128)(2,1)S(1)} %get-tuple-element.338), channel_id=1, source_target_pairs={{10,0},{2,1},{8,2},{0,3},{11,8},{3,9},{9,10},{1,11},{14,4},{6,5},{... | collective-permute-start | bytes 491528 | tf_op jit(solution)/shard_map/ppermute | solution.py:359
  (192 other events, 1663.7 us)
Sparse Core Ops, SparseCore 0:
  54.1 50.8 all-gather.3
  107.1 43.8 all-gather.5
  175.8 86.8 all-gather.7
  487.8 44.5 reduce-scatter.4
  534.6 78.1 reduce-scatter.6
  619.1 45.6 reduce-scatter.8
  686.7 25.0 reduce-scatter.10

commit v5 on v4

--- a/solution.py
+++ b/solution.py
@@ -789,11 +789,11 @@
             return [a for pair in grads for a in pair]
 
         grad, g_ffn_two, gain_ffn_two = ffn_backward(
-            last_grad.astype(f32), ffn_two, gains[3], kept_ffn_two, kinds, (output,)
+            last_grad.astype(f32), ffn_two, gains[3], kept_ffn_two, kinds, ()
         )
         r_ffn_two = return_ffn_two(*g_ffn_two)
         grad, g_attn_two, gain_attn_two, extra, done_attn_two = attn_backward(
-            grad, attn_two, gains[2], kept_attn_two, None, tuple(leaves(g_ffn_two)), (r_ffn_two[1], r_ffn_two[3])
+            grad, attn_two, gains[2], kept_attn_two, None, tuple(leaves(g_ffn_two)), (r_ffn_two[1], r_ffn_two[3], output)
         )
         r_attn_two = return_attn_two(g_attn_two)
         sent_attn_two = (r_attn_two[1], r_attn_two[3])
@@ -811,7 +811,7 @@
         gain_rows = jnp.stack([gain_attn_one, gain_ffn_one, gain_attn_two, gain_ffn_two])
         gain_rows = jnp.pad(gain_rows, ((0, 12), (0, 0))).astype(bf16)
         r_attn_one = return_attn(g_attn_one, gain_rows)
-        p_ffn_one = pack_parts(last_ffn(r_ffn_one, t_attn_two, t_ffn_two, *r_attn_one.near))
+        p_ffn_one = pack_parts(last_ffn(r_ffn_one, *r_attn_one.near))
         t_ffn_one = scatter(p_ffn_one)
         r_attn_one.second((p_ffn_one,))
         b_ffn_two = finish_ffn_two(t_ffn_two, p_ffn_one)

time: 744 us -> 731 us (0.983)
  waiting for transfers between devices: 230 us -> 209 us
  matrix products: 97.3 us -> 86.7 us
  starting transfers between devices: 80.3 us -> 89.3 us
  local copies, waits for them, and re-layouts: 51.9 us -> 59.4 us
    ppermute x25, starting transfers between devices: 7.01 us -> 20.2 us  [swap_core(): return lax.ppermute(value, 'core', SWAP)]
    ppermute x18, waiting for transfers between devices: 87.4 us -> 77.2 us  [swap_x(): return lax.ppermute(value, 'xi', SWAP)]
    unnamed x316 -> x322, local copies, waits for them, and re-layouts: 19.6 us -> 24.7 us
  transfers between devices with their start and end apart: 86 -> 86, of which waited for: 38 -> 35; matrix products, arithmetic and copies ran while one was open for 26% -> 28% of each run, Pallas kernels for 18% -> 18%
where the time goes in v5:
time: 731 us; the launch traced here: 723 us
  waiting for transfers between devices  209 us (29%)
  Pallas kernels  130 us (18%)
  other arithmetic  95.8 us (13%)
  starting transfers between devices  89.3 us (12%)
  matrix products  86.7 us (12%)
  local copies, waits for them, and re-layouts  59.4 us (8%)
  blocking collectives  33.8 us (5%)
  between operations  19 us (3%)
    ppermute x18, waiting for transfers between devices, swap_x(): return lax.ppermute(value, 'xi', SWAP)  77.2 us
    ppermute x16, waiting for transfers between devices, swap_y(): return lax.ppermute(value, 'row', SWAP)  50.9 us
    pallas_call x2, Pallas kernels, attend_back(): pl.pallas_call(kernel, grid=(pairs,), in_specs=in_specs, out_specs=[pair_...  48.1 us
    all_gather x2, blocking collectives, gather_col(): return lax.all_gather(block, 'col', axis=0, tiled=True)  33.8 us
    dot_general x22, matrix products, dot_tn(): lax.dot_general(left, right, (((0,), (0,)), ((), ())), preferred_element_...  32 us
    pallas_call x2, Pallas kernels, attend(): pl.pallas_call(kernel, grid=(pairs,), in_specs=[pair_block(n, 0), pair_bl...  29.9 us
    pallas_call x4, Pallas kernels, project(): pl.pallas_call(kernel, grid=(turned + plain,), in_specs=in_specs, out_spe...  28.1 us
    dot_general x8, matrix products, dot_nt(): lax.dot_general(left, right, (((1,), (1,)), ((), ())), preferred_element_...  27.4 us
  transfers between devices with their start and end apart: 86, of which 35 were waited for; matrix products, arithmetic and copies ran while one was open for 28% of the time, Pallas kernels for 18%

profile of v5, /device:TPU:0, one launch (start us, length us, event | category | flops | bytes accessed | tf_op | source)
XLA Modules:
  0.0 723.1 jit_solution(17479426271861030037)
XLA Ops:
  10.5 17.4 %all_gather.15 = bf16[1024,256]{1,0:T(8,128)(2,1)S(1)} all-gather(bf16[256,256]{1,0:T(8,128)(2,1)S(1)} %pad_maximum_fusion.76), channel_id=1, replica_groups=mesh['xo'=1,'xi'=2,'core'=2,'row'=2,'col'=4] {'col'}, dimensions={0}, use_global_device_ids=true | all-gather | bytes 655360 | tf_op jit(solution)/shard_map/all_gather | solution.py:381
  28.7 16.4 %all_gather.16 = bf16[1024,256]{1,0:T(8,128)(2,1)S(1)} all-gather(bf16[256,256]{1,0:T(8,128)(2,1)S(1)} %pad_maximum_fusion.77), channel_id=1, replica_groups=mesh['xo'=1,'xi'=2,'core'=2,'row'=2,'col'=4] {'col'}, dimensions={0}, use_global_device_ids=true | all-gather | bytes 655360 | tf_op jit(solution)/shard_map/all_gather | solution.py:381
  50.3 3.3 collective-permute-start.7
  65.8 3.7 fusion.135
  77.6 5.7 collective-permute-done.8.low_ref
  83.3 5.6 collective-permute-done.9.high_ref
  93.2 9.6 %all-gather.4.cloned.1.call-done.whole_ref = bf16[4224,256]{1,0:T(8,128)(2,1)} async-done(((bf16[1056,256]{1,0:T(8,128)(2,1)}), bf16[4224,256]{1,0:T(8,128)(2,1)}) %all-gather.4.cloned.1.call-update) | async-done | bytes 2162704 | tf_op jit(solution)/shard_map/all_gather | solution.py:381
  104.5 5.1 collective-permute-start.11
  120.4 4.7 shard_map.365
  125.1 8.0 %shard_map.366.q_ref.kb_ref.vb_ref.rest_0_ = bf16[640,1536]{1,0:T(8,128)(2,1)} custom-call(bf16[640,1024]{1,0:T(8,128)(2,1)} %pad_maximum_fusion.14.n_ref, bf16[1024,1024]{1,0:T(8,128)(2,1)} %bitcast.425, bf16[512,1024]{1,0:T(8,128)(2,1)} %bitcast.430, f32[640,128]{1,0:T(8,128)} %get-tuple-element.469.cos_ref.co_ref, f32[640,128]{1,0:T(8,128)} %get-tuple-element.472.sin_ref), custom_call_target="tpu_custom_call" | custom-call | flops 1 | bytes 1 | tf_op jit(solution)/shard_map/pallas_call | solution.py:104
  133.1 5.9 shard_map.367.ka_ref.va_ref.rest_0_
  139.0 15.0 %shard_map.368 = (bf16[640,512]{1,0:T(8,128)(2,1)}, f32[4,2,1,640]{3,2,1,0:T(1,128)}) custom-call(bf16[640,1536]{1,0:T(8,128)(2,1)} %shard_map.366.q_ref.kb_ref.vb_ref.rest_0_, bf16[640,1024]{1,0:T(8,128)(2,1)} %shard_map.367.ka_ref.va_ref.rest_0_, bf16[640,1536]{1,0:T(8,128)(2,1)} %shard_map.366.q_ref.kb_ref.vb_ref.rest_0_, ...), custom_call_target="tpu_custom_call" | custom-call | flops 1 | bytes 1 | tf_op jit(solution)/shard_map/pallas_call | solution.py:217
  153.9 8.4 %collective-permute-done.12.x_ref = bf16[4224,256]{1,0:T(8,128)(2,1)} collective-permute-done((bf16[4224,256]{1,0:T(8,128)(2,1)S(1)}, bf16[4224,256]{1,0:T(8,128)(2,1)}, u32[]{:S(2)}, u32[]{:S(2)}) %collective-permute-start.12) | collective-permute-done | bytes 2162720 | tf_op jit(solution)/shard_map/ppermute | solution.py:38
  178.0 19.8 %collective-permute-done.17.low_ref = bf16[2112,256]{1,0:T(8,128)(2,1)} collective-permute-done((bf16[2112,256]{1,0:T(8,128)(2,1)}, bf16[2112,256]{1,0:T(8,128)(2,1)}, u32[]{:S(2)}, u32[]{:S(2)}) %collective-permute-start.17) | collective-permute-done | bytes 1081376 | tf_op jit(solution)/shard_map/ppermute | solution.py:38
  203.9 7.3 %shard_map.369 = (bf16[1,1408,1024]{2,1,0:T(8,128)(2,1)}, bf16[1,1408,1024]{2,1,0:T(8,128)(2,1)}, bf16[1,1408,1024]{2,1,0:T(8,128)(2,1)}) custom-call(bf16[4224,256]{1,0:T(8,128)(2,1)} %all-gather.4.cloned.1.call-done.whole_ref, bf16[4224,256]{1,0:T(8,128)(2,1)} %collective-permute-done.13.y_ref, bf16[4224,256]{1,0:T(8,128)(2,1)} %collective-permute-done.12.x_ref, ...), custom_call_target="tpu_custom_call" | custom-call | flops 1 | bytes 1 | tf_op jit(solution)/shard_map/pallas_call | solution.py:141
  211.3 4.3 fusion.28
  215.7 4.3 multiply_convert_fusion.5
  219.9 4.8 collective-permute-done.19.xf_ref
  232.2 3.7 collective-permute-start.23
  235.9 14.2 %collective-permute-done.23 = bf16[320,1024]{1,0:T(8,128)(2,1)S(1)} collective-permute-done((bf16[320,1024]{1,0:T(8,128)(2,1)S(1)}, bf16[320,1024]{1,0:T(8,128)(2,1)S(1)}, u32[]{:S(2)}, u32[]{:S(2)}) %collective-permute-start.23) | collective-permute-done | bytes 655392 | tf_op jit(solution)/shard_map/ppermute | solution.py:676
  253.6 7.2 all-gather.8.cloned.1.call-done
  271.2 4.3 collective-permute-done.30
  277.2 4.7 shard_map.370
  283.1 8.1 %shard_map.371.q_ref.kb_ref.vb_ref = bf16[640,1536]{1,0:T(8,128)(2,1)} custom-call(bf16[640,1024]{1,0:T(8,128)(2,1)} %pad_maximum_fusion.16.n_ref, bf16[1024,1024]{1,0:T(8,128)(2,1)} %bitcast.427, bf16[512,1024]{1,0:T(8,128)(2,1)} %bitcast.432, f32[640,128]{1,0:T(8,128)} %get-tuple-element.469.cos_ref.co_ref, f32[640,128]{1,0:T(8,128)} %get-tuple-element.472.sin_ref, ...), custom_call_target="tpu_custom_call" | custom-call | flops 1 | bytes 1 | tf_op jit(solution)/shard_map/pallas_call | solution.py:104
  291.2 6.1 shard_map.372.ka_ref.va_ref
  297.3 14.9 %shard_map.373 = (bf16[640,512]{1,0:T(8,128)(2,1)}, f32[4,2,1,640]{3,2,1,0:T(1,128)}) custom-call(bf16[640,1536]{1,0:T(8,128)(2,1)} %shard_map.371.q_ref.kb_ref.vb_ref, bf16[640,1024]{1,0:T(8,128)(2,1)} %shard_map.372.ka_ref.va_ref, bf16[640,1536]{1,0:T(8,128)(2,1)} %shard_map.371.q_ref.kb_ref.vb_ref, bf16[640,1024]{1,0:T(8,128)(2,1)} %shard_map.372.ka_ref.va_ref, ...), custom_call_target="tpu_custom_call" | custom-call | flops 1 | bytes 1 | tf_op jit(solution)/shard_map/pallas_call | solution.py:217
  317.0 5.7 collective-permute-start.31
  328.6 7.4 %shard_map.374 = (bf16[1,1408,1024]{2,1,0:T(8,128)(2,1)}, bf16[1,1408,1024]{2,1,0:T(8,128)(2,1)}, bf16[1,1408,1024]{2,1,0:T(8,128)(2,1)}) custom-call(bf16[2112,512]{1,0:T(8,128)(2,1)} %bitcast.441, bf16[2112,512]{1,0:T(8,128)(2,1)} %collective-permute-done.25.xf_ref, bf16[2112,512]{1,0:T(8,128)(2,1)} %bitcast.439, ...), custom_call_target="tpu_custom_call" | custom-call | flops 1 | bytes 1 | tf_op jit(solution)/shard_map/pallas_call | solution.py:179
  336.0 4.3 fusion.6
  342.6 4.6 multiply_convert_fusion.3
  375.4 9.0 %collective-permute-done.37 = bf16[320,256]{1,0:T(8,128)(2,1)S(1)} collective-permute-done((bf16[320,256]{1,0:T(8,128)(2,1)S(1)}, bf16[320,256]{1,0:T(8,128)(2,1)S(1)}, u32[]{:S(2)}, u32[]{:S(2)}) %collective-permute-start.37) | collective-permute-done | bytes 163872 | tf_op jit(solution)/shard_map/ppermute | solution.py:359
  393.6 24.0 %shard_map.375 = (bf16[640,512]{1,0:T(8,128)(2,1)}, bf16[640,512]{1,0:T(8,128)(2,1)}, bf16[640,512]{1,0:T(8,128)(2,1)}, bf16[640,512]{1,0:T(8,128)(2,1)}, bf16[640,512]{1,0:T(8,128)(2,1)}) custom-call(bf16[640,1536]{1,0:T(8,128)(2,1)} %shard_map.371.q_ref.kb_ref.vb_ref, bf16[640,1024]{1,0:T(8,128)(2,1)} %shard_map.372.ka_ref.va_ref, ...), custom_call_target="tpu_custom_call" | custom-call | flops 1 | bytes 1 | tf_op jit(solution)/shard_map/pallas_call | solution.py:302
  423.2 3.5 collective-permute-start.44
  436.8 11.4 %collective-permute-done.45 = bf16[320,1024]{1,0:T(8,128)(2,1)S(1)} collective-permute-done((bf16[320,1024]{1,0:T(8,128)(2,1)S(1)}, bf16[320,1024]{1,0:T(8,128)(2,1)S(1)}, u32[]{:S(2)}, u32[]{:S(2)}) %collective-permute-start.45) | collective-permute-done | bytes 655392 | tf_op jit(solution)/shard_map/ppermute | solution.py:723
  454.9 4.2 multiply_convert_fusion.1
  503.6 24.1 %shard_map.376 = (bf16[640,512]{1,0:T(8,128)(2,1)}, bf16[640,512]{1,0:T(8,128)(2,1)}, bf16[640,512]{1,0:T(8,128)(2,1)}, bf16[640,512]{1,0:T(8,128)(2,1)}, bf16[640,512]{1,0:T(8,128)(2,1)}) custom-call(bf16[640,1536]{1,0:T(8,128)(2,1)} %shard_map.366.q_ref.kb_ref.vb_ref.rest_0_, bf16[640,1024]{1,0:T(8,128)(2,1)} %shard_map.367.ka_ref.va_ref.rest_0_, ...), custom_call_target="tpu_custom_call" | custom-call | flops 1 | bytes 1 | tf_op jit(solution)/shard_map/pallas_call | solution.py:302
  533.8 3.7 collective-permute-done.53
  556.3 9.2 %collective-permute-done.55 = bf16[320,1024]{1,0:T(8,128)(2,1)S(1)} collective-permute-done((bf16[320,1024]{1,0:T(8,128)(2,1)S(1)}, bf16[320,1024]{1,0:T(8,128)(2,1)S(1)}, u32[]{:S(2)}, u32[]{:S(2)}) %collective-permute-start.55) | collective-permute-done | bytes 655392 | tf_op jit(solution)/shard_map/ppermute | solution.py:723
  572.8 19.6 %collective-permute-done.56 = bf16[2112,256]{1,0:T(8,128)(2,1)S(1)} collective-permute-done((bf16[2112,256]{1,0:T(8,128)(2,1)S(1)}, bf16[2112,256]{1,0:T(8,128)(2,1)S(1)}, u32[]{:S(2)}, u32[]{:S(2)}) %collective-permute-start.56) | collective-permute-done | bytes 1081376 | tf_op jit(solution)/shard_map/ppermute | solution.py:42
  604.2 10.2 %collective-permute-done.63 = bf16[1088,512]{1,0:T(8,128)(2,1)} collective-permute-done((bf16[1088,512]{1,0:T(8,128)(2,1)}, bf16[1088,512]{1,0:T(8,128)(2,1)}, u32[]{:S(2)}, u32[]{:S(2)}) %collective-permute-start.63) | collective-permute-done | bytes 1114144 | tf_op jit(solution)/shard_map/ppermute | solution.py:42
  621.8 3.6 collective-permute-done.71
  630.2 5.8 collective-permute-done.66
  637.5 6.5 collective-permute-done.68
  644.7 4.4 collective-permute-done.67
  660.6 7.7 %collective-permute-done.65 = bf16[1088,256]{1,0:T(8,128)(2,1)} collective-permute-done((bf16[1088,256]{1,0:T(8,128)(2,1)S(1)}, bf16[1088,256]{1,0:T(8,128)(2,1)}, u32[]{:S(2)}, u32[]{:S(2)}) %collective-permute-start.65) | collective-permute-done | bytes 557088 | tf_op jit(solution)/shard_map/ppermute | solution.py:38
  673.0 9.4 %collective-permute-done.77 = bf16[1056,256]{1,0:T(8,128)(2,1)S(1)} collective-permute-done((bf16[1056,256]{1,0:T(8,128)(2,1)}, bf16[1056,256]{1,0:T(8,128)(2,1)S(1)}, u32[]{:S(2)}, u32[]{:S(2)}) %collective-permute-start.77) | collective-permute-done | bytes 540704 | tf_op jit(solution)/shard_map/ppermute | solution.py:38
  694.5 4.7 reduce-scatter.11.cloned.1.call-done
  702.0 5.5 collective-permute-done.74
  (776 shorter events, 303.2 us)
Async XLA Ops:
  7.2 95.6 %all-gather.4.cloned.1.call-start = ((), (), s32[]{:S(2)}) async-start(), calls=%async_computation.4 | async-start | bytes 2703360 | tf_op jit(solution)/shard_map/all_gather | solution.py:381
  45.3 27.6 %collective-permute-start.5 = (bf16[2048,256]{1,0:T(8,128)(2,1)S(1)}, bf16[2048,256]{1,0:T(8,128)(2,1)}, u32[]{:S(2)}, u32[]{:S(2)}) collective-permute-start(bf16[2048,256]{1,0:T(8,128)(2,1)S(1)} %bitcast.459), channel_id=1, source_target_pairs={{0,16},{16,0},{1,17},{17,1},{2,18},{18,2},{3,19},{19,3},{4,20},{20... | collective-permute-start | bytes 3145736 | tf_op jit(solution)/shard_map/ppermute | solution.py:38
  46.8 26.1 %collective-permute-start.6 = (bf16[2048,256]{1,0:T(8,128)(2,1)S(1)}, bf16[2048,256]{1,0:T(8,128)(2,1)}, u32[]{:S(2)}, u32[]{:S(2)}) collective-permute-start(bf16[2048,256]{1,0:T(8,128)(2,1)S(1)} %bitcast.460), channel_id=1, source_target_pairs={{0,4},{4,0},{1,5},{5,1},{2,6},{6,2},{3,7},{7,3},{8,12},{12,8},{9,1... | collective-permute-start | bytes 3145736 | tf_op jit(solution)/shard_map/ppermute | solution.py:42
  49.5 15.6 %collective-permute-start.3 = (bf16[336,256]{1,0:T(8,128)(2,1)}, bf16[336,256]{1,0:T(8,128)(2,1)}, u32[]{:S(2)}, u32[]{:S(2)}) collective-permute-start(bf16[336,256]{1,0:T(8,128)(2,1)} %get-tuple-element.328), channel_id=1, source_target_pairs={{0,10},{1,2},{2,8},{3,0},{8,11},{9,3},{10,9},{11,1},{4,14},{5,6},{... | collective-permute-start | bytes 516104 | tf_op jit(solution)/shard_map/ppermute | solution.py:433
  49.5 21.4 %collective-permute-start.2 = (bf16[336,256]{1,0:T(8,128)(2,1)}, bf16[336,256]{1,0:T(8,128)(2,1)}, u32[]{:S(2)}, u32[]{:S(2)}) collective-permute-start(bf16[336,256]{1,0:T(8,128)(2,1)} %get-tuple-element.329), channel_id=1, source_target_pairs={{0,2},{1,10},{2,0},{3,8},{8,3},{9,11},{10,1},{11,9},{4,6},{5,14},{... | collective-permute-start | bytes 516104 | tf_op jit(solution)/shard_map/ppermute | solution.py:433
  56.2 108.2 %all-gather.6.cloned.1.call-start = ((), (), s32[]{:S(2)}) async-start(), calls=%async_computation.5 | async-start | bytes 2621440 | tf_op jit(solution)/shard_map/all_gather | solution.py:381
  70.9 21.4 %collective-permute-start.14 = (bf16[784,256]{1,0:T(8,128)(2,1)}, bf16[784,256]{1,0:T(8,128)(2,1)S(1)}, u32[]{:S(2)}, u32[]{:S(2)}) collective-permute-start(bf16[784,256]{1,0:T(8,128)(2,1)} %pad_maximum_fusion.61), channel_id=1, source_target_pairs={{0,4},{4,0},{1,5},{5,1},{2,6},{6,2},{3,7},{7,3},{8,12},{12,8},{9,1... | collective-permute-start | bytes 1204232 | tf_op jit(solution)/shard_map/ppermute | solution.py:42
  102.9 157.9 %all-gather.8.cloned.1.call-start = ((), (), s32[]{:S(2)}) async-start(), calls=%async_computation.6 | async-start | bytes 5406720 | tf_op jit(solution)/shard_map/all_gather | solution.py:381
  112.5 49.8 %collective-permute-start.12 = (bf16[4224,256]{1,0:T(8,128)(2,1)S(1)}, bf16[4224,256]{1,0:T(8,128)(2,1)}, u32[]{:S(2)}, u32[]{:S(2)}) collective-permute-start(bf16[4224,256]{1,0:T(8,128)(2,1)S(1)} %copy-done.49), channel_id=1, source_target_pairs={{0,16},{16,0},{1,17},{17,1},{2,18},{18,2},{3,19},{19,3},{4,20},{20... | collective-permute-start | bytes 6488072 | tf_op jit(solution)/shard_map/ppermute | solution.py:38
  114.7 49.7 %collective-permute-start.13 = (bf16[4224,256]{1,0:T(8,128)(2,1)S(1)}, bf16[4224,256]{1,0:T(8,128)(2,1)}, u32[]{:S(2)}, u32[]{:S(2)}) collective-permute-start(bf16[4224,256]{1,0:T(8,128)(2,1)S(1)} %copy-done.49), channel_id=1, source_target_pairs={{0,4},{4,0},{1,5},{5,1},{2,6},{6,2},{3,7},{7,3},{8,12},{12,8},{9,1... | collective-permute-start | bytes 6488072 | tf_op jit(solution)/shard_map/ppermute | solution.py:42
  171.5 26.4 %collective-permute-start.17 = (bf16[2112,256]{1,0:T(8,128)(2,1)}, bf16[2112,256]{1,0:T(8,128)(2,1)}, u32[]{:S(2)}, u32[]{:S(2)}) collective-permute-start(bf16[2112,256]{1,0:T(8,128)(2,1)} %slice.794), channel_id=1, source_target_pairs={{0,16},{16,0},{1,17},{17,1},{2,18},{18,2},{3,19},{19,3},{4,20},{20... | collective-permute-start | bytes 3244040 | tf_op jit(solution)/shard_map/ppermute | solution.py:38
  174.0 26.1 %collective-permute-start.18 = (bf16[2112,256]{1,0:T(8,128)(2,1)}, bf16[2112,256]{1,0:T(8,128)(2,1)}, u32[]{:S(2)}, u32[]{:S(2)}) collective-permute-start(bf16[2112,256]{1,0:T(8,128)(2,1)} %slice.795), channel_id=1, source_target_pairs={{0,4},{4,0},{1,5},{5,1},{2,6},{6,2},{3,7},{7,3},{8,12},{12,8},{9,1... | collective-permute-start | bytes 3244040 | tf_op jit(solution)/shard_map/ppermute | solution.py:42
  175.8 424.8 %reduce-scatter.9.cloned.1.call-start = ((), (), s32[]{:S(2)}) async-start(), calls=%async_computation.9 | async-start | bytes 2621440 | tf_op jit(solution)/shard_map/reduce_scatter | solution.py:497
  177.9 33.3 %collective-permute-start.16 = (bf16[320,1024]{1,0:T(8,128)(2,1)S(1)}, bf16[320,1024]{1,0:T(8,128)(2,1)S(1)}, u32[]{:S(2)}, u32[]{:S(2)}) collective-permute-start(bf16[320,1024]{1,0:T(8,128)(2,1)S(1)} %multiply_convert_fusion.8), channel_id=1, source_target_pairs={{0,8},{8,0},{1,9},{9,1},{2,10},{10,2},{3,11},{11,3},{4,12},{12,4},... | collective-permute-start | bytes 1966088 | tf_op jit(solution)/shard_map/ppermute | solution.py:34
  200.4 24.3 %collective-permute-start.19 = (bf16[1024,512]{1,0:T(8,128)(2,1)S(1)}, bf16[1024,512]{1,0:T(8,128)(2,1)S(1)}, u32[]{:S(2)}, u32[]{:S(2)}) collective-permute-start(bf16[1024,512]{1,0:T(8,128)(2,1)S(1)} %bitcast.464), channel_id=1, source_target_pairs={{0,16},{16,0},{1,17},{17,1},{2,18},{18,2},{3,19},{19,3},{4,20},{20... | collective-permute-start | bytes 3145736 | tf_op jit(solution)/shard_map/ppermute | solution.py:38
  202.2 24.0 %collective-permute-start.20 = (bf16[1024,512]{1,0:T(8,128)(2,1)S(1)}, bf16[1024,512]{1,0:T(8,128)(2,1)S(1)}, u32[]{:S(2)}, u32[]{:S(2)}) collective-permute-start(bf16[1024,512]{1,0:T(8,128)(2,1)S(1)} %bitcast.462), channel_id=1, source_target_pairs={{0,4},{4,0},{1,5},{5,1},{2,6},{6,2},{3,7},{7,3},{8,12},{12,8},{9,1... | collective-permute-start | bytes 3145736 | tf_op jit(solution)/shard_map/ppermute | solution.py:42
  232.2 17.9 %collective-permute-start.23 = (bf16[320,1024]{1,0:T(8,128)(2,1)S(1)}, bf16[320,1024]{1,0:T(8,128)(2,1)S(1)}, u32[]{:S(2)}, u32[]{:S(2)}) collective-permute-start(bf16[320,1024]{1,0:T(8,128)(2,1)S(1)} %multiply_convert_fusion.7), channel_id=1, source_target_pairs={{0,4},{1,5},{2,6},{3,7},{8,12},{9,13},{10,14},{11,15},{16,20},{17,... | collective-permute-start | bytes 1966088 | tf_op jit(solution)/shard_map/ppermute | solution.py:676
  263.4 51.1 %collective-permute-start.25 = (bf16[2112,512]{1,0:T(8,128)(2,1)S(1)}, bf16[2112,512]{1,0:T(8,128)(2,1)}, u32[]{:S(2)}, u32[]{:S(2)}) collective-permute-start(bf16[2112,512]{1,0:T(8,128)(2,1)S(1)} %bitcast.440), channel_id=1, source_target_pairs={{0,16},{16,0},{1,17},{17,1},{2,18},{18,2},{3,19},{19,3},{4,20},{20... | collective-permute-start | bytes 6488072 | tf_op jit(solution)/shard_map/ppermute | solution.py:38
  265.0 49.5 %collective-permute-start.26 = (bf16[2112,512]{1,0:T(8,128)(2,1)S(1)}, bf16[2112,512]{1,0:T(8,128)(2,1)}, u32[]{:S(2)}, u32[]{:S(2)}) collective-permute-start(bf16[2112,512]{1,0:T(8,128)(2,1)S(1)} %bitcast.438), channel_id=1, source_target_pairs={{0,4},{4,0},{1,5},{5,1},{2,6},{6,2},{3,7},{7,3},{8,12},{12,8},{9,1... | collective-permute-start | bytes 6488072 | tf_op jit(solution)/shard_map/ppermute | solution.py:42
  268.2 44.0 %collective-permute-start.29 = (bf16[320,256]{1,0:T(8,128)(2,1)}, bf16[320,256]{1,0:T(8,128)(2,1)S(1)}, u32[]{:S(2)}, u32[]{:S(2)}) collective-permute-start(bf16[320,256]{1,0:T(8,128)(2,1)} %get-tuple-element.369), channel_id=1, source_target_pairs={{0,2},{1,10},{2,0},{3,8},{8,3},{9,11},{10,1},{11,9},{4,6},{5,14},{... | collective-permute-start | bytes 491528 | tf_op jit(solution)/shard_map/ppermute | solution.py:433
  270.3 41.9 %collective-permute-start.28 = (bf16[320,256]{1,0:T(8,128)(2,1)}, bf16[320,256]{1,0:T(8,128)(2,1)}, u32[]{:S(2)}, u32[]{:S(2)}) collective-permute-start(bf16[320,256]{1,0:T(8,128)(2,1)} %get-tuple-element.370), channel_id=1, source_target_pairs={{0,8},{1,0},{2,10},{3,2},{8,9},{9,1},{10,11},{11,3},{4,12},{5,4},{... | collective-permute-start | bytes 491528 | tf_op jit(solution)/shard_map/ppermute | solution.py:433
  275.4 36.8 %collective-permute-start.27 = (bf16[320,256]{1,0:T(8,128)(2,1)S(1)}, bf16[320,256]{1,0:T(8,128)(2,1)}, u32[]{:S(2)}, u32[]{:S(2)}) collective-permute-start(bf16[320,256]{1,0:T(8,128)(2,1)S(1)} %get-tuple-element.367), channel_id=1, source_target_pairs={{0,0},{1,8},{2,2},{3,10},{8,1},{9,9},{10,3},{11,11},{4,4},{5,12},{... | collective-permute-start | bytes 491528 | tf_op jit(solution)/shard_map/ppermute | solution.py:433
  351.7 16.8 %collective-permute-start.39 = (bf16[320,1024]{1,0:T(8,128)(2,1)S(1)}, bf16[320,1024]{1,0:T(8,128)(2,1)S(1)}, u32[]{:S(2)}, u32[]{:S(2)}) collective-permute-start(bf16[320,1024]{1,0:T(8,128)(2,1)S(1)} %slice.1096), channel_id=1, source_target_pairs={{0,8},{8,0},{1,9},{9,1},{2,10},{10,2},{3,11},{11,3},{4,12},{12,4},... | collective-permute-start | bytes 1966088 | tf_op jit(solution)/shard_map/ppermute | solution.py:34
  361.5 59.1 %collective-permute-start.42 = (bf16[2112,512]{1,0:T(8,128)(2,1)}, bf16[2112,512]{1,0:T(8,128)(2,1)}, u32[]{:S(2)}, u32[]{:S(2)}) collective-permute-start(bf16[2112,512]{1,0:T(8,128)(2,1)} %bitcast.86), channel_id=1, source_target_pairs={{0,16},{16,0},{1,17},{17,1},{2,18},{18,2},{3,19},{19,3},{4,20},{20... | collective-permute-start | bytes 6488072 | tf_op jit(solution)/shard_map/ppermute | solution.py:38
  365.1 55.4 %collective-permute-start.43 = (bf16[2112,512]{1,0:T(8,128)(2,1)}, bf16[2112,512]{1,0:T(8,128)(2,1)}, u32[]{:S(2)}, u32[]{:S(2)}) collective-permute-start(bf16[2112,512]{1,0:T(8,128)(2,1)} %bitcast.90), channel_id=1, source_target_pairs={{0,4},{4,0},{1,5},{5,1},{2,6},{6,2},{3,7},{7,3},{8,12},{12,8},{9,1... | collective-permute-start | bytes 6488072 | tf_op jit(solution)/shard_map/ppermute | solution.py:42
  372.2 16.2 %collective-permute-start.36 = (bf16[320,256]{1,0:T(8,128)(2,1)S(1)}, bf16[320,256]{1,0:T(8,128)(2,1)S(1)}, u32[]{:S(2)}, u32[]{:S(2)}) collective-permute-start(bf16[320,256]{1,0:T(8,128)(2,1)S(1)} %get-tuple-element.357), channel_id=1, source_target_pairs={{2,0},{10,1},{0,2},{8,3},{3,8},{11,9},{1,10},{9,11},{6,4},{14,5},{... | collective-permute-start | bytes 491528 | tf_op jit(solution)/shard_map/ppermute | solution.py:359
  373.8 17.9 %collective-permute-start.40 = (bf16[320,1024]{1,0:T(8,128)(2,1)S(1)}, bf16[320,1024]{1,0:T(8,128)(2,1)S(1)}, u32[]{:S(2)}, u32[]{:S(2)}) collective-permute-start(bf16[320,1024]{1,0:T(8,128)(2,1)S(1)} %get-tuple-element.240), channel_id=1, source_target_pairs={{0,8},{8,0},{1,9},{9,1},{2,10},{10,2},{3,11},{11,3},{4,12},{12,4},... | collective-permute-start | bytes 1966088 | tf_op jit(solution)/shard_map/ppermute | solution.py:34
  427.7 20.5 %collective-permute-start.41 = (bf16[320,1024]{1,0:T(8,128)(2,1)S(1)}, bf16[320,1024]{1,0:T(8,128)(2,1)S(1)}, u32[]{:S(2)}, u32[]{:S(2)}) collective-permute-start(bf16[320,1024]{1,0:T(8,128)(2,1)S(1)} %slice.1095), channel_id=1, source_target_pairs={{0,8},{8,0},{1,9},{9,1},{2,10},{10,2},{3,11},{11,3},{4,12},{12,4},... | collective-permute-start | bytes 1966088 | tf_op jit(solution)/shard_map/ppermute | solution.py:34
  429.4 18.8 %collective-permute-start.45 = (bf16[320,1024]{1,0:T(8,128)(2,1)S(1)}, bf16[320,1024]{1,0:T(8,128)(2,1)S(1)}, u32[]{:S(2)}, u32[]{:S(2)}) collective-permute-start(bf16[320,1024]{1,0:T(8,128)(2,1)S(1)} %fusion.53), channel_id=1, source_target_pairs={{4,0},{5,1},{6,2},{7,3},{12,8},{13,9},{14,10},{15,11},{20,16},{21,... | collective-permute-start | bytes 1966088 | tf_op jit(solution)/shard_map/ppermute | solution.py:723
  434.3 42.6 %collective-permute-start.49 = (bf16[1024,512]{1,0:T(8,128)(2,1)S(1)}, bf16[1024,512]{1,0:T(8,128)(2,1)S(1)}, u32[]{:S(2)}, u32[]{:S(2)}) collective-permute-start(bf16[1024,512]{1,0:T(8,128)(2,1)S(1)} %concatenate.577), channel_id=1, source_target_pairs={{0,16},{16,0},{1,17},{17,1},{2,18},{18,2},{3,19},{19,3},{4,20},{20... | collective-permute-start | bytes 3145736 | tf_op jit(solution)/shard_map/ppermute | solution.py:38
  451.3 25.6 %collective-permute-start.50 = (bf16[1024,512]{1,0:T(8,128)(2,1)S(1)}, bf16[1024,512]{1,0:T(8,128)(2,1)S(1)}, u32[]{:S(2)}, u32[]{:S(2)}) collective-permute-start(bf16[1024,512]{1,0:T(8,128)(2,1)S(1)} %pad_maximum_fusion.30), channel_id=1, source_target_pairs={{0,4},{4,0},{1,5},{5,1},{2,6},{6,2},{3,7},{7,3},{8,12},{12,8},{9,1... | collective-permute-start | bytes 3145736 | tf_op jit(solution)/shard_map/ppermute | solution.py:42
  464.7 26.7 %collective-permute-start.47 = (bf16[320,1024]{1,0:T(8,128)(2,1)}, bf16[320,1024]{1,0:T(8,128)(2,1)}, u32[]{:S(2)}, u32[]{:S(2)}) collective-permute-start(bf16[320,1024]{1,0:T(8,128)(2,1)} %slice.1093), channel_id=1, source_target_pairs={{0,8},{8,0},{1,9},{9,1},{2,10},{10,2},{3,11},{11,3},{4,12},{12,4},... | collective-permute-start | bytes 1966088 | tf_op jit(solution)/shard_map/ppermute | solution.py:34
  480.3 145.4 %reduce-scatter.7.cloned.1.call-start = ((), (), s32[]{:S(2)}) async-start(), calls=%async_computation.8 | async-start | bytes 5406720 | tf_op jit(solution)/shard_map/reduce_scatter | solution.py:497
  483.8 50.0 %collective-permute-start.52 = (bf16[2112,512]{1,0:T(8,128)(2,1)}, bf16[2112,512]{1,0:T(8,128)(2,1)}, u32[]{:S(2)}, u32[]{:S(2)}) collective-permute-start(bf16[2112,512]{1,0:T(8,128)(2,1)} %pad_maximum_fusion.8), channel_id=1, source_target_pairs={{0,16},{16,0},{1,17},{17,1},{2,18},{18,2},{3,19},{19,3},{4,20},{20... | collective-permute-start | bytes 6488072 | tf_op jit(solution)/shard_map/ppermute | solution.py:38
  488.0 49.5 %collective-permute-start.53 = (bf16[2112,512]{1,0:T(8,128)(2,1)}, bf16[2112,512]{1,0:T(8,128)(2,1)}, u32[]{:S(2)}, u32[]{:S(2)}) collective-permute-start(bf16[2112,512]{1,0:T(8,128)(2,1)} %fusion.31), channel_id=1, source_target_pairs={{0,4},{4,0},{1,5},{5,1},{2,6},{6,2},{3,7},{7,3},{8,12},{12,8},{9,1... | collective-permute-start | bytes 6488072 | tf_op jit(solution)/shard_map/ppermute | solution.py:42
  500.6 167.7 %reduce-scatter.5.cloned.1.call-start = ((), (), s32[]{:S(2)}) async-start(), calls=%async_computation.7 | async-start | bytes 2703360 | tf_op jit(solution)/shard_map/reduce_scatter | solution.py:497
  532.4 33.2 %collective-permute-start.51 = (bf16[320,1024]{1,0:T(8,128)(2,1)S(1)}, bf16[320,1024]{1,0:T(8,128)(2,1)S(1)}, u32[]{:S(2)}, u32[]{:S(2)}) collective-permute-start(bf16[320,1024]{1,0:T(8,128)(2,1)S(1)} %slice.1092), channel_id=1, source_target_pairs={{0,8},{8,0},{1,9},{9,1},{2,10},{10,2},{3,11},{11,3},{4,12},{12,4},... | collective-permute-start | bytes 1966088 | tf_op jit(solution)/shard_map/ppermute | solution.py:34
  546.0 26.8 %collective-permute-start.57 = (bf16[2112,256]{1,0:T(8,128)(2,1)S(1)}, bf16[2112,256]{1,0:T(8,128)(2,1)S(1)}, u32[]{:S(2)}, u32[]{:S(2)}) collective-permute-start(bf16[2112,256]{1,0:T(8,128)(2,1)S(1)} %slice.865), channel_id=1, source_target_pairs={{0,16},{16,0},{1,17},{17,1},{2,18},{18,2},{3,19},{19,3},{4,20},{20... | collective-permute-start | bytes 3244040 | tf_op jit(solution)/shard_map/ppermute | solution.py:38
  547.0 18.6 %collective-permute-start.55 = (bf16[320,1024]{1,0:T(8,128)(2,1)S(1)}, bf16[320,1024]{1,0:T(8,128)(2,1)S(1)}, u32[]{:S(2)}, u32[]{:S(2)}) collective-permute-start(bf16[320,1024]{1,0:T(8,128)(2,1)S(1)} %fusion.51), channel_id=1, source_target_pairs={{4,0},{5,1},{6,2},{7,3},{12,8},{13,9},{14,10},{15,11},{20,16},{21,... | collective-permute-start | bytes 1966088 | tf_op jit(solution)/shard_map/ppermute | solution.py:723
  552.9 49.9 %collective-permute-start.62 = (bf16[1024,512]{1,0:T(8,128)(2,1)}, bf16[1024,512]{1,0:T(8,128)(2,1)}, u32[]{:S(2)}, u32[]{:S(2)}) collective-permute-start(bf16[1024,512]{1,0:T(8,128)(2,1)} %concatenate.584), channel_id=1, source_target_pairs={{0,16},{16,0},{1,17},{17,1},{2,18},{18,2},{3,19},{19,3},{4,20},{20... | collective-permute-start | bytes 3145736 | tf_op jit(solution)/shard_map/ppermute | solution.py:38
  565.5 26.8 %collective-permute-start.56 = (bf16[2112,256]{1,0:T(8,128)(2,1)S(1)}, bf16[2112,256]{1,0:T(8,128)(2,1)S(1)}, u32[]{:S(2)}, u32[]{:S(2)}) collective-permute-start(bf16[2112,256]{1,0:T(8,128)(2,1)S(1)} %slice.864), channel_id=1, source_target_pairs={{0,4},{4,0},{1,5},{5,1},{2,6},{6,2},{3,7},{7,3},{8,12},{12,8},{9,1... | collective-permute-start | bytes 3244040 | tf_op jit(solution)/shard_map/ppermute | solution.py:42
  568.8 45.6 %collective-permute-start.63 = (bf16[1088,512]{1,0:T(8,128)(2,1)}, bf16[1088,512]{1,0:T(8,128)(2,1)}, u32[]{:S(2)}, u32[]{:S(2)}) collective-permute-start(bf16[1088,512]{1,0:T(8,128)(2,1)} %pad_maximum_fusion.23), channel_id=1, source_target_pairs={{0,4},{4,0},{1,5},{5,1},{2,6},{6,2},{3,7},{7,3},{8,12},{12,8},{9,1... | collective-permute-start | bytes 3342344 | tf_op jit(solution)/shard_map/ppermute | solution.py:42
  597.3 86.3 %collective-permute-start.61 = (bf16[320,256]{1,0:T(8,128)(2,1)}, bf16[320,256]{1,0:T(8,128)(2,1)}, u32[]{:S(2)}, u32[]{:S(2)}) collective-permute-start(bf16[320,256]{1,0:T(8,128)(2,1)} %get-tuple-element.336), channel_id=1, source_target_pairs={{10,0},{2,1},{8,2},{0,3},{11,8},{3,9},{9,10},{1,11},{14,4},{6,5},{... | collective-permute-start | bytes 491528 | tf_op jit(solution)/shard_map/ppermute | solution.py:359
  598.9 84.8 %collective-permute-start.60 = (bf16[320,256]{1,0:T(8,128)(2,1)}, bf16[320,256]{1,0:T(8,128)(2,1)}, u32[]{:S(2)}, u32[]{:S(2)}) collective-permute-start(bf16[320,256]{1,0:T(8,128)(2,1)} %get-tuple-element.337), channel_id=1, source_target_pairs={{2,0},{10,1},{0,2},{8,3},{3,8},{11,9},{1,10},{9,11},{6,4},{14,5},{... | collective-permute-start | bytes 491528 | tf_op jit(solution)/shard_map/ppermute | solution.py:359
  600.4 83.3 %collective-permute-start.59 = (bf16[320,256]{1,0:T(8,128)(2,1)}, bf16[320,256]{1,0:T(8,128)(2,1)}, u32[]{:S(2)}, u32[]{:S(2)}) collective-permute-start(bf16[320,256]{1,0:T(8,128)(2,1)} %get-tuple-element.338), channel_id=1, source_target_pairs={{8,0},{0,1},{10,2},{2,3},{9,8},{1,9},{11,10},{3,11},{12,4},{4,5},{... | collective-permute-start | bytes 491528 | tf_op jit(solution)/shard_map/ppermute | solution.py:359
  600.5 98.6 %reduce-scatter.11.cloned.1.call-start = ((), (), s32[]{:S(2)}) async-start(), calls=%async_computation.10 | async-start | bytes 1351680 | tf_op jit(solution)/shard_map/reduce_scatter | solution.py:497
  602.8 18.9 %collective-permute-start.72 = (bf16[256,512]{1,0:T(8,128)(2,1)S(1)}, bf16[256,512]{1,0:T(8,128)(2,1)S(1)}, u32[]{:S(2)}, u32[]{:S(2)}) collective-permute-start(bf16[256,512]{1,0:T(8,128)(2,1)S(1)} %maximum_select_fusion.15), channel_id=1, source_target_pairs={{0,16},{16,0},{1,17},{17,1},{2,18},{18,2},{3,19},{19,3},{4,20},{20... | collective-permute-start | bytes 786440 | tf_op jit(solution)/shard_map/ppermute | solution.py:38
  658.8 24.9 %collective-permute-start.58 = (bf16[320,256]{1,0:T(8,128)(2,1)}, bf16[320,256]{1,0:T(8,128)(2,1)S(1)}, u32[]{:S(2)}, u32[]{:S(2)}) collective-permute-start(bf16[320,256]{1,0:T(8,128)(2,1)} %get-tuple-element.335), channel_id=1, source_target_pairs={{0,0},{8,1},{2,2},{10,3},{1,8},{9,9},{3,10},{11,11},{4,4},{12,5},{... | collective-permute-start | bytes 491528 | tf_op jit(solution)/shard_map/ppermute | solution.py:359
  (195 other events, 1984.1 us)
Sparse Core Ops, SparseCore 0:
  56.3 46.5 all-gather.3
  105.0 44.9 all-gather.5
  175.9 84.8 all-gather.7
  480.4 42.7 reduce-scatter.8
  525.5 80.6 reduce-scatter.6
  608.4 50.3 reduce-scatter.4
  673.2 25.9 reduce-scatter.10

commit v6 on v5

--- a/solution.py
+++ b/solution.py
@@ -443,7 +443,7 @@
         by_piece = lambda array: array.reshape(col_count, own_rows, quarter)
         got = spread(
             [by_piece(tokens), jnp.broadcast_to(small[None], (col_count,) + small.shape)],
-            vo_whole_one,
+            vo_whole_one, ffn_local_one,
         )
         residual = got[:own_rows].astype(f32)
         small = got[own_rows:].astype(f32)

time: 731 us -> 738 us (level)
    unnamed x322 -> x330, local copies, waits for them, and re-layouts: 24.7 us -> 27.6 us
  transfers between devices with their start and end apart: 86 -> 86, of which waited for: 35 -> 37; matrix products, arithmetic and copies ran while one was open for 28% -> 28% of each run, Pallas kernels for 18% -> 18%
where the time goes in v6:
time: 738 us; the launch traced here: 730 us
  waiting for transfers between devices  209 us (28%)
  Pallas kernels  130 us (18%)
  other arithmetic  99.9 us (14%)
  starting transfers between devices  89.2 us (12%)
  matrix products  86.7 us (12%)
  local copies, waits for them, and re-layouts  62.2 us (8%)
  blocking collectives  33.6 us (5%)
  between operations  19 us (3%)
    ppermute x18, waiting for transfers between devices, swap_x(): return lax.ppermute(value, 'xi', SWAP)  80.6 us
    pallas_call x2, Pallas kernels, attend_back(): pl.pallas_call(kernel, grid=(pairs,), in_specs=in_specs, out_specs=[pair_...  48.1 us
    ppermute x16, waiting for transfers between devices, swap_y(): return lax.ppermute(value, 'row', SWAP)  45 us
    all_gather x2, blocking collectives, gather_col(): return lax.all_gather(block, 'col', axis=0, tiled=True)  33.6 us
    dot_general x22, matrix products, dot_tn(): lax.dot_general(left, right, (((0,), (0,)), ((), ())), preferred_element_...  32 us
    pallas_call x2, Pallas kernels, attend(): pl.pallas_call(kernel, grid=(pairs,), in_specs=[pair_block(n, 0), pair_bl...  29.9 us
    pallas_call x4, Pallas kernels, project(): pl.pallas_call(kernel, grid=(turned + plain,), in_specs=in_specs, out_spe...  28.1 us
    unnamed x330, local copies, waits for them, and re-layouts  27.6 us
  transfers between devices with their start and end apart: 86, of which 37 were waited for; matrix products, arithmetic and copies ran while one was open for 28% of the time, Pallas kernels for 18%

profile of v6, /device:TPU:0, one launch (start us, length us, event | category | flops | bytes accessed | tf_op | source)
XLA Modules:
  0.0 730.2 jit_solution(15788694702173618700)
XLA Ops:
  10.5 17.4 %all_gather.15 = bf16[1024,256]{1,0:T(8,128)(2,1)S(1)} all-gather(bf16[256,256]{1,0:T(8,128)(2,1)S(1)} %pad_maximum_fusion.76), channel_id=1, replica_groups=mesh['xo'=1,'xi'=2,'core'=2,'row'=2,'col'=4] {'col'}, dimensions={0}, use_global_device_ids=true | all-gather | bytes 655360 | tf_op jit(solution)/shard_map/all_gather | solution.py:381
  28.7 16.3 %all_gather.16 = bf16[1024,256]{1,0:T(8,128)(2,1)S(1)} all-gather(bf16[256,256]{1,0:T(8,128)(2,1)S(1)} %pad_maximum_fusion.77), channel_id=1, replica_groups=mesh['xo'=1,'xi'=2,'core'=2,'row'=2,'col'=4] {'col'}, dimensions={0}, use_global_device_ids=true | all-gather | bytes 655360 | tf_op jit(solution)/shard_map/all_gather | solution.py:381
  72.9 3.7 fusion.135
  78.5 4.8 collective-permute-done.1
  87.6 8.7 %collective-permute-done.8.low_ref = bf16[1024,256]{1,0:T(8,128)(2,1)S(1)} collective-permute-done((bf16[1024,256]{1,0:T(8,128)(2,1)S(1)}, bf16[1024,256]{1,0:T(8,128)(2,1)S(1)}, u32[]{:S(2)}, u32[]{:S(2)}) %collective-permute-start.8) | collective-permute-done | bytes 524320 | tf_op jit(solution)/shard_map/ppermute | solution.py:38
  100.2 6.2 all-gather.4.cloned.1.call-done.whole_ref
  106.6 4.0 collective-permute-done.10
  110.9 9.0 %collective-permute-start.11 = (bf16[320,1024]{1,0:T(8,128)(2,1)S(1)}, bf16[320,1024]{1,0:T(8,128)(2,1)S(1)}, u32[]{:S(2)}, u32[]{:S(2)}) collective-permute-start(bf16[320,1024]{1,0:T(8,128)(2,1)S(1)} %pad_maximum_fusion.49), channel_id=1, source_target_pairs={{0,8},{8,0},{1,9},{9,1},{2,10},{10,2},{3,11},{11,3},{4,12},{12,4},... | collective-permute-start | bytes 1966088 | tf_op jit(solution)/shard_map/ppermute | solution.py:34
  129.7 4.7 shard_map.365
  134.5 7.9 %shard_map.366.q_ref.kb_ref.vb_ref.rest_0_ = bf16[640,1536]{1,0:T(8,128)(2,1)} custom-call(bf16[640,1024]{1,0:T(8,128)(2,1)} %pad_maximum_fusion.14.n_ref, bf16[1024,1024]{1,0:T(8,128)(2,1)} %bitcast.425, bf16[512,1024]{1,0:T(8,128)(2,1)} %bitcast.430, f32[640,128]{1,0:T(8,128)} %get-tuple-element.469.cos_ref.co_ref, f32[640,128]{1,0:T(8,128)} %get-tuple-element.472.sin_ref), custom_call_target="tpu_custom_call" | custom-call | flops 1 | bytes 1 | tf_op jit(solution)/shard_map/pallas_call | solution.py:104
  142.4 5.9 shard_map.367.ka_ref.va_ref.rest_0_
  148.3 15.0 %shard_map.368 = (bf16[640,512]{1,0:T(8,128)(2,1)}, f32[4,2,1,640]{3,2,1,0:T(1,128)}) custom-call(bf16[640,1536]{1,0:T(8,128)(2,1)} %shard_map.366.q_ref.kb_ref.vb_ref.rest_0_, bf16[640,1024]{1,0:T(8,128)(2,1)} %shard_map.367.ka_ref.va_ref.rest_0_, bf16[640,1536]{1,0:T(8,128)(2,1)} %shard_map.366.q_ref.kb_ref.vb_ref.rest_0_, ...), custom_call_target="tpu_custom_call" | custom-call | flops 1 | bytes 1 | tf_op jit(solution)/shard_map/pallas_call | solution.py:217
  163.3 8.9 %collective-permute-done.12.x_ref = bf16[4224,256]{1,0:T(8,128)(2,1)} collective-permute-done((bf16[4224,256]{1,0:T(8,128)(2,1)S(1)}, bf16[4224,256]{1,0:T(8,128)(2,1)}, u32[]{:S(2)}, u32[]{:S(2)}) %collective-permute-start.12) | collective-permute-done | bytes 2162720 | tf_op jit(solution)/shard_map/ppermute | solution.py:38
  187.8 19.5 %collective-permute-done.17.low_ref = bf16[2112,256]{1,0:T(8,128)(2,1)} collective-permute-done((bf16[2112,256]{1,0:T(8,128)(2,1)}, bf16[2112,256]{1,0:T(8,128)(2,1)}, u32[]{:S(2)}, u32[]{:S(2)}) %collective-permute-start.17) | collective-permute-done | bytes 1081376 | tf_op jit(solution)/shard_map/ppermute | solution.py:38
  213.3 7.4 %shard_map.369 = (bf16[1,1408,1024]{2,1,0:T(8,128)(2,1)}, bf16[1,1408,1024]{2,1,0:T(8,128)(2,1)}, bf16[1,1408,1024]{2,1,0:T(8,128)(2,1)}) custom-call(bf16[4224,256]{1,0:T(8,128)(2,1)} %all-gather.4.cloned.1.call-done.whole_ref, bf16[4224,256]{1,0:T(8,128)(2,1)} %collective-permute-done.13.y_ref, bf16[4224,256]{1,0:T(8,128)(2,1)} %collective-permute-done.12.x_ref, ...), custom_call_target="tpu_custom_call" | custom-call | flops 1 | bytes 1 | tf_op jit(solution)/shard_map/pallas_call | solution.py:141
  220.8 4.3 fusion.28
  225.1 4.3 multiply_convert_fusion.5
  229.4 5.1 collective-permute-done.19.xf_ref
  241.6 3.7 collective-permute-start.23
  245.3 14.2 %collective-permute-done.23 = bf16[320,1024]{1,0:T(8,128)(2,1)S(1)} collective-permute-done((bf16[320,1024]{1,0:T(8,128)(2,1)S(1)}, bf16[320,1024]{1,0:T(8,128)(2,1)S(1)}, u32[]{:S(2)}, u32[]{:S(2)}) %collective-permute-start.23) | collective-permute-done | bytes 655392 | tf_op jit(solution)/shard_map/ppermute | solution.py:676
  263.0 4.9 all-gather.8.cloned.1.call-done
  278.2 4.3 collective-permute-done.30
  284.3 4.7 shard_map.370
  290.1 8.1 %shard_map.371.q_ref.kb_ref.vb_ref = bf16[640,1536]{1,0:T(8,128)(2,1)} custom-call(bf16[640,1024]{1,0:T(8,128)(2,1)} %pad_maximum_fusion.16.n_ref, bf16[1024,1024]{1,0:T(8,128)(2,1)} %bitcast.427, bf16[512,1024]{1,0:T(8,128)(2,1)} %bitcast.432, f32[640,128]{1,0:T(8,128)} %get-tuple-element.469.cos_ref.co_ref, f32[640,128]{1,0:T(8,128)} %get-tuple-element.472.sin_ref, ...), custom_call_target="tpu_custom_call" | custom-call | flops 1 | bytes 1 | tf_op jit(solution)/shard_map/pallas_call | solution.py:104
  298.3 6.1 shard_map.372.ka_ref.va_ref
  304.4 14.9 %shard_map.373 = (bf16[640,512]{1,0:T(8,128)(2,1)}, f32[4,2,1,640]{3,2,1,0:T(1,128)}) custom-call(bf16[640,1536]{1,0:T(8,128)(2,1)} %shard_map.371.q_ref.kb_ref.vb_ref, bf16[640,1024]{1,0:T(8,128)(2,1)} %shard_map.372.ka_ref.va_ref, bf16[640,1536]{1,0:T(8,128)(2,1)} %shard_map.371.q_ref.kb_ref.vb_ref, bf16[640,1024]{1,0:T(8,128)(2,1)} %shard_map.372.ka_ref.va_ref, ...), custom_call_target="tpu_custom_call" | custom-call | flops 1 | bytes 1 | tf_op jit(solution)/shard_map/pallas_call | solution.py:217
  324.1 5.7 collective-permute-start.31
  335.7 7.4 %shard_map.374 = (bf16[1,1408,1024]{2,1,0:T(8,128)(2,1)}, bf16[1,1408,1024]{2,1,0:T(8,128)(2,1)}, bf16[1,1408,1024]{2,1,0:T(8,128)(2,1)}) custom-call(bf16[2112,512]{1,0:T(8,128)(2,1)} %bitcast.441, bf16[2112,512]{1,0:T(8,128)(2,1)} %collective-permute-done.25.xf_ref, bf16[2112,512]{1,0:T(8,128)(2,1)} %bitcast.439, ...), custom_call_target="tpu_custom_call" | custom-call | flops 1 | bytes 1 | tf_op jit(solution)/shard_map/pallas_call | solution.py:179
  343.1 4.3 fusion.6
  349.7 4.6 multiply_convert_fusion.3
  382.6 9.0 %collective-permute-done.37 = bf16[320,256]{1,0:T(8,128)(2,1)S(1)} collective-permute-done((bf16[320,256]{1,0:T(8,128)(2,1)S(1)}, bf16[320,256]{1,0:T(8,128)(2,1)S(1)}, u32[]{:S(2)}, u32[]{:S(2)}) %collective-permute-start.37) | collective-permute-done | bytes 163872 | tf_op jit(solution)/shard_map/ppermute | solution.py:359
  400.8 24.0 %shard_map.375 = (bf16[640,512]{1,0:T(8,128)(2,1)}, bf16[640,512]{1,0:T(8,128)(2,1)}, bf16[640,512]{1,0:T(8,128)(2,1)}, bf16[640,512]{1,0:T(8,128)(2,1)}, bf16[640,512]{1,0:T(8,128)(2,1)}) custom-call(bf16[640,1536]{1,0:T(8,128)(2,1)} %shard_map.371.q_ref.kb_ref.vb_ref, bf16[640,1024]{1,0:T(8,128)(2,1)} %shard_map.372.ka_ref.va_ref, ...), custom_call_target="tpu_custom_call" | custom-call | flops 1 | bytes 1 | tf_op jit(solution)/shard_map/pallas_call | solution.py:302
  430.3 3.5 collective-permute-start.44
  443.9 11.4 %collective-permute-done.45 = bf16[320,1024]{1,0:T(8,128)(2,1)S(1)} collective-permute-done((bf16[320,1024]{1,0:T(8,128)(2,1)S(1)}, bf16[320,1024]{1,0:T(8,128)(2,1)S(1)}, u32[]{:S(2)}, u32[]{:S(2)}) %collective-permute-start.45) | collective-permute-done | bytes 655392 | tf_op jit(solution)/shard_map/ppermute | solution.py:723
  462.0 4.2 multiply_convert_fusion.1
  510.7 24.1 %shard_map.376 = (bf16[640,512]{1,0:T(8,128)(2,1)}, bf16[640,512]{1,0:T(8,128)(2,1)}, bf16[640,512]{1,0:T(8,128)(2,1)}, bf16[640,512]{1,0:T(8,128)(2,1)}, bf16[640,512]{1,0:T(8,128)(2,1)}) custom-call(bf16[640,1536]{1,0:T(8,128)(2,1)} %shard_map.366.q_ref.kb_ref.vb_ref.rest_0_, bf16[640,1024]{1,0:T(8,128)(2,1)} %shard_map.367.ka_ref.va_ref.rest_0_, ...), custom_call_target="tpu_custom_call" | custom-call | flops 1 | bytes 1 | tf_op jit(solution)/shard_map/pallas_call | solution.py:302
  540.9 3.8 collective-permute-done.53
  563.4 9.2 %collective-permute-done.55 = bf16[320,1024]{1,0:T(8,128)(2,1)S(1)} collective-permute-done((bf16[320,1024]{1,0:T(8,128)(2,1)S(1)}, bf16[320,1024]{1,0:T(8,128)(2,1)S(1)}, u32[]{:S(2)}, u32[]{:S(2)}) %collective-permute-start.55) | collective-permute-done | bytes 655392 | tf_op jit(solution)/shard_map/ppermute | solution.py:723
  579.9 19.5 %collective-permute-done.56 = bf16[2112,256]{1,0:T(8,128)(2,1)S(1)} collective-permute-done((bf16[2112,256]{1,0:T(8,128)(2,1)S(1)}, bf16[2112,256]{1,0:T(8,128)(2,1)S(1)}, u32[]{:S(2)}, u32[]{:S(2)}) %collective-permute-start.56) | collective-permute-done | bytes 1081376 | tf_op jit(solution)/shard_map/ppermute | solution.py:42
  611.3 10.2 %collective-permute-done.63 = bf16[1088,512]{1,0:T(8,128)(2,1)} collective-permute-done((bf16[1088,512]{1,0:T(8,128)(2,1)}, bf16[1088,512]{1,0:T(8,128)(2,1)}, u32[]{:S(2)}, u32[]{:S(2)}) %collective-permute-start.63) | collective-permute-done | bytes 1114144 | tf_op jit(solution)/shard_map/ppermute | solution.py:42
  628.9 3.6 collective-permute-done.71
  637.3 5.8 collective-permute-done.66
  644.6 6.5 collective-permute-done.68
  651.8 4.4 collective-permute-done.67
  667.7 7.7 %collective-permute-done.65 = bf16[1088,256]{1,0:T(8,128)(2,1)} collective-permute-done((bf16[1088,256]{1,0:T(8,128)(2,1)S(1)}, bf16[1088,256]{1,0:T(8,128)(2,1)}, u32[]{:S(2)}, u32[]{:S(2)}) %collective-permute-start.65) | collective-permute-done | bytes 557088 | tf_op jit(solution)/shard_map/ppermute | solution.py:38
  680.2 9.4 %collective-permute-done.77 = bf16[1056,256]{1,0:T(8,128)(2,1)S(1)} collective-permute-done((bf16[1056,256]{1,0:T(8,128)(2,1)}, bf16[1056,256]{1,0:T(8,128)(2,1)S(1)}, u32[]{:S(2)}, u32[]{:S(2)}) %collective-permute-start.77) | collective-permute-done | bytes 540704 | tf_op jit(solution)/shard_map/ppermute | solution.py:38
  701.6 4.7 reduce-scatter.11.cloned.1.call-done
  709.1 5.4 collective-permute-done.74
  (784 shorter events, 309.0 us)
Async XLA Ops:
  7.2 99.1 %all-gather.4.cloned.1.call-start = ((), (), s32[]{:S(2)}) async-start(), calls=%async_computation.4 | async-start | bytes 2703360 | tf_op jit(solution)/shard_map/all_gather | solution.py:381
  45.1 40.4 %collective-permute-start.5 = (bf16[2048,256]{1,0:T(8,128)(2,1)S(1)}, bf16[2048,256]{1,0:T(8,128)(2,1)S(1)}, u32[]{:S(2)}, u32[]{:S(2)}) collective-permute-start(bf16[2048,256]{1,0:T(8,128)(2,1)S(1)} %bitcast.459), channel_id=1, source_target_pairs={{0,16},{16,0},{1,17},{17,1},{2,18},{18,2},{3,19},{19,3},{4,20},{20... | collective-permute-start | bytes 3145736 | tf_op jit(solution)/shard_map/ppermute | solution.py:38
  46.7 38.9 %collective-permute-start.6 = (bf16[2048,256]{1,0:T(8,128)(2,1)S(1)}, bf16[2048,256]{1,0:T(8,128)(2,1)}, u32[]{:S(2)}, u32[]{:S(2)}) collective-permute-start(bf16[2048,256]{1,0:T(8,128)(2,1)S(1)} %bitcast.460), channel_id=1, source_target_pairs={{0,4},{4,0},{1,5},{5,1},{2,6},{6,2},{3,7},{7,3},{8,12},{12,8},{9,1... | collective-permute-start | bytes 3145736 | tf_op jit(solution)/shard_map/ppermute | solution.py:42
  53.4 18.7 %collective-permute-start.3 = (bf16[336,256]{1,0:T(8,128)(2,1)}, bf16[336,256]{1,0:T(8,128)(2,1)}, u32[]{:S(2)}, u32[]{:S(2)}) collective-permute-start(bf16[336,256]{1,0:T(8,128)(2,1)} %get-tuple-element.328), channel_id=1, source_target_pairs={{0,10},{1,2},{2,8},{3,0},{8,11},{9,3},{10,9},{11,1},{4,14},{5,6},{... | collective-permute-start | bytes 516104 | tf_op jit(solution)/shard_map/ppermute | solution.py:433
  53.4 24.6 %collective-permute-start.2 = (bf16[336,256]{1,0:T(8,128)(2,1)}, bf16[336,256]{1,0:T(8,128)(2,1)}, u32[]{:S(2)}, u32[]{:S(2)}) collective-permute-start(bf16[336,256]{1,0:T(8,128)(2,1)} %get-tuple-element.329), channel_id=1, source_target_pairs={{0,2},{1,10},{2,0},{3,8},{8,3},{9,11},{10,1},{11,9},{4,6},{5,14},{... | collective-permute-start | bytes 516104 | tf_op jit(solution)/shard_map/ppermute | solution.py:433
  58.0 115.8 %all-gather.6.cloned.1.call-start = ((), (), s32[]{:S(2)}) async-start(), calls=%async_computation.5 | async-start | bytes 2621440 | tf_op jit(solution)/shard_map/all_gather | solution.py:381
  65.4 17.8 %collective-permute-start.1 = (bf16[336,256]{1,0:T(8,128)(2,1)}, bf16[336,256]{1,0:T(8,128)(2,1)S(1)}, u32[]{:S(2)}, u32[]{:S(2)}) collective-permute-start(bf16[336,256]{1,0:T(8,128)(2,1)} %get-tuple-element.330), channel_id=1, source_target_pairs={{0,8},{1,0},{2,10},{3,2},{8,9},{9,1},{10,11},{11,3},{4,12},{5,4},{... | collective-permute-start | bytes 516104 | tf_op jit(solution)/shard_map/ppermute | solution.py:433
  78.0 20.6 %collective-permute-start.14 = (bf16[784,256]{1,0:T(8,128)(2,1)S(1)}, bf16[784,256]{1,0:T(8,128)(2,1)S(1)}, u32[]{:S(2)}, u32[]{:S(2)}) collective-permute-start(bf16[784,256]{1,0:T(8,128)(2,1)S(1)} %copy-done.112), channel_id=1, source_target_pairs={{0,4},{4,0},{1,5},{5,1},{2,6},{6,2},{3,7},{7,3},{8,12},{12,8},{9,1... | collective-permute-start | bytes 1204232 | tf_op jit(solution)/shard_map/ppermute | solution.py:42
  106.4 161.4 %all-gather.8.cloned.1.call-start = ((), (), s32[]{:S(2)}) async-start(), calls=%async_computation.6 | async-start | bytes 5406720 | tf_op jit(solution)/shard_map/all_gather | solution.py:381
  122.8 49.4 %collective-permute-start.12 = (bf16[4224,256]{1,0:T(8,128)(2,1)S(1)}, bf16[4224,256]{1,0:T(8,128)(2,1)}, u32[]{:S(2)}, u32[]{:S(2)}) collective-permute-start(bf16[4224,256]{1,0:T(8,128)(2,1)S(1)} %copy-done.50), channel_id=1, source_target_pairs={{0,16},{16,0},{1,17},{17,1},{2,18},{18,2},{3,19},{19,3},{4,20},{20... | collective-permute-start | bytes 6488072 | tf_op jit(solution)/shard_map/ppermute | solution.py:38
  124.2 49.6 %collective-permute-start.13 = (bf16[4224,256]{1,0:T(8,128)(2,1)S(1)}, bf16[4224,256]{1,0:T(8,128)(2,1)}, u32[]{:S(2)}, u32[]{:S(2)}) collective-permute-start(bf16[4224,256]{1,0:T(8,128)(2,1)S(1)} %copy-done.50), channel_id=1, source_target_pairs={{0,4},{4,0},{1,5},{5,1},{2,6},{6,2},{3,7},{7,3},{8,12},{12,8},{9,1... | collective-permute-start | bytes 6488072 | tf_op jit(solution)/shard_map/ppermute | solution.py:42
  180.8 26.4 %collective-permute-start.17 = (bf16[2112,256]{1,0:T(8,128)(2,1)}, bf16[2112,256]{1,0:T(8,128)(2,1)}, u32[]{:S(2)}, u32[]{:S(2)}) collective-permute-start(bf16[2112,256]{1,0:T(8,128)(2,1)} %slice.794), channel_id=1, source_target_pairs={{0,16},{16,0},{1,17},{17,1},{2,18},{18,2},{3,19},{19,3},{4,20},{20... | collective-permute-start | bytes 3244040 | tf_op jit(solution)/shard_map/ppermute | solution.py:38
  183.8 26.1 %collective-permute-start.18 = (bf16[2112,256]{1,0:T(8,128)(2,1)}, bf16[2112,256]{1,0:T(8,128)(2,1)}, u32[]{:S(2)}, u32[]{:S(2)}) collective-permute-start(bf16[2112,256]{1,0:T(8,128)(2,1)} %slice.795), channel_id=1, source_target_pairs={{0,4},{4,0},{1,5},{5,1},{2,6},{6,2},{3,7},{7,3},{8,12},{12,8},{9,1... | collective-permute-start | bytes 3244040 | tf_op jit(solution)/shard_map/ppermute | solution.py:42
  185.5 422.2 %reduce-scatter.9.cloned.1.call-start = ((), (), s32[]{:S(2)}) async-start(), calls=%async_computation.9 | async-start | bytes 2621440 | tf_op jit(solution)/shard_map/reduce_scatter | solution.py:497
  187.7 33.1 %collective-permute-start.16 = (bf16[320,1024]{1,0:T(8,128)(2,1)S(1)}, bf16[320,1024]{1,0:T(8,128)(2,1)S(1)}, u32[]{:S(2)}, u32[]{:S(2)}) collective-permute-start(bf16[320,1024]{1,0:T(8,128)(2,1)S(1)} %multiply_convert_fusion.8), channel_id=1, source_target_pairs={{0,8},{8,0},{1,9},{9,1},{2,10},{10,2},{3,11},{11,3},{4,12},{12,4},... | collective-permute-start | bytes 1966088 | tf_op jit(solution)/shard_map/ppermute | solution.py:34
  210.1 24.3 %collective-permute-start.19 = (bf16[1024,512]{1,0:T(8,128)(2,1)S(1)}, bf16[1024,512]{1,0:T(8,128)(2,1)S(1)}, u32[]{:S(2)}, u32[]{:S(2)}) collective-permute-start(bf16[1024,512]{1,0:T(8,128)(2,1)S(1)} %bitcast.464), channel_id=1, source_target_pairs={{0,16},{16,0},{1,17},{17,1},{2,18},{18,2},{3,19},{19,3},{4,20},{20... | collective-permute-start | bytes 3145736 | tf_op jit(solution)/shard_map/ppermute | solution.py:38
  211.6 24.0 %collective-permute-start.20 = (bf16[1024,512]{1,0:T(8,128)(2,1)S(1)}, bf16[1024,512]{1,0:T(8,128)(2,1)S(1)}, u32[]{:S(2)}, u32[]{:S(2)}) collective-permute-start(bf16[1024,512]{1,0:T(8,128)(2,1)S(1)} %bitcast.462), channel_id=1, source_target_pairs={{0,4},{4,0},{1,5},{5,1},{2,6},{6,2},{3,7},{7,3},{8,12},{12,8},{9,1... | collective-permute-start | bytes 3145736 | tf_op jit(solution)/shard_map/ppermute | solution.py:42
  241.6 17.9 %collective-permute-start.23 = (bf16[320,1024]{1,0:T(8,128)(2,1)S(1)}, bf16[320,1024]{1,0:T(8,128)(2,1)S(1)}, u32[]{:S(2)}, u32[]{:S(2)}) collective-permute-start(bf16[320,1024]{1,0:T(8,128)(2,1)S(1)} %multiply_convert_fusion.7), channel_id=1, source_target_pairs={{0,4},{1,5},{2,6},{3,7},{8,12},{9,13},{10,14},{11,15},{16,20},{17,... | collective-permute-start | bytes 1966088 | tf_op jit(solution)/shard_map/ppermute | solution.py:676
  270.5 51.2 %collective-permute-start.25 = (bf16[2112,512]{1,0:T(8,128)(2,1)S(1)}, bf16[2112,512]{1,0:T(8,128)(2,1)}, u32[]{:S(2)}, u32[]{:S(2)}) collective-permute-start(bf16[2112,512]{1,0:T(8,128)(2,1)S(1)} %bitcast.440), channel_id=1, source_target_pairs={{0,16},{16,0},{1,17},{17,1},{2,18},{18,2},{3,19},{19,3},{4,20},{20... | collective-permute-start | bytes 6488072 | tf_op jit(solution)/shard_map/ppermute | solution.py:38
  272.0 49.6 %collective-permute-start.26 = (bf16[2112,512]{1,0:T(8,128)(2,1)S(1)}, bf16[2112,512]{1,0:T(8,128)(2,1)}, u32[]{:S(2)}, u32[]{:S(2)}) collective-permute-start(bf16[2112,512]{1,0:T(8,128)(2,1)S(1)} %bitcast.438), channel_id=1, source_target_pairs={{0,4},{4,0},{1,5},{5,1},{2,6},{6,2},{3,7},{7,3},{8,12},{12,8},{9,1... | collective-permute-start | bytes 6488072 | tf_op jit(solution)/shard_map/ppermute | solution.py:42
  275.3 44.0 %collective-permute-start.29 = (bf16[320,256]{1,0:T(8,128)(2,1)}, bf16[320,256]{1,0:T(8,128)(2,1)S(1)}, u32[]{:S(2)}, u32[]{:S(2)}) collective-permute-start(bf16[320,256]{1,0:T(8,128)(2,1)} %get-tuple-element.369), channel_id=1, source_target_pairs={{0,2},{1,10},{2,0},{3,8},{8,3},{9,11},{10,1},{11,9},{4,6},{5,14},{... | collective-permute-start | bytes 491528 | tf_op jit(solution)/shard_map/ppermute | solution.py:433
  277.3 42.0 %collective-permute-start.28 = (bf16[320,256]{1,0:T(8,128)(2,1)}, bf16[320,256]{1,0:T(8,128)(2,1)}, u32[]{:S(2)}, u32[]{:S(2)}) collective-permute-start(bf16[320,256]{1,0:T(8,128)(2,1)} %get-tuple-element.370), channel_id=1, source_target_pairs={{0,8},{1,0},{2,10},{3,2},{8,9},{9,1},{10,11},{11,3},{4,12},{5,4},{... | collective-permute-start | bytes 491528 | tf_op jit(solution)/shard_map/ppermute | solution.py:433
  282.5 36.8 %collective-permute-start.27 = (bf16[320,256]{1,0:T(8,128)(2,1)S(1)}, bf16[320,256]{1,0:T(8,128)(2,1)}, u32[]{:S(2)}, u32[]{:S(2)}) collective-permute-start(bf16[320,256]{1,0:T(8,128)(2,1)S(1)} %get-tuple-element.367), channel_id=1, source_target_pairs={{0,0},{1,8},{2,2},{3,10},{8,1},{9,9},{10,3},{11,11},{4,4},{5,12},{... | collective-permute-start | bytes 491528 | tf_op jit(solution)/shard_map/ppermute | solution.py:433
  358.8 16.8 %collective-permute-start.39 = (bf16[320,1024]{1,0:T(8,128)(2,1)S(1)}, bf16[320,1024]{1,0:T(8,128)(2,1)S(1)}, u32[]{:S(2)}, u32[]{:S(2)}) collective-permute-start(bf16[320,1024]{1,0:T(8,128)(2,1)S(1)} %slice.1096), channel_id=1, source_target_pairs={{0,8},{8,0},{1,9},{9,1},{2,10},{10,2},{3,11},{11,3},{4,12},{12,4},... | collective-permute-start | bytes 1966088 | tf_op jit(solution)/shard_map/ppermute | solution.py:34
  368.6 59.0 %collective-permute-start.42 = (bf16[2112,512]{1,0:T(8,128)(2,1)}, bf16[2112,512]{1,0:T(8,128)(2,1)}, u32[]{:S(2)}, u32[]{:S(2)}) collective-permute-start(bf16[2112,512]{1,0:T(8,128)(2,1)} %bitcast.86), channel_id=1, source_target_pairs={{0,16},{16,0},{1,17},{17,1},{2,18},{18,2},{3,19},{19,3},{4,20},{20... | collective-permute-start | bytes 6488072 | tf_op jit(solution)/shard_map/ppermute | solution.py:38
  372.3 55.4 %collective-permute-start.43 = (bf16[2112,512]{1,0:T(8,128)(2,1)}, bf16[2112,512]{1,0:T(8,128)(2,1)}, u32[]{:S(2)}, u32[]{:S(2)}) collective-permute-start(bf16[2112,512]{1,0:T(8,128)(2,1)} %bitcast.90), channel_id=1, source_target_pairs={{0,4},{4,0},{1,5},{5,1},{2,6},{6,2},{3,7},{7,3},{8,12},{12,8},{9,1... | collective-permute-start | bytes 6488072 | tf_op jit(solution)/shard_map/ppermute | solution.py:42
  380.9 17.8 %collective-permute-start.40 = (bf16[320,1024]{1,0:T(8,128)(2,1)S(1)}, bf16[320,1024]{1,0:T(8,128)(2,1)S(1)}, u32[]{:S(2)}, u32[]{:S(2)}) collective-permute-start(bf16[320,1024]{1,0:T(8,128)(2,1)S(1)} %get-tuple-element.240), channel_id=1, source_target_pairs={{0,8},{8,0},{1,9},{9,1},{2,10},{10,2},{3,11},{11,3},{4,12},{12,4},... | collective-permute-start | bytes 1966088 | tf_op jit(solution)/shard_map/ppermute | solution.py:34
  434.8 20.5 %collective-permute-start.41 = (bf16[320,1024]{1,0:T(8,128)(2,1)S(1)}, bf16[320,1024]{1,0:T(8,128)(2,1)S(1)}, u32[]{:S(2)}, u32[]{:S(2)}) collective-permute-start(bf16[320,1024]{1,0:T(8,128)(2,1)S(1)} %slice.1095), channel_id=1, source_target_pairs={{0,8},{8,0},{1,9},{9,1},{2,10},{10,2},{3,11},{11,3},{4,12},{12,4},... | collective-permute-start | bytes 1966088 | tf_op jit(solution)/shard_map/ppermute | solution.py:34
  436.5 18.8 %collective-permute-start.45 = (bf16[320,1024]{1,0:T(8,128)(2,1)S(1)}, bf16[320,1024]{1,0:T(8,128)(2,1)S(1)}, u32[]{:S(2)}, u32[]{:S(2)}) collective-permute-start(bf16[320,1024]{1,0:T(8,128)(2,1)S(1)} %fusion.53), channel_id=1, source_target_pairs={{4,0},{5,1},{6,2},{7,3},{12,8},{13,9},{14,10},{15,11},{20,16},{21,... | collective-permute-start | bytes 1966088 | tf_op jit(solution)/shard_map/ppermute | solution.py:723
  441.4 42.6 %collective-permute-start.49 = (bf16[1024,512]{1,0:T(8,128)(2,1)S(1)}, bf16[1024,512]{1,0:T(8,128)(2,1)S(1)}, u32[]{:S(2)}, u32[]{:S(2)}) collective-permute-start(bf16[1024,512]{1,0:T(8,128)(2,1)S(1)} %concatenate.577), channel_id=1, source_target_pairs={{0,16},{16,0},{1,17},{17,1},{2,18},{18,2},{3,19},{19,3},{4,20},{20... | collective-permute-start | bytes 3145736 | tf_op jit(solution)/shard_map/ppermute | solution.py:38
  458.4 25.6 %collective-permute-start.50 = (bf16[1024,512]{1,0:T(8,128)(2,1)S(1)}, bf16[1024,512]{1,0:T(8,128)(2,1)S(1)}, u32[]{:S(2)}, u32[]{:S(2)}) collective-permute-start(bf16[1024,512]{1,0:T(8,128)(2,1)S(1)} %pad_maximum_fusion.30), channel_id=1, source_target_pairs={{0,4},{4,0},{1,5},{5,1},{2,6},{6,2},{3,7},{7,3},{8,12},{12,8},{9,1... | collective-permute-start | bytes 3145736 | tf_op jit(solution)/shard_map/ppermute | solution.py:42
  471.8 26.7 %collective-permute-start.47 = (bf16[320,1024]{1,0:T(8,128)(2,1)}, bf16[320,1024]{1,0:T(8,128)(2,1)}, u32[]{:S(2)}, u32[]{:S(2)}) collective-permute-start(bf16[320,1024]{1,0:T(8,128)(2,1)} %slice.1093), channel_id=1, source_target_pairs={{0,8},{8,0},{1,9},{9,1},{2,10},{10,2},{3,11},{11,3},{4,12},{12,4},... | collective-permute-start | bytes 1966088 | tf_op jit(solution)/shard_map/ppermute | solution.py:34
  487.4 145.4 %reduce-scatter.7.cloned.1.call-start = ((), (), s32[]{:S(2)}) async-start(), calls=%async_computation.8 | async-start | bytes 5406720 | tf_op jit(solution)/shard_map/reduce_scatter | solution.py:497
  490.9 49.9 %collective-permute-start.52 = (bf16[2112,512]{1,0:T(8,128)(2,1)}, bf16[2112,512]{1,0:T(8,128)(2,1)}, u32[]{:S(2)}, u32[]{:S(2)}) collective-permute-start(bf16[2112,512]{1,0:T(8,128)(2,1)} %pad_maximum_fusion.8), channel_id=1, source_target_pairs={{0,16},{16,0},{1,17},{17,1},{2,18},{18,2},{3,19},{19,3},{4,20},{20... | collective-permute-start | bytes 6488072 | tf_op jit(solution)/shard_map/ppermute | solution.py:38
  495.1 49.5 %collective-permute-start.53 = (bf16[2112,512]{1,0:T(8,128)(2,1)}, bf16[2112,512]{1,0:T(8,128)(2,1)}, u32[]{:S(2)}, u32[]{:S(2)}) collective-permute-start(bf16[2112,512]{1,0:T(8,128)(2,1)} %fusion.31), channel_id=1, source_target_pairs={{0,4},{4,0},{1,5},{5,1},{2,6},{6,2},{3,7},{7,3},{8,12},{12,8},{9,1... | collective-permute-start | bytes 6488072 | tf_op jit(solution)/shard_map/ppermute | solution.py:42
  507.7 167.7 %reduce-scatter.5.cloned.1.call-start = ((), (), s32[]{:S(2)}) async-start(), calls=%async_computation.7 | async-start | bytes 2703360 | tf_op jit(solution)/shard_map/reduce_scatter | solution.py:497
  539.5 33.2 %collective-permute-start.51 = (bf16[320,1024]{1,0:T(8,128)(2,1)S(1)}, bf16[320,1024]{1,0:T(8,128)(2,1)S(1)}, u32[]{:S(2)}, u32[]{:S(2)}) collective-permute-start(bf16[320,1024]{1,0:T(8,128)(2,1)S(1)} %slice.1092), channel_id=1, source_target_pairs={{0,8},{8,0},{1,9},{9,1},{2,10},{10,2},{3,11},{11,3},{4,12},{12,4},... | collective-permute-start | bytes 1966088 | tf_op jit(solution)/shard_map/ppermute | solution.py:34
  553.1 26.8 %collective-permute-start.57 = (bf16[2112,256]{1,0:T(8,128)(2,1)S(1)}, bf16[2112,256]{1,0:T(8,128)(2,1)S(1)}, u32[]{:S(2)}, u32[]{:S(2)}) collective-permute-start(bf16[2112,256]{1,0:T(8,128)(2,1)S(1)} %slice.865), channel_id=1, source_target_pairs={{0,16},{16,0},{1,17},{17,1},{2,18},{18,2},{3,19},{19,3},{4,20},{20... | collective-permute-start | bytes 3244040 | tf_op jit(solution)/shard_map/ppermute | solution.py:38
  554.1 18.6 %collective-permute-start.55 = (bf16[320,1024]{1,0:T(8,128)(2,1)S(1)}, bf16[320,1024]{1,0:T(8,128)(2,1)S(1)}, u32[]{:S(2)}, u32[]{:S(2)}) collective-permute-start(bf16[320,1024]{1,0:T(8,128)(2,1)S(1)} %fusion.51), channel_id=1, source_target_pairs={{4,0},{5,1},{6,2},{7,3},{12,8},{13,9},{14,10},{15,11},{20,16},{21,... | collective-permute-start | bytes 1966088 | tf_op jit(solution)/shard_map/ppermute | solution.py:723
  560.0 49.9 %collective-permute-start.62 = (bf16[1024,512]{1,0:T(8,128)(2,1)}, bf16[1024,512]{1,0:T(8,128)(2,1)}, u32[]{:S(2)}, u32[]{:S(2)}) collective-permute-start(bf16[1024,512]{1,0:T(8,128)(2,1)} %concatenate.584), channel_id=1, source_target_pairs={{0,16},{16,0},{1,17},{17,1},{2,18},{18,2},{3,19},{19,3},{4,20},{20... | collective-permute-start | bytes 3145736 | tf_op jit(solution)/shard_map/ppermute | solution.py:38
  572.6 26.8 %collective-permute-start.56 = (bf16[2112,256]{1,0:T(8,128)(2,1)S(1)}, bf16[2112,256]{1,0:T(8,128)(2,1)S(1)}, u32[]{:S(2)}, u32[]{:S(2)}) collective-permute-start(bf16[2112,256]{1,0:T(8,128)(2,1)S(1)} %slice.864), channel_id=1, source_target_pairs={{0,4},{4,0},{1,5},{5,1},{2,6},{6,2},{3,7},{7,3},{8,12},{12,8},{9,1... | collective-permute-start | bytes 3244040 | tf_op jit(solution)/shard_map/ppermute | solution.py:42
  575.9 45.6 %collective-permute-start.63 = (bf16[1088,512]{1,0:T(8,128)(2,1)}, bf16[1088,512]{1,0:T(8,128)(2,1)}, u32[]{:S(2)}, u32[]{:S(2)}) collective-permute-start(bf16[1088,512]{1,0:T(8,128)(2,1)} %pad_maximum_fusion.23), channel_id=1, source_target_pairs={{0,4},{4,0},{1,5},{5,1},{2,6},{6,2},{3,7},{7,3},{8,12},{12,8},{9,1... | collective-permute-start | bytes 3342344 | tf_op jit(solution)/shard_map/ppermute | solution.py:42
  604.4 86.4 %collective-permute-start.61 = (bf16[320,256]{1,0:T(8,128)(2,1)}, bf16[320,256]{1,0:T(8,128)(2,1)}, u32[]{:S(2)}, u32[]{:S(2)}) collective-permute-start(bf16[320,256]{1,0:T(8,128)(2,1)} %get-tuple-element.336), channel_id=1, source_target_pairs={{10,0},{2,1},{8,2},{0,3},{11,8},{3,9},{9,10},{1,11},{14,4},{6,5},{... | collective-permute-start | bytes 491528 | tf_op jit(solution)/shard_map/ppermute | solution.py:359
  606.0 84.8 %collective-permute-start.60 = (bf16[320,256]{1,0:T(8,128)(2,1)}, bf16[320,256]{1,0:T(8,128)(2,1)}, u32[]{:S(2)}, u32[]{:S(2)}) collective-permute-start(bf16[320,256]{1,0:T(8,128)(2,1)} %get-tuple-element.337), channel_id=1, source_target_pairs={{2,0},{10,1},{0,2},{8,3},{3,8},{11,9},{1,10},{9,11},{6,4},{14,5},{... | collective-permute-start | bytes 491528 | tf_op jit(solution)/shard_map/ppermute | solution.py:359
  607.5 83.3 %collective-permute-start.59 = (bf16[320,256]{1,0:T(8,128)(2,1)}, bf16[320,256]{1,0:T(8,128)(2,1)}, u32[]{:S(2)}, u32[]{:S(2)}) collective-permute-start(bf16[320,256]{1,0:T(8,128)(2,1)} %get-tuple-element.338), channel_id=1, source_target_pairs={{8,0},{0,1},{10,2},{2,3},{9,8},{1,9},{11,10},{3,11},{12,4},{4,5},{... | collective-permute-start | bytes 491528 | tf_op jit(solution)/shard_map/ppermute | solution.py:359
  607.6 98.6 %reduce-scatter.11.cloned.1.call-start = ((), (), s32[]{:S(2)}) async-start(), calls=%async_computation.10 | async-start | bytes 1351680 | tf_op jit(solution)/shard_map/reduce_scatter | solution.py:497
  609.9 18.9 %collective-permute-start.72 = (bf16[256,512]{1,0:T(8,128)(2,1)S(1)}, bf16[256,512]{1,0:T(8,128)(2,1)S(1)}, u32[]{:S(2)}, u32[]{:S(2)}) collective-permute-start(bf16[256,512]{1,0:T(8,128)(2,1)S(1)} %maximum_select_fusion.15), channel_id=1, source_target_pairs={{0,16},{16,0},{1,17},{17,1},{2,18},{18,2},{3,19},{19,3},{4,20},{20... | collective-permute-start | bytes 786440 | tf_op jit(solution)/shard_map/ppermute | solution.py:38
  665.9 24.8 %collective-permute-start.58 = (bf16[320,256]{1,0:T(8,128)(2,1)}, bf16[320,256]{1,0:T(8,128)(2,1)S(1)}, u32[]{:S(2)}, u32[]{:S(2)}) collective-permute-start(bf16[320,256]{1,0:T(8,128)(2,1)} %get-tuple-element.335), channel_id=1, source_target_pairs={{0,0},{8,1},{2,2},{10,3},{1,8},{9,9},{3,10},{11,11},{4,4},{12,5},{... | collective-permute-start | bytes 491528 | tf_op jit(solution)/shard_map/ppermute | solution.py:359
  (199 other events, 1923.3 us)
Sparse Core Ops, SparseCore 0:
  58.1 48.2 all-gather.3
  108.5 49.7 all-gather.5
  185.7 82.1 all-gather.7
  487.6 42.7 reduce-scatter.8
  532.7 80.6 reduce-scatter.6
  615.6 50.3 reduce-scatter.4
  680.3 25.9 reduce-scatter.10
